TPU v7x, 32 devices: a whole 2x2x4 slice. The times are simulated.
32 devices in a mesh: batch: 8 (over z, x), narrow: 4 (over y, core).
Axes of the slice: x: 2, y: 2, z: 4, core: 2. Of those that a mesh axis runs over, the one named last changes fastest.
Arguments:
- inputs: bfloat16 [128, 16, 16, 1024], P('batch', 'narrow'), may hold values from -6 to 6
- image_class: int32 [128], P('batch'), may hold values from 0 to 2
- weight_reduce: bfloat16 [1024, 256], replicated, may hold values from -0.1875 to 0.1875
- gain_reduce: float32 [256], replicated, may hold values from 0.5 to 1.5
- shift_reduce: float32 [256], replicated, may hold values from -3 to 3
- weight_split: bfloat16 [3, 3, 2, 128, 256], replicated, may hold values from -0.1875 to 0.1875
- gain_split: float32 [512], replicated, may hold values from 0.5 to 1.5
- shift_split: float32 [512], replicated, may hold values from -3 to 3
- weight_squeeze: float32 [256, 128], replicated, may hold values from -0.375 to 0.375
- gain_squeeze: float32 [128], replicated, may hold values from 0.5 to 1.5
- shift_squeeze: float32 [128], replicated, may hold values from -3 to 3
- weight_excite: float32 [128, 512], replicated, may hold values from -0.5 to 0.5
- bias_excite: float32 [512], replicated, may hold values from -4 to 4
- weight_expand: bfloat16 [256, 1024], replicated, may hold values from -0.375 to 0.375
- gain_expand: float32 [1024], replicated, may hold values from 0.5 to 1.5
- shift_expand: float32 [1024], replicated, may hold values from -3 to 3
- cotangent: bfloat16 [128, 16, 16, 1024], P('batch', 'narrow'), may hold values from -6 to 6
Outputs:
- block_output: bfloat16 [128, 16, 16, 1024], P('batch', 'narrow')
- input_grad: bfloat16 [128, 16, 16, 1024], P('batch', 'narrow')
- grad_weight_reduce: float32 [1024, 256], replicated
- grad_gain_reduce: float32 [256], replicated
- grad_shift_reduce: float32 [256], replicated
- grad_weight_split: float32 [3, 3, 2, 128, 256], replicated
- grad_gain_split: float32 [512], replicated
- grad_shift_split: float32 [512], replicated
- grad_weight_squeeze: float32 [256, 128], replicated
- grad_gain_squeeze: float32 [128], replicated
- grad_shift_squeeze: float32 [128], replicated
- grad_weight_excite: float32 [128, 512], replicated
- grad_bias_excite: float32 [512], replicated
- grad_weight_expand: float32 [256, 1024], replicated
- grad_gain_expand: float32 [1024], replicated
- grad_shift_expand: float32 [1024], replicated
Inputs may be any that keep to these rules, and one draw needn't show every extreme that they name: `image_class`: an image's side is 12 + 2 times its class; rows and columns from that side up to 16 lie outside it.
All inputs are finite; a program needn't handle non-finite values.
Results may differ from a plain program's by a relative error of at most 0.011.
Values may be sent and summed in bfloat16 or wider, within the bound.
No kernel may reach another device: no remote copies, remote signals or barrier semaphores. Data moves between devices by JAX's collectives and lax.ppermute only.
A program may use at most 128 MiB of HBM per device.

v0:
```python
import jax
import jax.numpy as jnp
from jax import lax
from jax.sharding import PartitionSpec as P

EPSILON = 1e-05
HIGHEST = lax.Precision.HIGHEST


def extended(block, sides, width):
    for axis, dim in sides:
        count = lax.axis_size(axis)
        forward = [(i, i + 1) for i in range(count - 1)]
        backward = [(target, source) for source, target in forward]
        low = lax.ppermute(
            lax.slice_in_dim(block, block.shape[dim] - width, None, axis=dim), axis, forward
        )
        high = lax.ppermute(lax.slice_in_dim(block, 0, width, axis=dim), axis, backward)
        block = jnp.concatenate([low, block, high], axis=dim)
    return block


def silu_slope(values):
    sigmoid_part = jax.nn.sigmoid(values)
    return sigmoid_part * (1.0 + values * (1.0 - sigmoid_part))


def side_mask(classes, first_row, row_count, col_count):
    image_side = 12 + 2 * classes
    row_ids = first_row + jnp.arange(row_count, dtype=jnp.int32)
    col_ids = jnp.arange(col_count, dtype=jnp.int32)
    row_inside = (row_ids[None, :] < image_side[:, None]).astype(jnp.float32)
    col_inside = (col_ids[None, :] < image_side[:, None]).astype(jnp.float32)
    return (row_inside[:, :, None] * col_inside[:, None, :])[..., None]


def norm_apply(values, totals, squares, counted, gains, shifts):
    center = totals / counted
    inv_std = lax.rsqrt(squares / counted - center * center + EPSILON)
    normed = (values - center) * inv_std
    return (normed, inv_std, normed * gains + shifts)


def norm_back(grad_z, normed, inv_std, gains, shift_sum, gain_sum, counted):
    return gains * inv_std * (grad_z - shift_sum / counted - normed * gain_sum / counted)


def conv_forward(padded, kernel, row_count, col_count):
    blocks = padded.shape[0]
    groups = kernel.shape[2]
    group_width = kernel.shape[3]
    accum = None
    for row_off in range(3):
        for col_off in range(3):
            window = padded[
                :, row_off : row_off + row_count, col_off : col_off + col_count, :
            ].reshape(blocks * row_count * col_count, groups, group_width)
            partial_value = jnp.einsum(
                "pgc,gco->pgo", window, kernel[row_off, col_off], preferred_element_type=jnp.float32
            )
            accum = partial_value if accum is None else accum + partial_value
    return accum.reshape(blocks * row_count * col_count, -1)


def conv_weight_grad(padded, grad_out, row_count, col_count, groups):
    blocks = padded.shape[0]
    group_width = padded.shape[3] // groups
    pieces = []
    for row_off in range(3):
        for col_off in range(3):
            window = padded[
                :, row_off : row_off + row_count, col_off : col_off + col_count, :
            ].reshape(blocks * row_count * col_count, groups, group_width)
            pieces.append(
                jnp.einsum("pgc,pgo->gco", window, grad_out, preferred_element_type=jnp.float32)
            )
    stacked = jnp.stack(pieces)
    return stacked.reshape(3, 3, groups, group_width, -1)


def conv_input_grad(padded_grad, kernel, row_count, col_count):
    blocks = padded_grad.shape[0]
    groups = kernel.shape[2]
    out_width = kernel.shape[4]
    accum = None
    for row_off in range(3):
        for col_off in range(3):
            window = padded_grad[
                :, 2 - row_off : 2 - row_off + row_count, 2 - col_off : 2 - col_off + col_count, :
            ].reshape(blocks * row_count * col_count, groups, out_width)
            partial_value = jnp.einsum(
                "pgo,gco->pgc", window, kernel[row_off, col_off], preferred_element_type=jnp.float32
            )
            accum = partial_value if accum is None else accum + partial_value
    return accum.reshape(blocks * row_count * col_count, -1)


def body(
    inputs,
    image_class,
    weight_reduce,
    gain_reduce,
    shift_reduce,
    weight_split,
    gain_split,
    shift_split,
    weight_squeeze,
    gain_squeeze,
    shift_squeeze,
    weight_excite,
    bias_excite,
    weight_expand,
    gain_expand,
    shift_expand,
    cotangent,
):
    blocks, row_count, col_count, channels = inputs.shape
    bottleneck = weight_reduce.shape[1]
    groups = weight_split.shape[2]
    parts = lax.axis_size("narrow")
    per_part = blocks // parts
    full_rows = row_count * parts
    pixels = blocks * row_count * col_count
    valid = side_mask(image_class, lax.axis_index("narrow") * row_count, row_count, col_count)
    flat_valid = valid.reshape(pixels, 1)
    masked = (inputs * valid.astype(jnp.bfloat16)).reshape(pixels, channels)
    own_class = lax.dynamic_slice_in_dim(image_class, lax.axis_index("narrow") * per_part, per_part)
    image_valid = side_mask(own_class, 0, full_rows, col_count)
    own_side = (12 + 2 * own_class).astype(jnp.float32)
    image_area = own_side * own_side
    pre_reduce = jnp.dot(masked, weight_reduce, preferred_element_type=jnp.float32)
    sum_reduce, square_reduce, pixel_count = lax.psum(
        (
            jnp.sum(pre_reduce * flat_valid, 0),
            jnp.sum(pre_reduce * pre_reduce * flat_valid, 0),
            jnp.sum(flat_valid),
        ),
        ("batch", "narrow"),
    )
    norm_reduce, inv_reduce, z_reduce = norm_apply(
        pre_reduce, sum_reduce, square_reduce, pixel_count, gain_reduce, shift_reduce
    )
    hidden_reduce = (
        (jax.nn.silu(z_reduce) * flat_valid)
        .astype(jnp.bfloat16)
        .reshape(blocks, row_count, col_count, bottleneck)
    )
    padded_reduce = extended(hidden_reduce, (("narrow", 1),), 1)
    padded_reduce = jnp.pad(padded_reduce, ((0, 0), (0, 0), (1, 1), (0, 0)))
    pre_split = conv_forward(padded_reduce, weight_split, row_count, col_count)
    sum_split, square_split = lax.psum(
        (jnp.sum(pre_split * flat_valid, 0), jnp.sum(pre_split * pre_split * flat_valid, 0)),
        ("batch", "narrow"),
    )
    norm_split, inv_split, z_split = norm_apply(
        pre_split, sum_split, square_split, pixel_count, gain_split, shift_split
    )
    hidden_split = (
        (jax.nn.silu(z_split) * flat_valid)
        .astype(jnp.bfloat16)
        .reshape(blocks, row_count, col_count, groups * bottleneck)
    )
    image_split = lax.all_to_all(hidden_split, "narrow", split_axis=0, concat_axis=1, tiled=True)
    first_half = image_split[..., :bottleneck]
    second_half = image_split[..., bottleneck:]
    summed = jnp.sum(image_split, axis=(1, 2), dtype=jnp.float32)
    pooled = (summed[:, :bottleneck] + summed[:, bottleneck:]) / image_area[:, None]
    pre_squeeze = jnp.dot(pooled, weight_squeeze, precision=HIGHEST)
    sum_squeeze, square_squeeze = lax.psum(
        (jnp.sum(pre_squeeze, 0), jnp.sum(pre_squeeze * pre_squeeze, 0)), ("batch", "narrow")
    )
    image_count = blocks * lax.axis_size("batch")
    norm_squeeze, inv_squeeze, z_squeeze = norm_apply(
        pre_squeeze, sum_squeeze, square_squeeze, image_count, gain_squeeze, shift_squeeze
    )
    hidden_squeeze = jax.nn.silu(z_squeeze)
    logits = jnp.dot(hidden_squeeze, weight_excite, precision=HIGHEST) + bias_excite
    logit_first = logits[:, :bottleneck]
    logit_second = logits[:, bottleneck:]
    ceiling = jnp.maximum(logit_first, logit_second)
    exp_first = jnp.exp(logit_first - ceiling)
    exp_second = jnp.exp(logit_second - ceiling)
    att_first = exp_first / (exp_first + exp_second)
    att_second = exp_second / (exp_first + exp_second)
    mixture = (
        att_first[:, None, None, :] * first_half + att_second[:, None, None, :] * second_half
    ).astype(jnp.bfloat16)
    flat_mix = mixture.reshape(-1, bottleneck)
    image_expand = (
        jnp.dot(flat_mix, weight_expand, preferred_element_type=jnp.float32)
        .astype(jnp.bfloat16)
        .reshape(per_part, full_rows, col_count, channels)
    )
    pre_expand = lax.all_to_all(
        image_expand, "narrow", split_axis=1, concat_axis=0, tiled=True
    ).reshape(pixels, channels)
    expand_values = pre_expand.astype(jnp.float32)
    sum_expand, square_expand = lax.psum(
        (
            jnp.sum(expand_values * flat_valid, 0),
            jnp.sum(expand_values * expand_values * flat_valid, 0),
        ),
        ("batch", "narrow"),
    )
    norm_expand, inv_expand, z_expand = norm_apply(
        expand_values, sum_expand, square_expand, pixel_count, gain_expand, shift_expand
    )
    residual = z_expand + masked
    block_output = (
        (jax.nn.silu(residual) * flat_valid)
        .astype(jnp.bfloat16)
        .reshape(blocks, row_count, col_count, channels)
    )
    grad_residual = cotangent.reshape(pixels, channels) * flat_valid * silu_slope(residual)
    shift_expand_grad, gain_expand_grad = lax.psum(
        (jnp.sum(grad_residual, 0), jnp.sum(grad_residual * norm_expand, 0)), ("batch", "narrow")
    )
    grad_expand = (
        flat_valid
        * norm_back(
            grad_residual,
            norm_expand,
            inv_expand,
            gain_expand,
            shift_expand_grad,
            gain_expand_grad,
            pixel_count,
        )
    ).astype(jnp.bfloat16)
    grad_images = lax.all_to_all(
        grad_expand.reshape(blocks, row_count, col_count, channels),
        "narrow",
        split_axis=0,
        concat_axis=1,
        tiled=True,
    ).reshape(-1, channels)
    expand_part = jnp.einsum("pc,pd->cd", flat_mix, grad_images, preferred_element_type=jnp.float32)
    grad_mixture = (
        jnp.einsum("pd,cd->pc", grad_images, weight_expand, preferred_element_type=jnp.float32)
        .astype(jnp.bfloat16)
        .reshape(per_part, full_rows, col_count, bottleneck)
    )
    grad_att_first = jnp.einsum(
        "ihwc,ihwc->ic", grad_mixture, first_half, preferred_element_type=jnp.float32
    )
    grad_att_second = jnp.einsum(
        "ihwc,ihwc->ic", grad_mixture, second_half, preferred_element_type=jnp.float32
    )
    inner = att_first * grad_att_first + att_second * grad_att_second
    grad_logits = jnp.concatenate(
        [att_first * (grad_att_first - inner), att_second * (grad_att_second - inner)], axis=1
    )
    bias_part = jnp.sum(grad_logits, 0)
    excite_part = jnp.einsum("ik,ic->kc", hidden_squeeze, grad_logits, precision=HIGHEST)
    grad_hidden_squeeze = jnp.einsum("ic,kc->ik", grad_logits, weight_excite, precision=HIGHEST)
    grad_z_squeeze = grad_hidden_squeeze * silu_slope(z_squeeze)
    shift_squeeze_grad, gain_squeeze_grad = lax.psum(
        (jnp.sum(grad_z_squeeze, 0), jnp.sum(grad_z_squeeze * norm_squeeze, 0)), ("batch", "narrow")
    )
    grad_pre_squeeze = norm_back(
        grad_z_squeeze,
        norm_squeeze,
        inv_squeeze,
        gain_squeeze,
        shift_squeeze_grad,
        gain_squeeze_grad,
        image_count,
    )
    squeeze_part = jnp.einsum("ic,ik->ck", pooled, grad_pre_squeeze, precision=HIGHEST)
    grad_pooled = (
        jnp.einsum("ik,ck->ic", grad_pre_squeeze, weight_squeeze, precision=HIGHEST)
        / image_area[:, None]
    )
    spread = grad_pooled[:, None, None, :] * image_valid
    grad_split_image = jnp.concatenate(
        [
            grad_mixture * att_first[:, None, None, :] + spread,
            grad_mixture * att_second[:, None, None, :] + spread,
        ],
        axis=-1,
    ).astype(jnp.bfloat16)
    grad_split_rows = lax.all_to_all(
        grad_split_image, "narrow", split_axis=1, concat_axis=0, tiled=True
    ).reshape(pixels, groups * bottleneck)
    grad_z_split = grad_split_rows * flat_valid * silu_slope(z_split)
    shift_split_grad, gain_split_grad = lax.psum(
        (jnp.sum(grad_z_split, 0), jnp.sum(grad_z_split * norm_split, 0)), ("batch", "narrow")
    )
    grad_split = (
        flat_valid
        * norm_back(
            grad_z_split,
            norm_split,
            inv_split,
            gain_split,
            shift_split_grad,
            gain_split_grad,
            pixel_count,
        )
    ).astype(jnp.bfloat16)
    split_part = conv_weight_grad(
        padded_reduce, grad_split.reshape(-1, groups, bottleneck), row_count, col_count, groups
    )
    padded_grad = extended(
        grad_split.reshape(blocks, row_count, col_count, groups * bottleneck), (("narrow", 1),), 1
    )
    padded_grad = jnp.pad(padded_grad, ((0, 0), (0, 0), (1, 1), (0, 0)))
    grad_hidden_reduce = conv_input_grad(padded_grad, weight_split, row_count, col_count)
    grad_z_reduce = grad_hidden_reduce * flat_valid * silu_slope(z_reduce)
    shift_reduce_grad, gain_reduce_grad = lax.psum(
        (jnp.sum(grad_z_reduce, 0), jnp.sum(grad_z_reduce * norm_reduce, 0)), ("batch", "narrow")
    )
    grad_reduce = (
        flat_valid
        * norm_back(
            grad_z_reduce,
            norm_reduce,
            inv_reduce,
            gain_reduce,
            shift_reduce_grad,
            gain_reduce_grad,
            pixel_count,
        )
    ).astype(jnp.bfloat16)
    reduce_part = jnp.einsum("pc,pd->cd", masked, grad_reduce, preferred_element_type=jnp.float32)
    grad_input = (
        jnp.einsum("pd,cd->pc", grad_reduce, weight_reduce, preferred_element_type=jnp.float32)
        + grad_residual
    )
    input_grad = (
        (grad_input * flat_valid)
        .astype(jnp.bfloat16)
        .reshape(blocks, row_count, col_count, channels)
    )
    reduce_total, split_total, squeeze_total, excite_total, bias_total, expand_total = lax.psum(
        (reduce_part, split_part, squeeze_part, excite_part, bias_part, expand_part),
        ("batch", "narrow"),
    )
    return (
        block_output,
        input_grad,
        reduce_total,
        gain_reduce_grad,
        shift_reduce_grad,
        split_total,
        gain_split_grad,
        shift_split_grad,
        squeeze_total,
        gain_squeeze_grad,
        shift_squeeze_grad,
        excite_total,
        bias_total,
        expand_total,
        gain_expand_grad,
        shift_expand_grad,
    )


def solution(mesh):
    return jax.shard_map(
        body,
        mesh=mesh,
        in_specs=(
            P("batch", "narrow", None, None),
            P("batch"),
            P(),
            P(),
            P(),
            P(),
            P(),
            P(),
            P(),
            P(),
            P(),
            P(),
            P(),
            P(),
            P(),
            P(),
            P("batch", "narrow", None, None),
        ),
        out_specs=(
            P("batch", "narrow", None, None),
            P("batch", "narrow", None, None),
            P(),
            P(),
            P(),
            P(),
            P(),
            P(),
            P(),
            P(),
            P(),
            P(),
            P(),
            P(),
            P(),
            P(),
        ),
        check_vma=False,
    )
```

profile of v0, /device:TPU:0, one launch (start us, length us, event | category | flops | bytes accessed | tf_op | source)
XLA Modules:
  0.0 761.8 jit_solution(4644260774192874272)
XLA Ops:
  12.0 42.2 %all-reduce.9 = (f32[256]{0:T(256)S(1)}, f32[]{:T(128)}, f32[256]{0:T(256)S(1)}) all-reduce(f32[256]{0:T(256)S(1)} %get-tuple-element.27, f32[]{:T(128)} %get-tuple-element.95, f32[256]{0:T(256)S(1)} %get-tuple-element.26), channel_id=1, replica_groups=mesh['batch'=8,'narrow'=4] {'batch','narrow'}, use_global_device_ids=true, to_apply=%region_1.0 | all-reduce | flops 513 | bytes 4104 | tf_op jit(solution)/shard_map/psum | solution.py:132
  59.0 2.9 fusion.75
  63.8 2.9 fusion.84
  71.9 2.9 fusion.64
  77.0 2.8 fusion.69
  83.1 2.8 fusion.72
  89.2 2.9 fusion.78
  94.4 2.9 fusion.81
  98.2 2.1 copy.149
  101.9 6.0 multiply_reduce_fusion.3
  109.4 2.9 copy.125
  112.3 3.0 reshape.623
  115.3 42.2 %all-reduce.8 = (f32[512]{0:T(512)S(1)}, f32[512]{0:T(512)S(1)}) all-reduce(f32[512]{0:T(512)S(1)} %bitcast.296, f32[512]{0:T(512)S(1)} %bitcast.295), channel_id=1, replica_groups=mesh['batch'=8,'narrow'=4] {'batch','narrow'}, use_global_device_ids=true, to_apply=%region_9.10 | all-reduce | flops 1024 | bytes 8192 | tf_op jit(solution)/shard_map/psum | solution.py:151
  160.4 4.2 all-to-all-start
  165.3 13.9 %all-to-all-done = bf16[16,4,16,512]{3,2,1,0:T(8,128)(2,1)} async-done(((bf16[16,4,16,512]{3,2,1,0:T(8,128)(2,1)}), bf16[16,4,16,512]{3,2,1,0:T(8,128)(2,1)}, u32[]{:S(2)}, u32[]{:S(2)}) %all-to-all-start) | async-done | bytes 1048608 | tf_op jit(solution)/shard_map/all_to_all | solution.py:163
  182.6 38.9 %all-reduce.7 = (f32[128]{0:T(128)S(1)}, f32[128]{0:T(128)S(1)}) all-reduce(f32[128]{0:T(128)S(1)} %get-tuple-element.33, f32[128]{0:T(128)S(1)} %get-tuple-element.32), channel_id=1, replica_groups=mesh['batch'=8,'narrow'=4] {'batch','narrow'}, use_global_device_ids=true, to_apply=%region_14.15 | all-reduce | flops 256 | bytes 2048 | tf_op jit(solution)/shard_map/psum | solution.py:169
  225.5 3.6 all-to-all-start.1
  229.5 25.3 %all-to-all-done.1 = bf16[4,16,16,1024]{3,2,0,1:T(8,128)(2,1)S(1)} async-done(((bf16[4,16,16,1024]{3,2,0,1:T(8,128)(2,1)}), bf16[4,16,16,1024]{3,2,0,1:T(8,128)(2,1)S(1)}, u32[]{:S(2)}, u32[]{:S(2)}) %all-to-all-start.1) | async-done | bytes 2097184 | tf_op jit(solution)/shard_map/all_to_all | solution.py:194
  256.1 40.0 %all-reduce.6 = (f32[1024]{0:T(1024)S(1)}, f32[1024]{0:T(1024)S(1)}) all-reduce(f32[1024]{0:T(1024)S(1)} %get-tuple-element.17, f32[1024]{0:T(1024)S(1)} %get-tuple-element.16), channel_id=1, replica_groups=mesh['batch'=8,'narrow'=4] {'batch','narrow'}, use_global_device_ids=true, to_apply=%region_16.17 | all-reduce | flops 2048 | bytes 16384 | tf_op jit(solution)/shard_map/psum | solution.py:198
  299.5 5.8 fusion.126
  305.3 40.2 %all-reduce.5 = (f32[1024]{0:T(1024)S(1)}, f32[1024]{0:T(1024)S(1)}) all-reduce(f32[1024]{0:T(1024)S(1)} %get-tuple-element.19, f32[1024]{0:T(1024)S(1)} %get-tuple-element.18), channel_id=1, replica_groups=mesh['batch'=8,'narrow'=4] {'batch','narrow'}, use_global_device_ids=true, to_apply=%region_22.23 | all-reduce | flops 2048 | bytes 16384 | tf_op jit(solution)/shard_map/psum | solution.py:215
  346.1 5.6 multiply_convert_fusion
  351.7 3.6 all-to-all-start.2
  355.5 25.5 %all-to-all-done.2 = bf16[16,4,16,1024]{3,2,1,0:T(8,128)(2,1)S(1)} async-done(((bf16[16,4,16,1024]{3,2,1,0:T(8,128)(2,1)}), bf16[16,4,16,1024]{3,2,1,0:T(8,128)(2,1)S(1)}, u32[]{:S(2)}, u32[]{:S(2)}) %all-to-all-start.2) | async-done | bytes 2097184 | tf_op jit(solution)/shard_map/all_to_all | solution.py:230
  383.8 40.3 %all-reduce.4 = (f32[128]{0:T(128)S(1)}, f32[128]{0:T(128)S(1)}) all-reduce(f32[128]{0:T(128)S(1)} %get-tuple-element.31, f32[128]{0:T(128)S(1)} %get-tuple-element.30), channel_id=1, replica_groups=mesh['batch'=8,'narrow'=4] {'batch','narrow'}, use_global_device_ids=true, to_apply=%region_26.27 | all-reduce | flops 256 | bytes 2048 | tf_op jit(solution)/shard_map/psum | solution.py:257
  425.9 4.2 all-to-all-start.3
  430.4 2.7 reshape.628
  435.4 3.3 fusion.138
  438.8 5.9 all-to-all-done.3
  448.8 38.9 %all-reduce.3 = (f32[512]{0:T(512)S(1)}, f32[512]{0:T(512)S(1)}) all-reduce(f32[512]{0:T(512)S(1)} %get-tuple-element.21, f32[512]{0:T(512)S(1)} %get-tuple-element.20), channel_id=1, replica_groups=mesh['batch'=8,'narrow'=4] {'batch','narrow'}, use_global_device_ids=true, to_apply=%region_30.31 | all-reduce | flops 1024 | bytes 8192 | tf_op jit(solution)/shard_map/psum | solution.py:286
  489.9 3.7 reshape.642
  493.6 3.8 fusion.24
  497.4 2.1 fusion.30
  506.9 4.1 collective-permute-done.3
  512.1 3.7 fusion.133
  515.8 2.2 reshape.629
  519.5 2.3 reshape.630
  521.8 2.7 fusion.56
  524.5 2.2 reshape.631
  526.6 2.1 reshape.632
  534.1 2.3 reshape.633
  537.5 2.2 reshape.635
  547.6 2.5 copy.172
  552.0 43.7 %all-reduce.2 = (f32[256]{0:T(256)S(1)}, f32[256]{0:T(256)S(1)}, f32[512]{0:T(512)}) all-reduce(f32[256]{0:T(256)S(1)} %get-tuple-element.29, f32[256]{0:T(256)S(1)} %get-tuple-element.28, f32[512]{0:T(512)S(1)} %fusion.113), channel_id=1, replica_groups=mesh['batch'=8,'narrow'=4] {'batch','narrow'}, use_global_device_ids=true, to_apply=%region_34.35 | all-reduce | flops 1024 | bytes 8192 | tf_op jit(solution)/shard_map/psum | solution.py:310
  600.8 5.8 fusion.9
  606.6 140.1 %all-reduce.13.cloned.1.call-done = (f32[1024,256]{1,0:T(8,128)}, f32[3,3,2,128,256]{4,3,2,1,0:T(8,128)}, f32[256,128]{1,0:T(8,128)}, f32[128,512]{1,0:T(8,128)}, f32[256,1024]{1,0:T(8,128)}) async-done(((f32[1024,256]{1,0:T(8,128)}, f32[3,3,2,128,256]{4,3,2,1,0:T(8,128)}, f32[256,128]{1,0:T(8,128)}, f32[128,512]{1,0:T(8,128)}, f32[256,1024]{1,0:T(8,128)}), (f32[1024,256]{1,0:T(8,128)}, ...) | async-done | bytes 4849680 | tf_op jit(solution)/shard_map/psum | solution.py:335
  746.7 2.3 copy.235
  749.0 3.4 copy.236
  (316 shorter events, 94.2 us)
Async XLA Ops:
  7.2 216.1 %copy-start = (bf16[256,1024]{1,0:T(8,128)(2,1)S(1)}, bf16[256,1024]{1,0:T(8,128)(2,1)}, u32[]{:S(2)}) copy-start(bf16[256,1024]{1,0:T(8,128)(2,1)} %param.30) | copy-start | bytes 1572868
  10.7 43.5 %copy-start.67 = (f32[256]{0:T(256)S(1)}, f32[256]{0:T(256)}, u32[]{:S(2)}) copy-start(f32[256]{0:T(256)} %param.20) | copy-start | bytes 3076
  10.7 44.7 %copy-start.84 = (f32[256]{0:T(256)S(1)}, f32[256]{0:T(256)}, u32[]{:S(2)}) copy-start(f32[256]{0:T(256)} %param.21) | copy-start | bytes 3076
  12.0 49.8 %copy-start.10 = (f32[1024,256]{1,0:T(8,128)}, f32[1024,256]{1,0:T(8,128)S(1)}, u32[]{:S(2)}) copy-start(f32[1024,256]{1,0:T(8,128)S(1)} %get-tuple-element.102) | copy-start | bytes 3145732
  56.0 5.9 collective-permute-start
  57.3 5.9 collective-permute-start.1
  59.0 4.3 copy-start.19
  71.8 5.1 copy-start.21
  77.0 6.1 copy-start.25
  83.1 6.1 copy-start.27
  89.2 5.1 copy-start.29
  112.3 45.2 %copy-start.55 = (f32[512]{0:T(512)S(1)}, f32[512]{0:T(512)}, u32[]{:S(2)}) copy-start(f32[512]{0:T(512)} %param.23) | copy-start | bytes 6148
  112.3 46.3 %copy-start.56 = (f32[512]{0:T(512)S(1)}, f32[512]{0:T(512)}, u32[]{:S(2)}) copy-start(f32[512]{0:T(512)} %param.24) | copy-start | bytes 6148
  115.3 45.1 %copy-start.5 = (f32[16,4,16,512]{3,2,1,0:T(8,128)}, f32[16,4,16,512]{3,2,1,0:T(8,128)S(1)}, u32[]{:S(2)}) copy-start(f32[16,4,16,512]{3,2,1,0:T(8,128)S(1)} %reshape.623) | copy-start | bytes 6291460
  158.7 6.0 copy-start.94
  160.4 18.8 %all-to-all-start = ((bf16[16,4,16,512]{3,2,1,0:T(8,128)(2,1)}), bf16[16,4,16,512]{3,2,1,0:T(8,128)(2,1)}, u32[]{:S(2)}, u32[]{:S(2)}) async-start(bf16[16,4,16,512]{3,2,1,0:T(8,128)(2,1)} %multiply_convert_fusion.2), calls=%async_computation | async-start | bytes 2097152 | tf_op jit(solution)/shard_map/all_to_all | solution.py:163
  164.6 17.7 %copy-start.51 = (f32[256,128]{1,0:T(8,128)S(1)}, f32[256,128]{1,0:T(8,128)}, u32[]{:S(2)}) copy-start(f32[256,128]{1,0:T(8,128)} %param.25) | copy-start | bytes 393220
  164.7 56.8 %copy-start.69 = (f32[128]{0:T(128)S(1)}, f32[128]{0:T(128)}, u32[]{:S(2)}) copy-start(f32[128]{0:T(128)} %param.26) | copy-start | bytes 1540
  164.7 57.3 %copy-start.50 = (f32[128,512]{1,0:T(8,128)S(1)}, f32[128,512]{1,0:T(8,128)}, u32[]{:S(2)}) copy-start(f32[128,512]{1,0:T(8,128)} %param.28) | copy-start | bytes 786436
  164.7 57.3 %copy-start.76 = (f32[128]{0:T(128)S(1)}, f32[128]{0:T(128)}, u32[]{:S(2)}) copy-start(f32[128]{0:T(128)} %param.27) | copy-start | bytes 1540
  164.7 57.3 %copy-start.88 = (f32[512]{0:T(512)S(1)}, f32[512]{0:T(512)}, u32[]{:S(2)}) copy-start(f32[512]{0:T(512)} %param.29) | copy-start | bytes 6148
  165.3 56.2 %copy-start.72 = (f32[4]{0:T(128)}, f32[4]{0:T(128)S(1)}, u32[]{:S(2)}) copy-start(f32[4]{0:T(128)S(1)} %get-tuple-element.68) | copy-start | bytes 52
  180.5 43.5 %copy-start.42 = (bf16[4,4,4,16,512]{4,3,2,1,0:T(8,128)(2,1)}, bf16[4,4,4,16,512]{4,3,2,1,0:T(8,128)(2,1)S(1)}, u32[]{:S(2)}) copy-start(bf16[4,4,4,16,512]{4,3,2,1,0:T(8,128)(2,1)S(1)} %copy.126) | copy-start | bytes 3145732
  225.5 29.3 %all-to-all-start.1 = ((bf16[4,16,16,1024]{3,2,0,1:T(8,128)(2,1)}), bf16[4,16,16,1024]{3,2,0,1:T(8,128)(2,1)S(1)}, u32[]{:S(2)}, u32[]{:S(2)}) async-start(bf16[4,16,16,1024]{3,2,0,1:T(8,128)(2,1)} %copy.127), calls=%async_computation.1 | async-start | bytes 4194304 | tf_op jit(solution)/shard_map/all_to_all | solution.py:194
  255.3 40.9 %copy-start.65 = (f32[1024]{0:T(1024)S(1)}, f32[1024]{0:T(1024)}, u32[]{:S(2)}) copy-start(f32[1024]{0:T(1024)} %param.31) | copy-start | bytes 12292
  299.5 5.9 copy-start.2
  345.5 6.2 copy-start.81
  345.5 6.2 copy-start.87
  351.7 29.3 %all-to-all-start.2 = ((bf16[16,4,16,1024]{3,2,1,0:T(8,128)(2,1)}), bf16[16,4,16,1024]{3,2,1,0:T(8,128)(2,1)S(1)}, u32[]{:S(2)}, u32[]{:S(2)}) async-start(bf16[16,4,16,1024]{3,2,1,0:T(8,128)(2,1)} %multiply_convert_fusion), calls=%async_computation.2 | async-start | bytes 4194304 | tf_op jit(solution)/shard_map/all_to_all | solution.py:230
  382.6 41.6 %copy-start.52 = (f32[256,128]{1,0:T(8,128)S(1)}, f32[256,128]{1,0:T(8,128)}, u32[]{:S(2)}) copy-start(f32[256,128]{1,0:T(8,128)} %param.25) | copy-start | bytes 393220
  382.6 41.6 %copy-start.73 = (f32[4]{0:T(128)S(1)}, f32[4]{0:T(128)}, u32[]{:S(2)}) copy-start(f32[4]{0:T(128)} %copy-done.72) | copy-start | bytes 52
  382.6 41.6 %copy-start.79 = (f32[128]{0:T(128)S(1)}, f32[128]{0:T(128)}, u32[]{:S(2)}) copy-start(f32[128]{0:T(128)} %get-tuple-element.63) | copy-start | bytes 1540
  424.1 9.0 %copy-start.89 = (f32[128]{0:T(128)}, f32[128]{0:T(128)S(1)}, u32[]{:S(2)}) copy-start(f32[128]{0:T(128)S(1)} %get-tuple-element.116) | copy-start | bytes 1540
  424.8 5.5 copy-start.7
  425.9 18.8 %all-to-all-start.3 = ((bf16[4,16,16,512]{3,2,0,1:T(8,128)(2,1)}), bf16[4,16,16,512]{3,2,0,1:T(8,128)(2,1)}, u32[]{:S(2)}, u32[]{:S(2)}) async-start(bf16[4,16,16,512]{3,2,0,1:T(8,128)(2,1)} %copy.133), calls=%async_computation.3 | async-start | bytes 2097152 | tf_op jit(solution)/shard_map/all_to_all | solution.py:282
  430.1 316.6 %all-reduce.13.cloned.1.call-start = ((), (), s32[]{:S(2)}) async-start(), calls=%async_computation.4 | async-start | bytes 9699328 | tf_op jit(solution)/shard_map/psum | solution.py:335
  430.4 5.1 copy-start.18
  487.8 5.8 copy-start.75
  497.3 13.6 %copy-start.8 = (bf16[16,4,16,512]{3,2,1,0:T(8,128)(2,1)}, bf16[16,4,16,512]{3,2,1,0:T(8,128)(2,1)S(1)}, u32[]{:S(2)}) copy-start(bf16[16,4,16,512]{3,2,1,0:T(8,128)(2,1)S(1)} %fusion.24) | copy-start | bytes 3145732
  503.7 3.1 collective-permute-start.2
  505.0 5.9 collective-permute-start.3
  506.8 9.0 %copy-start.44 = (f32[9,2,128,256]{3,2,1,0:T(8,128)}, f32[9,2,128,256]{3,2,1,0:T(8,128)S(1)}, u32[]{:S(2)}) copy-start(f32[9,2,128,256]{3,2,1,0:T(8,128)S(1)} %fusion.37) | copy-start | bytes 7077892
  537.5 4.4 copy-start.35
  546.1 4.0 copy-start.85
  550.2 46.3 %copy-start.86 = (f32[256]{0:T(256)S(1)}, f32[256]{0:T(256)}, u32[]{:S(2)}) copy-start(f32[256]{0:T(256)} %get-tuple-element.57) | copy-start | bytes 3076
  749.0 4.1 copy-start.53
  749.0 4.8 copy-start.49
  749.0 5.8 copy-start.1
  (59 other events, 131.5 us)
Sparse Core Ops, SparseCore 0:
  599.3 147.4 all-reduce.12
where the time goes:
time: 767 us; the launch traced here: 762 us
  blocking collectives  326 us (43%)
  waiting for transfers between devices  216 us (28%)
  local copies, waits for them, and re-layouts  83.1 us (11%)
  matrix products  58.3 us (8%)
  other arithmetic  41 us (5%)
  starting transfers between devices  21.3 us (3%)
  between operations  15.5 us (2%)
    psum x1, waiting for transfers between devices, body(): lax.psum((reduce_part, split_part, squeeze_part, excite_part, bias_part,...  140 us
    psum x1, blocking collectives, body(): lax.psum((jnp.sum(grad_z_reduce, 0), jnp.sum(grad_z_reduce * norm_reduce,...  43.7 us
    psum x1, blocking collectives, body(): lax.psum((jnp.sum(pre_split * flat_valid, 0), jnp.sum(pre_split * pre_spl...  42.2 us
    psum x1, blocking collectives, body(): lax.psum((jnp.sum(pre_reduce * flat_valid, 0), jnp.sum(pre_reduce * pre_r...  42.2 us
    psum x1, blocking collectives, body(): lax.psum((jnp.sum(grad_z_squeeze, 0), jnp.sum(grad_z_squeeze * norm_squee...  40.3 us
    psum x1, blocking collectives, body(): lax.psum((jnp.sum(grad_residual, 0), jnp.sum(grad_residual * norm_expand,...  40.2 us
    psum x1, blocking collectives, body(): lax.psum((jnp.sum(expand_values * flat_valid, 0), jnp.sum(expand_values *...  40 us
    psum x1, blocking collectives, body(): lax.psum((jnp.sum(grad_z_split, 0), jnp.sum(grad_z_split * norm_split, 0)...  38.9 us
  transfers between devices with their start and end apart: 9, of which 7 were waited for; matrix products, arithmetic and copies ran while one was open for 2% of the time, Pallas kernels for 0%

commit v1 on v0

v1 whole, which is shorter than its diff:
```python
import jax
import jax.numpy as jnp
from jax import lax
from jax.sharding import PartitionSpec as P

EPSILON = 1e-05
HIGHEST = lax.Precision.HIGHEST
ALL = ("batch", "narrow")


def device_count():
    return lax.axis_size("batch") * lax.axis_size("narrow")


def gather_all(block):
    count = device_count()
    return lax.all_to_all(jnp.broadcast_to(block[None], (count,) + block.shape), ALL, 0, 0)


def sum_all(*vectors):
    flat = jnp.concatenate(vectors)
    size = flat.shape[0]
    rows = -(-size // 128)
    flat = jnp.pad(flat, (0, rows * 128 - size)).reshape(rows, 128)
    total = jnp.sum(gather_all(flat), 0).reshape(-1)
    outs, start = [], 0
    for vector in vectors:
        outs.append(total[start : start + vector.shape[0]])
        start += vector.shape[0]
    return outs


def sum_weights(*parts):
    count = device_count()
    flat = jnp.concatenate([part.astype(jnp.bfloat16).reshape(-1, 128) for part in parts])
    rows = flat.shape[0]
    per = -(-rows // (count * 16)) * 16
    flat = jnp.pad(flat, ((0, per * count - rows), (0, 0))).reshape(count, per, 128)
    mine = jnp.sum(lax.all_to_all(flat, ALL, 0, 0).astype(jnp.float32), 0)
    full = gather_all(mine.astype(jnp.bfloat16)).reshape(-1, 128)
    outs, start = [], 0
    for part in parts:
        length = part.size // 128
        outs.append(full[start : start + length].astype(jnp.float32).reshape(part.shape))
        start += length
    return outs


def halo(block):
    count = lax.axis_size("narrow")
    forward = [(i, i + 1) for i in range(count - 1)]
    backward = [(i + 1, i) for i in range(count - 1)]
    low = lax.ppermute(block[:, -1:], "narrow", forward)
    high = lax.ppermute(block[:, :1], "narrow", backward)
    return low, high


def silu_slope(values):
    sigmoid_part = jax.nn.sigmoid(values)
    return sigmoid_part * (1.0 + values * (1.0 - sigmoid_part))


def side_mask(classes, first_row, row_count, col_count):
    image_side = 12 + 2 * classes
    row_ids = first_row + jnp.arange(row_count, dtype=jnp.int32)
    col_ids = jnp.arange(col_count, dtype=jnp.int32)
    row_inside = (row_ids[None, :] < image_side[:, None]) & (row_ids >= 0)[None, :]
    col_inside = col_ids[None, :] < image_side[:, None]
    return (row_inside[:, :, None] & col_inside[:, None, :]).astype(jnp.float32)[..., None]


def moments(totals, squares, counted):
    center = totals / counted
    return center, lax.rsqrt(squares / counted - center * center + EPSILON)


def conv_forward(padded, kernel, row_count, col_count):
    blocks = padded.shape[0]
    groups = kernel.shape[2]
    group_width = kernel.shape[3]
    accum = None
    for row_off in range(3):
        for col_off in range(3):
            window = padded[
                :, row_off : row_off + row_count, col_off : col_off + col_count, :
            ].reshape(blocks * row_count * col_count, groups, group_width)
            partial_value = jnp.einsum(
                "pgc,gco->pgo", window, kernel[row_off, col_off], preferred_element_type=jnp.float32
            )
            accum = partial_value if accum is None else accum + partial_value
    return accum.reshape(blocks, row_count, col_count, -1)


def conv_weight_grad(padded, grad_out, row_count, col_count, groups):
    blocks = padded.shape[0]
    group_width = padded.shape[3] // groups
    pieces = []
    for row_off in range(3):
        for col_off in range(3):
            window = padded[
                :, row_off : row_off + row_count, col_off : col_off + col_count, :
            ].reshape(blocks * row_count * col_count, groups, group_width)
            pieces.append(
                jnp.einsum("pgc,pgo->gco", window, grad_out, preferred_element_type=jnp.float32)
            )
    stacked = jnp.stack(pieces)
    return stacked.reshape(3, 3, groups, group_width, -1)


def conv_input_grad(padded_grad, kernel, row_count, col_count):
    blocks = padded_grad.shape[0]
    groups = kernel.shape[2]
    out_width = kernel.shape[4]
    accum = None
    for row_off in range(3):
        for col_off in range(3):
            window = padded_grad[
                :, 2 - row_off : 2 - row_off + row_count, 2 - col_off : 2 - col_off + col_count, :
            ].reshape(blocks * row_count * col_count, groups, out_width)
            partial_value = jnp.einsum(
                "pgo,gco->pgc", window, kernel[row_off, col_off], preferred_element_type=jnp.float32
            )
            accum = partial_value if accum is None else accum + partial_value
    return accum.reshape(blocks, row_count, col_count, -1)


def body(
    inputs,
    image_class,
    weight_reduce,
    gain_reduce,
    shift_reduce,
    weight_split,
    gain_split,
    shift_split,
    weight_squeeze,
    gain_squeeze,
    shift_squeeze,
    weight_excite,
    bias_excite,
    weight_expand,
    gain_expand,
    shift_expand,
    cotangent,
):
    blocks, row_count, col_count, channels = inputs.shape
    bottleneck = weight_reduce.shape[1]
    groups = weight_split.shape[2]
    parts = lax.axis_size("narrow")
    bands = lax.axis_size("batch")
    pixels = blocks * row_count * col_count
    first_row = lax.axis_index("narrow") * row_count
    tall = side_mask(image_class, first_row - 1, row_count + 2, col_count)
    valid = tall[:, 1:-1]
    flat_valid = valid.reshape(pixels, 1)
    side = (12 + 2 * image_class).astype(jnp.float32)
    image_area = side * side
    masked = inputs * valid.astype(jnp.bfloat16)
    flat_masked = masked.reshape(pixels, channels)

    pre_reduce = jnp.dot(flat_masked, weight_reduce, preferred_element_type=jnp.float32)
    low, high = halo(pre_reduce.reshape(blocks, row_count, col_count, bottleneck))
    sum_reduce, square_reduce, pixel_count = sum_all(
        jnp.sum(pre_reduce * flat_valid, 0),
        jnp.sum(pre_reduce * pre_reduce * flat_valid, 0),
        jnp.sum(flat_valid)[None],
    )
    center_reduce, inv_reduce = moments(sum_reduce, square_reduce, pixel_count)
    tall_reduce = jnp.concatenate(
        [low, pre_reduce.reshape(blocks, row_count, col_count, bottleneck), high], axis=1
    )
    tall_norm = (tall_reduce - center_reduce) * inv_reduce
    tall_z = tall_norm * gain_reduce + shift_reduce
    padded_reduce = jnp.pad(
        (jax.nn.silu(tall_z) * tall).astype(jnp.bfloat16), ((0, 0), (0, 0), (1, 1), (0, 0))
    )
    norm_reduce = tall_norm[:, 1:-1].reshape(pixels, -1)
    z_reduce = tall_z[:, 1:-1].reshape(pixels, -1)

    pre_split = conv_forward(padded_reduce, weight_split, row_count, col_count)
    low_split, high_split = halo(pre_split)
    flat_split = pre_split.reshape(pixels, -1)
    sum_split, square_split = sum_all(
        jnp.sum(flat_split * flat_valid, 0), jnp.sum(flat_split * flat_split * flat_valid, 0)
    )
    center_split, inv_split = moments(sum_split, square_split, pixel_count)
    tall_norm_split = (
        jnp.concatenate([low_split, pre_split, high_split], axis=1) - center_split
    ) * inv_split
    tall_z_split = tall_norm_split * gain_split + shift_split
    hidden_split = (jax.nn.silu(tall_z_split[:, 1:-1]) * valid).astype(jnp.bfloat16)
    first_half = hidden_split[..., :bottleneck]
    second_half = hidden_split[..., bottleneck:]
    summed = jnp.sum(hidden_split, axis=(1, 2), dtype=jnp.float32)
    pooled = (summed[:, :bottleneck] + summed[:, bottleneck:]) / image_area[:, None]
    squeeze_part = jnp.dot(pooled, weight_squeeze, precision=HIGHEST)
    all_squeeze = jnp.sum(
        gather_all(squeeze_part).reshape(bands, parts, blocks, -1), 1
    )
    image_count = bands * blocks
    center_squeeze, inv_squeeze = moments(
        jnp.sum(all_squeeze, (0, 1)), jnp.sum(all_squeeze * all_squeeze, (0, 1)), image_count
    )
    all_norm_squeeze = (all_squeeze - center_squeeze) * inv_squeeze
    all_z_squeeze = all_norm_squeeze * gain_squeeze + shift_squeeze
    band = lax.axis_index("batch")
    z_squeeze = lax.dynamic_index_in_dim(all_z_squeeze, band, keepdims=False)
    hidden_squeeze = jax.nn.silu(z_squeeze)
    logits = jnp.dot(hidden_squeeze, weight_excite, precision=HIGHEST) + bias_excite
    logit_first = logits[:, :bottleneck]
    logit_second = logits[:, bottleneck:]
    ceiling = jnp.maximum(logit_first, logit_second)
    exp_first = jnp.exp(logit_first - ceiling)
    exp_second = jnp.exp(logit_second - ceiling)
    att_first = exp_first / (exp_first + exp_second)
    att_second = exp_second / (exp_first + exp_second)
    mixture = (
        att_first[:, None, None, :] * first_half + att_second[:, None, None, :] * second_half
    ).astype(jnp.bfloat16)
    flat_mix = mixture.reshape(pixels, bottleneck)
    pre_expand = jnp.dot(flat_mix, weight_expand, preferred_element_type=jnp.float32).astype(
        jnp.bfloat16
    )
    expand_values = pre_expand.astype(jnp.float32)
    sum_expand, square_expand = sum_all(
        jnp.sum(expand_values * flat_valid, 0),
        jnp.sum(expand_values * expand_values * flat_valid, 0),
    )
    center_expand, inv_expand = moments(sum_expand, square_expand, pixel_count)
    norm_expand = (expand_values - center_expand) * inv_expand
    residual = norm_expand * gain_expand + shift_expand + flat_masked
    block_output = (
        (jax.nn.silu(residual) * flat_valid)
        .astype(jnp.bfloat16)
        .reshape(blocks, row_count, col_count, channels)
    )
    grad_residual = cotangent.reshape(pixels, channels) * flat_valid * silu_slope(residual)
    shift_expand_grad, gain_expand_grad = sum_all(
        jnp.sum(grad_residual, 0), jnp.sum(grad_residual * norm_expand, 0)
    )
    grad_expand = (
        flat_valid
        * gain_expand
        * inv_expand
        * (
            grad_residual
            - shift_expand_grad / pixel_count
            - norm_expand * gain_expand_grad / pixel_count
        )
    ).astype(jnp.bfloat16)
    expand_part = jnp.einsum("pc,pd->cd", flat_mix, grad_expand, preferred_element_type=jnp.float32)
    grad_mixture = (
        jnp.einsum("pd,cd->pc", grad_expand, weight_expand, preferred_element_type=jnp.float32)
        .astype(jnp.bfloat16)
        .reshape(blocks, row_count, col_count, bottleneck)
    )
    low_mix, high_mix = halo(grad_mixture)
    grad_att_first = jnp.einsum(
        "ihwc,ihwc->ic", grad_mixture, first_half, preferred_element_type=jnp.float32
    )
    grad_att_second = jnp.einsum(
        "ihwc,ihwc->ic", grad_mixture, second_half, preferred_element_type=jnp.float32
    )
    inner = att_first * grad_att_first + att_second * grad_att_second
    grad_logits = jnp.concatenate(
        [att_first * (grad_att_first - inner), att_second * (grad_att_second - inner)], axis=1
    )
    bias_part = jnp.sum(grad_logits, 0)
    excite_part = jnp.einsum("ik,ic->kc", hidden_squeeze, grad_logits, precision=HIGHEST)
    hidden_part = jnp.einsum("ic,kc->ik", grad_logits, weight_excite, precision=HIGHEST)
    all_hidden = jnp.sum(gather_all(hidden_part).reshape(bands, parts, blocks, -1), 1)
    all_grad_z = all_hidden * silu_slope(all_z_squeeze)
    shift_squeeze_grad = jnp.sum(all_grad_z, (0, 1))
    gain_squeeze_grad = jnp.sum(all_grad_z * all_norm_squeeze, (0, 1))
    grad_z_squeeze = lax.dynamic_index_in_dim(all_grad_z, band, keepdims=False)
    norm_squeeze = lax.dynamic_index_in_dim(all_norm_squeeze, band, keepdims=False)
    grad_pre_squeeze = (
        gain_squeeze
        * inv_squeeze
        * (
            grad_z_squeeze
            - shift_squeeze_grad / image_count
            - norm_squeeze * gain_squeeze_grad / image_count
        )
    )
    squeeze_grad_part = jnp.einsum("ic,ik->ck", pooled, grad_pre_squeeze, precision=HIGHEST)
    grad_pooled = (
        jnp.einsum("ik,ck->ic", grad_pre_squeeze, weight_squeeze, precision=HIGHEST)
        / image_area[:, None]
    )
    tall_mix = jnp.concatenate([low_mix, grad_mixture, high_mix], axis=1)
    spread = grad_pooled[:, None, None, :] * tall
    tall_hidden = jnp.concatenate(
        [
            tall_mix * att_first[:, None, None, :] + spread,
            tall_mix * att_second[:, None, None, :] + spread,
        ],
        axis=-1,
    ).astype(jnp.bfloat16)
    tall_grad_z = tall_hidden * tall * silu_slope(tall_z_split)
    own_grad_z = tall_grad_z[:, 1:-1].reshape(pixels, -1)
    own_norm_split = tall_norm_split[:, 1:-1].reshape(pixels, -1)
    shift_split_grad, gain_split_grad = sum_all(
        jnp.sum(own_grad_z, 0), jnp.sum(own_grad_z * own_norm_split, 0)
    )
    tall_grad_split = (
        tall
        * gain_split
        * inv_split
        * (
            tall_grad_z
            - shift_split_grad / pixel_count
            - tall_norm_split * gain_split_grad / pixel_count
        )
    ).astype(jnp.bfloat16)
    grad_split = tall_grad_split[:, 1:-1].reshape(-1, groups, bottleneck)
    split_part = conv_weight_grad(padded_reduce, grad_split, row_count, col_count, groups)
    padded_grad = jnp.pad(tall_grad_split, ((0, 0), (0, 0), (1, 1), (0, 0)))
    grad_hidden_reduce = conv_input_grad(padded_grad, weight_split, row_count, col_count).reshape(
        pixels, -1
    )
    grad_z_reduce = grad_hidden_reduce * flat_valid * silu_slope(z_reduce)
    shift_reduce_grad, gain_reduce_grad, bias_total = sum_all(
        jnp.sum(grad_z_reduce, 0), jnp.sum(grad_z_reduce * norm_reduce, 0), bias_part
    )
    grad_reduce = (
        flat_valid
        * gain_reduce
        * inv_reduce
        * (
            grad_z_reduce
            - shift_reduce_grad / pixel_count
            - norm_reduce * gain_reduce_grad / pixel_count
        )
    ).astype(jnp.bfloat16)
    reduce_part = jnp.einsum(
        "pc,pd->cd", flat_masked, grad_reduce, preferred_element_type=jnp.float32
    )
    grad_input = (
        jnp.einsum("pd,cd->pc", grad_reduce, weight_reduce, preferred_element_type=jnp.float32)
        + grad_residual
    )
    input_grad = (
        (grad_input * flat_valid)
        .astype(jnp.bfloat16)
        .reshape(blocks, row_count, col_count, channels)
    )
    expand_total, squeeze_total, excite_total = sum_weights(
        expand_part, squeeze_grad_part, excite_part
    )
    (split_total,) = sum_weights(split_part)
    (reduce_total,) = sum_weights(reduce_part)
    return (
        block_output,
        input_grad,
        reduce_total,
        gain_reduce_grad,
        shift_reduce_grad,
        split_total,
        gain_split_grad,
        shift_split_grad,
        squeeze_total,
        gain_squeeze_grad,
        shift_squeeze_grad,
        excite_total,
        bias_total,
        expand_total,
        gain_expand_grad,
        shift_expand_grad,
    )


def solution(mesh):
    rows = P("batch", "narrow", None, None)
    return jax.shard_map(
        body,
        mesh=mesh,
        in_specs=(rows, P("batch")) + (P(),) * 14 + (rows,),
        out_specs=(rows, rows) + (P(),) * 14,
        check_vma=False,
    )
```

time: 767 us -> 432 us (0.56)
  blocking collectives: 326 us -> 26 us
  waiting for transfers between devices: 216 us -> 120 us
  starting transfers between devices: 21.3 us -> 76.5 us
  local copies, waits for them, and re-layouts: 83.1 us -> 101 us
  other arithmetic: 41 us -> 58.8 us
  matrix products: 58.3 us -> 41 us
  between operations: 15.5 us -> 2.19 us
    psum x8 -> x0, blocking collectives: 326 us -> none  [the longest x1 43.7 us: body(): lax.psum((jnp.sum(grad_z_reduce, 0), jnp.sum(grad_z_reduce * norm_reduce,...]
    psum x1 -> x0, waiting for transfers between devices: 140 us -> none  [body(): lax.psum((reduce_part, split_part, squeeze_part, excite_part, bias_part,...]
    all_to_all x4 -> x12, starting transfers between devices: 15.7 us -> 65.3 us  [the longest x9 53.1 us: gather_all(): lax.all_to_all(jnp.broadcast_to(block[None], (count,) + block.shape), ALL...]
    all_to_all x4 -> x12, waiting for transfers between devices: 70.6 us -> 118 us  [the longest x9 76.9 us: gather_all(): lax.all_to_all(jnp.broadcast_to(block[None], (count,) + block.shape), ALL...]
    all_to_all x0 -> x2, blocking collectives: none -> 26 us  [gather_all(): lax.all_to_all(jnp.broadcast_to(block[None], (count,) + block.shape), ALL...]
    dot_general x9, matrix products: 27.7 us -> 7.13 us  [conv_forward(): jnp.einsum('pgc,gco->pgo', window, kernel[row_off, col_off], preferred_el...]
    dot_general x9, matrix products: 2.73 us -> 15.6 us  [conv_weight_grad(): jnp.einsum('pgc,pgo->gco', window, grad_out, preferred_element_type=jnp.f...]
    reshape x17 -> x18, local copies, waits for them, and re-layouts: 17.6 us -> 29.5 us  [conv_forward(): window = padded[:, row_off:row_off + row_count, col_off:col_off + col_cou...]
  transfers between devices with their start and end apart: 9 -> 18, of which waited for: 7 -> 12; matrix products, arithmetic and copies ran while one was open for 2% -> 15% of each run, Pallas kernels for 0% -> 0%
where the time goes in v1:
time: 432 us; the launch traced here: 426 us
  waiting for transfers between devices  120 us (28%)
  local copies, waits for them, and re-layouts  101 us (23%)
  starting transfers between devices  76.5 us (18%)
  other arithmetic  58.8 us (14%)
  matrix products  41 us (9%)
  blocking collectives  26 us (6%)
    all_to_all x9, waiting for transfers between devices, gather_all(): lax.all_to_all(jnp.broadcast_to(block[None], (count,) + block.shape), ALL...  76.9 us
    all_to_all x9, starting transfers between devices, gather_all(): lax.all_to_all(jnp.broadcast_to(block[None], (count,) + block.shape), ALL...  53.1 us
    all_to_all x3, waiting for transfers between devices, sum_weights(): mine = jnp.sum(lax.all_to_all(flat, ALL, 0, 0).astype(jnp.float32), 0)  41.5 us
    reshape x18, local copies, waits for them, and re-layouts, conv_forward(): window = padded[:, row_off:row_off + row_count, col_off:col_off + col_cou...  29.5 us
    all_to_all x2, blocking collectives, gather_all(): lax.all_to_all(jnp.broadcast_to(block[None], (count,) + block.shape), ALL...  26 us
    reshape x9, local copies, waits for them, and re-layouts, conv_input_grad(): window = padded_grad[:, 2 - row_off:2 - row_off + row_count, 2 - col_off:...  16.6 us
    dot_general x9, matrix products, conv_weight_grad(): jnp.einsum('pgc,pgo->gco', window, grad_out, preferred_element_type=jnp.f...  15.6 us
    all_to_all x3, starting transfers between devices, sum_weights(): mine = jnp.sum(lax.all_to_all(flat, ALL, 0, 0).astype(jnp.float32), 0)  12.3 us
  transfers between devices with their start and end apart: 18, of which 12 were waited for; matrix products, arithmetic and copies ran while one was open for 15% of the time, Pallas kernels for 0%

profile of v1, /device:TPU:0, one launch (start us, length us, event | category | flops | bytes accessed | tf_op | source)
XLA Modules:
  0.0 425.6 jit_solution(13549810580445236767)
XLA Ops:
  7.0 7.3 %all-to-all-start = ((f32[32,5,128]{2,1,0:T(8,128)}), f32[32,5,128]{2,1,0:T(8,128)S(1)}, u32[]{:S(2)}, u32[]{:S(2)}) async-start(f32[32,5,128]{2,1,0:T(8,128)} %broadcast_in_dim.30), calls=%async_computation | async-start | bytes 262144 | tf_op jit(solution)/shard_map/all_to_all | solution.py:17
  17.9 4.6 %all-to-all-done = f32[32,5,128]{2,1,0:T(8,128)S(1)} async-done(((f32[32,5,128]{2,1,0:T(8,128)}), f32[32,5,128]{2,1,0:T(8,128)S(1)}, u32[]{:S(2)}, u32[]{:S(2)}) %all-to-all-start) | async-done | bytes 81952 | tf_op jit(solution)/shard_map/all_to_all | solution.py:17
  25.2 2.3 multiply_convert_fusion.4
  27.5 2.4 pad_slice_fusion.6
  67.6 5.2 %all-to-all-start.1 = ((f32[32,8,128]{2,1,0:T(8,128)}), f32[32,8,128]{2,1,0:T(8,128)S(1)}, u32[]{:S(2)}, u32[]{:S(2)}) async-start(f32[32,8,128]{2,1,0:T(8,128)} %broadcast_in_dim.31), calls=%async_computation.1 | async-start | bytes 262144 | tf_op jit(solution)/shard_map/all_to_all | solution.py:17
  72.8 2.9 copy.140
  75.7 2.9 reshape.497
  79.7 3.1 collective-permute-start.2
  87.3 3.4 multiply_add_fusion
  94.3 11.4 %all-to-all-start.2 = ((f32[32,16,128]{2,1,0:T(8,128)}), f32[32,16,128]{2,1,0:T(8,128)S(1)}, u32[]{:S(2)}, u32[]{:S(2)}) async-start(f32[32,16,128]{2,1,0:T(8,128)} %broadcast_in_dim.32), calls=%async_computation.2 | async-start | bytes 524288 | tf_op jit(solution)/shard_map/all_to_all | solution.py:17
  105.7 10.6 %all-to-all-done.2 = f32[32,16,128]{2,1,0:T(8,128)S(1)} async-done(((f32[32,16,128]{2,1,0:T(8,128)}), f32[32,16,128]{2,1,0:T(8,128)S(1)}, u32[]{:S(2)}, u32[]{:S(2)}) %all-to-all-start.2) | async-done | bytes 262176 | tf_op jit(solution)/shard_map/all_to_all | solution.py:17
  119.5 13.0 %all_to_all.70 = f32[32,16,128]{2,1,0:T(8,128)} all-to-all(f32[32,16,128]{2,1,0:T(8,128)S(1)} %broadcast_in_dim.33), channel_id=1, replica_groups=mesh['batch'=8,'narrow'=4] {'batch','narrow'}, dimensions={0} | all-to-all | bytes 524288 | tf_op jit(solution)/shard_map/all_to_all | solution.py:17
  134.9 6.9 %fusion.150 = (f32[1024]{0:T(1024)S(1)}, f32[1024]{0:T(1024)S(1)}, f32[1024,1024]{1,0:T(8,128)}, bf16[1024,1024]{1,0:T(8,128)(2,1)}) fusion(f32[1024]{0:T(1024)S(1)} %fusion.124, f32[1024]{0:T(1024)S(1)} %fusion.125, bf16[1024,1024]{1,0:T(8,128)(2,1)S(1)} %get-tuple-element.96, bf16[16,4,16,1024]{3,2,1,0:T(8,128)(2,1)} %copy-done.5, f32[1024]{0:T(1024)} %param.32, ...), kind=kLoop, calls=%fused_computation.286 | loop fusion | flops 24115200 | bytes 12611584 | tf_op jit(solution)/shard_map/reduce_sum | solution.py:239
  141.9 13.0 %all_to_all.71 = f32[32,16,128]{2,1,0:T(8,128)} all-to-all(f32[32,16,128]{2,1,0:T(8,128)S(1)} %broadcast_in_dim.34), channel_id=1, replica_groups=mesh['batch'=8,'narrow'=4] {'batch','narrow'}, dimensions={0} | all-to-all | bytes 524288 | tf_op jit(solution)/shard_map/all_to_all | solution.py:17
  157.1 4.2 fusion.14
  163.8 2.6 all-to-all-start.5
  166.4 2.3 convolution_convert_fusion.1
  172.9 4.0 all-to-all-done.5
  178.8 2.9 multiply_multiply_fusion
  184.1 13.7 %all-to-all-start.6 = ((f32[32,8,128]{2,1,0:T(8,128)}), f32[32,8,128]{2,1,0:T(8,128)S(1)}, u32[]{:S(2)}, u32[]{:S(2)}) async-start(f32[32,8,128]{2,1,0:T(8,128)} %broadcast_in_dim.36), calls=%async_computation.6 | async-start | bytes 262144 | tf_op jit(solution)/shard_map/all_to_all | solution.py:17
  198.7 7.1 %all-to-all-done.6 = f32[32,8,128]{2,1,0:T(8,128)S(1)} async-done(((f32[32,8,128]{2,1,0:T(8,128)}), f32[32,8,128]{2,1,0:T(8,128)S(1)}, u32[]{:S(2)}, u32[]{:S(2)}) %all-to-all-start.6) | async-done | bytes 131104 | tf_op jit(solution)/shard_map/all_to_all | solution.py:17
  207.1 4.3 %multiply_convert_fusion.2 = bf16[16,6,16,512]{3,2,1,0:T(8,128)(2,1)S(1)} fusion(f32[16,6,16,512]{3,2,1,0:T(8,128)} %get-tuple-element.49, f32[16,6,16,512]{3,2,1,0:T(8,128)} %copy-done.2, f32[]{:T(128)} %bitcast.10, f32[512]{0:T(512)S(1)} %slice_bitcast_fusion.3, f32[512]{0:T(512)S(1)} %get-tuple-element.36, f32[16,6,16]{2,1,0:T(8,128)S(1)} %and_convert_fusion, ...), kind=kLoop, calls=%fused_computation.24 | loop fusion | flops 6291456 | bytes 7878660 | tf_op jit(solution)/shard_map/convert_element_type | solution.py:315
  211.4 3.7 pad_slice_fusion
  245.2 3.2 multiply_reduce_fusion.2
  252.2 2.6 fusion.152
  255.5 2.6 all-to-all-start.7
  258.1 2.8 reshape.516
  266.3 5.1 %all-to-all-start.12 = ((bf16[32,96,128]{2,1,0:T(8,128)(2,1)}), bf16[32,96,128]{2,1,0:T(8,128)(2,1)S(1)}, u32[]{:S(2)}, u32[]{:S(2)}) async-start(bf16[32,96,128]{2,1,0:T(8,128)(2,1)} %bitcast.69), calls=%async_computation.12 | async-start | bytes 1572864 | tf_op jit(solution)/shard_map/all_to_all | solution.py:39
  271.5 2.3 fusion.28
  273.8 2.4 fusion.30
  278.1 2.6 multiply_convert_fusion.5
  284.3 7.8 %all-to-all-done.12 = bf16[32,96,128]{2,1,0:T(8,128)(2,1)S(1)} async-done(((bf16[32,96,128]{2,1,0:T(8,128)(2,1)}), bf16[32,96,128]{2,1,0:T(8,128)(2,1)S(1)}, u32[]{:S(2)}, u32[]{:S(2)}) %all-to-all-start.12) | async-done | bytes 786464 | tf_op jit(solution)/shard_map/all_to_all | solution.py:39
  292.0 3.8 all-to-all-start.8
  295.8 2.3 fusion.34
  298.1 2.4 fusion.36
  302.5 3.0 convert_element_type.158
  305.5 5.8 %all-to-all-done.8 = bf16[32,64,128]{2,1,0:T(8,128)(2,1)} async-done(((bf16[32,64,128]{2,1,0:T(8,128)(2,1)}), bf16[32,64,128]{2,1,0:T(8,128)(2,1)}, u32[]{:S(2)}, u32[]{:S(2)}) %all-to-all-start.8) | async-done | bytes 524320 | tf_op jit(solution)/shard_map/all_to_all | solution.py:39
  311.3 3.4 all-to-all-start.10
  315.8 27.9 %all-to-all-done.10 = bf16[32,144,128]{2,1,0:T(8,128)(2,1)} async-done(((bf16[32,144,128]{2,1,0:T(8,128)(2,1)}), bf16[32,144,128]{2,1,0:T(8,128)(2,1)}, u32[]{:S(2)}, u32[]{:S(2)}) %all-to-all-start.10) | async-done | bytes 1179680 | tf_op jit(solution)/shard_map/all_to_all | solution.py:39
  344.7 3.5 all-to-all-start.9
  348.3 15.4 %all-to-all-done.9 = bf16[32,64,128]{2,1,0:T(8,128)(2,1)S(1)} async-done(((bf16[32,64,128]{2,1,0:T(8,128)(2,1)}), bf16[32,64,128]{2,1,0:T(8,128)(2,1)S(1)}, u32[]{:S(2)}, u32[]{:S(2)}) %all-to-all-start.9) | async-done | bytes 524320 | tf_op jit(solution)/shard_map/all_to_all | solution.py:17
  364.7 3.1 all-to-all-start.13
  369.2 19.2 %all-to-all-done.13 = bf16[32,96,128]{2,1,0:T(8,128)(2,1)S(1)} async-done(((bf16[32,96,128]{2,1,0:T(8,128)(2,1)}), bf16[32,96,128]{2,1,0:T(8,128)(2,1)S(1)}, u32[]{:S(2)}, u32[]{:S(2)}) %all-to-all-start.13) | async-done | bytes 786464 | tf_op jit(solution)/shard_map/all_to_all | solution.py:17
  389.6 3.7 all-to-all-start.11
  396.5 2.9 fusion.62
  399.3 4.3 %multiply_convert_fusion = bf16[1024,1024]{1,0:T(8,128)(2,1)} fusion(f32[1024,1024]{1,0:T(8,128)} %get-tuple-element.43, bf16[1024,256]{1,0:T(8,128)(2,1)S(1)} %fusion.62, bf16[1024,256]{1,0:T(8,128)(2,1)S(1)} %copy-done.39, f32[1024]{0:T(1024)S(1)} %mul.513), kind=kOutput, calls=%fused_computation.18 | convolution fusion | flops 540016640 | bytes 7344128 | tf_op jit(solution)/shard_map/pd,cd->pc/dot_general | solution.py:340
  407.4 15.1 %all-to-all-done.11 = bf16[32,144,128]{2,1,0:T(8,128)(2,1)} async-done(((bf16[32,144,128]{2,1,0:T(8,128)(2,1)}), bf16[32,144,128]{2,1,0:T(8,128)(2,1)}, u32[]{:S(2)}, u32[]{:S(2)}) %all-to-all-start.11) | async-done | bytes 1179680 | tf_op jit(solution)/shard_map/all_to_all | solution.py:17
  422.4 3.0 reshape.528
  (311 shorter events, 139.7 us)
Async XLA Ops:
  0.6 117.8 %copy-start = (bf16[256,1024]{1,0:T(8,128)(2,1)S(1)}, bf16[256,1024]{1,0:T(8,128)(2,1)}, u32[]{:S(2)}) copy-start(bf16[256,1024]{1,0:T(8,128)(2,1)} %param.30) | copy-start | bytes 1572868
  2.4 88.3 %copy-start.43 = (f32[16,4,16]{2,1,0:T(4,128)}, f32[16,4,16]{2,1,0:T(4,128)S(1)}, u32[]{:S(2)}) copy-start(f32[16,4,16]{2,1,0:T(4,128)S(1)} %get-tuple-element.92) | copy-start | bytes 12292
  4.4 20.8 %copy-start.55 = (f32[256]{0:T(256)S(1)}, f32[256]{0:T(256)}, u32[]{:S(2)}) copy-start(f32[256]{0:T(256)} %param.20) | copy-start | bytes 3076
  4.4 20.8 %copy-start.71 = (f32[256]{0:T(256)S(1)}, f32[256]{0:T(256)}, u32[]{:S(2)}) copy-start(f32[256]{0:T(256)} %param.21) | copy-start | bytes 3076
  7.0 15.5 %all-to-all-start = ((f32[32,5,128]{2,1,0:T(8,128)}), f32[32,5,128]{2,1,0:T(8,128)S(1)}, u32[]{:S(2)}, u32[]{:S(2)}) async-start(f32[32,5,128]{2,1,0:T(8,128)} %broadcast_in_dim.30), calls=%async_computation | async-start | bytes 262144 | tf_op jit(solution)/shard_map/all_to_all | solution.py:17
  14.4 10.8 %collective-permute-start = (f32[16,1,16,256]{3,2,1,0:T(8,128)S(1)}, f32[16,1,16,256]{3,2,1,0:T(8,128)S(1)}, u32[]{:S(2)}, u32[]{:S(2)}) collective-permute-start(f32[16,1,16,256]{3,2,1,0:T(8,128)S(1)} %get-tuple-element.68), channel_id=1, source_target_pairs={{0,1},{1,2},{2,3},{4,5},{5,6},{6,7},{8,9},{9,10},{10,11},{12,13},{... | collective-permute-start | bytes 786440 | tf_op jit(solution)/shard_map/ppermute | solution.py:53
  16.6 8.6 %collective-permute-start.1 = (f32[16,1,16,256]{3,2,1,0:T(8,128)S(1)}, f32[16,1,16,256]{3,2,1,0:T(8,128)S(1)}, u32[]{:S(2)}, u32[]{:S(2)}) collective-permute-start(f32[16,1,16,256]{3,2,1,0:T(8,128)S(1)} %get-tuple-element.69), channel_id=1, source_target_pairs={{1,0},{2,1},{3,2},{5,4},{6,5},{7,6},{9,8},{10,9},{11,10},{13,12},{... | collective-permute-start | bytes 786440 | tf_op jit(solution)/shard_map/ppermute | solution.py:54
  32.0 32.6 %copy-start.22 = (bf16[1024,2,128]{0,2,1:T(8,128)(2,1)}, bf16[1024,2,128]{0,2,1:T(8,128)(2,1)S(1)}, u32[]{:S(2)}) copy-start(bf16[1024,2,128]{0,2,1:T(8,128)(2,1)S(1)} %copy.171) | copy-start | bytes 1572868
  52.3 7.0 %copy-start.8 = (bf16[3,3,2,128,256]{4,3,2,1,0:T(8,128)(2,1)S(1)}, bf16[3,3,2,128,256]{4,3,2,1,0:T(8,128)(2,1)}, u32[]{:S(2)}) copy-start(bf16[3,3,2,128,256]{4,3,2,1,0:T(8,128)(2,1)} %param.22) | copy-start | bytes 3538948
  67.6 16.6 %all-to-all-start.1 = ((f32[32,8,128]{2,1,0:T(8,128)}), f32[32,8,128]{2,1,0:T(8,128)S(1)}, u32[]{:S(2)}, u32[]{:S(2)}) async-start(f32[32,8,128]{2,1,0:T(8,128)} %broadcast_in_dim.31), calls=%async_computation.1 | async-start | bytes 262144 | tf_op jit(solution)/shard_map/all_to_all | solution.py:17
  78.6 8.6 %copy-start.60 = (f32[512]{0:T(512)S(1)}, f32[512]{0:T(512)}, u32[]{:S(2)}) copy-start(f32[512]{0:T(512)} %param.23) | copy-start | bytes 6148
  78.7 8.6 %copy-start.70 = (f32[512]{0:T(512)S(1)}, f32[512]{0:T(512)}, u32[]{:S(2)}) copy-start(f32[512]{0:T(512)} %param.24) | copy-start | bytes 6148
  79.7 5.9 %collective-permute-start.2 = (f32[16,1,16,512]{3,2,1,0:T(8,128)}, f32[16,1,16,512]{3,2,1,0:T(8,128)}, u32[]{:S(2)}, u32[]{:S(2)}) collective-permute-start(f32[16,1,16,512]{3,2,1,0:T(8,128)} %get-tuple-element.54), channel_id=1, source_target_pairs={{0,1},{1,2},{2,3},{4,5},{5,6},{6,7},{8,9},{9,10},{10,11},{12,13},{... | collective-permute-start | bytes 1572872 | tf_op jit(solution)/shard_map/ppermute | solution.py:53
  82.8 4.5 %collective-permute-start.3 = (f32[16,1,16,512]{3,2,1,0:T(8,128)}, f32[16,1,16,512]{3,2,1,0:T(8,128)}, u32[]{:S(2)}, u32[]{:S(2)}) collective-permute-start(f32[16,1,16,512]{3,2,1,0:T(8,128)} %get-tuple-element.55), channel_id=1, source_target_pairs={{1,0},{2,1},{3,2},{5,4},{6,5},{7,6},{9,8},{10,9},{11,10},{13,12},{... | collective-permute-start | bytes 1572872 | tf_op jit(solution)/shard_map/ppermute | solution.py:54
  84.1 9.1 %copy-start.66 = (f32[16]{0:T(128)}, f32[16]{0:T(128)S(1)}, u32[]{:S(2)}) copy-start(f32[16]{0:T(128)S(1)} %convert_multiply_fusion.7) | copy-start | bytes 196
  84.9 5.8 %copy-start.52 = (f32[512]{0:T(512)}, f32[512]{0:T(512)S(1)}, u32[]{:S(2)}) copy-start(f32[512]{0:T(512)S(1)} %fusion.128) | copy-start | bytes 6148
  92.5 23.9 %copy-start.68 = (f32[128]{0:T(128)S(1)}, f32[128]{0:T(128)}, u32[]{:S(2)}) copy-start(f32[128]{0:T(128)} %param.26) | copy-start | bytes 1540
  92.5 24.5 %copy-start.72 = (f32[128]{0:T(128)S(1)}, f32[128]{0:T(128)}, u32[]{:S(2)}) copy-start(f32[128]{0:T(128)} %param.27) | copy-start | bytes 1540
  92.5 25.1 %copy-start.37 = (f32[128,512]{1,0:T(8,128)S(1)}, f32[128,512]{1,0:T(8,128)}, u32[]{:S(2)}) copy-start(f32[128,512]{1,0:T(8,128)} %param.28) | copy-start | bytes 786436
  92.5 25.1 %copy-start.64 = (f32[512]{0:T(512)S(1)}, f32[512]{0:T(512)}, u32[]{:S(2)}) copy-start(f32[512]{0:T(512)} %param.29) | copy-start | bytes 6148
  93.2 23.7 %copy-start.49 = (f32[16,512]{1,0:T(8,128)}, f32[16,512]{1,0:T(8,128)S(1)}, u32[]{:S(2)}) copy-start(f32[16,512]{1,0:T(8,128)S(1)} %get-tuple-element.46) | copy-start | bytes 98308
  93.2 24.9 %copy-start.13 = (bf16[16,4,16,512]{3,2,1,0:T(8,128)(2,1)}, bf16[16,4,16,512]{3,2,1,0:T(8,128)(2,1)S(1)}, u32[]{:S(2)}) copy-start(bf16[16,4,16,512]{3,2,1,0:T(8,128)(2,1)S(1)} %get-tuple-element.47) | copy-start | bytes 3145732
  94.3 22.0 %all-to-all-start.2 = ((f32[32,16,128]{2,1,0:T(8,128)}), f32[32,16,128]{2,1,0:T(8,128)S(1)}, u32[]{:S(2)}, u32[]{:S(2)}) async-start(f32[32,16,128]{2,1,0:T(8,128)} %broadcast_in_dim.32), calls=%async_computation.2 | async-start | bytes 524288 | tf_op jit(solution)/shard_map/all_to_all | solution.py:17
  134.9 7.0 %copy-start.51 = (f32[1024]{0:T(1024)}, f32[1024]{0:T(1024)S(1)}, u32[]{:S(2)}) copy-start(f32[1024]{0:T(1024)S(1)} %fusion.125) | copy-start | bytes 12292
  163.8 13.2 %all-to-all-start.5 = ((f32[32,16,128]{2,1,0:T(8,128)}), f32[32,16,128]{2,1,0:T(8,128)S(1)}, u32[]{:S(2)}, u32[]{:S(2)}) async-start(f32[32,16,128]{2,1,0:T(8,128)} %broadcast_in_dim.35), calls=%async_computation.5 | async-start | bytes 524288 | tf_op jit(solution)/shard_map/all_to_all | solution.py:17
  166.4 10.6 %copy-start.42 = (f32[8,16,128]{2,1,0:T(8,128)S(1)}, f32[8,16,128]{2,1,0:T(8,128)}, u32[]{:S(2)}) copy-start(f32[8,16,128]{2,1,0:T(8,128)} %get-tuple-element.45) | copy-start | bytes 196612
  168.7 8.8 %copy-start.41 = (f32[256,128]{1,0:T(8,128)S(1)}, f32[256,128]{1,0:T(8,128)}, u32[]{:S(2)}) copy-start(f32[256,128]{1,0:T(8,128)} %param.25) | copy-start | bytes 393220
  168.7 8.8 %copy-start.67 = (f32[16]{0:T(128)S(1)}, f32[16]{0:T(128)}, u32[]{:S(2)}) copy-start(f32[16]{0:T(128)} %copy-done.66) | copy-start | bytes 196
  168.7 8.8 %copy-start.69 = (f32[128]{0:T(128)S(1)}, f32[128]{0:T(128)}, u32[]{:S(2)}) copy-start(f32[128]{0:T(128)} %get-tuple-element.38) | copy-start | bytes 1540
  168.8 9.0 %copy-start.50 = (f32[16,512]{1,0:T(8,128)S(1)}, f32[16,512]{1,0:T(8,128)}, u32[]{:S(2)}) copy-start(f32[16,512]{1,0:T(8,128)} %copy-done.49) | copy-start | bytes 98308
  169.6 8.7 %collective-permute-start.4 = (bf16[16,1,16,256]{3,2,1,0:T(8,128)(2,1)S(1)}, bf16[16,1,16,256]{3,2,1,0:T(8,128)(2,1)S(1)}, u32[]{:S(2)}, u32[]{:S(2)}) collective-permute-start(bf16[16,1,16,256]{3,2,1,0:T(8,128)(2,1)S(1)} %get-tuple-element.81), channel_id=1, source_target_pairs={{0,1},{1,2},{2,3},{4,5},{5,6},{6,7},{8,9},{9,10},{10,11},{12,13},{... | collective-permute-start | bytes 393224 | tf_op jit(solution)/shard_map/ppermute | solution.py:53
  171.6 6.7 %collective-permute-start.5 = (bf16[16,1,16,256]{3,2,1,0:T(8,128)(2,1)S(1)}, bf16[16,1,16,256]{3,2,1,0:T(8,128)(2,1)S(1)}, u32[]{:S(2)}, u32[]{:S(2)}) collective-permute-start(bf16[16,1,16,256]{3,2,1,0:T(8,128)(2,1)S(1)} %get-tuple-element.82), channel_id=1, source_target_pairs={{1,0},{2,1},{3,2},{5,4},{6,5},{7,6},{9,8},{10,9},{11,10},{13,12},{... | collective-permute-start | bytes 393224 | tf_op jit(solution)/shard_map/ppermute | solution.py:54
  181.7 25.4 %copy-start.53 = (f32[512]{0:T(512)S(1)}, f32[512]{0:T(512)}, u32[]{:S(2)}) copy-start(f32[512]{0:T(512)} %copy-done.52) | copy-start | bytes 6148
  181.7 25.4 %copy-start.61 = (f32[512]{0:T(512)S(1)}, f32[512]{0:T(512)}, u32[]{:S(2)}) copy-start(f32[512]{0:T(512)} %param.23) | copy-start | bytes 6148
  184.1 21.7 %all-to-all-start.6 = ((f32[32,8,128]{2,1,0:T(8,128)}), f32[32,8,128]{2,1,0:T(8,128)S(1)}, u32[]{:S(2)}, u32[]{:S(2)}) async-start(f32[32,8,128]{2,1,0:T(8,128)} %broadcast_in_dim.36), calls=%async_computation.6 | async-start | bytes 262144 | tf_op jit(solution)/shard_map/all_to_all | solution.py:17
  217.6 19.9 %copy-start.10 = (bf16[1024,2,256]{2,1,0:T(2,128)(2,1)}, bf16[1024,2,256]{2,1,0:T(2,128)(2,1)S(1)}, u32[]{:S(2)}) copy-start(bf16[1024,2,256]{2,1,0:T(2,128)(2,1)S(1)} %reshape.507) | copy-start | bytes 3145732
  255.5 10.8 %all-to-all-start.7 = ((f32[32,8,128]{2,1,0:T(8,128)}), f32[32,8,128]{2,1,0:T(8,128)S(1)}, u32[]{:S(2)}, u32[]{:S(2)}) async-start(f32[32,8,128]{2,1,0:T(8,128)} %broadcast_in_dim.38), calls=%async_computation.7 | async-start | bytes 262144 | tf_op jit(solution)/shard_map/all_to_all | solution.py:17
  263.1 8.3 %copy-start.30 = (bf16[1024,2,128]{0,2,1:T(8,128)(2,1)S(1)}, bf16[1024,2,128]{0,2,1:T(8,128)(2,1)}, u32[]{:S(2)}) copy-start(bf16[1024,2,128]{0,2,1:T(8,128)(2,1)} %copy.159) | copy-start | bytes 1572868
  266.3 25.7 %all-to-all-start.12 = ((bf16[32,96,128]{2,1,0:T(8,128)(2,1)}), bf16[32,96,128]{2,1,0:T(8,128)(2,1)S(1)}, u32[]{:S(2)}, u32[]{:S(2)}) async-start(bf16[32,96,128]{2,1,0:T(8,128)(2,1)} %bitcast.69), calls=%async_computation.12 | async-start | bytes 1572864 | tf_op jit(solution)/shard_map/all_to_all | solution.py:39
  278.0 118.4 %copy-start.63 = (f32[256]{0:T(256)}, f32[256]{0:T(256)S(1)}, u32[]{:S(2)}) copy-start(f32[256]{0:T(256)S(1)} %get-tuple-element.88) | copy-start | bytes 3076
  282.2 13.6 %copy-start.25 = (bf16[1024,2,128]{0,2,1:T(8,128)(2,1)S(1)}, bf16[1024,2,128]{0,2,1:T(8,128)(2,1)}, u32[]{:S(2)}) copy-start(bf16[1024,2,128]{0,2,1:T(8,128)(2,1)} %copy.165) | copy-start | bytes 1572868
  292.0 19.3 %all-to-all-start.8 = ((bf16[32,64,128]{2,1,0:T(8,128)(2,1)}), bf16[32,64,128]{2,1,0:T(8,128)(2,1)}, u32[]{:S(2)}, u32[]{:S(2)}) async-start(bf16[32,64,128]{2,1,0:T(8,128)(2,1)} %reshape.517), calls=%async_computation.8 | async-start | bytes 1048576 | tf_op jit(solution)/shard_map/all_to_all | solution.py:39
  311.3 32.4 %all-to-all-start.10 = ((bf16[32,144,128]{2,1,0:T(8,128)(2,1)}), bf16[32,144,128]{2,1,0:T(8,128)(2,1)}, u32[]{:S(2)}, u32[]{:S(2)}) async-start(bf16[32,144,128]{2,1,0:T(8,128)(2,1)} %convert_element_type.158), calls=%async_computation.10 | async-start | bytes 2359296 | tf_op jit(solution)/shard_map/all_to_all | solution.py:39
  344.7 19.1 %all-to-all-start.9 = ((bf16[32,64,128]{2,1,0:T(8,128)(2,1)}), bf16[32,64,128]{2,1,0:T(8,128)(2,1)S(1)}, u32[]{:S(2)}, u32[]{:S(2)}) async-start(bf16[32,64,128]{2,1,0:T(8,128)(2,1)} %broadcast_in_dim.39), calls=%async_computation.9 | async-start | bytes 1048576 | tf_op jit(solution)/shard_map/all_to_all | solution.py:17
  364.7 23.7 %all-to-all-start.13 = ((bf16[32,96,128]{2,1,0:T(8,128)(2,1)}), bf16[32,96,128]{2,1,0:T(8,128)(2,1)S(1)}, u32[]{:S(2)}, u32[]{:S(2)}) async-start(bf16[32,96,128]{2,1,0:T(8,128)(2,1)} %broadcast_in_dim.41), calls=%async_computation.13 | async-start | bytes 1572864 | tf_op jit(solution)/shard_map/all_to_all | solution.py:17
  389.6 6.9 %copy-start.58 = (f32[256]{0:T(256)S(1)}, f32[256]{0:T(256)}, u32[]{:S(2)}) copy-start(f32[256]{0:T(256)} %copy-done.57) | copy-start | bytes 3076
  389.6 32.8 %all-to-all-start.11 = ((bf16[32,144,128]{2,1,0:T(8,128)(2,1)}), bf16[32,144,128]{2,1,0:T(8,128)(2,1)}, u32[]{:S(2)}, u32[]{:S(2)}) async-start(bf16[32,144,128]{2,1,0:T(8,128)(2,1)} %broadcast_in_dim.40), calls=%async_computation.11 | async-start | bytes 2359296 | tf_op jit(solution)/shard_map/all_to_all | solution.py:17
  405.5 19.9 %copy-start.1 = (bf16[256,1024]{1,0:T(8,128)(2,1)S(1)}, bf16[256,1024]{1,0:T(8,128)(2,1)}, u32[]{:S(2)}) copy-start(bf16[256,1024]{1,0:T(8,128)(2,1)} %param.30) | copy-start | bytes 1572868
  (45 other events, 117.0 us)

commit v2 on v1

v2 whole, which is shorter than its diff:
```python
import functools

import jax
import jax.numpy as jnp
from jax import lax
from jax.experimental import pallas as pl
from jax.experimental.pallas import tpu as pltpu
from jax.sharding import PartitionSpec as P

EPSILON = 1e-05
HIGHEST = lax.Precision.HIGHEST
ALL = ("batch", "narrow")
F32 = jnp.float32
BF16 = jnp.bfloat16
COLS = 16
LANES = 128


def device_count():
    return lax.axis_size("batch") * lax.axis_size("narrow")


def halo(top, bottom):
    count = lax.axis_size("narrow")
    low = lax.ppermute(bottom, "narrow", [(i, i + 1) for i in range(count - 1)])
    high = lax.ppermute(top, "narrow", [(i + 1, i) for i in range(count - 1)])
    return low, high


def exchange(block):
    return lax.all_to_all(block, ALL, 0, 0)


def sum_weights(*parts):
    count = device_count()
    flat = jnp.concatenate([part.astype(BF16).reshape(-1, LANES) for part in parts])
    rows = flat.shape[0]
    per = -(-rows // (count * 16)) * 16
    flat = jnp.pad(flat, ((0, per * count - rows), (0, 0))).reshape(count, per, LANES)
    mine = jnp.sum(exchange(flat).astype(F32), 0).astype(BF16)
    full = exchange(jnp.broadcast_to(mine[None], (count,) + mine.shape)).reshape(-1, LANES)
    outs, start = [], 0
    for part in parts:
        length = part.size // LANES
        outs.append(full[start : start + length].astype(F32).reshape(part.shape))
        start += length
    return outs


def sigmoid(values):
    return 0.5 * jnp.tanh(0.5 * values) + 0.5


def wide(mask, width):
    return jnp.concatenate([mask] * (width // LANES), axis=1) if width > LANES else mask


def inside(meta, image, start, count):
    pixel = lax.broadcasted_iota(jnp.int32, (count * COLS, LANES), 0)
    row = (pixel >> 4) + (meta[0] + start)
    col = pixel & (COLS - 1)
    side = 12 + 2 * meta[2 + image]
    return jnp.where((row < side) & (row >= 0) & (col < side), 1.0, 0.0).astype(F32)


def area_of(meta, image):
    side = (12 + 2 * meta[2 + image]).astype(F32)
    return side * side


def row_of(block, first, count):
    return jnp.concatenate([block[first + k : first + k + 1] for k in range(count)], axis=1)


def put_row(ref, first, vector):
    for k in range(vector.shape[1] // LANES):
        ref[0, first + k : first + k + 1, :] = vector[:, k * LANES : (k + 1) * LANES]


def spread(ref):
    block = ref[0]

    def step(k, carry):
        ref[k] = block
        return carry

    lax.fori_loop(1, ref.shape[0], step, 0)


def fold(values):
    return jnp.sum(values.reshape(-1, 8, values.shape[-1]), 0)


def total(block):
    return jnp.sum(block, 0, keepdims=True)


def stats(totals, squares, counted):
    center = totals / counted
    return center, lax.rsqrt(squares / counted - center * center + EPSILON)


def shifted(values):
    count, width = values.shape
    col = lax.broadcasted_iota(jnp.int32, (count, LANES), 0) & (COLS - 1)
    has_left = wide(jnp.where(col > 0, 1.0, 0.0).astype(F32), width)
    has_right = wide(jnp.where(col < COLS - 1, 1.0, 0.0).astype(F32), width)
    left = pltpu.roll(values, 1, 0) * has_left
    right = pltpu.roll(values, count - 1, 0) * has_right
    return left.astype(BF16), values.astype(BF16), right.astype(BF16)


def dot(a, b, dims=((1,), (0,)), precision=None):
    return lax.dot_general(a, b, (dims, ((), ())), precision=precision, preferred_element_type=F32)


def call(kernel, outs, args, scratch=(), megabytes=32, flops=0, **sizes):
    moved = sum(a.size * a.dtype.itemsize for a in args) + sum(
        functools.reduce(lambda x, y: x * y, s) * jnp.dtype(t).itemsize for s, t in outs
    )
    return pl.pallas_call(
        functools.partial(kernel, **sizes),
        out_shape=[jax.ShapeDtypeStruct(s, t) for s, t in outs],
        in_specs=[pl.BlockSpec(memory_space=pltpu.SMEM)]
        + [pl.BlockSpec(memory_space=pltpu.VMEM)] * (len(args) - 1),
        out_specs=[pl.BlockSpec(memory_space=pltpu.VMEM)] * len(outs),
        scratch_shapes=[pltpu.VMEM(s, t) for s, t in scratch],
        compiler_params=pltpu.CompilerParams(vmem_limit_bytes=megabytes << 20),
        cost_estimate=pl.CostEstimate(flops=flops, bytes_accessed=moved, transcendentals=0),
    )(*args)


def reduce_kernel(meta, x, w, pre, top, bottom, pay, acc, *, blocks, rows):
    slab = rows * COLS
    acc[...] = jnp.zeros_like(acc)
    group = 4

    def step(g, carry):
        base = pl.multiple_of(g * group * slab, group * slab)
        out = dot(x[pl.ds(base, group * slab), :], w[...])
        for j in range(group):
            image = g * group + j
            mask = inside(meta, image, 0, rows)
            part = out[j * slab : (j + 1) * slab] * wide(mask, out.shape[1])
            pre[pl.ds(pl.multiple_of(image * slab, slab), slab), :] = part
            edge = pl.ds(pl.multiple_of(image * COLS, COLS), COLS)
            top[edge, :] = part[:COLS]
            bottom[edge, :] = part[slab - COLS :]
            acc[0] += fold(part)
            acc[1] += fold(part * part)
            acc[2, :, :LANES] += fold(mask)
        return carry

    lax.fori_loop(0, blocks // group, step, 0)
    put_row(pay, 0, total(acc[0]))
    put_row(pay, 2, total(acc[1]))
    put_row(pay, 4, total(acc[2, :, :LANES]))
    pay[0, 5:8, :] = jnp.zeros((3, LANES), F32)
    spread(pay)


def split_kernel(
    meta, got, pre, low, high, gain, shift, w, hid, out, top, bottom, pay, stat, acc, *, blocks, rows
):
    slab = rows * COLS
    sums = jnp.sum(got[...], 0)
    counted = row_of(jnp.concatenate([sums[4:5]] * 2, 0), 0, 2)
    center, inv = stats(row_of(sums, 0, 2), row_of(sums, 2, 2), counted)
    stat[...] = jnp.zeros_like(stat)
    stat[0:1] = center
    stat[1:2] = inv
    stat[2:3] = counted
    scale = inv * gain[...]
    offset = shift[...]

    def prepare(i, carry):
        edge = pl.ds(pl.multiple_of(i * COLS, COLS), COLS)
        own = pl.ds(pl.multiple_of(i * slab, slab), slab)
        tall = jnp.concatenate([low[edge, :], pre[own, :], high[edge, :]], axis=0)
        z = (tall - center) * scale + offset
        mask = wide(inside(meta, i, -1, rows + 2), z.shape[1])
        left, middle, right = shifted(z * sigmoid(z) * mask)
        hid[0, i] = left
        hid[1, i] = middle
        hid[2, i] = right
        return carry

    lax.fori_loop(0, blocks, prepare, 0)
    acc[...] = jnp.zeros_like(acc)
    group = 4

    def step(g, carry):
        for half in range(2):
            lanes = slice(half * 128, half * 128 + 128)
            outs = slice(half * 256, half * 256 + 256)
            lhs = jnp.concatenate(
                [
                    hid[dx, pl.ds(g * group, group), dy * COLS : dy * COLS + slab, lanes].reshape(
                        group * slab, 128
                    )
                    for dy in range(3)
                    for dx in range(3)
                ],
                axis=1,
            )
            value = dot(lhs, w[:, :, half].reshape(9 * 128, 256))
            for j in range(group):
                image = g * group + j
                mask = inside(meta, image, 0, rows)
                part = value[j * slab : (j + 1) * slab] * wide(mask, 256)
                out[pl.ds(pl.multiple_of(image * slab, slab), slab), outs] = part
                edge = pl.ds(pl.multiple_of(image * COLS, COLS), COLS)
                top[edge, outs] = part[:COLS]
                bottom[edge, outs] = part[slab - COLS :]
                acc[0, :, outs] += fold(part)
                acc[1, :, outs] += fold(part * part)
        return carry

    lax.fori_loop(0, blocks // group, step, 0)
    put_row(pay, 0, total(acc[0]))
    put_row(pay, 4, total(acc[1]))
    spread(pay)


def pool_kernel(
    meta, got, stat, pre, gain, shift, w, hid, pooled, pay, stat2, *, blocks, rows
):
    slab = rows * COLS
    sums = jnp.sum(got[...], 0)
    counted = jnp.concatenate([stat[2:3]] * 2, axis=1)
    center, inv = stats(row_of(sums, 0, 4), row_of(sums, 4, 4), counted)
    stat2[...] = jnp.zeros_like(stat2)
    stat2[0:1] = center
    stat2[1:2] = inv
    stat2[2:3] = counted
    scale = inv * gain[...]
    offset = shift[...]

    def step(i, carry):
        own = pl.ds(pl.multiple_of(i * slab, slab), slab)
        mask = wide(inside(meta, i, 0, rows), 256)
        summed = None
        for half in range(2):
            lanes = slice(half * 256, half * 256 + 256)
            z = (pre[own, lanes] - center[:, lanes]) * scale[:, lanes] + offset[:, lanes]
            value = (z * sigmoid(z) * mask).astype(BF16)
            hid[own, lanes] = value
            part = fold(value.astype(F32))
            summed = part if summed is None else summed + part
        pooled[pl.ds(i, 1), :] = total(summed) / area_of(meta, i)
        return carry

    lax.fori_loop(0, blocks, step, 0)
    pay[0] = dot(pooled[...], w[...], precision=HIGHEST)
    spread(pay)


def squeeze_stats(block):
    return stats(total(block), total(block * block), float(block.shape[0]))


def expand_kernel(
    meta, got, hid, gain, shift, we, bias, w, mix, pre, att, hsq, znorm, zall, pay, stat_sq, acc, *, blocks, rows, parts
):
    slab = rows * COLS
    bands = got.shape[0] // parts
    for b in range(bands):
        block = got[b * parts]
        for k in range(1, parts):
            block = block + got[b * parts + k]
        znorm[b * blocks : (b + 1) * blocks, :] = block
    center, inv = squeeze_stats(znorm[...])
    stat_sq[...] = jnp.zeros_like(stat_sq)
    stat_sq[0:1] = center
    stat_sq[1:2] = inv
    normed = (znorm[...] - center) * inv
    znorm[...] = normed
    zall[...] = normed * gain[...] + shift[...]
    own_z = zall[pl.ds(pl.multiple_of(meta[1] * blocks, blocks), blocks), :]
    hidden = own_z * jax.nn.sigmoid(own_z)
    hsq[...] = hidden
    logits = dot(hidden, we[...], precision=HIGHEST) + bias[...]
    first = logits[:, :256]
    second = logits[:, 256:]
    ceiling = jnp.maximum(first, second)
    exp_first = jnp.exp(first - ceiling)
    exp_second = jnp.exp(second - ceiling)
    att[:, :256] = exp_first / (exp_first + exp_second)
    att[:, 256:] = exp_second / (exp_first + exp_second)
    acc[...] = jnp.zeros_like(acc)
    group = 4

    def step(g, carry):
        for j in range(group):
            image = g * group + j
            own = pl.ds(pl.multiple_of(image * slab, slab), slab)
            weights = att[pl.ds(image, 1), :]
            mix[own, :] = (
                weights[:, :256] * hid[own, :256].astype(F32)
                + weights[:, 256:] * hid[own, 256:].astype(F32)
            ).astype(BF16)
        many = pl.ds(pl.multiple_of(g * group * slab, group * slab), group * slab)
        for k in range(4):
            lanes = slice(k * 256, k * 256 + 256)
            value = dot(mix[many, :], w[:, lanes]).astype(BF16)
            pre[many, lanes] = value
            value = value.astype(F32)
            acc[0, :, lanes] += fold(value)
            acc[1, :, lanes] += fold(value * value)
        return carry

    lax.fori_loop(0, blocks // group, step, 0)
    put_row(pay, 0, total(acc[0]))
    put_row(pay, 8, total(acc[1]))
    spread(pay)


def residual_kernel(
    meta, got, stat, x, pre, cot, gain, shift, out, grad, pay, stat3, acc, *, blocks, rows
):
    slab = rows * COLS
    sums = jnp.sum(got[...], 0)
    counted = jnp.concatenate([stat[2:3]] * 4, axis=1)
    center, inv = stats(row_of(sums, 0, 8), row_of(sums, 8, 8), counted)
    stat3[...] = jnp.zeros_like(stat3)
    stat3[0:1] = center
    stat3[1:2] = inv
    stat3[2:3] = counted
    acc[...] = jnp.zeros_like(acc)

    def step(i, carry):
        own = pl.ds(pl.multiple_of(i * slab, slab), slab)
        mask = wide(inside(meta, i, 0, rows), 256)
        for k in range(4):
            lanes = slice(k * 256, k * 256 + 256)
            normed = (pre[own, lanes].astype(F32) - center[:, lanes]) * inv[:, lanes]
            value = normed * gain[:, lanes] + shift[:, lanes] + x[own, lanes].astype(F32)
            part = sigmoid(value)
            silu = value * part
            out[own, lanes] = (silu * mask).astype(BF16)
            slope = part + silu * (1.0 - part)
            back = cot[own, lanes].astype(F32) * mask * slope
            grad[own, lanes] = back
            acc[0, :, lanes] += fold(back)
            acc[1, :, lanes] += fold(back * normed)
        return carry

    lax.fori_loop(0, blocks, step, 0)
    put_row(pay, 0, total(acc[0]))
    put_row(pay, 8, total(acc[1]))
    spread(pay)


def back_terms(stat, gain, shift_sum, gain_sum):
    center, inv, counted = stat[0:1], stat[1:2], stat[2:3]
    a = gain * inv
    d = -a * inv * (gain_sum / counted)
    b = -a * (shift_sum / counted) - d * center
    return a, b, d


def mixture_kernel(
    meta, got, stat3, pre, grad, gain, w, hid, att, we, gexp, gmix, top, bottom, glog, pay, sums_out, *, blocks, rows
):
    slab = rows * COLS
    sums = jnp.sum(got[...], 0)
    shift_sum, gain_sum = row_of(sums, 0, 8), row_of(sums, 8, 8)
    sums_out[0:1] = shift_sum
    sums_out[1:2] = gain_sum
    a, b, d = back_terms(stat3, gain[...], shift_sum, gain_sum)
    group = 4

    def step(g, carry):
        many = pl.ds(pl.multiple_of(g * group * slab, group * slab), group * slab)
        for j in range(group):
            image = g * group + j
            own = pl.ds(pl.multiple_of(image * slab, slab), slab)
            mask = wide(inside(meta, image, 0, rows), 256)
            for k in range(4):
                lanes = slice(k * 256, k * 256 + 256)
                gexp[own, lanes] = (
                    mask
                    * (
                        a[:, lanes] * grad[own, lanes]
                        + b[:, lanes]
                        + d[:, lanes] * pre[own, lanes].astype(F32)
                    )
                ).astype(BF16)
        value = dot(gexp[many, :], w[...], ((1,), (1,))).astype(BF16)
        gmix[many, :] = value
        value = value.astype(F32)
        for j in range(group):
            image = g * group + j
            own = pl.ds(pl.multiple_of(image * slab, slab), slab)
            edge = pl.ds(pl.multiple_of(image * COLS, COLS), COLS)
            part = value[j * slab : (j + 1) * slab]
            top[edge, :] = part[:COLS].astype(BF16)
            bottom[edge, :] = part[slab - COLS :].astype(BF16)
            for half in range(2):
                lanes = slice(half * 256, half * 256 + 256)
                glog[pl.ds(image, 1), lanes] = total(fold(part * hid[own, lanes].astype(F32)))
        return carry

    lax.fori_loop(0, blocks // group, step, 0)
    first, second = att[:, :256], att[:, 256:]
    inner = first * glog[:, :256] + second * glog[:, 256:]
    logits = jnp.concatenate(
        [first * (glog[:, :256] - inner), second * (glog[:, 256:] - inner)], axis=1
    )
    glog[...] = logits
    pay[0] = dot(logits, we[...], ((1,), (1,)), HIGHEST)
    spread(pay)


def expand_grad_kernel(meta, mix, gexp, hsq, glog, out, excite, bias):
    for k in range(4):
        lanes = slice(k * 256, k * 256 + 256)
        out[:, lanes] = dot(mix[...], gexp[:, lanes], ((0,), (0,))).astype(BF16)
    excite[...] = dot(hsq[...], glog[...], ((0,), (0,)), HIGHEST)
    bias[...] = jnp.zeros_like(bias)
    put = total(glog[...])
    for k in range(4):
        bias[k : k + 1, :] = put[:, k * LANES : (k + 1) * LANES]


def hidden_kernel(
    meta, got, znorm, zall, hsq_gain, stat_sq, pooled, wsq, att, gmix, pre, stat2, gain, shift,
    dz, gpool, squeeze, pay, sums_out, acc, full, *, blocks, rows, parts
):
    slab = rows * COLS
    bands = got.shape[0] // parts
    for b in range(bands):
        block = got[b * parts]
        for k in range(1, parts):
            block = block + got[b * parts + k]
        full[b * blocks : (b + 1) * blocks, :] = block
    z = zall[...]
    part = jax.nn.sigmoid(z)
    grad_z = full[...] * (part * (1.0 + z * (1.0 - part)))
    full[...] = grad_z
    images = float(bands * blocks)
    shift_sum = total(grad_z)
    gain_sum = total(grad_z * znorm[...])
    sums_out[...] = jnp.zeros_like(sums_out)
    sums_out[0:1] = shift_sum
    sums_out[1:2] = gain_sum
    mine = pl.ds(pl.multiple_of(meta[1] * blocks, blocks), blocks)
    grad_pre = (
        hsq_gain[...]
        * stat_sq[1:2]
        * (full[mine, :] - shift_sum / images - znorm[mine, :] * (gain_sum / images))
    )
    squeeze[...] = dot(pooled[...], grad_pre, ((0,), (0,)), HIGHEST)
    gpool[...] = dot(grad_pre, wsq[...], ((1,), (1,)), HIGHEST)
    for i in range(blocks):
        gpool[i : i + 1, :] = gpool[i : i + 1, :] / area_of(meta, i)
    center, inv = stat2[0:1], stat2[1:2]
    acc[...] = jnp.zeros_like(acc)

    def step(i, carry):
        own = pl.ds(pl.multiple_of(i * slab, slab), slab)
        mask = wide(inside(meta, i, 0, rows), 256)
        mixed = gmix[own, :].astype(F32)
        pool = gpool[pl.ds(i, 1), :]
        for half in range(2):
            lanes = slice(half * 256, half * 256 + 256)
            normed = (pre[own, lanes] - center[:, lanes]) * inv[:, lanes]
            value = normed * gain[:, lanes] + shift[:, lanes]
            sig = sigmoid(value)
            slope = sig * (1.0 + value * (1.0 - sig))
            hidden = (mixed * att[pl.ds(i, 1), lanes] + pool).astype(BF16).astype(F32)
            back = hidden * mask * slope
            dz[own, lanes] = back
            acc[0, :, lanes] += fold(back)
            acc[1, :, lanes] += fold(back * normed)
        return carry

    lax.fori_loop(0, blocks, step, 0)
    put_row(pay, 0, total(acc[0]))
    put_row(pay, 4, total(acc[1]))
    spread(pay)


def conv_kernel(
    meta, got, stat2, gain2, shift2, dz, pre2, low2, high2, lowm, highm, att, gpool, w, pre, stat, gain, shift,
    gsplit, out, pay, sums_out, tall, acc, *, blocks, rows
):
    slab = rows * COLS
    sums = jnp.sum(got[...], 0)
    shift_sum, gain_sum = row_of(sums, 0, 4), row_of(sums, 4, 4)
    sums_out[0:1] = shift_sum
    sums_out[1:2] = gain_sum
    a, b, d = back_terms(stat2, gain2[...], shift_sum, gain_sum)
    center2, inv2 = stat2[0:1], stat2[1:2]

    def prepare(i, carry):
        own = pl.ds(pl.multiple_of(i * slab, slab), slab)
        edge = pl.ds(pl.multiple_of(i * COLS, COLS), COLS)
        mask = inside(meta, i, -1, rows + 2)
        for half in range(2):
            lanes = slice(half * 256, half * 256 + 256)

            def edge_grad(values, mixed, keep):
                z = (values[edge, lanes] - center2[:, lanes]) * inv2[:, lanes]
                z = z * gain2[:, lanes] + shift2[:, lanes]
                sig = sigmoid(z)
                slope = sig * (1.0 + z * (1.0 - sig))
                hidden = (
                    mixed[edge, :].astype(F32) * att[pl.ds(i, 1), lanes] + gpool[pl.ds(i, 1), :]
                ).astype(BF16)
                return hidden.astype(F32) * keep * slope

            keep_low = wide(mask[:COLS], 256)
            keep_high = wide(mask[slab + COLS :], 256)
            grads = jnp.concatenate(
                [edge_grad(low2, lowm, keep_low), dz[own, lanes], edge_grad(high2, highm, keep_high)],
                axis=0,
            )
            values = jnp.concatenate([low2[edge, lanes], pre2[own, lanes], high2[edge, lanes]], axis=0)
            back = wide(mask, 256) * (a[:, lanes] * grads + b[:, lanes] + d[:, lanes] * values)
            left, middle, right = shifted(back)
            tall[0, i, :, lanes] = left
            tall[1, i, :, lanes] = middle
            tall[2, i, :, lanes] = right
            gsplit[own, lanes] = middle[COLS : COLS + slab]
        return carry

    lax.fori_loop(0, blocks, prepare, 0)
    acc[...] = jnp.zeros_like(acc)
    center, inv = stat[0:1], stat[1:2]
    group = 4

    def step(g, carry):
        for half in range(2):
            lanes = slice(half * 256, half * 256 + 256)
            outs = slice(half * 128, half * 128 + 128)
            value = None
            for dy in range(3):
                for dx in range(3):
                    lhs = tall[
                        2 - dx, pl.ds(g * group, group), (2 - dy) * COLS : (2 - dy) * COLS + slab, lanes
                    ].reshape(group * slab, 256)
                    part = dot(lhs, w[dy, dx, half], ((1,), (1,)))
                    value = part if value is None else value + part
            for j in range(group):
                image = g * group + j
                own = pl.ds(pl.multiple_of(image * slab, slab), slab)
                mask = inside(meta, image, 0, rows)
                normed = (pre[own, outs] - center[:, outs]) * inv[:, outs]
                z = normed * gain[:, outs] + shift[:, outs]
                sig = sigmoid(z)
                slope = sig * (1.0 + z * (1.0 - sig))
                back = value[j * slab : (j + 1) * slab] * mask * slope
                out[own, outs] = back
                acc[0, :, outs] += fold(back)
                acc[1, :, outs] += fold(back * normed)
        return carry

    lax.fori_loop(0, blocks // group, step, 0)
    put_row(pay, 0, total(acc[0]))
    put_row(pay, 2, total(acc[1]))
    pay[0, 4:8, :] = jnp.zeros((4, LANES), F32)
    spread(pay)


def split_grad_kernel(meta, hid, gsplit, out, *, blocks, rows):
    slab = rows * COLS
    for half in range(2):
        lanes = slice(half * 128, half * 128 + 128)
        grads = gsplit[:, half * 256 : half * 256 + 256]
        for dy in range(3):
            lhs = jnp.concatenate(
                [
                    hid[dx, :, dy * COLS : dy * COLS + slab, lanes].reshape(blocks * slab, 128)
                    for dx in range(3)
                ],
                axis=1,
            )
            value = dot(lhs, grads, ((0,), (0,))).astype(BF16)
            for dx in range(3):
                out[dy, dx, half] = value[dx * 128 : (dx + 1) * 128]


def input_kernel(meta, got, stat, gain, dz, pre, w, x, grad, out, wgrad, sums_out, small, *, blocks, rows):
    slab = rows * COLS
    sums = jnp.sum(got[...], 0)
    shift_sum, gain_sum = row_of(sums, 0, 2), row_of(sums, 2, 2)
    sums_out[0:1] = shift_sum
    sums_out[1:2] = gain_sum
    a, b, d = back_terms(stat, gain[...], shift_sum, gain_sum)
    group = 4

    def step(g, carry):
        many = pl.ds(pl.multiple_of(g * group * slab, group * slab), group * slab)
        for j in range(group):
            image = g * group + j
            own = pl.ds(pl.multiple_of(image * slab, slab), slab)
            mask = wide(inside(meta, image, 0, rows), 256)
            small[own, :] = (mask * (a * dz[own, :] + b + d * pre[own, :])).astype(BF16)
        for k in range(4):
            lanes = slice(k * 256, k * 256 + 256)
            value = dot(small[many, :], w[lanes, :], ((1,), (1,)))
            for j in range(group):
                image = g * group + j
                own = pl.ds(pl.multiple_of(image * slab, slab), slab)
                mask = wide(inside(meta, image, 0, rows), 256)
                out[own, lanes] = (
                    (value[j * slab : (j + 1) * slab] + grad[own, lanes]) * mask
                ).astype(BF16)
        return carry

    lax.fori_loop(0, blocks // group, step, 0)
    wgrad[...] = dot(x[...], small[...], ((0,), (0,))).astype(BF16)


def body(
    inputs,
    image_class,
    weight_reduce,
    gain_reduce,
    shift_reduce,
    weight_split,
    gain_split,
    shift_split,
    weight_squeeze,
    gain_squeeze,
    shift_squeeze,
    weight_excite,
    bias_excite,
    weight_expand,
    gain_expand,
    shift_expand,
    cotangent,
):
    blocks, rows, cols, channels = inputs.shape
    mid = weight_reduce.shape[1]
    inter = weight_squeeze.shape[1]
    parts = lax.axis_size("narrow")
    count = device_count()
    pixels = blocks * rows * cols
    slab = rows * cols
    edge = blocks * cols
    images = blocks * lax.axis_size("batch")
    meta = jnp.concatenate(
        [
            (lax.axis_index("narrow") * rows).astype(jnp.int32)[None],
            lax.axis_index("batch").astype(jnp.int32)[None],
            image_class,
        ]
    )
    x = inputs.reshape(pixels, channels)
    cot = cotangent.reshape(pixels, channels)
    row = lambda v: v.reshape(1, -1)
    gain1, shift1 = row(gain_reduce), row(shift_reduce)
    gain2, shift2 = row(gain_split), row(shift_split)
    gain3, shift3 = row(gain_expand), row(shift_expand)
    gain_sq, shift_sq = row(gain_squeeze), row(shift_squeeze)
    sizes = dict(blocks=blocks, rows=rows)
    small = 2 * pixels * channels * mid
    large = 2 * pixels * 9 * 128 * 512

    pre1, top, bottom, pay = call(
        reduce_kernel,
        [((pixels, mid), F32), ((edge, mid), F32), ((edge, mid), F32), ((count, 8, LANES), F32)],
        [meta, x, weight_reduce],
        [((3, 8, mid), F32)],
        flops=small,
        **sizes,
    )
    low, high = halo(top, bottom)
    hid1, pre2, top, bottom, pay, stat1 = call(
        split_kernel,
        [
            ((3, blocks, slab + 2 * cols, mid), BF16),
            ((pixels, 2 * mid), F32),
            ((edge, 2 * mid), F32),
            ((edge, 2 * mid), F32),
            ((count, 8, LANES), F32),
            ((8, mid), F32),
        ],
        [meta, exchange(pay), pre1, low, high, gain1, shift1, weight_split],
        [((2, 8, 2 * mid), F32)],
        flops=large,
        **sizes,
    )
    low2, high2 = halo(top, bottom)
    hid2, pooled, pay, stat2 = call(
        pool_kernel,
        [
            ((pixels, 2 * mid), BF16),
            ((blocks, mid), F32),
            ((count, blocks, inter), F32),
            ((8, 2 * mid), F32),
        ],
        [meta, exchange(pay), stat1, pre2, gain2, shift2, weight_squeeze],
        **sizes,
    )
    mix, pre3, att, hsq, znorm, zall, pay, stat_sq = call(
        expand_kernel,
        [
            ((pixels, mid), BF16),
            ((pixels, channels), BF16),
            ((blocks, 2 * mid), F32),
            ((blocks, inter), F32),
            ((images, inter), F32),
            ((images, inter), F32),
            ((count, 16, LANES), F32),
            ((8, inter), F32),
        ],
        [
            meta,
            exchange(pay),
            hid2,
            gain_sq,
            shift_sq,
            weight_excite,
            row(bias_excite),
            weight_expand,
        ],
        [((2, 8, channels), F32)],
        flops=small,
        parts=parts,
        **sizes,
    )
    out, grad_res, pay, stat3 = call(
        residual_kernel,
        [
            ((pixels, channels), BF16),
            ((pixels, channels), F32),
            ((count, 16, LANES), F32),
            ((8, channels), F32),
        ],
        [meta, exchange(pay), stat1, x, pre3, cot, gain3, shift3],
        [((2, 8, channels), F32)],
        **sizes,
    )
    gexp, gmix, top, bottom, glog, pay, sums3 = call(
        mixture_kernel,
        [
            ((pixels, channels), BF16),
            ((pixels, mid), BF16),
            ((edge, mid), BF16),
            ((edge, mid), BF16),
            ((blocks, 2 * mid), F32),
            ((count, blocks, inter), F32),
            ((2, channels), F32),
        ],
        [meta, exchange(pay), stat3, pre3, grad_res, gain3, weight_expand, hid2, att, weight_excite],
        flops=small,
        **sizes,
    )
    lowm, highm = halo(top, bottom)
    expand_part, excite_part, bias_part = call(
        expand_grad_kernel,
        [((mid, channels), BF16), ((inter, 2 * mid), F32), ((8, LANES), F32)],
        [meta, mix, gexp, hsq, glog],
        flops=small,
    )
    dz2, gpool, squeeze_part, pay, sums_sq = call(
        hidden_kernel,
        [
            ((pixels, 2 * mid), F32),
            ((blocks, mid), F32),
            ((mid, inter), F32),
            ((count, 8, LANES), F32),
            ((8, inter), F32),
        ],
        [
            meta,
            exchange(pay),
            znorm,
            zall,
            gain_sq,
            stat_sq,
            pooled,
            weight_squeeze,
            att,
            gmix,
            pre2,
            stat2,
            gain2,
            shift2,
        ],
        [((2, 8, 2 * mid), F32), ((images, inter), F32)],
        parts=parts,
        **sizes,
    )
    gsplit, dz1, pay, sums2 = call(
        conv_kernel,
        [
            ((pixels, 2 * mid), BF16),
            ((pixels, mid), F32),
            ((count, 8, LANES), F32),
            ((2, 2 * mid), F32),
        ],
        [
            meta,
            exchange(pay),
            stat2,
            gain2,
            shift2,
            dz2,
            pre2,
            low2,
            high2,
            lowm,
            highm,
            att,
            gpool,
            weight_split,
            pre1,
            stat1,
            gain1,
            shift1,
        ],
        [((3, blocks, slab + 2 * cols, 2 * mid), BF16), ((2, 8, mid), F32)],
        flops=large,
        **sizes,
    )
    (split_part,) = call(
        split_grad_kernel,
        [(weight_split.shape, BF16)],
        [meta, hid1, gsplit],
        flops=large,
        **sizes,
    )
    input_grad, reduce_part, sums1 = call(
        input_kernel,
        [((pixels, channels), BF16), ((channels, mid), BF16), ((2, mid), F32)],
        [meta, exchange(pay), stat1, gain1, dz1, pre1, weight_reduce, x, grad_res],
        [((pixels, mid), BF16)],
        flops=2 * small,
        **sizes,
    )
    per = -(-(squeeze_part.size // LANES + 8) // count)
    flat = jnp.concatenate([squeeze_part, bias_part])
    flat = jnp.pad(flat, ((0, per * count - flat.shape[0]), (0, 0))).reshape(count, per, LANES)
    mine = jnp.sum(exchange(flat), 0)
    full = exchange(jnp.broadcast_to(mine[None], (count,) + mine.shape)).reshape(-1, LANES)
    squeeze_total = full[:mid]
    bias_total = full[mid : mid + 4].reshape(-1)
    expand_total, excite_total = sum_weights(expand_part, excite_part)
    (split_total,) = sum_weights(split_part)
    (reduce_total,) = sum_weights(reduce_part)
    return (
        out.reshape(inputs.shape),
        input_grad.reshape(inputs.shape),
        reduce_total,
        sums1[1],
        sums1[0],
        split_total,
        sums2[1],
        sums2[0],
        squeeze_total,
        sums_sq[1],
        sums_sq[0],
        excite_total,
        bias_total,
        expand_total,
        sums3[1],
        sums3[0],
    )


def solution(mesh):
    rows = P("batch", "narrow", None, None)
    return jax.shard_map(
        body,
        mesh=mesh,
        in_specs=(rows, P("batch")) + (P(),) * 14 + (rows,),
        out_specs=(rows, rows) + (P(),) * 14,
        check_vma=False,
    )
```

time: 432 us -> 348 us (0.81)
  other arithmetic: 58.8 us -> 8.94 us
  local copies, waits for them, and re-layouts: 101 us -> 58.3 us
  matrix products: 41 us -> 0 us
  blocking collectives: 26 us -> 65.3 us
  Pallas kernels: 0 us -> 38.1 us
  starting transfers between devices: 76.5 us -> 53.9 us
    reshape x37 -> x9, local copies, waits for them, and re-layouts: 62 us -> 10.4 us  [the longest x2 3.25 us: sum_weights(): jnp.pad(flat, ((0, per * count - rows), (0, 0))).reshape(count, per, LANES)]
    dot_general x39 -> x0, matrix products: 41 us -> none  [the longest x9 15.6 us: conv_weight_grad(): jnp.einsum('pgc,pgo->gco', window, grad_out, preferred_element_type=jnp.f...]
    all_to_all x2 -> x5, blocking collectives: 26 us -> 65.3 us  [exchange(): return lax.all_to_all(block, ALL, 0, 0)]
    pallas_call x0 -> x11, Pallas kernels: none -> 38.1 us  [call(): pl.pallas_call(functools.partial(kernel, **sizes), out_shape=[jax.ShapeDt...]
    unnamed x150 -> x158, local copies, waits for them, and re-layouts: 9.6 us -> 37.7 us
    all_to_all x12 -> x11, starting transfers between devices: 65.3 us -> 42.7 us  [exchange(): return lax.all_to_all(block, ALL, 0, 0)]
    reduce_sum x21 -> x4, other arithmetic: 19.9 us -> 2.59 us  [the longest x3 1.46 us: sum_weights(): mine = jnp.sum(exchange(flat).astype(F32), 0).astype(BF16)]
    convert_element_type x8 -> x1, other arithmetic: 17.1 us -> 0.97 us  [sum_weights(): part.astype(BF16).reshape(-1, LANES)]
  transfers between devices with their start and end apart: 18 -> 17, of which waited for: 12 -> 10; matrix products, arithmetic and copies ran while one was open for 15% -> 7% of each run, Pallas kernels for 0% -> 5%
where the time goes in v2:
time: 348 us; the launch traced here: 346 us
  waiting for transfers between devices  120 us (34%)
  blocking collectives  65.3 us (19%)
  local copies, waits for them, and re-layouts  58.3 us (17%)
  starting transfers between devices  53.9 us (15%)
  Pallas kernels  38.1 us (11%)
  other arithmetic  8.94 us (3%)
    all_to_all x11, waiting for transfers between devices, exchange(): return lax.all_to_all(block, ALL, 0, 0)  117 us
    all_to_all x5, blocking collectives, exchange(): return lax.all_to_all(block, ALL, 0, 0)  65.3 us
    all_to_all x11, starting transfers between devices, exchange(): return lax.all_to_all(block, ALL, 0, 0)  42.7 us
    pallas_call x11, Pallas kernels, call(): pl.pallas_call(functools.partial(kernel, **sizes), out_shape=[jax.ShapeDt...  38.1 us
    unnamed x158, local copies, waits for them, and re-layouts  37.7 us
    ppermute x3, starting transfers between devices, halo(): low = lax.ppermute(bottom, 'narrow', [(i, i + 1) for i in range(count - 1)])  7.32 us
  transfers between devices with their start and end apart: 17, of which 10 were waited for; matrix products, arithmetic and copies ran while one was open for 7% of the time, Pallas kernels for 5%

profile of v2, /device:TPU:0, one launch (start us, length us, event | category | flops | bytes accessed | tf_op | source)
XLA Modules:
  0.0 345.7 jit_solution(11012613984567896921)
XLA Ops:
  1.4 1.6 copy-done
  4.0 1.9 shard_map.288
  6.0 2.4 collective-permute-start
  9.7 17.2 %all_to_all.80.got = f32[32,8,128]{2,1,0:T(8,128)S(1)} all-to-all(f32[32,8,128]{2,1,0:T(8,128)S(1)} %get-tuple-element.64), channel_id=1, replica_groups=mesh['batch'=8,'narrow'=4] {'batch','narrow'}, dimensions={0} | all-to-all | bytes 262144 | tf_op jit(solution)/shard_map/all_to_all | solution.py:31
  27.0 4.1 %shard_map.289 = (bf16[3,16,96,256]{3,2,1,0:T(8,128)(2,1)S(1)}, f32[1024,512]{1,0:T(8,128)S(1)}, f32[256,512]{1,0:T(8,128)S(1)}, f32[256,512]{1,0:T(8,128)S(1)},...) custom-call(s32[18]{0:T(128)S(1)} %pad_add_fusion.meta, f32[32,8,128]{2,1,0:T(8,128)S(1)} %all_to_all.80.got, ...), custom_call_target="tpu_custom_call" | custom-call | flops 1207959552 | bytes 8529992 | tf_op jit(solution)/shard_map/pallas_call | solution.py:121
  32.6 10.1 %all_to_all.81.got = f32[32,8,128]{2,1,0:T(8,128)S(1)} all-to-all(f32[32,8,128]{2,1,0:T(8,128)S(1)} %get-tuple-element.68), channel_id=1, replica_groups=mesh['batch'=8,'narrow'=4] {'batch','narrow'}, dimensions={0} | all-to-all | bytes 262144 | tf_op jit(solution)/shard_map/all_to_all | solution.py:31
  42.7 2.2 shard_map.290
  44.9 12.4 %all_to_all.82.got = f32[32,16,128]{2,1,0:T(8,128)S(1)} all-to-all(f32[32,16,128]{2,1,0:T(8,128)S(1)} %get-tuple-element.71), channel_id=1, replica_groups=mesh['batch'=8,'narrow'=4] {'batch','narrow'}, dimensions={0} | all-to-all | bytes 524288 | tf_op jit(solution)/shard_map/all_to_all | solution.py:31
  57.4 2.6 shard_map.291
  60.1 12.7 %all_to_all.83.got = f32[32,16,128]{2,1,0:T(8,128)S(1)} all-to-all(f32[32,16,128]{2,1,0:T(8,128)S(1)} %get-tuple-element.73), channel_id=1, replica_groups=mesh['batch'=8,'narrow'=4] {'batch','narrow'}, dimensions={0} | all-to-all | bytes 524288 | tf_op jit(solution)/shard_map/all_to_all | solution.py:31
  72.8 5.5 %shard_map.292 = (bf16[1024,1024]{1,0:T(8,128)(2,1)}, f32[1024,1024]{1,0:T(8,128)S(1)}, f32[32,16,128]{2,1,0:T(8,128)S(1)}, f32[8,1024]{1,0:T(8,128)S(1)}) custom-call(s32[18]{0:T(128)S(1)} %pad_add_fusion.meta, f32[32,16,128]{2,1,0:T(8,128)S(1)} %all_to_all.83.got, f32[8,256]{1,0:T(8,128)S(1)} %get-tuple-element.69.stat, bf16[1024,1024]{1,0:T(8,128)(2,1)S(1)} %bitcast.32, ...), custom_call_target="tpu_custom_call" | custom-call | bytes 13156424 | tf_op jit(solution)/shard_map/pallas_call | solution.py:121
  78.4 12.8 %all_to_all.84.got = f32[32,16,128]{2,1,0:T(8,128)S(1)} all-to-all(f32[32,16,128]{2,1,0:T(8,128)S(1)} %get-tuple-element.76), channel_id=1, replica_groups=mesh['batch'=8,'narrow'=4] {'batch','narrow'}, dimensions={0} | all-to-all | bytes 524288 | tf_op jit(solution)/shard_map/all_to_all | solution.py:31
  91.2 3.4 shard_map.293
  100.0 2.6 all-to-all-start.5
  102.6 2.9 collective-permute-start.2
  106.7 6.6 %all-to-all-done.5.got = f32[32,16,128]{2,1,0:T(8,128)S(1)} async-done(((f32[32,16,128]{2,1,0:T(8,128)}), f32[32,16,128]{2,1,0:T(8,128)S(1)}, u32[]{:S(2)}, u32[]{:S(2)}) %all-to-all-start.5) | async-done | bytes 262176 | tf_op jit(solution)/shard_map/all_to_all | solution.py:31
  120.2 3.0 shard_map.294
  127.1 2.7 all-to-all-start.6
  129.8 1.6 copy-done.11
  137.6 1.6 reshape.143
  139.2 6.0 %all-to-all-start.12 = ((f32[32,9,128]{2,1,0:T(8,128)}), f32[32,9,128]{2,1,0:T(8,128)}, u32[]{:S(2)}, u32[]{:S(2)}) async-start(f32[32,9,128]{2,1,0:T(8,128)} %reshape.143), calls=%async_computation.12 | async-start | bytes 524288 | tf_op jit(solution)/shard_map/all_to_all | solution.py:31
  145.2 2.1 collective-permute-start.4
  148.6 3.3 collective-permute-done.5.highm
  151.9 1.6 copy-done.8
  154.8 7.8 %shard_map.295 = (bf16[1024,512]{1,0:T(8,128)(2,1)S(1)}, f32[1024,256]{1,0:T(8,128)S(1)}, f32[32,8,128]{2,1,0:T(8,128)}, f32[2,512]{1,0:T(2,128)S(1)}) custom-call(s32[18]{0:T(128)S(1)} %pad_add_fusion.meta, f32[32,8,128]{2,1,0:T(8,128)S(1)} %all-to-all-done.6.got, f32[8,512]{1,0:T(8,128)S(1)} %copy-done.39, f32[1,512]{1,0:T(1,128)S(1)} %bitcast.37, ...), custom_call_target="tpu_custom_call" | custom-call | flops 1207959552 | bytes 10176584 | tf_op jit(solution)/shard_map/pallas_call | solution.py:121
  165.1 7.8 %all-to-all-start.7 = ((f32[32,8,128]{2,1,0:T(8,128)}), f32[32,8,128]{2,1,0:T(8,128)S(1)}, u32[]{:S(2)}, u32[]{:S(2)}) async-start(f32[32,8,128]{2,1,0:T(8,128)} %get-tuple-element.94), calls=%async_computation.7 | async-start | bytes 262144 | tf_op jit(solution)/shard_map/all_to_all | solution.py:31
  174.0 2.1 reshape.145
  177.2 4.0 %all-to-all-done.7.got = f32[32,8,128]{2,1,0:T(8,128)S(1)} async-done(((f32[32,8,128]{2,1,0:T(8,128)}), f32[32,8,128]{2,1,0:T(8,128)S(1)}, u32[]{:S(2)}, u32[]{:S(2)}) %all-to-all-start.7) | async-done | bytes 131104 | tf_op jit(solution)/shard_map/all_to_all | solution.py:31
  181.8 3.3 all-to-all-start.13
  185.2 1.9 pad_maximum_fusion
  187.1 8.6 %all-to-all-done.13 = f32[32,9,128]{2,1,0:T(8,128)} async-done(((f32[32,9,128]{2,1,0:T(8,128)}), f32[32,9,128]{2,1,0:T(8,128)}, u32[]{:S(2)}, u32[]{:S(2)}) %all-to-all-start.13) | async-done | bytes 147488 | tf_op jit(solution)/shard_map/all_to_all | solution.py:31
  195.7 3.3 all-to-all-start.14
  199.1 2.2 copy-done.4
  203.5 4.0 %shard_map.296 = (bf16[1024,1024]{1,0:T(8,128)(2,1)}, bf16[1024,256]{1,0:T(8,128)(2,1)S(1)}, f32[2,256]{1,0:T(2,128)S(1)}) custom-call(s32[18]{0:T(128)S(1)} %pad_add_fusion.meta, f32[32,8,128]{2,1,0:T(8,128)S(1)} %all-to-all-done.7.got, f32[8,256]{1,0:T(8,128)S(1)} %get-tuple-element.69.stat, f32[1,256]{1,0:T(1,128)S(1)} %bitcast.45, ...), custom_call_target="tpu_custom_call" | custom-call | flops 1073741824 | bytes 11676744 | tf_op jit(solution)/shard_map/pallas_call | solution.py:121
  208.3 2.0 reshape.141
  210.3 6.6 %all-to-all-done.14 = bf16[32,80,128]{2,1,0:T(8,128)(2,1)} async-done(((bf16[32,80,128]{2,1,0:T(8,128)(2,1)}), bf16[32,80,128]{2,1,0:T(8,128)(2,1)}, u32[]{:S(2)}, u32[]{:S(2)}) %all-to-all-start.14) | async-done | bytes 655392 | tf_op jit(solution)/shard_map/all_to_all | solution.py:31
  217.0 3.4 all-to-all-start.8
  221.6 14.4 %all-to-all-done.8 = bf16[32,64,128]{2,1,0:T(8,128)(2,1)S(1)} async-done(((bf16[32,64,128]{2,1,0:T(8,128)(2,1)}), bf16[32,64,128]{2,1,0:T(8,128)(2,1)S(1)}, u32[]{:S(2)}, u32[]{:S(2)}) %all-to-all-start.8) | async-done | bytes 524320 | tf_op jit(solution)/shard_map/all_to_all | solution.py:31
  237.0 3.5 %all-to-all-start.15 = ((bf16[32,80,128]{2,1,0:T(8,128)(2,1)}), bf16[32,80,128]{2,1,0:T(8,128)(2,1)}, u32[]{:S(2)}, u32[]{:S(2)}) async-start(bf16[32,80,128]{2,1,0:T(8,128)(2,1)} %broadcast_in_dim.17), calls=%async_computation.15 | async-start | bytes 1310720 | tf_op jit(solution)/shard_map/all_to_all | solution.py:31
  241.7 2.0 shard_map.297
  244.9 13.3 %all-to-all-done.15 = bf16[32,80,128]{2,1,0:T(8,128)(2,1)} async-done(((bf16[32,80,128]{2,1,0:T(8,128)(2,1)}), bf16[32,80,128]{2,1,0:T(8,128)(2,1)}, u32[]{:S(2)}, u32[]{:S(2)}) %all-to-all-start.15) | async-done | bytes 655392 | tf_op jit(solution)/shard_map/all_to_all | solution.py:31
  258.2 3.4 all-to-all-start.10
  261.7 29.0 %all-to-all-done.10 = bf16[32,144,128]{2,1,0:T(8,128)(2,1)S(1)} async-done(((bf16[32,144,128]{2,1,0:T(8,128)(2,1)}), bf16[32,144,128]{2,1,0:T(8,128)(2,1)S(1)}, u32[]{:S(2)}, u32[]{:S(2)}) %all-to-all-start.10) | async-done | bytes 1179680 | tf_op jit(solution)/shard_map/all_to_all | solution.py:31
  291.6 3.6 %all-to-all-start.9 = ((bf16[32,64,128]{2,1,0:T(8,128)(2,1)}), bf16[32,64,128]{2,1,0:T(8,128)(2,1)S(1)}, u32[]{:S(2)}, u32[]{:S(2)}) async-start(bf16[32,64,128]{2,1,0:T(8,128)(2,1)} %broadcast_in_dim.14), calls=%async_computation.9 | async-start | bytes 1048576 | tf_op jit(solution)/shard_map/all_to_all | solution.py:31
  295.4 15.4 %all-to-all-done.9 = bf16[32,64,128]{2,1,0:T(8,128)(2,1)S(1)} async-done(((bf16[32,64,128]{2,1,0:T(8,128)(2,1)}), bf16[32,64,128]{2,1,0:T(8,128)(2,1)S(1)}, u32[]{:S(2)}, u32[]{:S(2)}) %all-to-all-start.9) | async-done | bytes 524320 | tf_op jit(solution)/shard_map/all_to_all | solution.py:31
  311.9 3.1 all-to-all-start.11
  325.3 18.8 %all-to-all-done.11 = bf16[32,144,128]{2,1,0:T(8,128)(2,1)S(1)} async-done(((bf16[32,144,128]{2,1,0:T(8,128)(2,1)}), bf16[32,144,128]{2,1,0:T(8,128)(2,1)S(1)}, u32[]{:S(2)}, u32[]{:S(2)}) %all-to-all-start.11) | async-done | bytes 1179680 | tf_op jit(solution)/shard_map/all_to_all | solution.py:31
  344.1 1.6 reshape.155
  (190 shorter events, 56.5 us)
Async XLA Ops:
  0.6 26.3 %copy-start.69 = (f32[256]{0:T(256)S(1)}, f32[256]{0:T(256)}, u32[]{:S(2)}) copy-start(f32[256]{0:T(256)} %param.21) | copy-start | bytes 3076
  0.7 26.3 %copy-start.61 = (f32[256]{0:T(256)S(1)}, f32[256]{0:T(256)}, u32[]{:S(2)}) copy-start(f32[256]{0:T(256)} %param.20) | copy-start | bytes 3076
  4.0 22.9 %copy-start.15 = (bf16[3,3,2,128,256]{4,3,2,1,0:T(8,128)(2,1)S(1)}, bf16[3,3,2,128,256]{4,3,2,1,0:T(8,128)(2,1)}, u32[]{:S(2)}) copy-start(bf16[3,3,2,128,256]{4,3,2,1,0:T(8,128)(2,1)} %w.12) | copy-start | bytes 3538948
  6.0 20.9 %collective-permute-start = (f32[256,256]{1,0:T(8,128)S(1)}, f32[256,256]{1,0:T(8,128)S(1)}, u32[]{:S(2)}, u32[]{:S(2)}) collective-permute-start(f32[256,256]{1,0:T(8,128)S(1)} %get-tuple-element.66), channel_id=1, source_target_pairs={{0,1},{1,2},{2,3},{4,5},{5,6},{6,7},{8,9},{9,10},{10,11},{12,13},{... | collective-permute-start | bytes 786440 | tf_op jit(solution)/shard_map/ppermute | solution.py:25
  8.4 18.5 %collective-permute-start.1 = (f32[256,256]{1,0:T(8,128)S(1)}, f32[256,256]{1,0:T(8,128)S(1)}, u32[]{:S(2)}, u32[]{:S(2)}) collective-permute-start(f32[256,256]{1,0:T(8,128)S(1)} %get-tuple-element.67), channel_id=1, source_target_pairs={{1,0},{2,1},{3,2},{5,4},{6,5},{7,6},{9,8},{10,9},{11,10},{13,12},{... | collective-permute-start | bytes 786440 | tf_op jit(solution)/shard_map/ppermute | solution.py:26
  32.5 27.5 %copy-start.73 = (f32[256,512]{1,0:T(8,128)}, f32[256,512]{1,0:T(8,128)S(1)}, u32[]{:S(2)}) copy-start(f32[256,512]{1,0:T(8,128)S(1)} %get-tuple-element.90) | copy-start | bytes 1572868
  32.5 27.5 %copy-start.74 = (f32[256,512]{1,0:T(8,128)}, f32[256,512]{1,0:T(8,128)S(1)}, u32[]{:S(2)}) copy-start(f32[256,512]{1,0:T(8,128)S(1)} %get-tuple-element.89) | copy-start | bytes 1572868
  32.5 24.9 %copy-start.14 = (bf16[256,1024]{1,0:T(8,128)(2,1)S(1)}, bf16[256,1024]{1,0:T(8,128)(2,1)}, u32[]{:S(2)}) copy-start(bf16[256,1024]{1,0:T(8,128)(2,1)} %w.11) | copy-start | bytes 1572868
  32.5 24.9 %copy-start.19 = (f32[128,512]{1,0:T(8,128)S(1)}, f32[128,512]{1,0:T(8,128)}, u32[]{:S(2)}) copy-start(f32[128,512]{1,0:T(8,128)} %we.3) | copy-start | bytes 786436
  32.5 24.9 %copy-start.66 = (f32[512]{0:T(512)S(1)}, f32[512]{0:T(512)}, u32[]{:S(2)}) copy-start(f32[512]{0:T(512)} %param.29) | copy-start | bytes 6148
  32.5 24.8 %copy-start.67 = (f32[128]{0:T(128)S(1)}, f32[128]{0:T(128)}, u32[]{:S(2)}) copy-start(f32[128]{0:T(128)} %param.26) | copy-start | bytes 1540
  32.6 24.8 %copy-start.71 = (f32[128]{0:T(128)S(1)}, f32[128]{0:T(128)}, u32[]{:S(2)}) copy-start(f32[128]{0:T(128)} %param.27) | copy-start | bytes 1540
  42.6 30.2 %copy-start.9 = (bf16[16,4,16,1024]{3,2,1,0:T(8,128)(2,1)S(1)}, bf16[16,4,16,1024]{3,2,1,0:T(8,128)(2,1)}, u32[]{:S(2)}) copy-start(bf16[16,4,16,1024]{3,2,1,0:T(8,128)(2,1)} %param.33) | copy-start | bytes 6291460
  44.9 33.4 %copy-start.37 = (f32[8,512]{1,0:T(8,128)}, f32[8,512]{1,0:T(8,128)S(1)}, u32[]{:S(2)}) copy-start(f32[8,512]{1,0:T(8,128)S(1)} %get-tuple-element.86.stat2) | copy-start | bytes 49156
  44.9 33.4 %copy-start.52 = (f32[16,256]{1,0:T(8,128)}, f32[16,256]{1,0:T(8,128)S(1)}, u32[]{:S(2)}) copy-start(f32[16,256]{1,0:T(8,128)S(1)} %get-tuple-element.84.pooled) | copy-start | bytes 49156
  44.9 27.9 %copy-start.1 = (bf16[16,4,16,1024]{3,2,1,0:T(8,128)(2,1)S(1)}, bf16[16,4,16,1024]{3,2,1,0:T(8,128)(2,1)}, u32[]{:S(2)}) copy-start(bf16[16,4,16,1024]{3,2,1,0:T(8,128)(2,1)} %param.17) | copy-start | bytes 6291460
  44.9 27.9 %copy-start.54 = (f32[1024]{0:T(1024)S(1)}, f32[1024]{0:T(1024)}, u32[]{:S(2)}) copy-start(f32[1024]{0:T(1024)} %param.31) | copy-start | bytes 12292
  44.9 27.9 %copy-start.65 = (f32[1024]{0:T(1024)S(1)}, f32[1024]{0:T(1024)}, u32[]{:S(2)}) copy-start(f32[1024]{0:T(1024)} %param.32) | copy-start | bytes 12292
  60.0 18.3 %copy-start.24 = (bf16[1024,256]{1,0:T(8,128)(2,1)}, bf16[1024,256]{1,0:T(8,128)(2,1)S(1)}, u32[]{:S(2)}) copy-start(bf16[1024,256]{1,0:T(8,128)(2,1)S(1)} %get-tuple-element.103.mix) | copy-start | bytes 1572868
  60.0 18.3 %copy-start.40 = (f32[128,128]{1,0:T(8,128)}, f32[128,128]{1,0:T(8,128)S(1)}, u32[]{:S(2)}) copy-start(f32[128,128]{1,0:T(8,128)S(1)} %get-tuple-element.81.znorm) | copy-start | bytes 196612
  60.0 18.3 %copy-start.42 = (f32[128,128]{1,0:T(8,128)}, f32[128,128]{1,0:T(8,128)S(1)}, u32[]{:S(2)}) copy-start(f32[128,128]{1,0:T(8,128)S(1)} %get-tuple-element.82.zall) | copy-start | bytes 196612
  60.1 18.3 %copy-start.55 = (f32[16,128]{1,0:T(8,128)}, f32[16,128]{1,0:T(8,128)S(1)}, u32[]{:S(2)}) copy-start(f32[16,128]{1,0:T(8,128)S(1)} %get-tuple-element.105.hsq) | copy-start | bytes 24580
  60.1 31.1 %copy-start.29 = (f32[16,512]{1,0:T(8,128)}, f32[16,512]{1,0:T(8,128)S(1)}, u32[]{:S(2)}) copy-start(f32[16,512]{1,0:T(8,128)S(1)} %get-tuple-element.79.att) | copy-start | bytes 98308
  100.0 13.3 %all-to-all-start.5 = ((f32[32,16,128]{2,1,0:T(8,128)}), f32[32,16,128]{2,1,0:T(8,128)S(1)}, u32[]{:S(2)}, u32[]{:S(2)}) async-start(f32[32,16,128]{2,1,0:T(8,128)} %copy-done.33), calls=%async_computation.5 | async-start | bytes 524288 | tf_op jit(solution)/shard_map/all_to_all | solution.py:31
  102.6 46.1 %collective-permute-start.2 = (f32[256,512]{1,0:T(8,128)}, f32[256,512]{1,0:T(8,128)}, u32[]{:S(2)}, u32[]{:S(2)}) collective-permute-start(f32[256,512]{1,0:T(8,128)} %copy-done.74), channel_id=1, source_target_pairs={{0,1},{1,2},{2,3},{4,5},{5,6},{6,7},{8,9},{9,10},{10,11},{12,13},{... | collective-permute-start | bytes 1572872 | tf_op jit(solution)/shard_map/ppermute | solution.py:25
  105.4 43.2 %collective-permute-start.3 = (f32[256,512]{1,0:T(8,128)}, f32[256,512]{1,0:T(8,128)}, u32[]{:S(2)}, u32[]{:S(2)}) collective-permute-start(f32[256,512]{1,0:T(8,128)} %copy-done.73), channel_id=1, source_target_pairs={{1,0},{2,1},{3,2},{5,4},{6,5},{7,6},{9,8},{10,9},{11,10},{13,12},{... | collective-permute-start | bytes 1572872 | tf_op jit(solution)/shard_map/ppermute | solution.py:26
  127.0 24.9 %copy-start.31 = (f32[16,512]{1,0:T(8,128)S(1)}, f32[16,512]{1,0:T(8,128)}, u32[]{:S(2)}) copy-start(f32[16,512]{1,0:T(8,128)} %copy-done.29) | copy-start | bytes 98308
  127.0 24.9 %copy-start.39 = (f32[8,512]{1,0:T(8,128)S(1)}, f32[8,512]{1,0:T(8,128)}, u32[]{:S(2)}) copy-start(f32[8,512]{1,0:T(8,128)} %copy-done.37) | copy-start | bytes 49156
  127.0 24.9 %copy-start.49 = (f32[512]{0:T(512)S(1)}, f32[512]{0:T(512)}, u32[]{:S(2)}) copy-start(f32[512]{0:T(512)} %param.24) | copy-start | bytes 6148
  127.0 24.9 %copy-start.62 = (f32[256]{0:T(256)S(1)}, f32[256]{0:T(256)}, u32[]{:S(2)}) copy-start(f32[256]{0:T(256)} %param.20) | copy-start | bytes 3076
  127.1 24.9 %copy-start.70 = (f32[256]{0:T(256)S(1)}, f32[256]{0:T(256)}, u32[]{:S(2)}) copy-start(f32[256]{0:T(256)} %param.21) | copy-start | bytes 3076
  127.1 24.9 %copy-start.51 = (f32[16,256]{1,0:T(8,128)S(1)}, f32[16,256]{1,0:T(8,128)}, u32[]{:S(2)}) copy-start(f32[16,256]{1,0:T(8,128)} %copy-done.50) | copy-start | bytes 49156
  127.1 12.2 %all-to-all-start.6 = ((f32[32,8,128]{2,1,0:T(8,128)}), f32[32,8,128]{2,1,0:T(8,128)S(1)}, u32[]{:S(2)}, u32[]{:S(2)}) async-start(f32[32,8,128]{2,1,0:T(8,128)} %copy-done.34), calls=%async_computation.6 | async-start | bytes 262144 | tf_op jit(solution)/shard_map/all_to_all | solution.py:31
  139.2 25.9 %all-to-all-start.12 = ((f32[32,9,128]{2,1,0:T(8,128)}), f32[32,9,128]{2,1,0:T(8,128)}, u32[]{:S(2)}, u32[]{:S(2)}) async-start(f32[32,9,128]{2,1,0:T(8,128)} %reshape.143), calls=%async_computation.12 | async-start | bytes 524288 | tf_op jit(solution)/shard_map/all_to_all | solution.py:31
  145.2 3.4 collective-permute-start.4
  147.3 4.6 %collective-permute-start.5 = (bf16[256,256]{1,0:T(8,128)(2,1)}, bf16[256,256]{1,0:T(8,128)(2,1)S(1)}, u32[]{:S(2)}, u32[]{:S(2)}) collective-permute-start(bf16[256,256]{1,0:T(8,128)(2,1)} %copy-done.75), channel_id=1, source_target_pairs={{1,0},{2,1},{3,2},{5,4},{6,5},{7,6},{9,8},{10,9},{11,10},{13,12},{... | collective-permute-start | bytes 393224 | tf_op jit(solution)/shard_map/ppermute | solution.py:26
  165.1 16.0 %all-to-all-start.7 = ((f32[32,8,128]{2,1,0:T(8,128)}), f32[32,8,128]{2,1,0:T(8,128)S(1)}, u32[]{:S(2)}, u32[]{:S(2)}) async-start(f32[32,8,128]{2,1,0:T(8,128)} %get-tuple-element.94), calls=%async_computation.7 | async-start | bytes 262144 | tf_op jit(solution)/shard_map/all_to_all | solution.py:31
  176.0 23.1 %copy-start.2 = (bf16[16,4,16,1024]{3,2,1,0:T(8,128)(2,1)S(1)}, bf16[16,4,16,1024]{3,2,1,0:T(8,128)(2,1)}, u32[]{:S(2)}) copy-start(bf16[16,4,16,1024]{3,2,1,0:T(8,128)(2,1)} %param.17) | copy-start | bytes 6291460
  181.8 13.9 %all-to-all-start.13 = ((f32[32,9,128]{2,1,0:T(8,128)}), f32[32,9,128]{2,1,0:T(8,128)}, u32[]{:S(2)}, u32[]{:S(2)}) async-start(f32[32,9,128]{2,1,0:T(8,128)} %broadcast_in_dim.16), calls=%async_computation.13 | async-start | bytes 524288 | tf_op jit(solution)/shard_map/all_to_all | solution.py:31
  195.7 21.2 %all-to-all-start.14 = ((bf16[32,80,128]{2,1,0:T(8,128)(2,1)}), bf16[32,80,128]{2,1,0:T(8,128)(2,1)}, u32[]{:S(2)}, u32[]{:S(2)}) async-start(bf16[32,80,128]{2,1,0:T(8,128)(2,1)} %bitcast.53), calls=%async_computation.14 | async-start | bytes 1310720 | tf_op jit(solution)/shard_map/all_to_all | solution.py:31
  210.3 30.2 %copy-start.6 = (bf16[3,16,96,256]{3,2,1,0:T(8,128)(2,1)S(1)}, bf16[3,16,96,256]{3,2,1,0:T(8,128)(2,1)}, u32[]{:S(2)}) copy-start(bf16[3,16,96,256]{3,2,1,0:T(8,128)(2,1)} %copy-done.5) | copy-start | bytes 7077892
  217.0 19.0 %all-to-all-start.8 = ((bf16[32,64,128]{2,1,0:T(8,128)(2,1)}), bf16[32,64,128]{2,1,0:T(8,128)(2,1)S(1)}, u32[]{:S(2)}, u32[]{:S(2)}) async-start(bf16[32,64,128]{2,1,0:T(8,128)(2,1)} %reshape.141), calls=%async_computation.8 | async-start | bytes 1048576 | tf_op jit(solution)/shard_map/all_to_all | solution.py:31
  237.0 21.2 %all-to-all-start.15 = ((bf16[32,80,128]{2,1,0:T(8,128)(2,1)}), bf16[32,80,128]{2,1,0:T(8,128)(2,1)}, u32[]{:S(2)}, u32[]{:S(2)}) async-start(bf16[32,80,128]{2,1,0:T(8,128)(2,1)} %broadcast_in_dim.17), calls=%async_computation.15 | async-start | bytes 1310720 | tf_op jit(solution)/shard_map/all_to_all | solution.py:31
  258.2 32.5 %all-to-all-start.10 = ((bf16[32,144,128]{2,1,0:T(8,128)(2,1)}), bf16[32,144,128]{2,1,0:T(8,128)(2,1)S(1)}, u32[]{:S(2)}, u32[]{:S(2)}) async-start(bf16[32,144,128]{2,1,0:T(8,128)(2,1)} %reshape.142), calls=%async_computation.10 | async-start | bytes 2359296 | tf_op jit(solution)/shard_map/all_to_all | solution.py:31
  291.6 19.1 %all-to-all-start.9 = ((bf16[32,64,128]{2,1,0:T(8,128)(2,1)}), bf16[32,64,128]{2,1,0:T(8,128)(2,1)S(1)}, u32[]{:S(2)}, u32[]{:S(2)}) async-start(bf16[32,64,128]{2,1,0:T(8,128)(2,1)} %broadcast_in_dim.14), calls=%async_computation.9 | async-start | bytes 1048576 | tf_op jit(solution)/shard_map/all_to_all | solution.py:31
  295.2 19.8 %copy-start.58 = (f32[2,1024]{1,0:T(2,128)S(1)}, f32[2,1024]{1,0:T(2,128)}, u32[]{:S(2)}) copy-start(f32[2,1024]{1,0:T(2,128)} %copy-done.57) | copy-start | bytes 24580
  295.4 21.5 %copy-start.64 = (f32[2,512]{1,0:T(2,128)S(1)}, f32[2,512]{1,0:T(2,128)}, u32[]{:S(2)}) copy-start(f32[2,512]{1,0:T(2,128)} %copy-done.63) | copy-start | bytes 12292
  311.9 32.2 %all-to-all-start.11 = ((bf16[32,144,128]{2,1,0:T(8,128)(2,1)}), bf16[32,144,128]{2,1,0:T(8,128)(2,1)S(1)}, u32[]{:S(2)}, u32[]{:S(2)}) async-start(bf16[32,144,128]{2,1,0:T(8,128)(2,1)} %broadcast_in_dim.15), calls=%async_computation.11 | async-start | bytes 2359296 | tf_op jit(solution)/shard_map/all_to_all | solution.py:31
  (48 other events, 151.6 us)

commit v3 on v2

--- a/solution.py
+++ b/solution.py
@@ -31,20 +31,15 @@
     return lax.all_to_all(block, ALL, 0, 0)
 
 
-def sum_weights(*parts):
+def swap_cores(block):
+    count = lax.axis_size("narrow")
+    return lax.ppermute(block, "narrow", [(i, i ^ 1) for i in range(count)])
+
+
+def exchange_chips(block):
     count = device_count()
-    flat = jnp.concatenate([part.astype(BF16).reshape(-1, LANES) for part in parts])
-    rows = flat.shape[0]
-    per = -(-rows // (count * 16)) * 16
-    flat = jnp.pad(flat, ((0, per * count - rows), (0, 0))).reshape(count, per, LANES)
-    mine = jnp.sum(exchange(flat).astype(F32), 0).astype(BF16)
-    full = exchange(jnp.broadcast_to(mine[None], (count,) + mine.shape)).reshape(-1, LANES)
-    outs, start = [], 0
-    for part in parts:
-        length = part.size // LANES
-        outs.append(full[start : start + length].astype(F32).reshape(part.shape))
-        start += length
-    return outs
+    groups = [[i for i in range(count) if i % 2 == core] for core in range(2)]
+    return lax.all_to_all(block, ALL, 0, 0, axis_index_groups=groups)
 
 
 def sigmoid(values):
@@ -59,12 +54,12 @@
     pixel = lax.broadcasted_iota(jnp.int32, (count * COLS, LANES), 0)
     row = (pixel >> 4) + (meta[0] + start)
     col = pixel & (COLS - 1)
-    side = 12 + 2 * meta[2 + image]
+    side = 12 + 2 * meta[3 + image]
     return jnp.where((row < side) & (row >= 0) & (col < side), 1.0, 0.0).astype(F32)
 
 
 def area_of(meta, image):
-    side = (12 + 2 * meta[2 + image]).astype(F32)
+    side = (12 + 2 * meta[3 + image]).astype(F32)
     return side * side
 
 
@@ -114,20 +109,32 @@
     return lax.dot_general(a, b, (dims, ((), ())), precision=precision, preferred_element_type=F32)
 
 
-def call(kernel, outs, args, scratch=(), megabytes=32, flops=0, **sizes):
+def whole(shape):
+    return pl.BlockSpec(shape, lambda step: (0,) * len(shape))
+
+
+def call(kernel, outs, args, scratch=(), megabytes=56, flops=0, after=(), local="", **sizes):
     moved = sum(a.size * a.dtype.itemsize for a in args) + sum(
         functools.reduce(lambda x, y: x * y, s) * jnp.dtype(t).itemsize for s, t in outs
     )
+    count = len(args)
+    vmem = pl.BlockSpec(memory_space=pltpu.VMEM)
+
+    def run(*refs):
+        kernel(*refs[:count], *refs[count + len(after) :], **sizes)
+
     return pl.pallas_call(
-        functools.partial(kernel, **sizes),
+        run,
+        grid=() if local == "in out" else (1,),
         out_shape=[jax.ShapeDtypeStruct(s, t) for s, t in outs],
         in_specs=[pl.BlockSpec(memory_space=pltpu.SMEM)]
-        + [pl.BlockSpec(memory_space=pltpu.VMEM)] * (len(args) - 1),
-        out_specs=[pl.BlockSpec(memory_space=pltpu.VMEM)] * len(outs),
+        + [vmem if "in" in local else whole(a.shape) for a in args[1:]]
+        + [pl.BlockSpec(memory_space=pl.ANY)] * len(after),
+        out_specs=[vmem if "out" in local else whole(s) for s, _ in outs],
         scratch_shapes=[pltpu.VMEM(s, t) for s, t in scratch],
-        compiler_params=pltpu.CompilerParams(vmem_limit_bytes=megabytes << 20),
+        compiler_params=pltpu.CompilerParams(vmem_limit_bytes=(24 if local else megabytes) << 20),
         cost_estimate=pl.CostEstimate(flops=flops, bytes_accessed=moved, transcendentals=0),
-    )(*args)
+    )(*args, *after)
 
 
 def reduce_kernel(meta, x, w, pre, top, bottom, pay, acc, *, blocks, rows):
@@ -360,13 +367,13 @@
 
 
 def mixture_kernel(
-    meta, got, stat3, pre, grad, gain, w, hid, att, we, gexp, gmix, top, bottom, glog, pay, sums_out, *, blocks, rows
+    meta, got, stat3, pre, grad, gain, w, hid, gexp, gmix, top, bottom, gatt, gain_out, shift_out, *, blocks, rows
 ):
     slab = rows * COLS
     sums = jnp.sum(got[...], 0)
     shift_sum, gain_sum = row_of(sums, 0, 8), row_of(sums, 8, 8)
-    sums_out[0:1] = shift_sum
-    sums_out[1:2] = gain_sum
+    shift_out[...] = shift_sum
+    gain_out[...] = gain_sum
     a, b, d = back_terms(stat3, gain[...], shift_sum, gain_sum)
     group = 4
 
@@ -394,38 +401,64 @@
             own = pl.ds(pl.multiple_of(image * slab, slab), slab)
             edge = pl.ds(pl.multiple_of(image * COLS, COLS), COLS)
             part = value[j * slab : (j + 1) * slab]
-            top[edge, :] = part[:COLS].astype(BF16)
-            bottom[edge, :] = part[slab - COLS :].astype(BF16)
+            top[edge, :] = part[:COLS]
+            bottom[edge, :] = part[slab - COLS :]
             for half in range(2):
                 lanes = slice(half * 256, half * 256 + 256)
-                glog[pl.ds(image, 1), lanes] = total(fold(part * hid[own, lanes].astype(F32)))
+                gatt[pl.ds(image, 1), lanes] = total(fold(part * hid[own, lanes].astype(F32)))
         return carry
 
     lax.fori_loop(0, blocks // group, step, 0)
+
+
+def logits_kernel(meta, gatt, att, we, glog, pay):
     first, second = att[:, :256], att[:, 256:]
-    inner = first * glog[:, :256] + second * glog[:, 256:]
+    inner = first * gatt[:, :256] + second * gatt[:, 256:]
     logits = jnp.concatenate(
-        [first * (glog[:, :256] - inner), second * (glog[:, 256:] - inner)], axis=1
+        [first * (gatt[:, :256] - inner), second * (gatt[:, 256:] - inner)], axis=1
     )
     glog[...] = logits
     pay[0] = dot(logits, we[...], ((1,), (1,)), HIGHEST)
     spread(pay)
 
 
-def expand_grad_kernel(meta, mix, gexp, hsq, glog, out, excite, bias):
-    for k in range(4):
-        lanes = slice(k * 256, k * 256 + 256)
-        out[:, lanes] = dot(mix[...], gexp[:, lanes], ((0,), (0,))).astype(BF16)
-    excite[...] = dot(hsq[...], glog[...], ((0,), (0,)), HIGHEST)
-    bias[...] = jnp.zeros_like(bias)
-    put = total(glog[...])
-    for k in range(4):
-        bias[k : k + 1, :] = put[:, k * LANES : (k + 1) * LANES]
+def expand_grad_kernel(meta, mix, gexp, hsq, glog, keep, send):
+    for ref, core in ((send, 1 - meta[2]), (keep, meta[2])):
+        for k in range(2):
+            lanes = pl.ds(pl.multiple_of(core * 512 + k * 256, 256), 256)
+            ref[k * 256 : k * 256 + 256, :] = dot(mix[...], gexp[:, lanes], ((0,), (0,))).astype(ref.dtype)
+        lanes = pl.ds(pl.multiple_of(core * 256, 256), 256)
+        ref[512:, :] = dot(hsq[...], glog[:, lanes], ((0,), (0,)), HIGHEST).astype(ref.dtype)
+
+
+def pack_kernel(meta, *refs):
+    out = refs[-1]
+    start = 0
+    for keep, got in zip(refs[:-1:2], refs[1:-1:2]):
+        share = keep.shape[0] // out.shape[0]
+        for chip in range(out.shape[0]):
+            rows = slice(chip * share, chip * share + share)
+            out[chip, start : start + share, :] = (keep[rows] + got[rows].astype(F32)).astype(BF16)
+        start += share
+
+
+def share_kernel(meta, shares, out):
+    value = shares[0].astype(F32)
+    for k in range(1, shares.shape[0]):
+        value = value + shares[k].astype(F32)
+    out[0] = value.astype(BF16)
+    block = out[0]
+
+    def step(k, carry):
+        out[k] = block
+        return carry
+
+    lax.fori_loop(1, out.shape[0], step, 0)
 
 
 def hidden_kernel(
     meta, got, znorm, zall, hsq_gain, stat_sq, pooled, wsq, att, gmix, pre, stat2, gain, shift,
-    dz, gpool, squeeze, pay, sums_out, acc, full, *, blocks, rows, parts
+    dz, gpool, pay, gain_out, shift_out, acc, full, squeeze, *, blocks, rows, parts
 ):
     slab = rows * COLS
     bands = got.shape[0] // parts
@@ -441,9 +474,8 @@
     images = float(bands * blocks)
     shift_sum = total(grad_z)
     gain_sum = total(grad_z * znorm[...])
-    sums_out[...] = jnp.zeros_like(sums_out)
-    sums_out[0:1] = shift_sum
-    sums_out[1:2] = gain_sum
+    shift_out[...] = shift_sum
+    gain_out[...] = gain_sum
     mine = pl.ds(pl.multiple_of(meta[1] * blocks, blocks), blocks)
     grad_pre = (
         hsq_gain[...]
@@ -478,18 +510,22 @@
     lax.fori_loop(0, blocks, step, 0)
     put_row(pay, 0, total(acc[0]))
     put_row(pay, 4, total(acc[1]))
+    pay[0, 8:, :] = jnp.zeros((pay.shape[1] - 8, LANES), F32)
     spread(pay)
+    share = pay.shape[1] - 8
+    for n in range(pay.shape[0]):
+        pay[n, 8:, :] = squeeze[n * share : (n + 1) * share, :]
 
 
 def conv_kernel(
-    meta, got, stat2, gain2, shift2, dz, pre2, low2, high2, lowm, highm, att, gpool, w, pre, stat, gain, shift,
-    gsplit, out, pay, sums_out, tall, acc, *, blocks, rows
+    meta, got, stat2, gain2, shift2, dz, pre2, low2, high2, lowm, highm, att, gpool, w, pre, stat,
+    gain, shift, glog, gsplit, out, pay, gain_out, shift_out, tall, acc, *, blocks, rows
 ):
     slab = rows * COLS
     sums = jnp.sum(got[...], 0)
     shift_sum, gain_sum = row_of(sums, 0, 4), row_of(sums, 4, 4)
-    sums_out[0:1] = shift_sum
-    sums_out[1:2] = gain_sum
+    shift_out[...] = shift_sum
+    gain_out[...] = gain_sum
     a, b, d = back_terms(stat2, gain2[...], shift_sum, gain_sum)
     center2, inv2 = stat2[0:1], stat2[1:2]
 
@@ -506,7 +542,7 @@
                 sig = sigmoid(z)
                 slope = sig * (1.0 + z * (1.0 - sig))
                 hidden = (
-                    mixed[edge, :].astype(F32) * att[pl.ds(i, 1), lanes] + gpool[pl.ds(i, 1), :]
+                    mixed[edge, :] * att[pl.ds(i, 1), lanes] + gpool[pl.ds(i, 1), :]
                 ).astype(BF16)
                 return hidden.astype(F32) * keep * slope
 
@@ -559,15 +595,16 @@
     lax.fori_loop(0, blocks // group, step, 0)
     put_row(pay, 0, total(acc[0]))
     put_row(pay, 2, total(acc[1]))
-    pay[0, 4:8, :] = jnp.zeros((4, LANES), F32)
+    put_row(pay, 4, total(glog[...]))
+    pay[0, 8:, :] = sums[8:]
     spread(pay)
 
 
-def split_grad_kernel(meta, hid, gsplit, out, *, blocks, rows):
-    slab = rows * COLS
-    for half in range(2):
-        lanes = slice(half * 128, half * 128 + 128)
-        grads = gsplit[:, half * 256 : half * 256 + 256]
+def split_grad_kernel(meta, hid, gsplit, keep, send, *, blocks, rows):
+    slab = rows * COLS
+    for ref, core in ((send, 1 - meta[2]), (keep, meta[2])):
+        lanes = pl.ds(pl.multiple_of(core * 128, 128), 128)
+        grads = gsplit[:, pl.ds(pl.multiple_of(core * 256, 256), 256)]
         for dy in range(3):
             lhs = jnp.concatenate(
                 [
@@ -576,27 +613,39 @@
                 ],
                 axis=1,
             )
-            value = dot(lhs, grads, ((0,), (0,))).astype(BF16)
-            for dx in range(3):
-                out[dy, dx, half] = value[dx * 128 : (dx + 1) * 128]
-
-
-def input_kernel(meta, got, stat, gain, dz, pre, w, x, grad, out, wgrad, sums_out, small, *, blocks, rows):
-    slab = rows * COLS
-    sums = jnp.sum(got[...], 0)
+            ref[dy * 384 : dy * 384 + 384, :] = dot(lhs, grads, ((0,), (0,))).astype(ref.dtype)
+
+
+def reduce_back_kernel(meta, got, stat, gain, dz, pre, x, small, keep, send, gain_out, shift_out, bias_out, squeeze, *, blocks, rows):
+    slab = rows * COLS
+    sums = jnp.sum(got[:, :8, :], 0)
+    share = got.shape[1] - 8
+    for n in range(got.shape[0]):
+        squeeze[n * share : (n + 1) * share, :] = got[n, 8:, :]
     shift_sum, gain_sum = row_of(sums, 0, 2), row_of(sums, 2, 2)
-    sums_out[0:1] = shift_sum
-    sums_out[1:2] = gain_sum
+    shift_out[...] = shift_sum
+    gain_out[...] = gain_sum
+    bias_out[...] = row_of(sums, 4, 4)
     a, b, d = back_terms(stat, gain[...], shift_sum, gain_sum)
+
+    def step(image, carry):
+        own = pl.ds(pl.multiple_of(image * slab, slab), slab)
+        mask = wide(inside(meta, image, 0, rows), 256)
+        small[own, :] = (mask * (a * dz[own, :] + b + d * pre[own, :])).astype(BF16)
+        return carry
+
+    lax.fori_loop(0, blocks, step, 0)
+    for ref, core in ((send, 1 - meta[2]), (keep, meta[2])):
+        lanes = pl.ds(pl.multiple_of(core * 512, 512), 512)
+        ref[...] = dot(x[:, lanes], small[...], ((0,), (0,))).astype(ref.dtype)
+
+
+def input_kernel(meta, small, w, grad, out, *, blocks, rows):
+    slab = rows * COLS
     group = 4
 
     def step(g, carry):
         many = pl.ds(pl.multiple_of(g * group * slab, group * slab), group * slab)
-        for j in range(group):
-            image = g * group + j
-            own = pl.ds(pl.multiple_of(image * slab, slab), slab)
-            mask = wide(inside(meta, image, 0, rows), 256)
-            small[own, :] = (mask * (a * dz[own, :] + b + d * pre[own, :])).astype(BF16)
         for k in range(4):
             lanes = slice(k * 256, k * 256 + 256)
             value = dot(small[many, :], w[lanes, :], ((1,), (1,)))
@@ -610,7 +659,24 @@
         return carry
 
     lax.fori_loop(0, blocks // group, step, 0)
-    wgrad[...] = dot(x[...], small[...], ((0,), (0,))).astype(BF16)
+
+
+def total_kernel(meta, own, other, expand, excite, split, reduce):
+    chips = own.shape[0]
+    size3, size2, size1 = 640 // chips, 1152 // chips, 512 // chips
+    for ref, core in ((own, meta[2]), (other, 1 - meta[2])):
+
+        def part(start, size, first, rows):
+            block = ref[:, start : start + size, :].reshape(chips * size, 256)
+            return block[first : first + rows].astype(F32)
+
+        for k in range(2):
+            lanes = pl.ds(pl.multiple_of(core * 512 + k * 256, 256), 256)
+            expand[:, lanes] = part(0, size3, k * 256, 256)
+        excite[:, pl.ds(pl.multiple_of(core * 256, 256), 256)] = part(0, size3, 512, 128)
+        for tap in range(9):
+            split[tap // 3, tap % 3, core] = part(size3, size2, tap * 128, 128)
+        reduce[pl.ds(pl.multiple_of(core * 512, 512), 512), :] = part(size3 + size2, size1, 0, 512)
 
 
 def body(
@@ -640,11 +706,13 @@
     pixels = blocks * rows * cols
     slab = rows * cols
     edge = blocks * cols
+    share = mid // count
     images = blocks * lax.axis_size("batch")
     meta = jnp.concatenate(
         [
             (lax.axis_index("narrow") * rows).astype(jnp.int32)[None],
             lax.axis_index("batch").astype(jnp.int32)[None],
+            (lax.axis_index("narrow") % 2).astype(jnp.int32)[None],
             image_class,
         ]
     )
@@ -665,6 +733,7 @@
         [meta, x, weight_reduce],
         [((3, 8, mid), F32)],
         flops=small,
+        local="in out",
         **sizes,
     )
     low, high = halo(top, bottom)
@@ -681,6 +750,7 @@
         [meta, exchange(pay), pre1, low, high, gain1, shift1, weight_split],
         [((2, 8, 2 * mid), F32)],
         flops=large,
+        local="in out",
         **sizes,
     )
     low2, high2 = halo(top, bottom)
@@ -693,6 +763,8 @@
             ((8, 2 * mid), F32),
         ],
         [meta, exchange(pay), stat1, pre2, gain2, shift2, weight_squeeze],
+        local="in out",
+        after=(low2, high2),
         **sizes,
     )
     mix, pre3, att, hsq, znorm, zall, pay, stat_sq = call(
@@ -720,6 +792,7 @@
         [((2, 8, channels), F32)],
         flops=small,
         parts=parts,
+        local="in out",
         **sizes,
     )
     out, grad_res, pay, stat3 = call(
@@ -732,38 +805,41 @@
         ],
         [meta, exchange(pay), stat1, x, pre3, cot, gain3, shift3],
         [((2, 8, channels), F32)],
-        **sizes,
-    )
-    gexp, gmix, top, bottom, glog, pay, sums3 = call(
+        local="in out",
+        **sizes,
+    )
+    gexp, gmix, top, bottom, gatt, gain3_grad, shift3_grad = call(
         mixture_kernel,
         [
             ((pixels, channels), BF16),
             ((pixels, mid), BF16),
-            ((edge, mid), BF16),
-            ((edge, mid), BF16),
+            ((edge, mid), F32),
+            ((edge, mid), F32),
             ((blocks, 2 * mid), F32),
-            ((count, blocks, inter), F32),
-            ((2, channels), F32),
-        ],
-        [meta, exchange(pay), stat3, pre3, grad_res, gain3, weight_expand, hid2, att, weight_excite],
+            ((1, channels), F32),
+            ((1, channels), F32),
+        ],
+        [meta, exchange(pay), stat3, pre3, grad_res, gain3, weight_expand, hid2],
         flops=small,
+        local="in out",
         **sizes,
     )
     lowm, highm = halo(top, bottom)
-    expand_part, excite_part, bias_part = call(
-        expand_grad_kernel,
-        [((mid, channels), BF16), ((inter, 2 * mid), F32), ((8, LANES), F32)],
-        [meta, mix, gexp, hsq, glog],
-        flops=small,
-    )
-    dz2, gpool, squeeze_part, pay, sums_sq = call(
+    glog, pay = call(
+        logits_kernel,
+        [((blocks, 2 * mid), F32), ((count, blocks, inter), F32)],
+        [meta, gatt, att, weight_excite],
+        after=(lowm, highm),
+        local="in out",
+    )
+    dz2, gpool, pay, gain_sq_grad, shift_sq_grad = call(
         hidden_kernel,
         [
             ((pixels, 2 * mid), F32),
             ((blocks, mid), F32),
-            ((mid, inter), F32),
-            ((count, 8, LANES), F32),
-            ((8, inter), F32),
+            ((count, 8 + share, LANES), F32),
+            ((1, inter), F32),
+            ((1, inter), F32),
         ],
         [
             meta,
@@ -781,17 +857,19 @@
             gain2,
             shift2,
         ],
-        [((2, 8, 2 * mid), F32), ((images, inter), F32)],
+        [((2, 8, 2 * mid), F32), ((images, inter), F32), ((mid, inter), F32)],
         parts=parts,
-        **sizes,
-    )
-    gsplit, dz1, pay, sums2 = call(
+        local="in out",
+        **sizes,
+    )
+    gsplit, dz1, pay, gain2_grad, shift2_grad = call(
         conv_kernel,
         [
             ((pixels, 2 * mid), BF16),
             ((pixels, mid), F32),
-            ((count, 8, LANES), F32),
-            ((2, 2 * mid), F32),
+            ((count, 8 + share, LANES), F32),
+            ((1, 2 * mid), F32),
+            ((1, 2 * mid), F32),
         ],
         [
             meta,
@@ -812,53 +890,89 @@
             stat1,
             gain1,
             shift1,
+            glog,
         ],
         [((3, blocks, slab + 2 * cols, 2 * mid), BF16), ((2, 8, mid), F32)],
         flops=large,
-        **sizes,
-    )
-    (split_part,) = call(
+        local="in",
+        **sizes,
+    )
+    keep2, send2 = call(
         split_grad_kernel,
-        [(weight_split.shape, BF16)],
+        [((9 * 128, 256), F32), ((9 * 128, 256), BF16)],
         [meta, hid1, gsplit],
         flops=large,
         **sizes,
     )
-    input_grad, reduce_part, sums1 = call(
+    keep3, send3 = call(
+        expand_grad_kernel,
+        [((2 * mid + inter, 256), F32), ((2 * mid + inter, 256), BF16)],
+        [meta, mix, gexp, hsq, glog],
+        flops=small,
+        after=(send2,),
+    )
+    small1, keep1, send1, gain1_grad, shift1_grad, bias_grad, squeeze_total = call(
+        reduce_back_kernel,
+        [
+            ((pixels, mid), BF16),
+            ((channels // 2, mid), F32),
+            ((channels // 2, mid), BF16),
+            ((1, mid), F32),
+            ((1, mid), F32),
+            ((1, 2 * mid), F32),
+            ((mid, inter), F32),
+        ],
+        [meta, exchange(pay), stat1, gain1, dz1, pre1, x],
+        flops=small,
+        after=(send2, send3),
+        **sizes,
+    )
+    chips = count // 2
+    share_rows = [keep.shape[0] // chips for keep in (keep3, keep2, keep1)]
+    (packed,) = call(
+        pack_kernel,
+        [((chips, sum(share_rows), 256), BF16)],
+        [meta, keep3, swap_cores(send3), keep2, swap_cores(send2), keep1, swap_cores(send1)],
+    )
+    (input_grad,) = call(
         input_kernel,
-        [((pixels, channels), BF16), ((channels, mid), BF16), ((2, mid), F32)],
-        [meta, exchange(pay), stat1, gain1, dz1, pre1, weight_reduce, x, grad_res],
-        [((pixels, mid), BF16)],
-        flops=2 * small,
-        **sizes,
-    )
-    per = -(-(squeeze_part.size // LANES + 8) // count)
-    flat = jnp.concatenate([squeeze_part, bias_part])
-    flat = jnp.pad(flat, ((0, per * count - flat.shape[0]), (0, 0))).reshape(count, per, LANES)
-    mine = jnp.sum(exchange(flat), 0)
-    full = exchange(jnp.broadcast_to(mine[None], (count,) + mine.shape)).reshape(-1, LANES)
-    squeeze_total = full[:mid]
-    bias_total = full[mid : mid + 4].reshape(-1)
-    expand_total, excite_total = sum_weights(expand_part, excite_part)
-    (split_total,) = sum_weights(split_part)
-    (reduce_total,) = sum_weights(reduce_part)
+        [((pixels, channels), BF16)],
+        [meta, small1, weight_reduce, grad_res],
+        flops=small,
+        after=(packed,),
+        **sizes,
+    )
+    (shared,) = call(share_kernel, [(packed.shape, BF16)], [meta, exchange_chips(packed)], after=(input_grad,), local="in out")
+    own = exchange_chips(shared)
+    expand_total, excite_total, split_total, reduce_total = call(
+        total_kernel,
+        [
+            ((mid, channels), F32),
+            ((inter, 2 * mid), F32),
+            (weight_split.shape, F32),
+            ((channels, mid), F32),
+        ],
+        [meta, own, swap_cores(own)],
+        local="in",
+    )
+    flat = lambda v: v.reshape(-1)
     return (
         out.reshape(inputs.shape),
         input_grad.reshape(inputs.shape),
         reduce_total,
-        sums1[1],
-        sums1[0],
+        flat(gain1_grad),
+        flat(shift1_grad),
         split_total,
-        sums2[1],
-        sums2[0],
+        flat(gain2_grad),
+        flat(shift2_grad),
         squeeze_total,
-        sums_sq[1],
-        sums_sq[0],
+        flat(gain_sq_grad),
+        flat(shift_sq_grad),
         excite_total,
-        bias_total,
+        flat(bias_grad),
         expand_total,
-        sums3[1],
-        sums3[0],
+        flat(gain3_grad),
+        flat(shift3_grad),
     )
 
 

time: 348 us -> 251 us (0.72)
  waiting for transfers between devices: 120 us -> 30.3 us
  blocking collectives: 65.3 us -> 133 us
  local copies, waits for them, and re-layouts: 58.3 us -> 11 us
  starting transfers between devices: 53.9 us -> 18.1 us
  Pallas kernels: 38.1 us -> 56.2 us
  other arithmetic: 8.94 us -> 0.73 us
    all_to_all x11 -> x1, waiting for transfers between devices: 117 us -> 2.06 us  [exchange(): return lax.all_to_all(block, ALL, 0, 0)]
    all_to_all x11 -> x1, starting transfers between devices: 42.7 us -> 2.59 us  [exchange(): return lax.all_to_all(block, ALL, 0, 0)]
    all_to_all x0 -> x1, blocking collectives: none -> 35.2 us  [exchange_chips(): return lax.all_to_all(block, ALL, 0, 0, axis_index_groups=groups)]
    all_to_all x5 -> x7, blocking collectives: 65.3 us -> 97.6 us  [exchange(): return lax.all_to_all(block, ALL, 0, 0)]
    unnamed x158 -> x68, local copies, waits for them, and re-layouts: 37.7 us -> 11 us
    all_to_all x0 -> x1, waiting for transfers between devices: none -> 21.5 us  [exchange_chips(): return lax.all_to_all(block, ALL, 0, 0, axis_index_groups=groups)]
    pallas_call x11 -> x16, Pallas kernels: 38.1 us -> 56.2 us  [call(): pl.pallas_call(run, grid=() if local == 'in out' else (1,), out_shape=[ja...]
    reshape x9 -> x0, local copies, waits for them, and re-layouts: 10.4 us -> none  [the longest x2 3.25 us: sum_weights(): jnp.pad(flat, ((0, per * count - rows), (0, 0))).reshape(count, per, LANES)]
  transfers between devices with their start and end apart: 17 -> 12, of which waited for: 10 -> 5; matrix products, arithmetic and copies ran while one was open for 7% -> 0% of each run, Pallas kernels for 5% -> 7%
where the time goes in v3:
time: 251 us; the launch traced here: 250 us
  blocking collectives  133 us (53%)
  Pallas kernels  56.2 us (22%)
  waiting for transfers between devices  30.3 us (12%)
  starting transfers between devices  18.1 us (7%)
  local copies, waits for them, and re-layouts  11 us (4%)
    all_to_all x7, blocking collectives, exchange(): return lax.all_to_all(block, ALL, 0, 0)  97.6 us
    pallas_call x16, Pallas kernels, call(): pl.pallas_call(run, grid=() if local == 'in out' else (1,), out_shape=[ja...  56.2 us
    all_to_all x1, blocking collectives, exchange_chips(): return lax.all_to_all(block, ALL, 0, 0, axis_index_groups=groups)  35.2 us
    all_to_all x1, waiting for transfers between devices, exchange_chips(): return lax.all_to_all(block, ALL, 0, 0, axis_index_groups=groups)  21.5 us
    unnamed x68, local copies, waits for them, and re-layouts  11 us
    ppermute x3, starting transfers between devices, halo(): low = lax.ppermute(bottom, 'narrow', [(i, i + 1) for i in range(count - 1)])  6.33 us
  transfers between devices with their start and end apart: 12, of which 5 were waited for; matrix products, arithmetic and copies ran while one was open for 0% of the time, Pallas kernels for 7%

profile of v3, /device:TPU:0, one launch (start us, length us, event | category | flops | bytes accessed | tf_op | source)
XLA Modules:
  0.0 250.3 jit_solution(12265482898180433049)
XLA Ops:
  0.7 0.7 pad_add_fusion.refs_0_
  1.4 1.6 copy-done
  3.0 1.0 copy-done.7
  4.1 1.9 shard_map.288
  6.0 2.4 collective-permute-start
  8.4 1.3 collective-permute-start.1
  9.7 17.2 %all_to_all.50.refs_1_ = f32[32,8,128]{2,1,0:T(8,128)S(1)} all-to-all(f32[32,8,128]{2,1,0:T(8,128)S(1)} %get-tuple-element.76), channel_id=1, replica_groups=mesh['batch'=8,'narrow'=4] {'batch','narrow'}, dimensions={0} | all-to-all | bytes 262144 | tf_op jit(solution)/shard_map/all_to_all | solution.py:31
  27.0 4.1 %shard_map.289 = (bf16[3,16,96,256]{3,2,1,0:T(8,128)(2,1)S(1)}, f32[1024,512]{1,0:T(8,128)S(1)}, f32[256,512]{1,0:T(8,128)S(1)}, f32[256,512]{1,0:T(8,128)S(1)},...) custom-call(s32[19]{0:T(128)S(1)} %pad_add_fusion.refs_0_, f32[32,8,128]{2,1,0:T(8,128)S(1)} %all_to_all.50.refs_1_, ...), custom_call_target="tpu_custom_call" | custom-call | flops 1207959552 | bytes 8529996 | tf_op jit(solution)/shard_map/pallas_call | solution.py:126
  31.1 1.4 copy-done.29
  32.5 2.1 collective-permute-start.2
  34.7 1.3 collective-permute-start.3
  36.1 12.1 %all_to_all.51.refs_1_ = f32[32,8,128]{2,1,0:T(8,128)S(1)} all-to-all(f32[32,8,128]{2,1,0:T(8,128)S(1)} %get-tuple-element.80), channel_id=1, replica_groups=mesh['batch'=8,'narrow'=4] {'batch','narrow'}, dimensions={0} | all-to-all | bytes 262144 | tf_op jit(solution)/shard_map/all_to_all | solution.py:31
  48.2 2.2 shard_map.290
  50.5 12.4 %all_to_all.52.refs_1_ = f32[32,16,128]{2,1,0:T(8,128)S(1)} all-to-all(f32[32,16,128]{2,1,0:T(8,128)S(1)} %get-tuple-element.85), channel_id=1, replica_groups=mesh['batch'=8,'narrow'=4] {'batch','narrow'}, dimensions={0} | all-to-all | bytes 524288 | tf_op jit(solution)/shard_map/all_to_all | solution.py:31
  62.9 2.6 %shard_map.291 = (bf16[1024,256]{1,0:T(8,128)(2,1)S(1)}, bf16[1024,1024]{1,0:T(8,128)(2,1)S(1)}, f32[16,512]{1,0:T(8,128)S(1)}, f32[16,128]{1,0:T(8,128)S(1)}, f...) custom-call(s32[19]{0:T(128)S(1)} %pad_add_fusion.refs_0_, ...), custom_call_target="tpu_custom_call" | custom-call | flops 536870912 | bytes 5160012 | tf_op jit(solution)/shard_map/pallas_call | solution.py:126
  65.5 0.6 copy-done.21
  66.1 12.7 %all_to_all.53.refs_1_ = f32[32,16,128]{2,1,0:T(8,128)S(1)} all-to-all(f32[32,16,128]{2,1,0:T(8,128)S(1)} %get-tuple-element.87), channel_id=1, replica_groups=mesh['batch'=8,'narrow'=4] {'batch','narrow'}, dimensions={0} | all-to-all | bytes 524288 | tf_op jit(solution)/shard_map/all_to_all | solution.py:31
  78.9 5.4 %shard_map.292 = (bf16[1024,1024]{1,0:T(8,128)(2,1)}, f32[1024,1024]{1,0:T(8,128)S(1)}, f32[32,16,128]{2,1,0:T(8,128)S(1)}, f32[8,1024]{1,0:T(8,128)S(1)}) custom-call(s32[19]{0:T(128)S(1)} %pad_add_fusion.refs_0_, f32[32,16,128]{2,1,0:T(8,128)S(1)} %all_to_all.53.refs_1_, f32[8,256]{1,0:T(8,128)S(1)} %get-tuple-element.81.refs_2_.refs_15_, ...), custom_call_target="tpu_custom_call" | custom-call | bytes 13156428 | tf_op jit(solution)/shard_map/pallas_call | solution.py:126
  84.3 12.8 %all_to_all.54.refs_1_ = f32[32,16,128]{2,1,0:T(8,128)S(1)} all-to-all(f32[32,16,128]{2,1,0:T(8,128)S(1)} %get-tuple-element.90), channel_id=1, replica_groups=mesh['batch'=8,'narrow'=4] {'batch','narrow'}, dimensions={0} | all-to-all | bytes 524288 | tf_op jit(solution)/shard_map/all_to_all | solution.py:31
  97.1 3.5 %shard_map.293 = (bf16[1024,1024]{1,0:T(8,128)(2,1)S(1)}, bf16[1024,256]{1,0:T(8,128)(2,1)S(1)}, f32[256,256]{1,0:T(8,128)S(1)}, f32[256,256]{1,0:T(8,128)S(1)},...) custom-call(s32[19]{0:T(128)S(1)} %pad_add_fusion.refs_0_, f32[32,16,128]{2,1,0:T(8,128)S(1)} %all_to_all.54.refs_1_, ...), custom_call_target="tpu_custom_call" | custom-call | flops 536870912 | bytes 11350092 | tf_op jit(solution)/shard_map/pallas_call | solution.py:126
  100.7 1.3 copy-done.6
  102.0 1.8 collective-permute-start.4
  103.8 1.3 collective-permute-start.5
  105.1 2.1 collective-permute-done.5.refs_5_.refs_10_
  107.3 1.0 shard_map.294
  108.2 17.4 %all_to_all.55.refs_1_ = f32[32,16,128]{2,1,0:T(8,128)S(1)} all-to-all(f32[32,16,128]{2,1,0:T(8,128)S(1)} %get-tuple-element.97), channel_id=1, replica_groups=mesh['batch'=8,'narrow'=4] {'batch','narrow'}, dimensions={0} | all-to-all | bytes 524288 | tf_op jit(solution)/shard_map/all_to_all | solution.py:31
  125.7 3.5 %shard_map.295 = (f32[1024,512]{1,0:T(8,128)S(1)}, f32[16,256]{1,0:T(8,128)S(1)}, f32[32,16,128]{2,1,0:T(8,128)S(1)}, f32[1,128]{1,0:T(1,128)}, f32[1,128]{1,0:T(1,128)}) custom-call(s32[19]{0:T(128)S(1)} %pad_add_fusion.refs_0_, f32[32,16,128]{2,1,0:T(8,128)S(1)} %all_to_all.55.refs_1_, f32[128,128]{1,0:T(8,128)S(1)} %get-tuple-element.98.refs_2_, ...), custom_call_target="tpu_custom_call" | custom-call | bytes 5596748 | tf_op jit(solution)/shard_map/pallas_call | solution.py:126
  129.2 12.8 %all_to_all.56.refs_1_ = f32[32,16,128]{2,1,0:T(8,128)S(1)} all-to-all(f32[32,16,128]{2,1,0:T(8,128)S(1)} %get-tuple-element.104), channel_id=1, replica_groups=mesh['batch'=8,'narrow'=4] {'batch','narrow'}, dimensions={0} | all-to-all | bytes 524288 | tf_op jit(solution)/shard_map/all_to_all | solution.py:31
  142.0 7.2 %shard_map.296 = (bf16[1024,512]{1,0:T(8,128)(2,1)S(1)}, f32[1024,256]{1,0:T(8,128)S(1)}, f32[32,16,128]{2,1,0:T(8,128)}, f32[1,512]{1,0:T(1,128)}, f32[1,512]{1,0:T(1,128)}) custom-call(s32[19]{0:T(128)S(1)} %pad_add_fusion.refs_0_, f32[32,16,128]{2,1,0:T(8,128)S(1)} %all_to_all.56.refs_1_, f32[8,512]{1,0:T(8,128)S(1)} %get-tuple-element.103.refs_11_.refs_2_, ...), custom_call_target="tpu_custom_call" | custom-call | flops 1207959552 | bytes 10733644 | tf_op jit(solution)/shard_map/pallas_call | solution.py:126
  149.2 1.0 copy-done.11
  150.2 1.0 copy-done.28
  151.2 2.6 %all-to-all-start.7 = ((f32[32,16,128]{2,1,0:T(8,128)}), f32[32,16,128]{2,1,0:T(8,128)S(1)}, u32[]{:S(2)}, u32[]{:S(2)}) async-start(f32[32,16,128]{2,1,0:T(8,128)} %get-tuple-element.108), calls=%async_computation.7 | async-start | bytes 524288 | tf_op jit(solution)/shard_map/all_to_all | solution.py:31
  153.8 4.5 %shard_map.297 = (f32[1152,256]{1,0:T(8,128)}, bf16[1152,256]{1,0:T(8,128)(2,1)}) custom-call(s32[19]{0:T(128)} %copy-done.16, bf16[3,16,96,256]{3,2,1,0:T(8,128)(2,1)} %copy-done.29, bf16[1024,512]{1,0:T(8,128)(2,1)} %copy-done.28), custom_call_target="tpu_custom_call" | custom-call | flops 1207959552 | bytes 5177420 | tf_op jit(solution)/shard_map/pallas_call | solution.py:126
  158.4 3.5 %shard_map.298 = (f32[640,256]{1,0:T(8,128)}, bf16[640,256]{1,0:T(8,128)(2,1)}) custom-call(s32[19]{0:T(128)} %copy-done.16, bf16[1024,256]{1,0:T(8,128)(2,1)} %copy-done.13, bf16[1024,1024]{1,0:T(8,128)(2,1)} %copy-done.6, f32[16,128]{1,0:T(8,128)} %copy-done.21, f32[16,512]{1,0:T(8,128)} %copy-done.14, bf16[1152,256]{1,0:T(8,128)(2,1)} %get-tuple-element.112.refs_5_.refs_7_), custom_call_target="tpu_custom_call" | custom-call | flops 536870912 | bytes 3645516 | tf_op jit(solution)/shard_map/pallas_call | solution.py:126
  162.3 2.1 all-to-all-done.7.refs_1_
  164.4 0.7 copy-done.30
  165.1 4.5 %shard_map.299 = (bf16[1024,256]{1,0:T(8,128)(2,1)}, f32[512,256]{1,0:T(8,128)}, bf16[512,256]{1,0:T(8,128)(2,1)}, f32[1,256]{1,0:T(1,128)}, f32[1,256]{1,0:T(1,...) custom-call(s32[19]{0:T(128)} %copy-done.16, f32[32,16,128]{2,1,0:T(8,128)} %copy-done.30, f32[8,256]{1,0:T(8,128)} %copy-done.15, ...), custom_call_target="tpu_custom_call" | custom-call | flops 536870912 | bytes 5911628 | tf_op jit(solution)/shard_map/pallas_call | solution.py:126
  169.6 1.7 collective-permute-done.8.refs_6_
  171.3 0.7 copy-done.33
  172.0 3.2 %shard_map.300.refs_4_ = bf16[16,144,256]{2,1,0:T(8,128)(2,1)} custom-call(s32[19]{0:T(128)} %copy-done.16, f32[640,256]{1,0:T(8,128)} %get-tuple-element.118.refs_1_, bf16[640,256]{1,0:T(8,128)(2,1)} %copy-done.32, f32[1152,256]{1,0:T(8,128)} %get-tuple-element.119.refs_3_, bf16[1152,256]{1,0:T(8,128)(2,1)} %copy-done.31, ...), custom_call_target="tpu_custom_call" | custom-call | bytes 4718668 | tf_op jit(solution)/shard_map/pallas_call | solution.py:126
  175.2 4.8 %all-to-all-start.8 = ((bf16[16,144,256]{2,1,0:T(8,128)(2,1)}), bf16[16,144,256]{2,1,0:T(8,128)(2,1)S(1)}, u32[]{:S(2)}, u32[]{:S(2)}) async-start(bf16[16,144,256]{2,1,0:T(8,128)(2,1)} %shard_map.300.refs_4_), calls=%async_computation.8 | async-start | bytes 2359296 | tf_op jit(solution)/shard_map/all_to_all | solution.py:42
  180.0 5.3 %shard_map.301.refs_2_ = bf16[1024,1024]{1,0:T(8,128)(2,1)} custom-call(s32[19]{0:T(128)} %copy-done.16, bf16[1024,256]{1,0:T(8,128)(2,1)} %get-tuple-element.117.refs_1_, bf16[1024,256]{1,0:T(8,128)(2,1)} %refs_2_.3, f32[1024,1024]{1,0:T(8,128)} %copy-done.2, bf16[16,144,256]{2,1,0:T(8,128)(2,1)} %shard_map.300.refs_4_), custom_call_target="tpu_custom_call" | custom-call | flops 536870912 | bytes 7340108 | tf_op jit(solution)/shard_map/pallas_call | solution.py:126
  185.3 21.5 %all-to-all-done.8.refs_1_ = bf16[16,144,256]{2,1,0:T(8,128)(2,1)S(1)} async-done(((bf16[16,144,256]{2,1,0:T(8,128)(2,1)}), bf16[16,144,256]{2,1,0:T(8,128)(2,1)S(1)}, u32[]{:S(2)}, u32[]{:S(2)}) %all-to-all-start.8) | async-done | bytes 1179680 | tf_op jit(solution)/shard_map/all_to_all | solution.py:42
  206.8 1.6 copy-done.3
  208.4 0.8 shard_map.302
  209.3 35.2 %all_to_all.57.refs_1_ = bf16[16,144,256]{2,1,0:T(8,128)(2,1)S(1)} all-to-all(bf16[16,144,256]{2,1,0:T(8,128)(2,1)S(1)} %shard_map.302), channel_id=1, replica_groups={{0,2,4,6,8,10,12,14,16,18,20,22,24,26,28,30},{1,3,5,7,9,11,13,15,17,19,..., dimensions={0} | all-to-all | bytes 2359296 | tf_op jit(solution)/shard_map/all_to_all | solution.py:42
  244.5 2.8 %collective-permute-done.9.refs_2_ = bf16[16,144,256]{2,1,0:T(8,128)(2,1)S(1)} collective-permute-done((bf16[16,144,256]{2,1,0:T(8,128)(2,1)S(1)}, bf16[16,144,256]{2,1,0:T(8,128)(2,1)S(1)}, u32[]{:S(2)}, u32[]{:S(2)}) %collective-permute-start.9) | collective-permute-done | bytes 1179680 | tf_op jit(solution)/shard_map/ppermute | solution.py:36
  247.3 2.9 %shard_map.303 = (f32[256,1024]{1,0:T(8,128)}, f32[128,512]{1,0:T(8,128)}, f32[3,3,2,128,256]{4,3,2,1,0:T(8,128)}, f32[1024,256]{1,0:T(8,128)}) custom-call(s32[19]{0:T(128)S(1)} %copy-done.17, bf16[16,144,256]{2,1,0:T(8,128)(2,1)S(1)} %all_to_all.57.refs_1_, bf16[16,144,256]{2,1,0:T(8,128)(2,1)S(1)} %collective-permute-done.9.refs_2_), custom_call_target="tpu_custom_call" | custom-call | bytes 7077964 | tf_op jit(solution)/shard_map/pallas_call | solution.py:126
  (69 shorter events, 0.7 us)
Async XLA Ops:
  0.6 26.3 %copy-start.26 = (f32[256]{0:T(256)S(1)}, f32[256]{0:T(256)}, u32[]{:S(2)}) copy-start(f32[256]{0:T(256)} %param.21) | copy-start | bytes 3076
  0.7 26.3 %copy-start.22 = (f32[256]{0:T(256)S(1)}, f32[256]{0:T(256)}, u32[]{:S(2)}) copy-start(f32[256]{0:T(256)} %param.20) | copy-start | bytes 3076
  1.4 140.6 %copy-start.16 = (s32[19]{0:T(128)}, s32[19]{0:T(128)S(1)}, u32[]{:S(2)}) copy-start(s32[19]{0:T(128)S(1)} %pad_add_fusion.refs_0_) | copy-start | bytes 232
  1.4 1.6 copy-start
  3.0 1.0 copy-start.7
  4.1 22.9 %copy-start.9 = (bf16[3,3,2,128,256]{4,3,2,1,0:T(8,128)(2,1)S(1)}, bf16[3,3,2,128,256]{4,3,2,1,0:T(8,128)(2,1)}, u32[]{:S(2)}) copy-start(bf16[3,3,2,128,256]{4,3,2,1,0:T(8,128)(2,1)} %refs_13_.1) | copy-start | bytes 3538948
  6.0 136.0 %copy-start.4 = (f32[1024,256]{1,0:T(8,128)}, f32[1024,256]{1,0:T(8,128)S(1)}, u32[]{:S(2)}) copy-start(f32[1024,256]{1,0:T(8,128)S(1)} %get-tuple-element.77.refs_2_.refs_14_.refs_5_) | copy-start | bytes 3145732
  6.0 20.9 %collective-permute-start = (f32[256,256]{1,0:T(8,128)S(1)}, f32[256,256]{1,0:T(8,128)S(1)}, u32[]{:S(2)}, u32[]{:S(2)}) collective-permute-start(f32[256,256]{1,0:T(8,128)S(1)} %get-tuple-element.78), channel_id=1, source_target_pairs={{0,1},{1,2},{2,3},{4,5},{5,6},{6,7},{8,9},{9,10},{10,11},{12,13},{... | collective-permute-start | bytes 786440 | tf_op jit(solution)/shard_map/ppermute | solution.py:25
  8.4 18.5 %collective-permute-start.1 = (f32[256,256]{1,0:T(8,128)S(1)}, f32[256,256]{1,0:T(8,128)S(1)}, u32[]{:S(2)}, u32[]{:S(2)}) collective-permute-start(f32[256,256]{1,0:T(8,128)S(1)} %get-tuple-element.79), channel_id=1, source_target_pairs={{1,0},{2,1},{3,2},{5,4},{6,5},{7,6},{9,8},{10,9},{11,10},{13,12},{... | collective-permute-start | bytes 786440 | tf_op jit(solution)/shard_map/ppermute | solution.py:26
  27.0 21.2 %copy-start.12 = (f32[256,128]{1,0:T(8,128)S(1)}, f32[256,128]{1,0:T(8,128)}, u32[]{:S(2)}) copy-start(f32[256,128]{1,0:T(8,128)} %refs_7_.5) | copy-start | bytes 393220
  27.0 21.2 %copy-start.18 = (f32[512]{0:T(512)S(1)}, f32[512]{0:T(512)}, u32[]{:S(2)}) copy-start(f32[512]{0:T(512)} %param.23) | copy-start | bytes 6148
  27.0 21.2 %copy-start.19 = (f32[512]{0:T(512)S(1)}, f32[512]{0:T(512)}, u32[]{:S(2)}) copy-start(f32[512]{0:T(512)} %param.24) | copy-start | bytes 6148
  31.1 1.4 copy-start.29
  32.5 109.5 %copy-start.15 = (f32[8,256]{1,0:T(8,128)}, f32[8,256]{1,0:T(8,128)S(1)}, u32[]{:S(2)}) copy-start(f32[8,256]{1,0:T(8,128)S(1)} %get-tuple-element.81.refs_2_.refs_15_) | copy-start | bytes 24580
  32.5 15.6 %collective-permute-start.2 = (f32[256,512]{1,0:T(8,128)S(1)}, f32[256,512]{1,0:T(8,128)S(1)}, u32[]{:S(2)}, u32[]{:S(2)}) collective-permute-start(f32[256,512]{1,0:T(8,128)S(1)} %get-tuple-element.83), channel_id=1, source_target_pairs={{0,1},{1,2},{2,3},{4,5},{5,6},{6,7},{8,9},{9,10},{10,11},{12,13},{... | collective-permute-start | bytes 1572872 | tf_op jit(solution)/shard_map/ppermute | solution.py:25
  34.7 13.5 %collective-permute-start.3 = (f32[256,512]{1,0:T(8,128)S(1)}, f32[256,512]{1,0:T(8,128)S(1)}, u32[]{:S(2)}, u32[]{:S(2)}) collective-permute-start(f32[256,512]{1,0:T(8,128)S(1)} %get-tuple-element.84), channel_id=1, source_target_pairs={{1,0},{2,1},{3,2},{5,4},{6,5},{7,6},{9,8},{10,9},{11,10},{13,12},{... | collective-permute-start | bytes 1572872 | tf_op jit(solution)/shard_map/ppermute | solution.py:26
  36.0 26.9 %copy-start.8 = (bf16[256,1024]{1,0:T(8,128)(2,1)S(1)}, bf16[256,1024]{1,0:T(8,128)(2,1)}, u32[]{:S(2)}) copy-start(bf16[256,1024]{1,0:T(8,128)(2,1)} %refs_6_.3) | copy-start | bytes 1572868
  36.0 26.9 %copy-start.10 = (f32[128,512]{1,0:T(8,128)S(1)}, f32[128,512]{1,0:T(8,128)}, u32[]{:S(2)}) copy-start(f32[128,512]{1,0:T(8,128)} %refs_3_.1) | copy-start | bytes 786436
  36.0 26.9 %copy-start.24 = (f32[512]{0:T(512)S(1)}, f32[512]{0:T(512)}, u32[]{:S(2)}) copy-start(f32[512]{0:T(512)} %param.29) | copy-start | bytes 6148
  36.0 26.9 %copy-start.25 = (f32[128]{0:T(128)S(1)}, f32[128]{0:T(128)}, u32[]{:S(2)}) copy-start(f32[128]{0:T(128)} %param.26) | copy-start | bytes 1540
  36.0 26.9 %copy-start.27 = (f32[128]{0:T(128)S(1)}, f32[128]{0:T(128)}, u32[]{:S(2)}) copy-start(f32[128]{0:T(128)} %param.27) | copy-start | bytes 1540
  48.2 30.7 %copy-start.5 = (bf16[16,4,16,1024]{3,2,1,0:T(8,128)(2,1)S(1)}, bf16[16,4,16,1024]{3,2,1,0:T(8,128)(2,1)}, u32[]{:S(2)}) copy-start(bf16[16,4,16,1024]{3,2,1,0:T(8,128)(2,1)} %param.33) | copy-start | bytes 6291460
  50.4 28.4 %copy-start.1 = (bf16[16,4,16,1024]{3,2,1,0:T(8,128)(2,1)S(1)}, bf16[16,4,16,1024]{3,2,1,0:T(8,128)(2,1)}, u32[]{:S(2)}) copy-start(bf16[16,4,16,1024]{3,2,1,0:T(8,128)(2,1)} %param.17) | copy-start | bytes 6291460
  50.5 28.4 %copy-start.20 = (f32[1024]{0:T(1024)S(1)}, f32[1024]{0:T(1024)}, u32[]{:S(2)}) copy-start(f32[1024]{0:T(1024)} %param.31) | copy-start | bytes 12292
  50.5 28.4 %copy-start.23 = (f32[1024]{0:T(1024)S(1)}, f32[1024]{0:T(1024)}, u32[]{:S(2)}) copy-start(f32[1024]{0:T(1024)} %param.32) | copy-start | bytes 12292
  65.5 0.6 copy-start.21
  66.1 18.2 %copy-start.13 = (bf16[1024,256]{1,0:T(8,128)(2,1)}, bf16[1024,256]{1,0:T(8,128)(2,1)S(1)}, u32[]{:S(2)}) copy-start(bf16[1024,256]{1,0:T(8,128)(2,1)S(1)} %get-tuple-element.113.refs_1_) | copy-start | bytes 1572868
  84.3 16.3 %copy-start.2 = (f32[1024,1024]{1,0:T(8,128)}, f32[1024,1024]{1,0:T(8,128)S(1)}, u32[]{:S(2)}) copy-start(f32[1024,1024]{1,0:T(8,128)S(1)} %get-tuple-element.92.refs_4_.refs_3_) | copy-start | bytes 12582916
  100.7 1.3 copy-start.6
  102.0 3.1 %collective-permute-start.4 = (f32[256,256]{1,0:T(8,128)S(1)}, f32[256,256]{1,0:T(8,128)S(1)}, u32[]{:S(2)}, u32[]{:S(2)}) collective-permute-start(f32[256,256]{1,0:T(8,128)S(1)} %get-tuple-element.95), channel_id=1, source_target_pairs={{0,1},{1,2},{2,3},{4,5},{5,6},{6,7},{8,9},{9,10},{10,11},{12,13},{... | collective-permute-start | bytes 786440 | tf_op jit(solution)/shard_map/ppermute | solution.py:25
  103.8 3.4 %collective-permute-start.5 = (f32[256,256]{1,0:T(8,128)S(1)}, f32[256,256]{1,0:T(8,128)S(1)}, u32[]{:S(2)}, u32[]{:S(2)}) collective-permute-start(f32[256,256]{1,0:T(8,128)S(1)} %get-tuple-element.96), channel_id=1, source_target_pairs={{1,0},{2,1},{3,2},{5,4},{6,5},{7,6},{9,8},{10,9},{11,10},{13,12},{... | collective-permute-start | bytes 786440 | tf_op jit(solution)/shard_map/ppermute | solution.py:26
  108.2 33.8 %copy-start.14 = (f32[16,512]{1,0:T(8,128)}, f32[16,512]{1,0:T(8,128)S(1)}, u32[]{:S(2)}) copy-start(f32[16,512]{1,0:T(8,128)S(1)} %get-tuple-element.107.refs_18_.refs_4_) | copy-start | bytes 98308
  149.2 1.0 copy-start.11
  150.2 1.0 copy-start.28
  151.2 13.2 %all-to-all-start.7 = ((f32[32,16,128]{2,1,0:T(8,128)}), f32[32,16,128]{2,1,0:T(8,128)S(1)}, u32[]{:S(2)}, u32[]{:S(2)}) async-start(f32[32,16,128]{2,1,0:T(8,128)} %get-tuple-element.108), calls=%async_computation.7 | async-start | bytes 524288 | tf_op jit(solution)/shard_map/all_to_all | solution.py:31
  158.2 11.4 %collective-permute-start.7 = (bf16[1152,256]{1,0:T(8,128)(2,1)}, bf16[1152,256]{1,0:T(8,128)(2,1)S(1)}, u32[]{:S(2)}, u32[]{:S(2)}) collective-permute-start(bf16[1152,256]{1,0:T(8,128)(2,1)} %get-tuple-element.112.refs_5_.refs_7_), channel_id=1, source_target_pairs={{0,1},{1,0},{2,3},{3,2},{4,5},{5,4},{6,7},{7,6},{8,9},{9,8},{10,11... | collective-permute-start | bytes 1769480 | tf_op jit(solution)/shard_map/ppermute | solution.py:36
  161.9 7.7 %collective-permute-start.6 = (bf16[640,256]{1,0:T(8,128)(2,1)}, bf16[640,256]{1,0:T(8,128)(2,1)S(1)}, u32[]{:S(2)}, u32[]{:S(2)}) collective-permute-start(bf16[640,256]{1,0:T(8,128)(2,1)} %get-tuple-element.116.refs_8_), channel_id=1, source_target_pairs={{0,1},{1,0},{2,3},{3,2},{4,5},{5,4},{6,7},{7,6},{8,9},{9,8},{10,11... | collective-permute-start | bytes 983048 | tf_op jit(solution)/shard_map/ppermute | solution.py:36
  164.4 0.7 copy-start.30
  169.6 1.7 collective-permute-start.8
  169.6 1.7 copy-start.32
  169.6 1.7 copy-start.31
  171.3 0.7 copy-start.33
  175.2 31.6 %all-to-all-start.8 = ((bf16[16,144,256]{2,1,0:T(8,128)(2,1)}), bf16[16,144,256]{2,1,0:T(8,128)(2,1)S(1)}, u32[]{:S(2)}, u32[]{:S(2)}) async-start(bf16[16,144,256]{2,1,0:T(8,128)(2,1)} %shard_map.300.refs_4_), calls=%async_computation.8 | async-start | bytes 2359296 | tf_op jit(solution)/shard_map/all_to_all | solution.py:42
  180.0 26.9 %copy-start.17 = (s32[19]{0:T(128)S(1)}, s32[19]{0:T(128)}, u32[]{:S(2)}) copy-start(s32[19]{0:T(128)} %copy-done.16) | copy-start | bytes 232
  206.8 1.6 copy-start.3
  244.5 2.8 %collective-permute-start.9 = (bf16[16,144,256]{2,1,0:T(8,128)(2,1)S(1)}, bf16[16,144,256]{2,1,0:T(8,128)(2,1)S(1)}, u32[]{:S(2)}, u32[]{:S(2)}) collective-permute-start(bf16[16,144,256]{2,1,0:T(8,128)(2,1)S(1)} %all_to_all.57.refs_1_), channel_id=1, source_target_pairs={{0,1},{1,0},{2,3},{3,2},{4,5},{5,4},{6,7},{7,6},{8,9},{9,8},{10,11... | collective-permute-start | bytes 3538952 | tf_op jit(solution)/shard_map/ppermute | solution.py:36

commit v4 on v3

--- a/solution.py
+++ b/solution.py
@@ -14,6 +14,7 @@
 BF16 = jnp.bfloat16
 COLS = 16
 LANES = 128
+TOKEN = ((8, LANES), F32, "hbm")
 
 
 def device_count():
@@ -31,9 +32,9 @@
     return lax.all_to_all(block, ALL, 0, 0)
 
 
-def swap_cores(block):
+def swap(block, bit):
     count = lax.axis_size("narrow")
-    return lax.ppermute(block, "narrow", [(i, i ^ 1) for i in range(count)])
+    return lax.ppermute(block, "narrow", [(i, i ^ bit) for i in range(count)])
 
 
 def exchange_chips(block):
@@ -54,12 +55,12 @@
     pixel = lax.broadcasted_iota(jnp.int32, (count * COLS, LANES), 0)
     row = (pixel >> 4) + (meta[0] + start)
     col = pixel & (COLS - 1)
-    side = 12 + 2 * meta[3 + image]
+    side = 12 + 2 * meta[4 + image]
     return jnp.where((row < side) & (row >= 0) & (col < side), 1.0, 0.0).astype(F32)
 
 
 def area_of(meta, image):
-    side = (12 + 2 * meta[3 + image]).astype(F32)
+    side = (12 + 2 * meta[4 + image]).astype(F32)
     return side * side
 
 
@@ -113,26 +114,37 @@
     return pl.BlockSpec(shape, lambda step: (0,) * len(shape))
 
 
-def call(kernel, outs, args, scratch=(), megabytes=56, flops=0, after=(), local="", **sizes):
+def call(
+    kernel, outs, args, scratch=(), megabytes=24, flops=0, after=(), local="", raw_in=(), raw_out=(), **sizes
+):
     moved = sum(a.size * a.dtype.itemsize for a in args) + sum(
-        functools.reduce(lambda x, y: x * y, s) * jnp.dtype(t).itemsize for s, t in outs
+        functools.reduce(lambda x, y: x * y, o[0]) * jnp.dtype(o[1]).itemsize for o in outs
     )
     count = len(args)
     vmem = pl.BlockSpec(memory_space=pltpu.VMEM)
+    anywhere = pl.BlockSpec(memory_space=pl.ANY)
+    in_hbm = lambda a: pltpu.with_memory_space_constraint(a, pltpu.HBM)
+    args = [in_hbm(a) if k in raw_in else a for k, a in enumerate(args)]
+    after = [in_hbm(a) if a.shape == TOKEN[0] else a for a in after]
 
     def run(*refs):
         kernel(*refs[:count], *refs[count + len(after) :], **sizes)
+
+    def spec(place, shape, kept, raws):
+        return anywhere if place in raws else vmem if kept else whole(shape)
 
     return pl.pallas_call(
         run,
         grid=() if local == "in out" else (1,),
-        out_shape=[jax.ShapeDtypeStruct(s, t) for s, t in outs],
+        out_shape=[
+            pltpu.HBM(o[0], o[1]) if len(o) > 2 else jax.ShapeDtypeStruct(o[0], o[1]) for o in outs
+        ],
         in_specs=[pl.BlockSpec(memory_space=pltpu.SMEM)]
-        + [vmem if "in" in local else whole(a.shape) for a in args[1:]]
-        + [pl.BlockSpec(memory_space=pl.ANY)] * len(after),
-        out_specs=[vmem if "out" in local else whole(s) for s, _ in outs],
-        scratch_shapes=[pltpu.VMEM(s, t) for s, t in scratch],
-        compiler_params=pltpu.CompilerParams(vmem_limit_bytes=(24 if local else megabytes) << 20),
+        + [spec(k, a.shape, "in" in local, raw_in) for k, a in enumerate(args) if k]
+        + [anywhere] * len(after),
+        out_specs=[spec(k, o[0], "out" in local, raw_out) for k, o in enumerate(outs)],
+        scratch_shapes=[pltpu.VMEM(*entry) if isinstance(entry, tuple) else entry for entry in scratch],
+        compiler_params=pltpu.CompilerParams(vmem_limit_bytes=megabytes << 20),
         cost_estimate=pl.CostEstimate(flops=flops, bytes_accessed=moved, transcendentals=0),
     )(*args, *after)
 
@@ -167,7 +179,7 @@
 
 
 def split_kernel(
-    meta, got, pre, low, high, gain, shift, w, hid, out, top, bottom, pay, stat, acc, *, blocks, rows
+    meta, got, pre, low, high, gain, shift, w, hid_out, out, top, bottom, pay, stat, acc, hid, sem, *, blocks, rows
 ):
     slab = rows * COLS
     sums = jnp.sum(got[...], 0)
@@ -193,6 +205,8 @@
         return carry
 
     lax.fori_loop(0, blocks, prepare, 0)
+    copy = pltpu.make_async_copy(hid, hid_out, sem)
+    copy.start()
     acc[...] = jnp.zeros_like(acc)
     group = 4
 
@@ -227,6 +241,7 @@
     put_row(pay, 0, total(acc[0]))
     put_row(pay, 4, total(acc[1]))
     spread(pay)
+    copy.wait()
 
 
 def pool_kernel(
@@ -367,7 +382,7 @@
 
 
 def mixture_kernel(
-    meta, got, stat3, pre, grad, gain, w, hid, gexp, gmix, top, bottom, gatt, gain_out, shift_out, *, blocks, rows
+    meta, got, stat3, pre, grad, gain, w, hid, att, gexp, gmix, top, bottom, glog, gain_out, shift_out, *, blocks, rows
 ):
     slab = rows * COLS
     sums = jnp.sum(got[...], 0)
@@ -405,48 +420,62 @@
             bottom[edge, :] = part[slab - COLS :]
             for half in range(2):
                 lanes = slice(half * 256, half * 256 + 256)
-                gatt[pl.ds(image, 1), lanes] = total(fold(part * hid[own, lanes].astype(F32)))
+                glog[pl.ds(image, 1), lanes] = total(fold(part * hid[own, lanes].astype(F32)))
         return carry
 
     lax.fori_loop(0, blocks // group, step, 0)
-
-
-def logits_kernel(meta, gatt, att, we, glog, pay):
     first, second = att[:, :256], att[:, 256:]
-    inner = first * gatt[:, :256] + second * gatt[:, 256:]
-    logits = jnp.concatenate(
-        [first * (gatt[:, :256] - inner), second * (gatt[:, 256:] - inner)], axis=1
-    )
-    glog[...] = logits
-    pay[0] = dot(logits, we[...], ((1,), (1,)), HIGHEST)
+    inner = first * glog[:, :256] + second * glog[:, 256:]
+    glog[...] = jnp.concatenate(
+        [first * (glog[:, :256] - inner), second * (glog[:, 256:] - inner)], axis=1
+    )
+
+
+def logits_kernel(meta, glog, we, pay):
+    pay[0] = dot(glog[...], we[...], ((1,), (1,)), HIGHEST)
     spread(pay)
 
 
 def expand_grad_kernel(meta, mix, gexp, hsq, glog, keep, send):
     for ref, core in ((send, 1 - meta[2]), (keep, meta[2])):
-        for k in range(2):
-            lanes = pl.ds(pl.multiple_of(core * 512 + k * 256, 256), 256)
-            ref[k * 256 : k * 256 + 256, :] = dot(mix[...], gexp[:, lanes], ((0,), (0,))).astype(ref.dtype)
+        lanes = pl.ds(pl.multiple_of(core * 512, 512), 512)
+        value = dot(mix[...], gexp[:, lanes], ((0,), (0,))).astype(ref.dtype)
         lanes = pl.ds(pl.multiple_of(core * 256, 256), 256)
-        ref[512:, :] = dot(hsq[...], glog[:, lanes], ((0,), (0,)), HIGHEST).astype(ref.dtype)
-
-
-def pack_kernel(meta, *refs):
-    out = refs[-1]
-    start = 0
-    for keep, got in zip(refs[:-1:2], refs[1:-1:2]):
-        share = keep.shape[0] // out.shape[0]
-        for chip in range(out.shape[0]):
-            rows = slice(chip * share, chip * share + share)
-            out[chip, start : start + share, :] = (keep[rows] + got[rows].astype(F32)).astype(BF16)
-        start += share
-
-
-def share_kernel(meta, shares, out):
-    value = shares[0].astype(F32)
-    for k in range(1, shares.shape[0]):
-        value = value + shares[k].astype(F32)
-    out[0] = value.astype(BF16)
+        excite = dot(hsq[...], glog[:, lanes], ((0,), (0,)), HIGHEST).astype(ref.dtype)
+        for q in range(2):
+            for k in range(2):
+                first = k * 256 + q * 128
+                ref[q, k * 256 : k * 256 + 256, :] = value[:, first : first + 128]
+            ref[q, 512:, :] = excite[:, q * 128 : q * 128 + 128]
+
+
+def add_kernel(meta, keep2, got2, keep3, got3, keep, send, token):
+    first = keep2.shape[1]
+    for ref, half in ((send, 1 - meta[3]), (keep, meta[3])):
+        ref[:first, :] = (keep2[half] + got2[half].astype(F32)).astype(ref.dtype)
+        ref[first:, :] = (keep3[half] + got3[half].astype(F32)).astype(ref.dtype)
+    token[...] = jnp.zeros_like(token)
+
+
+def pack_kernel(meta, keep, got, keep1, got1, out):
+    chips = out.shape[0]
+    large, small = keep.shape[0] // chips, keep1.shape[0] // chips
+    out[:, :large, :] = (keep[...] + got[...].astype(F32)).astype(BF16).reshape(chips, large, LANES)
+    out[:, large:, :] = (keep1[...] + got1[...].astype(F32)).astype(BF16).reshape(chips, small, LANES)
+
+
+def share_kernel(meta, shares, out, *, large):
+    chips, rows, _ = shares.shape
+
+    def add(first, last, start, step):
+        value = shares[start, first:last, :].astype(F32)
+        for k in range(start + step, chips, step):
+            value = value + shares[k, first:last, :].astype(F32)
+        return value.astype(BF16)
+
+    out[0, :large, :] = add(0, large, 0, 2)
+    out[0, large : 2 * large, :] = add(0, large, 1, 2)
+    out[0, 2 * large :, :] = add(large, rows, 0, 1)
     block = out[0]
 
     def step(k, carry):
@@ -519,9 +548,12 @@
 
 def conv_kernel(
     meta, got, stat2, gain2, shift2, dz, pre2, low2, high2, lowm, highm, att, gpool, w, pre, stat,
-    gain, shift, glog, gsplit, out, pay, gain_out, shift_out, tall, acc, *, blocks, rows
+    gain, shift, glog, hid_in, out_hbm, keep_hbm, send_hbm, pay, gain_out, shift_out, tall, acc,
+    hid, out, keep, send, sems, *, blocks, rows
 ):
     slab = rows * COLS
+    fetch = pltpu.make_async_copy(hid_in, hid, sems.at[0])
+    fetch.start()
     sums = jnp.sum(got[...], 0)
     shift_sum, gain_sum = row_of(sums, 0, 4), row_of(sums, 4, 4)
     shift_out[...] = shift_sum
@@ -558,10 +590,33 @@
             tall[0, i, :, lanes] = left
             tall[1, i, :, lanes] = middle
             tall[2, i, :, lanes] = right
-            gsplit[own, lanes] = middle[COLS : COLS + slab]
         return carry
 
     lax.fori_loop(0, blocks, prepare, 0)
+    fetch.wait()
+
+    def weights(dy, carry):
+        rows_at = pl.ds(pl.multiple_of(dy * COLS, COLS), slab)
+        for ref, core in ((send, 1 - meta[2]), (keep, meta[2])):
+            lanes = pl.ds(pl.multiple_of(core * 128, 128), 128)
+            wide_lanes = pl.ds(pl.multiple_of(core * 256, 256), 256)
+            grads = tall[1, :, COLS : COLS + slab, wide_lanes].reshape(blocks * slab, 256)
+            lhs = jnp.concatenate(
+                [hid[dx, :, rows_at, lanes].reshape(blocks * slab, 128) for dx in range(3)], axis=1
+            )
+            value = dot(lhs, grads, ((0,), (0,))).astype(ref.dtype)
+            at = pl.ds(pl.multiple_of(dy * 384, 384), 384)
+            for q in range(2):
+                ref[q, at, :] = value[:, q * 128 : q * 128 + 128]
+        return carry
+
+    lax.fori_loop(0, 3, weights, 0)
+    stores = [
+        pltpu.make_async_copy(send, send_hbm, sems.at[1]),
+        pltpu.make_async_copy(keep, keep_hbm, sems.at[2]),
+    ]
+    for store in stores:
+        store.start()
     acc[...] = jnp.zeros_like(acc)
     center, inv = stat[0:1], stat[1:2]
     group = 4
@@ -593,31 +648,28 @@
         return carry
 
     lax.fori_loop(0, blocks // group, step, 0)
+    stores.append(pltpu.make_async_copy(out, out_hbm, sems.at[3]))
+    stores[-1].start()
     put_row(pay, 0, total(acc[0]))
     put_row(pay, 2, total(acc[1]))
     put_row(pay, 4, total(glog[...]))
     pay[0, 8:, :] = sums[8:]
     spread(pay)
-
-
-def split_grad_kernel(meta, hid, gsplit, keep, send, *, blocks, rows):
+    for store in stores:
+        store.wait()
+
+
+def reduce_back_kernel(
+    meta, got, stat, gain, dz_in, pre_in, x_in, small_out, keep, send, gain_out, shift_out, bias_out, squeeze,
+    dz, pre, x, small, sems, *, blocks, rows
+):
     slab = rows * COLS
-    for ref, core in ((send, 1 - meta[2]), (keep, meta[2])):
-        lanes = pl.ds(pl.multiple_of(core * 128, 128), 128)
-        grads = gsplit[:, pl.ds(pl.multiple_of(core * 256, 256), 256)]
-        for dy in range(3):
-            lhs = jnp.concatenate(
-                [
-                    hid[dx, :, dy * COLS : dy * COLS + slab, lanes].reshape(blocks * slab, 128)
-                    for dx in range(3)
-                ],
-                axis=1,
-            )
-            ref[dy * 384 : dy * 384 + 384, :] = dot(lhs, grads, ((0,), (0,))).astype(ref.dtype)
-
-
-def reduce_back_kernel(meta, got, stat, gain, dz, pre, x, small, keep, send, gain_out, shift_out, bias_out, squeeze, *, blocks, rows):
-    slab = rows * COLS
+    fetches = [
+        pltpu.make_async_copy(source, target, sems.at[k])
+        for k, (source, target) in enumerate(((dz_in, dz), (pre_in, pre), (x_in, x)))
+    ]
+    for fetch in fetches:
+        fetch.start()
     sums = jnp.sum(got[:, :8, :], 0)
     share = got.shape[1] - 8
     for n in range(got.shape[0]):
@@ -627,6 +679,8 @@
     gain_out[...] = gain_sum
     bias_out[...] = row_of(sums, 4, 4)
     a, b, d = back_terms(stat, gain[...], shift_sum, gain_sum)
+    fetches[0].wait()
+    fetches[1].wait()
 
     def step(image, carry):
         own = pl.ds(pl.multiple_of(image * slab, slab), slab)
@@ -635,13 +689,20 @@
         return carry
 
     lax.fori_loop(0, blocks, step, 0)
+    store = pltpu.make_async_copy(small, small_out, sems.at[3])
+    store.start()
+    fetches[2].wait()
     for ref, core in ((send, 1 - meta[2]), (keep, meta[2])):
         lanes = pl.ds(pl.multiple_of(core * 512, 512), 512)
-        ref[...] = dot(x[:, lanes], small[...], ((0,), (0,))).astype(ref.dtype)
-
-
-def input_kernel(meta, small, w, grad, out, *, blocks, rows):
+        value = dot(x[:, lanes], small[...], ((0,), (0,))).astype(ref.dtype)
+        for q in range(2):
+            ref[q * 512 : q * 512 + 512, :] = value[:, q * 128 : q * 128 + 128]
+    store.wait()
+
+
+def input_kernel(meta, small, w, grad, out, token, *, blocks, rows):
     slab = rows * COLS
+    token[...] = jnp.zeros_like(token)
     group = 4
 
     def step(g, carry):
@@ -661,22 +722,24 @@
     lax.fori_loop(0, blocks // group, step, 0)
 
 
-def total_kernel(meta, own, other, expand, excite, split, reduce):
-    chips = own.shape[0]
-    size3, size2, size1 = 640 // chips, 1152 // chips, 512 // chips
+def total_kernel(meta, own, other, expand, excite, split, reduce, *, large):
+    chips, rows, _ = own.shape
     for ref, core in ((own, meta[2]), (other, 1 - meta[2])):
-
-        def part(start, size, first, rows):
-            block = ref[:, start : start + size, :].reshape(chips * size, 256)
-            return block[first : first + rows].astype(F32)
-
-        for k in range(2):
-            lanes = pl.ds(pl.multiple_of(core * 512 + k * 256, 256), 256)
-            expand[:, lanes] = part(0, size3, k * 256, 256)
-        excite[:, pl.ds(pl.multiple_of(core * 256, 256), 256)] = part(0, size3, 512, 128)
-        for tap in range(9):
-            split[tap // 3, tap % 3, core] = part(size3, size2, tap * 128, 128)
-        reduce[pl.ds(pl.multiple_of(core * 512, 512), 512), :] = part(size3 + size2, size1, 0, 512)
+        for q in range(2):
+            lanes = slice(q * 128, q * 128 + 128)
+            block = ref[:, q * large : q * large + large, :].reshape(chips * large, LANES)
+            for tap in range(9):
+                split[tap // 3, tap % 3, core, :, lanes] = block[tap * 128 : tap * 128 + 128].astype(F32)
+            for k in range(2):
+                first = 1152 + k * 256
+                out = pl.ds(pl.multiple_of(core * 512 + (k * 256 + q * 128), 128), 128)
+                expand[:, out] = block[first : first + 256].astype(F32)
+            out = pl.ds(pl.multiple_of(core * 256 + q * 128, 128), 128)
+            excite[:, out] = block[1664:].astype(F32)
+        block = ref[:, 2 * large :, :].reshape(chips * (rows - 2 * large), LANES)
+        own_rows = pl.ds(pl.multiple_of(core * 512, 512), 512)
+        for q in range(2):
+            reduce[own_rows, q * 128 : q * 128 + 128] = block[q * 512 : q * 512 + 512].astype(F32)
 
 
 def body(
@@ -713,6 +776,7 @@
             (lax.axis_index("narrow") * rows).astype(jnp.int32)[None],
             lax.axis_index("batch").astype(jnp.int32)[None],
             (lax.axis_index("narrow") % 2).astype(jnp.int32)[None],
+            (lax.axis_index("narrow") // 2 % 2).astype(jnp.int32)[None],
             image_class,
         ]
     )
@@ -740,7 +804,7 @@
     hid1, pre2, top, bottom, pay, stat1 = call(
         split_kernel,
         [
-            ((3, blocks, slab + 2 * cols, mid), BF16),
+            ((3, blocks, slab + 2 * cols, mid), BF16, "hbm"),
             ((pixels, 2 * mid), F32),
             ((edge, 2 * mid), F32),
             ((edge, 2 * mid), F32),
@@ -748,7 +812,8 @@
             ((8, mid), F32),
         ],
         [meta, exchange(pay), pre1, low, high, gain1, shift1, weight_split],
-        [((2, 8, 2 * mid), F32)],
+        [((2, 8, 2 * mid), F32), ((3, blocks, slab + 2 * cols, mid), BF16), pltpu.SemaphoreType.DMA],
+        raw_out=(0,),
         flops=large,
         local="in out",
         **sizes,
@@ -808,7 +873,7 @@
         local="in out",
         **sizes,
     )
-    gexp, gmix, top, bottom, gatt, gain3_grad, shift3_grad = call(
+    gexp, gmix, top, bottom, glog, gain3_grad, shift3_grad = call(
         mixture_kernel,
         [
             ((pixels, channels), BF16),
@@ -819,17 +884,24 @@
             ((1, channels), F32),
             ((1, channels), F32),
         ],
-        [meta, exchange(pay), stat3, pre3, grad_res, gain3, weight_expand, hid2],
+        [meta, exchange(pay), stat3, pre3, grad_res, gain3, weight_expand, hid2, att],
         flops=small,
         local="in out",
         **sizes,
     )
     lowm, highm = halo(top, bottom)
-    glog, pay = call(
+    keep3, send3 = call(
+        expand_grad_kernel,
+        [((2, 2 * mid + inter, LANES), F32), ((2, 2 * mid + inter, LANES), BF16)],
+        [meta, mix, gexp, hsq, glog],
+        flops=small,
+        local="in out",
+    )
+    (pay,) = call(
         logits_kernel,
-        [((blocks, 2 * mid), F32), ((count, blocks, inter), F32)],
-        [meta, gatt, att, weight_excite],
-        after=(lowm, highm),
+        [((count, blocks, inter), F32)],
+        [meta, glog, weight_excite],
+        after=(lowm, highm, send3),
         local="in out",
     )
     dz2, gpool, pay, gain_sq_grad, shift_sq_grad = call(
@@ -862,12 +934,13 @@
         local="in out",
         **sizes,
     )
-    gsplit, dz1, pay, gain2_grad, shift2_grad = call(
+    dz1, keep2, send2, pay, gain2_grad, shift2_grad = call(
         conv_kernel,
         [
-            ((pixels, 2 * mid), BF16),
-            ((pixels, mid), F32),
-            ((count, 8 + share, LANES), F32),
+            ((pixels, mid), F32, "hbm"),
+            ((2, 9 * 128, LANES), F32, "hbm"),
+            ((2, 9 * 128, LANES), BF16, "hbm"),
+            ((count, 8 + share, LANES), F32, "hbm"),
             ((1, 2 * mid), F32),
             ((1, 2 * mid), F32),
         ],
@@ -891,58 +964,78 @@
             gain1,
             shift1,
             glog,
-        ],
-        [((3, blocks, slab + 2 * cols, 2 * mid), BF16), ((2, 8, mid), F32)],
-        flops=large,
+            hid1,
+        ],
+        [
+            ((3, blocks, slab + 2 * cols, 2 * mid), BF16),
+            ((2, 8, mid), F32),
+            (hid1.shape, BF16),
+            ((pixels, mid), F32),
+            ((2, 9 * 128, LANES), F32),
+            ((2, 9 * 128, LANES), BF16),
+            pltpu.SemaphoreType.DMA((4,)),
+        ],
+        raw_in=(19,),
+        raw_out=(0, 1, 2),
+        flops=2 * large,
         local="in",
         **sizes,
     )
-    keep2, send2 = call(
-        split_grad_kernel,
-        [((9 * 128, 256), F32), ((9 * 128, 256), BF16)],
-        [meta, hid1, gsplit],
-        flops=large,
-        **sizes,
-    )
-    keep3, send3 = call(
-        expand_grad_kernel,
-        [((2 * mid + inter, 256), F32), ((2 * mid + inter, 256), BF16)],
-        [meta, mix, gexp, hsq, glog],
-        flops=small,
-        after=(send2,),
+    quarter = 9 * 128 + 2 * mid + inter
+    keep, send, token = call(
+        add_kernel,
+        [((quarter, LANES), F32, "hbm"), ((quarter, LANES), BF16, "hbm"), TOKEN],
+        [meta, keep2, swap(send2, 1), keep3, swap(send3, 1)],
     )
     small1, keep1, send1, gain1_grad, shift1_grad, bias_grad, squeeze_total = call(
         reduce_back_kernel,
         [
-            ((pixels, mid), BF16),
-            ((channels // 2, mid), F32),
-            ((channels // 2, mid), BF16),
+            ((pixels, mid), BF16, "hbm"),
+            ((channels, mid // 2), F32),
+            ((channels, mid // 2), BF16),
             ((1, mid), F32),
             ((1, mid), F32),
             ((1, 2 * mid), F32),
             ((mid, inter), F32),
         ],
         [meta, exchange(pay), stat1, gain1, dz1, pre1, x],
+        [
+            ((pixels, mid), F32),
+            ((pixels, mid), F32),
+            ((pixels, channels), BF16),
+            ((pixels, mid), BF16),
+            pltpu.SemaphoreType.DMA((4,)),
+        ],
+        raw_in=(4, 5, 6),
+        raw_out=(0,),
         flops=small,
-        after=(send2, send3),
+        after=(token,),
+        local="in",
         **sizes,
     )
     chips = count // 2
-    share_rows = [keep.shape[0] // chips for keep in (keep3, keep2, keep1)]
+    large = quarter // chips
     (packed,) = call(
         pack_kernel,
-        [((chips, sum(share_rows), 256), BF16)],
-        [meta, keep3, swap_cores(send3), keep2, swap_cores(send2), keep1, swap_cores(send1)],
-    )
-    (input_grad,) = call(
+        [((chips, large + channels // chips, LANES), BF16, "hbm")],
+        [meta, keep, swap(send, 2), keep1, swap(send1, 1)],
+    )
+    input_grad, token = call(
         input_kernel,
-        [((pixels, channels), BF16)],
+        [((pixels, channels), BF16, "hbm"), TOKEN],
         [meta, small1, weight_reduce, grad_res],
         flops=small,
         after=(packed,),
         **sizes,
     )
-    (shared,) = call(share_kernel, [(packed.shape, BF16)], [meta, exchange_chips(packed)], after=(input_grad,), local="in out")
+    (shared,) = call(
+        share_kernel,
+        [((chips, 2 * large + channels // chips, LANES), BF16)],
+        [meta, exchange_chips(packed)],
+        after=(token,),
+        local="out",
+        large=large,
+    )
     own = exchange_chips(shared)
     expand_total, excite_total, split_total, reduce_total = call(
         total_kernel,
@@ -952,8 +1045,9 @@
             (weight_split.shape, F32),
             ((channels, mid), F32),
         ],
-        [meta, own, swap_cores(own)],
+        [meta, own, swap(own, 1)],
         local="in",
+        large=large,
     )
     flat = lambda v: v.reshape(-1)
     return (

time: 251 us -> 236 us (0.940)
  waiting for transfers between devices: 30.3 us -> 23.8 us
  Pallas kernels: 56.2 us -> 50.3 us
  starting transfers between devices: 18.1 us -> 21.1 us
  local copies, waits for them, and re-layouts: 11 us -> 8.04 us
    all_to_all x1, waiting for transfers between devices: 21.5 us -> 11.4 us  [exchange_chips(): return lax.all_to_all(block, ALL, 0, 0, axis_index_groups=groups)]
    pallas_call x16, Pallas kernels: 56.2 us -> 50.3 us  [call(): pl.pallas_call(run, grid=() if local == 'in out' else (1,), out_shape=[pl...]
    unnamed x68 -> x50, local copies, waits for them, and re-layouts: 11 us -> 7.3 us
    ppermute x4 -> x5, waiting for transfers between devices: 4.54 us -> 7.48 us  [swap(): return lax.ppermute(block, 'narrow', [(i, i ^ bit) for i in range(count)])]
  transfers between devices with their start and end apart: 12 -> 13, of which waited for: 5 -> 7; matrix products, arithmetic and copies ran while one was open for 0% -> 0% of each run, Pallas kernels for 7% -> 5%
where the time goes in v4:
time: 236 us; the launch traced here: 235 us
  blocking collectives  131 us (56%)
  Pallas kernels  50.3 us (21%)
  waiting for transfers between devices  23.8 us (10%)
  starting transfers between devices  21.1 us (9%)
  local copies, waits for them, and re-layouts  8.04 us (3%)
    all_to_all x7, blocking collectives, exchange(): return lax.all_to_all(block, ALL, 0, 0)  97.6 us
    pallas_call x16, Pallas kernels, call(): pl.pallas_call(run, grid=() if local == 'in out' else (1,), out_shape=[pl...  50.3 us
    all_to_all x1, blocking collectives, exchange_chips(): return lax.all_to_all(block, ALL, 0, 0, axis_index_groups=groups)  33.4 us
    all_to_all x1, waiting for transfers between devices, exchange_chips(): return lax.all_to_all(block, ALL, 0, 0, axis_index_groups=groups)  11.4 us
    ppermute x5, waiting for transfers between devices, swap(): return lax.ppermute(block, 'narrow', [(i, i ^ bit) for i in range(count)])  7.48 us
    unnamed x50, local copies, waits for them, and re-layouts  7.3 us
    ppermute x3, starting transfers between devices, halo(): low = lax.ppermute(bottom, 'narrow', [(i, i + 1) for i in range(count - 1)])  6.35 us
    all_to_all x1, starting transfers between devices, exchange_chips(): return lax.all_to_all(block, ALL, 0, 0, axis_index_groups=groups)  6.13 us
  transfers between devices with their start and end apart: 13, of which 7 were waited for; matrix products, arithmetic and copies ran while one was open for 0% of the time, Pallas kernels for 5%

profile of v4, /device:TPU:0, one launch (start us, length us, event | category | flops | bytes accessed | tf_op | source)
XLA Modules:
  0.0 235.3 jit_solution(2174436208962134001)
XLA Ops:
  0.7 0.7 concatenate.3.refs_0_
  1.4 1.6 copy-done
  3.0 1.0 copy-done.7
  4.1 1.9 shard_map.288
  6.0 2.4 %collective-permute-start = (f32[256,256]{1,0:T(8,128)S(1)}, f32[256,256]{1,0:T(8,128)S(1)}, u32[]{:S(2)}, u32[]{:S(2)}) collective-permute-start(f32[256,256]{1,0:T(8,128)S(1)} %get-tuple-element.80), channel_id=1, source_target_pairs={{0,1},{1,2},{2,3},{4,5},{5,6},{6,7},{8,9},{9,10},{10,11},{12,13},{... | collective-permute-start | bytes 786440 | tf_op jit(solution)/shard_map/ppermute | solution.py:26
  8.4 1.3 collective-permute-start.1
  9.7 17.2 %all_to_all.50.refs_1_ = f32[32,8,128]{2,1,0:T(8,128)S(1)} all-to-all(f32[32,8,128]{2,1,0:T(8,128)S(1)} %get-tuple-element.78), channel_id=1, replica_groups=mesh['batch'=8,'narrow'=4] {'batch','narrow'}, dimensions={0} | all-to-all | bytes 262144 | tf_op jit(solution)/shard_map/all_to_all | solution.py:32
  27.0 4.1 %shard_map.289 = (bf16[3,16,96,256]{3,2,1,0:T(8,128)(2,1)}, f32[1024,512]{1,0:T(8,128)S(1)}, f32[256,512]{1,0:T(8,128)S(1)}, f32[256,512]{1,0:T(8,128)S(1)}, f32...) custom-call(s32[20]{0:T(128)S(1)} %concatenate.3.refs_0_, f32[32,8,128]{2,1,0:T(8,128)S(1)} %all_to_all.50.refs_1_, ...), custom_call_target="tpu_custom_call" | custom-call | flops 1207959552 | bytes 8530000 | tf_op jit(solution)/shard_map/pallas_call | solution.py:136
  31.2 2.2 collective-permute-start.2
  33.3 1.3 collective-permute-start.3
  34.7 12.1 %all_to_all.51.refs_1_ = f32[32,8,128]{2,1,0:T(8,128)S(1)} all-to-all(f32[32,8,128]{2,1,0:T(8,128)S(1)} %get-tuple-element.82), channel_id=1, replica_groups=mesh['batch'=8,'narrow'=4] {'batch','narrow'}, dimensions={0} | all-to-all | bytes 262144 | tf_op jit(solution)/shard_map/all_to_all | solution.py:32
  46.8 2.2 shard_map.290
  49.1 12.4 %all_to_all.52.refs_1_ = f32[32,16,128]{2,1,0:T(8,128)S(1)} all-to-all(f32[32,16,128]{2,1,0:T(8,128)S(1)} %get-tuple-element.87), channel_id=1, replica_groups=mesh['batch'=8,'narrow'=4] {'batch','narrow'}, dimensions={0} | all-to-all | bytes 524288 | tf_op jit(solution)/shard_map/all_to_all | solution.py:32
  61.6 2.6 %shard_map.291 = (bf16[1024,256]{1,0:T(8,128)(2,1)S(1)}, bf16[1024,1024]{1,0:T(8,128)(2,1)S(1)}, f32[16,512]{1,0:T(8,128)S(1)}, f32[16,128]{1,0:T(8,128)S(1)}, f...) custom-call(s32[20]{0:T(128)S(1)} %concatenate.3.refs_0_, ...), custom_call_target="tpu_custom_call" | custom-call | flops 536870912 | bytes 5160016 | tf_op jit(solution)/shard_map/pallas_call | solution.py:136
  64.2 12.7 %all_to_all.53.refs_1_ = f32[32,16,128]{2,1,0:T(8,128)S(1)} all-to-all(f32[32,16,128]{2,1,0:T(8,128)S(1)} %get-tuple-element.89), channel_id=1, replica_groups=mesh['batch'=8,'narrow'=4] {'batch','narrow'}, dimensions={0} | all-to-all | bytes 524288 | tf_op jit(solution)/shard_map/all_to_all | solution.py:32
  76.9 5.5 %shard_map.292 = (bf16[1024,1024]{1,0:T(8,128)(2,1)}, f32[1024,1024]{1,0:T(8,128)S(1)}, f32[32,16,128]{2,1,0:T(8,128)S(1)}, f32[8,1024]{1,0:T(8,128)S(1)}) custom-call(s32[20]{0:T(128)S(1)} %concatenate.3.refs_0_, f32[32,16,128]{2,1,0:T(8,128)S(1)} %all_to_all.53.refs_1_, f32[8,256]{1,0:T(8,128)S(1)} %get-tuple-element.83.refs_2_.refs_15_, ...), custom_call_target="tpu_custom_call" | custom-call | bytes 13156432 | tf_op jit(solution)/shard_map/pallas_call | solution.py:136
  82.4 12.8 %all_to_all.54.refs_1_ = f32[32,16,128]{2,1,0:T(8,128)S(1)} all-to-all(f32[32,16,128]{2,1,0:T(8,128)S(1)} %get-tuple-element.92), channel_id=1, replica_groups=mesh['batch'=8,'narrow'=4] {'batch','narrow'}, dimensions={0} | all-to-all | bytes 524288 | tf_op jit(solution)/shard_map/all_to_all | solution.py:32
  95.2 3.3 %shard_map.293 = (bf16[1024,1024]{1,0:T(8,128)(2,1)S(1)}, bf16[1024,256]{1,0:T(8,128)(2,1)S(1)}, f32[256,256]{1,0:T(8,128)S(1)}, f32[256,256]{1,0:T(8,128)S(1)},...) custom-call(s32[20]{0:T(128)S(1)} %concatenate.3.refs_0_, f32[32,16,128]{2,1,0:T(8,128)S(1)} %all_to_all.54.refs_1_, ...), custom_call_target="tpu_custom_call" | custom-call | flops 536870912 | bytes 11382864 | tf_op jit(solution)/shard_map/pallas_call | solution.py:136
  98.5 1.8 collective-permute-start.4
  100.4 1.3 collective-permute-start.5
  101.7 1.5 shard_map.294
  103.2 0.6 collective-permute-done.5.refs_4_.refs_10_
  103.8 1.0 shard_map.295
  104.8 17.4 %all_to_all.55.refs_1_ = f32[32,16,128]{2,1,0:T(8,128)S(1)} all-to-all(f32[32,16,128]{2,1,0:T(8,128)S(1)} %shard_map.295), channel_id=1, replica_groups=mesh['batch'=8,'narrow'=4] {'batch','narrow'}, dimensions={0} | all-to-all | bytes 524288 | tf_op jit(solution)/shard_map/all_to_all | solution.py:32
  122.2 3.5 %shard_map.296 = (f32[1024,512]{1,0:T(8,128)S(1)}, f32[16,256]{1,0:T(8,128)S(1)}, f32[32,16,128]{2,1,0:T(8,128)S(1)}, f32[1,128]{1,0:T(1,128)}, f32[1,128]{1,0:T(1,128)}) custom-call(s32[20]{0:T(128)S(1)} %concatenate.3.refs_0_, f32[32,16,128]{2,1,0:T(8,128)S(1)} %all_to_all.55.refs_1_, f32[128,128]{1,0:T(8,128)S(1)} %get-tuple-element.103.refs_2_, ...), custom_call_target="tpu_custom_call" | custom-call | bytes 5596752 | tf_op jit(solution)/shard_map/pallas_call | solution.py:136
  125.8 12.8 %all_to_all.56.refs_1_ = f32[32,16,128]{2,1,0:T(8,128)S(1)} all-to-all(f32[32,16,128]{2,1,0:T(8,128)S(1)} %get-tuple-element.109), channel_id=1, replica_groups=mesh['batch'=8,'narrow'=4] {'batch','narrow'}, dimensions={0} | all-to-all | bytes 524288 | tf_op jit(solution)/shard_map/all_to_all | solution.py:32
  138.6 9.8 %shard_map.297 = (f32[1024,256]{1,0:T(8,128)}, f32[2,1152,128]{2,1,0:T(8,128)}, bf16[2,1152,128]{2,1,0:T(8,128)(2,1)}, f32[32,16,128]{2,1,0:T(8,128)}, f32[1,512]{1,0:T(1,128)}, /*index=5*/f32[1,512]{1,0:T(1,128)}) custom-call(s32[20]{0:T(128)S(1)} %concatenate.3.refs_0_, f32[32,16,128]{2,1,0:T(8,128)S(1)} %all_to_all.56.refs_1_, ...), custom_call_target="tpu_custom_call" | custom-call | flops 2415919104 | bytes 13813840 | tf_op jit(solution)/shard_map/pallas_call | solution.py:136
  148.5 2.6 %all-to-all-start.7 = ((f32[32,16,128]{2,1,0:T(8,128)}), f32[32,16,128]{2,1,0:T(8,128)S(1)}, u32[]{:S(2)}, u32[]{:S(2)}) async-start(f32[32,16,128]{2,1,0:T(8,128)} %get-tuple-element.113), calls=%async_computation.7 | async-start | bytes 524288 | tf_op jit(solution)/shard_map/all_to_all | solution.py:32
  151.1 0.3 collective-permute-start.7
  151.4 1.4 collective-permute-done.7.refs_4_
  152.8 1.3 copy-done.11
  154.1 1.8 shard_map.298
  155.9 1.7 collective-permute-start.8
  157.5 4.3 %all-to-all-done.7.refs_1_ = f32[32,16,128]{2,1,0:T(8,128)S(1)} async-done(((f32[32,16,128]{2,1,0:T(8,128)}), f32[32,16,128]{2,1,0:T(8,128)S(1)}, u32[]{:S(2)}, u32[]{:S(2)}) %all-to-all-start.7) | async-done | bytes 262176 | tf_op jit(solution)/shard_map/all_to_all | solution.py:32
  161.8 4.3 %shard_map.299 = (bf16[1024,256]{1,0:T(8,128)(2,1)}, f32[1024,128]{1,0:T(8,128)S(1)}, bf16[1024,128]{1,0:T(8,128)(2,1)S(1)}, f32[1,256]{1,0:T(1,128)}, f32[1,256...) custom-call(s32[20]{0:T(128)S(1)} %concatenate.3.refs_0_, f32[32,16,128]{2,1,0:T(8,128)S(1)} %all-to-all-done.7.refs_1_, ...), custom_call_target="tpu_custom_call" | custom-call | flops 536870912 | bytes 5911632 | tf_op jit(solution)/shard_map/pallas_call | solution.py:136
  166.1 0.1 collective-permute-start.9
  166.1 1.5 collective-permute-done.9.refs_4_
  167.7 1.7 collective-permute-done.8.refs_2_
  169.4 1.6 shard_map.300.refs_4_
  170.9 6.1 %all-to-all-start.8 = ((bf16[16,176,128]{2,1,0:T(8,128)(2,1)}), bf16[16,176,128]{2,1,0:T(8,128)(2,1)S(1)}, u32[]{:S(2)}, u32[]{:S(2)}) async-start(bf16[16,176,128]{2,1,0:T(8,128)(2,1)} %shard_map.300.refs_4_), calls=%async_computation.8 | async-start | bytes 1441792 | tf_op jit(solution)/shard_map/all_to_all | solution.py:43
  177.1 2.2 copy-done.3
  179.3 1.1 copy-done.4
  180.4 3.4 %shard_map.301 = (bf16[1024,1024]{1,0:T(8,128)(2,1)}, f32[8,128]{1,0:T(8,128)}) custom-call(s32[20]{0:T(128)S(1)} %concatenate.3.refs_0_, bf16[1024,256]{1,0:T(8,128)(2,1)S(1)} %copy-done.14, bf16[1024,256]{1,0:T(8,128)(2,1)S(1)} %copy-done.8, f32[1024,1024]{1,0:T(8,128)S(1)} %copy-done.3, bf16[16,176,128]{2,1,0:T(8,128)(2,1)S(1)} %copy-done.4), custom_call_target="tpu_custom_call" | custom-call | flops 536870912 | bytes 7344208 | tf_op jit(solution)/shard_map/pallas_call | solution.py:136
  183.8 11.4 %all-to-all-done.8.refs_1_ = bf16[16,176,128]{2,1,0:T(8,128)(2,1)S(1)} async-done(((bf16[16,176,128]{2,1,0:T(8,128)(2,1)}), bf16[16,176,128]{2,1,0:T(8,128)(2,1)S(1)}, u32[]{:S(2)}, u32[]{:S(2)}) %all-to-all-start.8) | async-done | bytes 720928 | tf_op jit(solution)/shard_map/all_to_all | solution.py:43
  195.2 0.8 shard_map.302
  196.0 33.4 %all_to_all.57.refs_1_ = bf16[16,288,128]{2,1,0:T(8,128)(2,1)S(1)} all-to-all(bf16[16,288,128]{2,1,0:T(8,128)(2,1)S(1)} %shard_map.302), channel_id=1, replica_groups={{0,2,4,6,8,10,12,14,16,18,20,22,24,26,28,30},{1,3,5,7,9,11,13,15,17,19,..., dimensions={0} | all-to-all | bytes 2359296 | tf_op jit(solution)/shard_map/all_to_all | solution.py:43
  229.4 2.8 %collective-permute-done.10.refs_2_ = bf16[16,288,128]{2,1,0:T(8,128)(2,1)S(1)} collective-permute-done((bf16[16,288,128]{2,1,0:T(8,128)(2,1)S(1)}, bf16[16,288,128]{2,1,0:T(8,128)(2,1)S(1)}, u32[]{:S(2)}, u32[]{:S(2)}) %collective-permute-start.10) | collective-permute-done | bytes 1179680 | tf_op jit(solution)/shard_map/ppermute | solution.py:37
  232.3 3.0 %shard_map.303 = (f32[256,1024]{1,0:T(8,128)}, f32[128,512]{1,0:T(8,128)}, f32[3,3,2,128,256]{4,3,2,1,0:T(8,128)}, f32[1024,256]{1,0:T(8,128)}) custom-call(s32[20]{0:T(128)S(1)} %concatenate.3.refs_0_, bf16[16,288,128]{2,1,0:T(8,128)(2,1)S(1)} %all_to_all.57.refs_1_, bf16[16,288,128]{2,1,0:T(8,128)(2,1)S(1)} %collective-permute-done.10.refs_2_), custom_call_target="tpu_custom_call" | custom-call | bytes 7077968 | tf_op jit(solution)/shard_map/pallas_call | solution.py:136
  (53 shorter events, 0.2 us)
Async XLA Ops:
  0.6 26.3 %copy-start.23 = (f32[256]{0:T(256)S(1)}, f32[256]{0:T(256)}, u32[]{:S(2)}) copy-start(f32[256]{0:T(256)} %param.21) | copy-start | bytes 3076
  0.7 26.3 %copy-start.19 = (f32[256]{0:T(256)S(1)}, f32[256]{0:T(256)}, u32[]{:S(2)}) copy-start(f32[256]{0:T(256)} %param.20) | copy-start | bytes 3076
  1.4 1.6 copy-start
  3.0 1.0 copy-start.7
  4.1 22.9 %copy-start.10 = (bf16[3,3,2,128,256]{4,3,2,1,0:T(8,128)(2,1)S(1)}, bf16[3,3,2,128,256]{4,3,2,1,0:T(8,128)(2,1)}, u32[]{:S(2)}) copy-start(bf16[3,3,2,128,256]{4,3,2,1,0:T(8,128)(2,1)} %refs_13_.1) | copy-start | bytes 3538948
  6.0 132.5 %copy-start.5 = (f32[1024,256]{1,0:T(8,128)}, f32[1024,256]{1,0:T(8,128)S(1)}, u32[]{:S(2)}) copy-start(f32[1024,256]{1,0:T(8,128)S(1)} %get-tuple-element.79.refs_2_.refs_14_.refs_5_) | copy-start | bytes 3145732
  6.0 20.9 %collective-permute-start = (f32[256,256]{1,0:T(8,128)S(1)}, f32[256,256]{1,0:T(8,128)S(1)}, u32[]{:S(2)}, u32[]{:S(2)}) collective-permute-start(f32[256,256]{1,0:T(8,128)S(1)} %get-tuple-element.80), channel_id=1, source_target_pairs={{0,1},{1,2},{2,3},{4,5},{5,6},{6,7},{8,9},{9,10},{10,11},{12,13},{... | collective-permute-start | bytes 786440 | tf_op jit(solution)/shard_map/ppermute | solution.py:26
  8.4 18.5 %collective-permute-start.1 = (f32[256,256]{1,0:T(8,128)S(1)}, f32[256,256]{1,0:T(8,128)S(1)}, u32[]{:S(2)}, u32[]{:S(2)}) collective-permute-start(f32[256,256]{1,0:T(8,128)S(1)} %get-tuple-element.81), channel_id=1, source_target_pairs={{1,0},{2,1},{3,2},{5,4},{6,5},{7,6},{9,8},{10,9},{11,10},{13,12},{... | collective-permute-start | bytes 786440 | tf_op jit(solution)/shard_map/ppermute | solution.py:27
  27.0 19.8 %copy-start.15 = (f32[256,128]{1,0:T(8,128)S(1)}, f32[256,128]{1,0:T(8,128)}, u32[]{:S(2)}) copy-start(f32[256,128]{1,0:T(8,128)} %refs_7_.5) | copy-start | bytes 393220
  27.0 19.8 %copy-start.16 = (f32[512]{0:T(512)S(1)}, f32[512]{0:T(512)}, u32[]{:S(2)}) copy-start(f32[512]{0:T(512)} %param.23) | copy-start | bytes 6148
  27.0 19.8 %copy-start.17 = (f32[512]{0:T(512)S(1)}, f32[512]{0:T(512)}, u32[]{:S(2)}) copy-start(f32[512]{0:T(512)} %param.24) | copy-start | bytes 6148
  31.2 15.6 %collective-permute-start.2 = (f32[256,512]{1,0:T(8,128)S(1)}, f32[256,512]{1,0:T(8,128)S(1)}, u32[]{:S(2)}, u32[]{:S(2)}) collective-permute-start(f32[256,512]{1,0:T(8,128)S(1)} %get-tuple-element.85), channel_id=1, source_target_pairs={{0,1},{1,2},{2,3},{4,5},{5,6},{6,7},{8,9},{9,10},{10,11},{12,13},{... | collective-permute-start | bytes 1572872 | tf_op jit(solution)/shard_map/ppermute | solution.py:26
  33.3 13.5 %collective-permute-start.3 = (f32[256,512]{1,0:T(8,128)S(1)}, f32[256,512]{1,0:T(8,128)S(1)}, u32[]{:S(2)}, u32[]{:S(2)}) collective-permute-start(f32[256,512]{1,0:T(8,128)S(1)} %get-tuple-element.86), channel_id=1, source_target_pairs={{1,0},{2,1},{3,2},{5,4},{6,5},{7,6},{9,8},{10,9},{11,10},{13,12},{... | collective-permute-start | bytes 1572872 | tf_op jit(solution)/shard_map/ppermute | solution.py:27
  34.6 26.9 %copy-start.9 = (bf16[256,1024]{1,0:T(8,128)(2,1)S(1)}, bf16[256,1024]{1,0:T(8,128)(2,1)}, u32[]{:S(2)}) copy-start(bf16[256,1024]{1,0:T(8,128)(2,1)} %refs_6_.3) | copy-start | bytes 1572868
  34.6 26.9 %copy-start.12 = (f32[128,512]{1,0:T(8,128)S(1)}, f32[128,512]{1,0:T(8,128)}, u32[]{:S(2)}) copy-start(f32[128,512]{1,0:T(8,128)} %refs_2_.4) | copy-start | bytes 786436
  34.6 26.9 %copy-start.21 = (f32[512]{0:T(512)S(1)}, f32[512]{0:T(512)}, u32[]{:S(2)}) copy-start(f32[512]{0:T(512)} %param.29) | copy-start | bytes 6148
  34.7 26.9 %copy-start.22 = (f32[128]{0:T(128)S(1)}, f32[128]{0:T(128)}, u32[]{:S(2)}) copy-start(f32[128]{0:T(128)} %param.26) | copy-start | bytes 1540
  34.7 26.9 %copy-start.24 = (f32[128]{0:T(128)S(1)}, f32[128]{0:T(128)}, u32[]{:S(2)}) copy-start(f32[128]{0:T(128)} %param.27) | copy-start | bytes 1540
  46.8 30.1 %copy-start.6 = (bf16[16,4,16,1024]{3,2,1,0:T(8,128)(2,1)S(1)}, bf16[16,4,16,1024]{3,2,1,0:T(8,128)(2,1)}, u32[]{:S(2)}) copy-start(bf16[16,4,16,1024]{3,2,1,0:T(8,128)(2,1)} %param.33) | copy-start | bytes 6291460
  49.1 27.9 %copy-start.1 = (bf16[16,4,16,1024]{3,2,1,0:T(8,128)(2,1)S(1)}, bf16[16,4,16,1024]{3,2,1,0:T(8,128)(2,1)}, u32[]{:S(2)}) copy-start(bf16[16,4,16,1024]{3,2,1,0:T(8,128)(2,1)} %param.17) | copy-start | bytes 6291460
  49.1 27.8 %copy-start.18 = (f32[1024]{0:T(1024)S(1)}, f32[1024]{0:T(1024)}, u32[]{:S(2)}) copy-start(f32[1024]{0:T(1024)} %param.31) | copy-start | bytes 12292
  49.1 27.8 %copy-start.20 = (f32[1024]{0:T(1024)S(1)}, f32[1024]{0:T(1024)}, u32[]{:S(2)}) copy-start(f32[1024]{0:T(1024)} %param.32) | copy-start | bytes 12292
  82.4 16.1 %copy-start.2 = (f32[1024,1024]{1,0:T(8,128)}, f32[1024,1024]{1,0:T(8,128)S(1)}, u32[]{:S(2)}) copy-start(f32[1024,1024]{1,0:T(8,128)S(1)} %get-tuple-element.94.refs_4_.refs_3_) | copy-start | bytes 12582916
  98.5 4.6 %collective-permute-start.4 = (f32[256,256]{1,0:T(8,128)S(1)}, f32[256,256]{1,0:T(8,128)S(1)}, u32[]{:S(2)}, u32[]{:S(2)}) collective-permute-start(f32[256,256]{1,0:T(8,128)S(1)} %get-tuple-element.97), channel_id=1, source_target_pairs={{0,1},{1,2},{2,3},{4,5},{5,6},{6,7},{8,9},{9,10},{10,11},{12,13},{... | collective-permute-start | bytes 786440 | tf_op jit(solution)/shard_map/ppermute | solution.py:26
  100.4 3.4 %collective-permute-start.5 = (f32[256,256]{1,0:T(8,128)S(1)}, f32[256,256]{1,0:T(8,128)S(1)}, u32[]{:S(2)}, u32[]{:S(2)}) collective-permute-start(f32[256,256]{1,0:T(8,128)S(1)} %get-tuple-element.98), channel_id=1, source_target_pairs={{1,0},{2,1},{3,2},{5,4},{6,5},{7,6},{9,8},{10,9},{11,10},{13,12},{... | collective-permute-start | bytes 786440 | tf_op jit(solution)/shard_map/ppermute | solution.py:27
  148.4 4.4 %collective-permute-start.6 = (bf16[2,1152,128]{2,1,0:T(8,128)(2,1)}, bf16[2,1152,128]{2,1,0:T(8,128)(2,1)S(1)}, u32[]{:S(2)}, u32[]{:S(2)}) collective-permute-start(bf16[2,1152,128]{2,1,0:T(8,128)(2,1)} %get-tuple-element.116), channel_id=1, source_target_pairs={{0,1},{1,0},{2,3},{3,2},{4,5},{5,4},{6,7},{7,6},{8,9},{9,8},{10,11... | collective-permute-start | bytes 1769480 | tf_op jit(solution)/shard_map/ppermute | solution.py:37
  148.5 13.3 %all-to-all-start.7 = ((f32[32,16,128]{2,1,0:T(8,128)}), f32[32,16,128]{2,1,0:T(8,128)S(1)}, u32[]{:S(2)}, u32[]{:S(2)}) async-start(f32[32,16,128]{2,1,0:T(8,128)} %get-tuple-element.113), calls=%async_computation.7 | async-start | bytes 524288 | tf_op jit(solution)/shard_map/all_to_all | solution.py:32
  151.1 1.7 collective-permute-start.7
  152.8 1.3 copy-start.11
  155.9 13.5 %collective-permute-start.8 = (bf16[1792,128]{1,0:T(8,128)(2,1)}, bf16[1792,128]{1,0:T(8,128)(2,1)S(1)}, u32[]{:S(2)}, u32[]{:S(2)}) collective-permute-start(bf16[1792,128]{1,0:T(8,128)(2,1)} %get-tuple-element.121), channel_id=1, source_target_pairs={{0,2},{1,3},{2,0},{3,1},{4,6},{5,7},{6,4},{7,5},{8,10},{9,11},{10,... | collective-permute-start | bytes 1376264 | tf_op jit(solution)/shard_map/ppermute | solution.py:37
  161.8 7.6 %copy-start.13 = (f32[1792,128]{1,0:T(8,128)S(1)}, f32[1792,128]{1,0:T(8,128)}, u32[]{:S(2)}) copy-start(f32[1792,128]{1,0:T(8,128)} %get-tuple-element.120.refs_1_) | copy-start | bytes 2752516
  166.1 1.6 collective-permute-start.9
  169.4 7.7 %copy-start.8 = (bf16[1024,256]{1,0:T(8,128)(2,1)S(1)}, bf16[1024,256]{1,0:T(8,128)(2,1)}, u32[]{:S(2)}) copy-start(bf16[1024,256]{1,0:T(8,128)(2,1)} %refs_2_.5) | copy-start | bytes 1572868
  169.4 7.7 %copy-start.14 = (bf16[1024,256]{1,0:T(8,128)(2,1)S(1)}, bf16[1024,256]{1,0:T(8,128)(2,1)}, u32[]{:S(2)}) copy-start(bf16[1024,256]{1,0:T(8,128)(2,1)} %get-tuple-element.119.refs_1_) | copy-start | bytes 1572868
  170.9 24.2 %all-to-all-start.8 = ((bf16[16,176,128]{2,1,0:T(8,128)(2,1)}), bf16[16,176,128]{2,1,0:T(8,128)(2,1)S(1)}, u32[]{:S(2)}, u32[]{:S(2)}) async-start(bf16[16,176,128]{2,1,0:T(8,128)(2,1)} %shard_map.300.refs_4_), calls=%async_computation.8 | async-start | bytes 1441792 | tf_op jit(solution)/shard_map/all_to_all | solution.py:43
  177.1 2.2 copy-start.3
  179.3 1.1 copy-start.4
  229.4 2.8 %collective-permute-start.10 = (bf16[16,288,128]{2,1,0:T(8,128)(2,1)S(1)}, bf16[16,288,128]{2,1,0:T(8,128)(2,1)S(1)}, u32[]{:S(2)}, u32[]{:S(2)}) collective-permute-start(bf16[16,288,128]{2,1,0:T(8,128)(2,1)S(1)} %all_to_all.57.refs_1_), channel_id=1, source_target_pairs={{0,1},{1,0},{2,3},{3,2},{4,5},{5,4},{6,7},{7,6},{8,9},{9,8},{10,11... | collective-permute-start | bytes 3538952 | tf_op jit(solution)/shard_map/ppermute | solution.py:37

commit v5 on v4

--- a/solution.py
+++ b/solution.py
@@ -1,4 +1,5 @@
 import functools
+from itertools import product
 
 import jax
 import jax.numpy as jnp
@@ -43,6 +44,21 @@
     return lax.all_to_all(block, ALL, 0, 0, axis_index_groups=groups)
 
 
+def gather_chips(share):
+    count = device_count()
+    bits = list(range(count.bit_length() - 2, 0, -1))
+    stages = [bits[k : k + 2] for k in range(0, len(bits), 2)]
+    block, places = share[None], [0]
+    for stage in stages:
+        steps = [sum(bit << stage[k] for k, bit in enumerate(pick)) for pick in product((0, 1), repeat=len(stage))]
+        blocks = [block] + [
+            lax.ppermute(block, ALL, [(i, i ^ step) for i in range(count)]) for step in steps[1:]
+        ]
+        lists = [[place ^ (step >> 1) for place in places] for step in steps]
+        block, places = jnp.concatenate(blocks), sum(lists, [])
+    return blocks, lists
+
+
 def sigmoid(values):
     return 0.5 * jnp.tanh(0.5 * values) + 0.5
 
@@ -55,12 +71,12 @@
     pixel = lax.broadcasted_iota(jnp.int32, (count * COLS, LANES), 0)
     row = (pixel >> 4) + (meta[0] + start)
     col = pixel & (COLS - 1)
-    side = 12 + 2 * meta[4 + image]
+    side = 12 + 2 * meta[5 + image]
     return jnp.where((row < side) & (row >= 0) & (col < side), 1.0, 0.0).astype(F32)
 
 
 def area_of(meta, image):
-    side = (12 + 2 * meta[4 + image]).astype(F32)
+    side = (12 + 2 * meta[5 + image]).astype(F32)
     return side * side
 
 
@@ -85,6 +101,11 @@
 
 def fold(values):
     return jnp.sum(values.reshape(-1, 8, values.shape[-1]), 0)
+
+
+def clear_from(ref, first):
+    if ref.shape[0] > first:
+        ref[first:, :] = jnp.zeros((ref.shape[0] - first, LANES), ref.dtype)
 
 
 def total(block):
@@ -453,7 +474,9 @@
     first = keep2.shape[1]
     for ref, half in ((send, 1 - meta[3]), (keep, meta[3])):
         ref[:first, :] = (keep2[half] + got2[half].astype(F32)).astype(ref.dtype)
-        ref[first:, :] = (keep3[half] + got3[half].astype(F32)).astype(ref.dtype)
+        last = first + keep3.shape[1]
+        ref[first:last, :] = (keep3[half] + got3[half].astype(F32)).astype(ref.dtype)
+        clear_from(ref, last)
     token[...] = jnp.zeros_like(token)
 
 
@@ -473,16 +496,9 @@
             value = value + shares[k, first:last, :].astype(F32)
         return value.astype(BF16)
 
-    out[0, :large, :] = add(0, large, 0, 2)
-    out[0, large : 2 * large, :] = add(0, large, 1, 2)
-    out[0, 2 * large :, :] = add(large, rows, 0, 1)
-    block = out[0]
-
-    def step(k, carry):
-        out[k] = block
-        return carry
-
-    lax.fori_loop(1, out.shape[0], step, 0)
+    out[:large, :] = add(0, large, 0, 2)
+    out[large : 2 * large, :] = add(0, large, 1, 2)
+    out[2 * large :, :] = add(large, rows, 0, 1)
 
 
 def hidden_kernel(
@@ -697,6 +713,7 @@
         value = dot(x[:, lanes], small[...], ((0,), (0,))).astype(ref.dtype)
         for q in range(2):
             ref[q * 512 : q * 512 + 512, :] = value[:, q * 128 : q * 128 + 128]
+        clear_from(ref, 1024)
     store.wait()
 
 
@@ -722,24 +739,32 @@
     lax.fori_loop(0, blocks // group, step, 0)
 
 
-def total_kernel(meta, own, other, expand, excite, split, reduce, *, large):
-    chips, rows, _ = own.shape
-    for ref, core in ((own, meta[2]), (other, 1 - meta[2])):
+def total_kernel(meta, *refs, places, large):
+    arrays = len(places)
+    expand, excite, split, reduce, wide_part, narrow_part = refs[2 * arrays :]
+    small = refs[0].shape[1] - 2 * large
+    for parts, core in ((refs[:arrays], meta[2]), (refs[arrays : 2 * arrays], 1 - meta[2])):
+        for part, chips in zip(parts, places):
+            for k, chip in enumerate(chips):
+                at = meta[4] ^ chip
+                for q in range(2):
+                    wide_part[q, pl.ds(pl.multiple_of(at * large, large), large), :] = part[
+                        k, q * large : q * large + large, :
+                    ]
+                narrow_part[pl.ds(pl.multiple_of(at * small, small), small), :] = part[k, 2 * large :, :]
         for q in range(2):
             lanes = slice(q * 128, q * 128 + 128)
-            block = ref[:, q * large : q * large + large, :].reshape(chips * large, LANES)
             for tap in range(9):
-                split[tap // 3, tap % 3, core, :, lanes] = block[tap * 128 : tap * 128 + 128].astype(F32)
+                split[tap // 3, tap % 3, core, :, lanes] = wide_part[q, tap * 128 : tap * 128 + 128].astype(F32)
             for k in range(2):
                 first = 1152 + k * 256
                 out = pl.ds(pl.multiple_of(core * 512 + (k * 256 + q * 128), 128), 128)
-                expand[:, out] = block[first : first + 256].astype(F32)
+                expand[:, out] = wide_part[q, first : first + 256].astype(F32)
             out = pl.ds(pl.multiple_of(core * 256 + q * 128, 128), 128)
-            excite[:, out] = block[1664:].astype(F32)
-        block = ref[:, 2 * large :, :].reshape(chips * (rows - 2 * large), LANES)
+            excite[:, out] = wide_part[q, 1664:1792].astype(F32)
         own_rows = pl.ds(pl.multiple_of(core * 512, 512), 512)
         for q in range(2):
-            reduce[own_rows, q * 128 : q * 128 + 128] = block[q * 512 : q * 512 + 512].astype(F32)
+            reduce[own_rows, q * 128 : q * 128 + 128] = narrow_part[q * 512 : q * 512 + 512].astype(F32)
 
 
 def body(
@@ -764,7 +789,6 @@
     blocks, rows, cols, channels = inputs.shape
     mid = weight_reduce.shape[1]
     inter = weight_squeeze.shape[1]
-    parts = lax.axis_size("narrow")
     count = device_count()
     pixels = blocks * rows * cols
     slab = rows * cols
@@ -777,6 +801,7 @@
             lax.axis_index("batch").astype(jnp.int32)[None],
             (lax.axis_index("narrow") % 2).astype(jnp.int32)[None],
             (lax.axis_index("narrow") // 2 % 2).astype(jnp.int32)[None],
+            (lax.axis_index(ALL) // 2).astype(jnp.int32)[None],
             image_class,
         ]
     )
@@ -856,7 +881,7 @@
         ],
         [((2, 8, channels), F32)],
         flops=small,
-        parts=parts,
+        parts=lax.axis_size("narrow"),
         local="in out",
         **sizes,
     )
@@ -930,7 +955,7 @@
             shift2,
         ],
         [((2, 8, 2 * mid), F32), ((images, inter), F32), ((mid, inter), F32)],
-        parts=parts,
+        parts=lax.axis_size("narrow"),
         local="in out",
         **sizes,
     )
@@ -981,18 +1006,19 @@
         local="in",
         **sizes,
     )
-    quarter = 9 * 128 + 2 * mid + inter
+    chips = count // 2
+    large, less = (-(-rows_in // (chips * 16)) * 16 for rows_in in (9 * 128 + 2 * mid + inter, channels))
     keep, send, token = call(
         add_kernel,
-        [((quarter, LANES), F32, "hbm"), ((quarter, LANES), BF16, "hbm"), TOKEN],
+        [((chips * large, LANES), F32, "hbm"), ((chips * large, LANES), BF16, "hbm"), TOKEN],
         [meta, keep2, swap(send2, 1), keep3, swap(send3, 1)],
     )
     small1, keep1, send1, gain1_grad, shift1_grad, bias_grad, squeeze_total = call(
         reduce_back_kernel,
         [
             ((pixels, mid), BF16, "hbm"),
-            ((channels, mid // 2), F32),
-            ((channels, mid // 2), BF16),
+            ((chips * less, LANES), F32),
+            ((chips * less, LANES), BF16),
             ((1, mid), F32),
             ((1, mid), F32),
             ((1, 2 * mid), F32),
@@ -1013,11 +1039,9 @@
         local="in",
         **sizes,
     )
-    chips = count // 2
-    large = quarter // chips
     (packed,) = call(
         pack_kernel,
-        [((chips, large + channels // chips, LANES), BF16, "hbm")],
+        [((chips, large + less, LANES), BF16, "hbm")],
         [meta, keep, swap(send, 2), keep1, swap(send1, 1)],
     )
     input_grad, token = call(
@@ -1030,13 +1054,13 @@
     )
     (shared,) = call(
         share_kernel,
-        [((chips, 2 * large + channels // chips, LANES), BF16)],
+        [((2 * large + less, LANES), BF16)],
         [meta, exchange_chips(packed)],
         after=(token,),
         local="out",
         large=large,
     )
-    own = exchange_chips(shared)
+    parts, places = gather_chips(shared)
     expand_total, excite_total, split_total, reduce_total = call(
         total_kernel,
         [
@@ -1045,8 +1069,10 @@
             (weight_split.shape, F32),
             ((channels, mid), F32),
         ],
-        [meta, own, swap(own, 1)],
+        [meta] + parts + [swap(part, 1) for part in parts],
+        [((2, chips * large, LANES), BF16), ((chips * less, LANES), BF16)],
         local="in",
+        places=places,
         large=large,
     )
     flat = lambda v: v.reshape(-1)

time: 236 us -> 224 us (0.949)
  blocking collectives: 131 us -> 97.6 us
  waiting for transfers between devices: 23.8 us -> 36.8 us
  starting transfers between devices: 21.1 us -> 29.1 us
    all_to_all x1 -> x0, blocking collectives: 33.4 us -> none  [exchange_chips(): return lax.all_to_all(block, ALL, 0, 0, axis_index_groups=groups)]
    ppermute x0 -> x6, waiting for transfers between devices: none -> 14.3 us  [gather_chips(): lax.ppermute(block, ALL, [(i, i ^ step) for i in range(count)])]
    ppermute x0 -> x6, starting transfers between devices: none -> 8.01 us  [gather_chips(): lax.ppermute(block, ALL, [(i, i ^ step) for i in range(count)])]
    ppermute x5 -> x8, waiting for transfers between devices: 7.48 us -> 6.17 us  [swap(): return lax.ppermute(block, 'narrow', [(i, i ^ bit) for i in range(count)])]
  transfers between devices with their start and end apart: 13 -> 22, of which waited for: 7 -> 13; matrix products, arithmetic and copies ran while one was open for 0% -> 0% of each run, Pallas kernels for 5% -> 5%
where the time goes in v5:
time: 224 us; the launch traced here: 223 us
  blocking collectives  97.6 us (44%)
  Pallas kernels  50.2 us (22%)
  waiting for transfers between devices  36.8 us (16%)
  starting transfers between devices  29.1 us (13%)
  local copies, waits for them, and re-layouts  8.04 us (4%)
    all_to_all x7, blocking collectives, exchange(): return lax.all_to_all(block, ALL, 0, 0)  97.6 us
    pallas_call x16, Pallas kernels, call(): pl.pallas_call(run, grid=() if local == 'in out' else (1,), out_shape=[pl...  50.2 us
    ppermute x6, waiting for transfers between devices, gather_chips(): lax.ppermute(block, ALL, [(i, i ^ step) for i in range(count)])  14.3 us
    all_to_all x1, waiting for transfers between devices, exchange_chips(): return lax.all_to_all(block, ALL, 0, 0, axis_index_groups=groups)  11.4 us
    ppermute x6, starting transfers between devices, gather_chips(): lax.ppermute(block, ALL, [(i, i ^ step) for i in range(count)])  8.01 us
    unnamed x50, local copies, waits for them, and re-layouts  7.3 us
    ppermute x3, starting transfers between devices, halo(): low = lax.ppermute(bottom, 'narrow', [(i, i + 1) for i in range(count - 1)])  6.34 us
    ppermute x8, waiting for transfers between devices, swap(): return lax.ppermute(block, 'narrow', [(i, i ^ bit) for i in range(count)])  6.17 us
  transfers between devices with their start and end apart: 22, of which 13 were waited for; matrix products, arithmetic and copies ran while one was open for 0% of the time, Pallas kernels for 5%

profile of v5, /device:TPU:0, one launch (start us, length us, event | category | flops | bytes accessed | tf_op | source)
XLA Modules:
  0.0 222.8 jit_solution(18230924899226695216)
XLA Ops:
  1.4 1.6 copy-done
  4.1 1.9 shard_map.288
  6.1 2.4 %collective-permute-start = (f32[256,256]{1,0:T(8,128)S(1)}, f32[256,256]{1,0:T(8,128)S(1)}, u32[]{:S(2)}, u32[]{:S(2)}) collective-permute-start(f32[256,256]{1,0:T(8,128)S(1)} %get-tuple-element.80), channel_id=1, source_target_pairs={{0,1},{1,2},{2,3},{4,5},{5,6},{6,7},{8,9},{9,10},{10,11},{12,13},{... | collective-permute-start | bytes 786440 | tf_op jit(solution)/shard_map/ppermute | solution.py:27
  8.4 1.3 collective-permute-start.1
  9.7 17.2 %all_to_all.45.refs_1_ = f32[32,8,128]{2,1,0:T(8,128)S(1)} all-to-all(f32[32,8,128]{2,1,0:T(8,128)S(1)} %get-tuple-element.78), channel_id=1, replica_groups=mesh['batch'=8,'narrow'=4] {'batch','narrow'}, dimensions={0} | all-to-all | bytes 262144 | tf_op jit(solution)/shard_map/all_to_all | solution.py:33
  27.0 4.1 %shard_map.289 = (bf16[3,16,96,256]{3,2,1,0:T(8,128)(2,1)}, f32[1024,512]{1,0:T(8,128)S(1)}, f32[256,512]{1,0:T(8,128)S(1)}, f32[256,512]{1,0:T(8,128)S(1)}, f32...) custom-call(s32[21]{0:T(128)S(1)} %concatenate.6.refs_0_, f32[32,8,128]{2,1,0:T(8,128)S(1)} %all_to_all.45.refs_1_, ...), custom_call_target="tpu_custom_call" | custom-call | flops 1207959552 | bytes 8530004 | tf_op jit(solution)/shard_map/pallas_call | solution.py:157
  31.2 2.2 collective-permute-start.2
  33.3 1.3 collective-permute-start.3
  34.7 12.1 %all_to_all.46.refs_1_ = f32[32,8,128]{2,1,0:T(8,128)S(1)} all-to-all(f32[32,8,128]{2,1,0:T(8,128)S(1)} %get-tuple-element.82), channel_id=1, replica_groups=mesh['batch'=8,'narrow'=4] {'batch','narrow'}, dimensions={0} | all-to-all | bytes 262144 | tf_op jit(solution)/shard_map/all_to_all | solution.py:33
  46.9 2.2 shard_map.290
  49.1 12.4 %all_to_all.47.refs_1_ = f32[32,16,128]{2,1,0:T(8,128)S(1)} all-to-all(f32[32,16,128]{2,1,0:T(8,128)S(1)} %get-tuple-element.87), channel_id=1, replica_groups=mesh['batch'=8,'narrow'=4] {'batch','narrow'}, dimensions={0} | all-to-all | bytes 524288 | tf_op jit(solution)/shard_map/all_to_all | solution.py:33
  61.6 2.6 %shard_map.291 = (bf16[1024,256]{1,0:T(8,128)(2,1)S(1)}, bf16[1024,1024]{1,0:T(8,128)(2,1)S(1)}, f32[16,512]{1,0:T(8,128)S(1)}, f32[16,128]{1,0:T(8,128)S(1)}, f...) custom-call(s32[21]{0:T(128)S(1)} %concatenate.6.refs_0_, ...), custom_call_target="tpu_custom_call" | custom-call | flops 536870912 | bytes 5160020 | tf_op jit(solution)/shard_map/pallas_call | solution.py:157
  64.2 12.7 %all_to_all.48.refs_1_ = f32[32,16,128]{2,1,0:T(8,128)S(1)} all-to-all(f32[32,16,128]{2,1,0:T(8,128)S(1)} %get-tuple-element.89), channel_id=1, replica_groups=mesh['batch'=8,'narrow'=4] {'batch','narrow'}, dimensions={0} | all-to-all | bytes 524288 | tf_op jit(solution)/shard_map/all_to_all | solution.py:33
  76.9 5.5 %shard_map.292 = (bf16[1024,1024]{1,0:T(8,128)(2,1)}, f32[1024,1024]{1,0:T(8,128)S(1)}, f32[32,16,128]{2,1,0:T(8,128)S(1)}, f32[8,1024]{1,0:T(8,128)S(1)}) custom-call(s32[21]{0:T(128)S(1)} %concatenate.6.refs_0_, f32[32,16,128]{2,1,0:T(8,128)S(1)} %all_to_all.48.refs_1_, f32[8,256]{1,0:T(8,128)S(1)} %get-tuple-element.83.refs_2_.refs_15_, ...), custom_call_target="tpu_custom_call" | custom-call | bytes 13156436 | tf_op jit(solution)/shard_map/pallas_call | solution.py:157
  82.4 12.8 %all_to_all.49.refs_1_ = f32[32,16,128]{2,1,0:T(8,128)S(1)} all-to-all(f32[32,16,128]{2,1,0:T(8,128)S(1)} %get-tuple-element.92), channel_id=1, replica_groups=mesh['batch'=8,'narrow'=4] {'batch','narrow'}, dimensions={0} | all-to-all | bytes 524288 | tf_op jit(solution)/shard_map/all_to_all | solution.py:33
  95.2 3.3 %shard_map.293 = (bf16[1024,1024]{1,0:T(8,128)(2,1)S(1)}, bf16[1024,256]{1,0:T(8,128)(2,1)S(1)}, f32[256,256]{1,0:T(8,128)S(1)}, f32[256,256]{1,0:T(8,128)S(1)},...) custom-call(s32[21]{0:T(128)S(1)} %concatenate.6.refs_0_, f32[32,16,128]{2,1,0:T(8,128)S(1)} %all_to_all.49.refs_1_, ...), custom_call_target="tpu_custom_call" | custom-call | flops 536870912 | bytes 11382868 | tf_op jit(solution)/shard_map/pallas_call | solution.py:157
  98.5 1.8 collective-permute-start.4
  100.3 1.3 collective-permute-start.5
  101.6 1.5 shard_map.294
  104.7 17.4 %all_to_all.50.refs_1_ = f32[32,16,128]{2,1,0:T(8,128)S(1)} all-to-all(f32[32,16,128]{2,1,0:T(8,128)S(1)} %shard_map.295), channel_id=1, replica_groups=mesh['batch'=8,'narrow'=4] {'batch','narrow'}, dimensions={0} | all-to-all | bytes 524288 | tf_op jit(solution)/shard_map/all_to_all | solution.py:33
  122.2 3.5 %shard_map.296 = (f32[1024,512]{1,0:T(8,128)S(1)}, f32[16,256]{1,0:T(8,128)S(1)}, f32[32,16,128]{2,1,0:T(8,128)S(1)}, f32[1,128]{1,0:T(1,128)}, f32[1,128]{1,0:T(1,128)}) custom-call(s32[21]{0:T(128)S(1)} %concatenate.6.refs_0_, f32[32,16,128]{2,1,0:T(8,128)S(1)} %all_to_all.50.refs_1_, f32[128,128]{1,0:T(8,128)S(1)} %get-tuple-element.103.refs_2_, ...), custom_call_target="tpu_custom_call" | custom-call | bytes 5596756 | tf_op jit(solution)/shard_map/pallas_call | solution.py:157
  125.7 12.8 %all_to_all.51.refs_1_ = f32[32,16,128]{2,1,0:T(8,128)S(1)} all-to-all(f32[32,16,128]{2,1,0:T(8,128)S(1)} %get-tuple-element.109), channel_id=1, replica_groups=mesh['batch'=8,'narrow'=4] {'batch','narrow'}, dimensions={0} | all-to-all | bytes 524288 | tf_op jit(solution)/shard_map/all_to_all | solution.py:33
  138.5 9.8 %shard_map.297 = (f32[1024,256]{1,0:T(8,128)}, f32[2,1152,128]{2,1,0:T(8,128)}, bf16[2,1152,128]{2,1,0:T(8,128)(2,1)}, f32[32,16,128]{2,1,0:T(8,128)}, f32[1,512]{1,0:T(1,128)}, /*index=5*/f32[1,512]{1,0:T(1,128)}) custom-call(s32[21]{0:T(128)S(1)} %concatenate.6.refs_0_, f32[32,16,128]{2,1,0:T(8,128)S(1)} %all_to_all.51.refs_1_, ...), custom_call_target="tpu_custom_call" | custom-call | flops 2415919104 | bytes 13813844 | tf_op jit(solution)/shard_map/pallas_call | solution.py:157
  148.5 2.6 %all-to-all-start.7 = ((f32[32,16,128]{2,1,0:T(8,128)}), f32[32,16,128]{2,1,0:T(8,128)S(1)}, u32[]{:S(2)}, u32[]{:S(2)}) async-start(f32[32,16,128]{2,1,0:T(8,128)} %get-tuple-element.113), calls=%async_computation.7 | async-start | bytes 524288 | tf_op jit(solution)/shard_map/all_to_all | solution.py:33
  151.4 1.4 collective-permute-done.7.refs_4_
  152.8 1.3 copy-done.11
  154.0 1.8 shard_map.298
  155.8 1.7 collective-permute-start.8
  157.5 4.3 %all-to-all-done.7.refs_1_ = f32[32,16,128]{2,1,0:T(8,128)S(1)} async-done(((f32[32,16,128]{2,1,0:T(8,128)}), f32[32,16,128]{2,1,0:T(8,128)S(1)}, u32[]{:S(2)}, u32[]{:S(2)}) %all-to-all-start.7) | async-done | bytes 262176 | tf_op jit(solution)/shard_map/all_to_all | solution.py:33
  161.8 4.3 %shard_map.299 = (bf16[1024,256]{1,0:T(8,128)(2,1)}, f32[1024,128]{1,0:T(8,128)S(1)}, bf16[1024,128]{1,0:T(8,128)(2,1)S(1)}, f32[1,256]{1,0:T(1,128)}, f32[1,256...) custom-call(s32[21]{0:T(128)S(1)} %concatenate.6.refs_0_, f32[32,16,128]{2,1,0:T(8,128)S(1)} %all-to-all-done.7.refs_1_, ...), custom_call_target="tpu_custom_call" | custom-call | flops 536870912 | bytes 5911636 | tf_op jit(solution)/shard_map/pallas_call | solution.py:157
  166.1 1.5 collective-permute-done.9.refs_4_
  167.6 1.7 collective-permute-done.8.refs_2_
  169.3 1.5 shard_map.300.refs_4_
  170.8 6.1 %all-to-all-start.8 = ((bf16[16,176,128]{2,1,0:T(8,128)(2,1)}), bf16[16,176,128]{2,1,0:T(8,128)(2,1)S(1)}, u32[]{:S(2)}, u32[]{:S(2)}) async-start(bf16[16,176,128]{2,1,0:T(8,128)(2,1)} %shard_map.300.refs_4_), calls=%async_computation.8 | async-start | bytes 1441792 | tf_op jit(solution)/shard_map/all_to_all | solution.py:44
  177.0 2.2 copy-done.3
  180.3 3.4 %shard_map.301 = (bf16[1024,1024]{1,0:T(8,128)(2,1)}, f32[8,128]{1,0:T(8,128)}) custom-call(s32[21]{0:T(128)S(1)} %concatenate.6.refs_0_, bf16[1024,256]{1,0:T(8,128)(2,1)S(1)} %copy-done.14, bf16[1024,256]{1,0:T(8,128)(2,1)S(1)} %copy-done.8, f32[1024,1024]{1,0:T(8,128)S(1)} %copy-done.3, bf16[16,176,128]{2,1,0:T(8,128)(2,1)S(1)} %copy-done.4), custom_call_target="tpu_custom_call" | custom-call | flops 536870912 | bytes 7344212 | tf_op jit(solution)/shard_map/pallas_call | solution.py:157
  183.6 11.4 %all-to-all-done.8.refs_1_ = bf16[16,176,128]{2,1,0:T(8,128)(2,1)S(1)} async-done(((bf16[16,176,128]{2,1,0:T(8,128)(2,1)}), bf16[16,176,128]{2,1,0:T(8,128)(2,1)S(1)}, u32[]{:S(2)}, u32[]{:S(2)}) %all-to-all-start.8) | async-done | bytes 720928 | tf_op jit(solution)/shard_map/all_to_all | solution.py:44
  195.7 2.2 collective-permute-start.12
  197.9 1.2 collective-permute-start.11
  200.2 2.1 collective-permute-done.12
  202.3 2.0 collective-permute-done.11
  204.3 1.5 collective-permute-start.15
  206.6 1.3 collective-permute-start.13
  207.9 7.1 %collective-permute-done.15.refs_4_ = bf16[4,288,128]{2,1,0:T(8,128)(2,1)S(1)} collective-permute-done((bf16[4,288,128]{2,1,0:T(8,128)(2,1)S(1)}, bf16[4,288,128]{2,1,0:T(8,128)(2,1)S(1)}, u32[]{:S(2)}, u32[]{:S(2)}) %collective-permute-start.15) | collective-permute-done | bytes 294944 | tf_op jit(solution)/shard_map/ppermute | solution.py:55
  215.0 1.7 collective-permute-done.14.refs_3_
  216.7 1.4 collective-permute-done.13.refs_2_
  218.3 1.4 collective-permute-done.17.refs_6_
  219.6 3.2 %shard_map.303 = (f32[256,1024]{1,0:T(8,128)}, f32[128,512]{1,0:T(8,128)}, f32[3,3,2,128,256]{4,3,2,1,0:T(8,128)}, f32[1024,256]{1,0:T(8,128)}) custom-call(s32[21]{0:T(128)S(1)} %concatenate.6.refs_0_, bf16[4,288,128]{2,1,0:T(8,128)(2,1)S(1)} %pad_maximum_fusion.refs_1_, bf16[4,288,128]{2,1,0:T(8,128)(2,1)S(1)} %collective-permute-done.13.refs_2_, ...), custom_call_target="tpu_custom_call" | custom-call | bytes 7077972 | tf_op jit(solution)/shard_map/pallas_call | solution.py:157
  (71 shorter events, 7.7 us)
Async XLA Ops:
  0.6 26.3 %copy-start.23 = (f32[256]{0:T(256)S(1)}, f32[256]{0:T(256)}, u32[]{:S(2)}) copy-start(f32[256]{0:T(256)} %param.21) | copy-start | bytes 3076
  0.7 26.3 %copy-start.19 = (f32[256]{0:T(256)S(1)}, f32[256]{0:T(256)}, u32[]{:S(2)}) copy-start(f32[256]{0:T(256)} %param.20) | copy-start | bytes 3076
  1.4 1.6 copy-start
  3.0 1.0 copy-start.7
  4.1 22.9 %copy-start.10 = (bf16[3,3,2,128,256]{4,3,2,1,0:T(8,128)(2,1)S(1)}, bf16[3,3,2,128,256]{4,3,2,1,0:T(8,128)(2,1)}, u32[]{:S(2)}) copy-start(bf16[3,3,2,128,256]{4,3,2,1,0:T(8,128)(2,1)} %refs_13_.1) | copy-start | bytes 3538948
  6.0 132.5 %copy-start.5 = (f32[1024,256]{1,0:T(8,128)}, f32[1024,256]{1,0:T(8,128)S(1)}, u32[]{:S(2)}) copy-start(f32[1024,256]{1,0:T(8,128)S(1)} %get-tuple-element.79.refs_2_.refs_14_.refs_5_) | copy-start | bytes 3145732
  6.1 20.9 %collective-permute-start = (f32[256,256]{1,0:T(8,128)S(1)}, f32[256,256]{1,0:T(8,128)S(1)}, u32[]{:S(2)}, u32[]{:S(2)}) collective-permute-start(f32[256,256]{1,0:T(8,128)S(1)} %get-tuple-element.80), channel_id=1, source_target_pairs={{0,1},{1,2},{2,3},{4,5},{5,6},{6,7},{8,9},{9,10},{10,11},{12,13},{... | collective-permute-start | bytes 786440 | tf_op jit(solution)/shard_map/ppermute | solution.py:27
  8.4 18.5 %collective-permute-start.1 = (f32[256,256]{1,0:T(8,128)S(1)}, f32[256,256]{1,0:T(8,128)S(1)}, u32[]{:S(2)}, u32[]{:S(2)}) collective-permute-start(f32[256,256]{1,0:T(8,128)S(1)} %get-tuple-element.81), channel_id=1, source_target_pairs={{1,0},{2,1},{3,2},{5,4},{6,5},{7,6},{9,8},{10,9},{11,10},{13,12},{... | collective-permute-start | bytes 786440 | tf_op jit(solution)/shard_map/ppermute | solution.py:28
  27.0 19.8 %copy-start.15 = (f32[256,128]{1,0:T(8,128)S(1)}, f32[256,128]{1,0:T(8,128)}, u32[]{:S(2)}) copy-start(f32[256,128]{1,0:T(8,128)} %refs_7_.5) | copy-start | bytes 393220
  27.0 19.8 %copy-start.16 = (f32[512]{0:T(512)S(1)}, f32[512]{0:T(512)}, u32[]{:S(2)}) copy-start(f32[512]{0:T(512)} %param.23) | copy-start | bytes 6148
  27.0 19.8 %copy-start.17 = (f32[512]{0:T(512)S(1)}, f32[512]{0:T(512)}, u32[]{:S(2)}) copy-start(f32[512]{0:T(512)} %param.24) | copy-start | bytes 6148
  31.2 15.6 %collective-permute-start.2 = (f32[256,512]{1,0:T(8,128)S(1)}, f32[256,512]{1,0:T(8,128)S(1)}, u32[]{:S(2)}, u32[]{:S(2)}) collective-permute-start(f32[256,512]{1,0:T(8,128)S(1)} %get-tuple-element.85), channel_id=1, source_target_pairs={{0,1},{1,2},{2,3},{4,5},{5,6},{6,7},{8,9},{9,10},{10,11},{12,13},{... | collective-permute-start | bytes 1572872 | tf_op jit(solution)/shard_map/ppermute | solution.py:27
  33.3 13.5 %collective-permute-start.3 = (f32[256,512]{1,0:T(8,128)S(1)}, f32[256,512]{1,0:T(8,128)S(1)}, u32[]{:S(2)}, u32[]{:S(2)}) collective-permute-start(f32[256,512]{1,0:T(8,128)S(1)} %get-tuple-element.86), channel_id=1, source_target_pairs={{1,0},{2,1},{3,2},{5,4},{6,5},{7,6},{9,8},{10,9},{11,10},{13,12},{... | collective-permute-start | bytes 1572872 | tf_op jit(solution)/shard_map/ppermute | solution.py:28
  34.6 26.9 %copy-start.9 = (bf16[256,1024]{1,0:T(8,128)(2,1)S(1)}, bf16[256,1024]{1,0:T(8,128)(2,1)}, u32[]{:S(2)}) copy-start(bf16[256,1024]{1,0:T(8,128)(2,1)} %refs_6_.3) | copy-start | bytes 1572868
  34.6 26.9 %copy-start.12 = (f32[128,512]{1,0:T(8,128)S(1)}, f32[128,512]{1,0:T(8,128)}, u32[]{:S(2)}) copy-start(f32[128,512]{1,0:T(8,128)} %refs_2_.4) | copy-start | bytes 786436
  34.7 26.9 %copy-start.21 = (f32[512]{0:T(512)S(1)}, f32[512]{0:T(512)}, u32[]{:S(2)}) copy-start(f32[512]{0:T(512)} %param.29) | copy-start | bytes 6148
  34.7 26.9 %copy-start.22 = (f32[128]{0:T(128)S(1)}, f32[128]{0:T(128)}, u32[]{:S(2)}) copy-start(f32[128]{0:T(128)} %param.26) | copy-start | bytes 1540
  34.7 26.9 %copy-start.24 = (f32[128]{0:T(128)S(1)}, f32[128]{0:T(128)}, u32[]{:S(2)}) copy-start(f32[128]{0:T(128)} %param.27) | copy-start | bytes 1540
  46.8 30.1 %copy-start.6 = (bf16[16,4,16,1024]{3,2,1,0:T(8,128)(2,1)S(1)}, bf16[16,4,16,1024]{3,2,1,0:T(8,128)(2,1)}, u32[]{:S(2)}) copy-start(bf16[16,4,16,1024]{3,2,1,0:T(8,128)(2,1)} %param.33) | copy-start | bytes 6291460
  49.1 27.9 %copy-start.1 = (bf16[16,4,16,1024]{3,2,1,0:T(8,128)(2,1)S(1)}, bf16[16,4,16,1024]{3,2,1,0:T(8,128)(2,1)}, u32[]{:S(2)}) copy-start(bf16[16,4,16,1024]{3,2,1,0:T(8,128)(2,1)} %param.17) | copy-start | bytes 6291460
  49.1 27.8 %copy-start.18 = (f32[1024]{0:T(1024)S(1)}, f32[1024]{0:T(1024)}, u32[]{:S(2)}) copy-start(f32[1024]{0:T(1024)} %param.31) | copy-start | bytes 12292
  49.1 27.8 %copy-start.20 = (f32[1024]{0:T(1024)S(1)}, f32[1024]{0:T(1024)}, u32[]{:S(2)}) copy-start(f32[1024]{0:T(1024)} %param.32) | copy-start | bytes 12292
  82.4 16.1 %copy-start.2 = (f32[1024,1024]{1,0:T(8,128)}, f32[1024,1024]{1,0:T(8,128)S(1)}, u32[]{:S(2)}) copy-start(f32[1024,1024]{1,0:T(8,128)S(1)} %get-tuple-element.94.refs_4_.refs_3_) | copy-start | bytes 12582916
  98.5 4.6 %collective-permute-start.4 = (f32[256,256]{1,0:T(8,128)S(1)}, f32[256,256]{1,0:T(8,128)S(1)}, u32[]{:S(2)}, u32[]{:S(2)}) collective-permute-start(f32[256,256]{1,0:T(8,128)S(1)} %get-tuple-element.97), channel_id=1, source_target_pairs={{0,1},{1,2},{2,3},{4,5},{5,6},{6,7},{8,9},{9,10},{10,11},{12,13},{... | collective-permute-start | bytes 786440 | tf_op jit(solution)/shard_map/ppermute | solution.py:27
  100.3 3.4 %collective-permute-start.5 = (f32[256,256]{1,0:T(8,128)S(1)}, f32[256,256]{1,0:T(8,128)S(1)}, u32[]{:S(2)}, u32[]{:S(2)}) collective-permute-start(f32[256,256]{1,0:T(8,128)S(1)} %get-tuple-element.98), channel_id=1, source_target_pairs={{1,0},{2,1},{3,2},{5,4},{6,5},{7,6},{9,8},{10,9},{11,10},{13,12},{... | collective-permute-start | bytes 786440 | tf_op jit(solution)/shard_map/ppermute | solution.py:28
  148.4 4.4 %collective-permute-start.6 = (bf16[2,1152,128]{2,1,0:T(8,128)(2,1)}, bf16[2,1152,128]{2,1,0:T(8,128)(2,1)S(1)}, u32[]{:S(2)}, u32[]{:S(2)}) collective-permute-start(bf16[2,1152,128]{2,1,0:T(8,128)(2,1)} %get-tuple-element.116), channel_id=1, source_target_pairs={{0,1},{1,0},{2,3},{3,2},{4,5},{5,4},{6,7},{7,6},{8,9},{9,8},{10,11... | collective-permute-start | bytes 1769480 | tf_op jit(solution)/shard_map/ppermute | solution.py:38
  148.5 13.3 %all-to-all-start.7 = ((f32[32,16,128]{2,1,0:T(8,128)}), f32[32,16,128]{2,1,0:T(8,128)S(1)}, u32[]{:S(2)}, u32[]{:S(2)}) async-start(f32[32,16,128]{2,1,0:T(8,128)} %get-tuple-element.113), calls=%async_computation.7 | async-start | bytes 524288 | tf_op jit(solution)/shard_map/all_to_all | solution.py:33
  151.1 1.7 collective-permute-start.7
  152.8 1.3 copy-start.11
  155.8 13.5 %collective-permute-start.8 = (bf16[1792,128]{1,0:T(8,128)(2,1)}, bf16[1792,128]{1,0:T(8,128)(2,1)S(1)}, u32[]{:S(2)}, u32[]{:S(2)}) collective-permute-start(bf16[1792,128]{1,0:T(8,128)(2,1)} %get-tuple-element.121), channel_id=1, source_target_pairs={{0,2},{1,3},{2,0},{3,1},{4,6},{5,7},{6,4},{7,5},{8,10},{9,11},{10,... | collective-permute-start | bytes 1376264 | tf_op jit(solution)/shard_map/ppermute | solution.py:38
  161.8 7.5 %copy-start.13 = (f32[1792,128]{1,0:T(8,128)S(1)}, f32[1792,128]{1,0:T(8,128)}, u32[]{:S(2)}) copy-start(f32[1792,128]{1,0:T(8,128)} %get-tuple-element.120.refs_1_) | copy-start | bytes 2752516
  166.0 1.6 collective-permute-start.9
  169.3 7.6 %copy-start.8 = (bf16[1024,256]{1,0:T(8,128)(2,1)S(1)}, bf16[1024,256]{1,0:T(8,128)(2,1)}, u32[]{:S(2)}) copy-start(bf16[1024,256]{1,0:T(8,128)(2,1)} %refs_2_.5) | copy-start | bytes 1572868
  169.3 7.7 %copy-start.14 = (bf16[1024,256]{1,0:T(8,128)(2,1)S(1)}, bf16[1024,256]{1,0:T(8,128)(2,1)}, u32[]{:S(2)}) copy-start(bf16[1024,256]{1,0:T(8,128)(2,1)} %get-tuple-element.119.refs_1_) | copy-start | bytes 1572868
  170.8 24.2 %all-to-all-start.8 = ((bf16[16,176,128]{2,1,0:T(8,128)(2,1)}), bf16[16,176,128]{2,1,0:T(8,128)(2,1)S(1)}, u32[]{:S(2)}, u32[]{:S(2)}) async-start(bf16[16,176,128]{2,1,0:T(8,128)(2,1)} %shard_map.300.refs_4_), calls=%async_computation.8 | async-start | bytes 1441792 | tf_op jit(solution)/shard_map/all_to_all | solution.py:44
  177.0 2.2 copy-start.3
  179.2 1.1 copy-start.4
  195.7 6.6 %collective-permute-start.12 = (bf16[1,288,128]{2,1,0:T(8,128)(2,1)S(1)}, bf16[1,288,128]{2,1,0:T(8,128)(2,1)S(1)}, u32[]{:S(2)}, u32[]{:S(2)}) collective-permute-start(bf16[1,288,128]{2,1,0:T(8,128)(2,1)S(1)} %bitcast.32), channel_id=1, source_target_pairs={{0,24},{1,25},{2,26},{3,27},{4,28},{5,29},{6,30},{7,31},{8,16},{9,... | collective-permute-start | bytes 221192 | tf_op jit(solution)/shard_map/ppermute | solution.py:55
  197.9 6.4 %collective-permute-start.11 = (bf16[1,288,128]{2,1,0:T(8,128)(2,1)S(1)}, bf16[1,288,128]{2,1,0:T(8,128)(2,1)S(1)}, u32[]{:S(2)}, u32[]{:S(2)}) collective-permute-start(bf16[1,288,128]{2,1,0:T(8,128)(2,1)S(1)} %bitcast.33), channel_id=1, source_target_pairs={{0,16},{1,17},{2,18},{3,19},{4,20},{5,21},{6,22},{7,23},{8,24},{9,... | collective-permute-start | bytes 221192 | tf_op jit(solution)/shard_map/ppermute | solution.py:55
  199.1 5.1 %collective-permute-start.10 = (bf16[1,288,128]{2,1,0:T(8,128)(2,1)S(1)}, bf16[1,288,128]{2,1,0:T(8,128)(2,1)S(1)}, u32[]{:S(2)}, u32[]{:S(2)}) collective-permute-start(bf16[1,288,128]{2,1,0:T(8,128)(2,1)S(1)} %bitcast.34), channel_id=1, source_target_pairs={{0,8},{1,9},{2,10},{3,11},{4,12},{5,13},{6,14},{7,15},{8,0},{9,1},... | collective-permute-start | bytes 221192 | tf_op jit(solution)/shard_map/ppermute | solution.py:55
  204.3 10.6 %collective-permute-start.15 = (bf16[4,288,128]{2,1,0:T(8,128)(2,1)S(1)}, bf16[4,288,128]{2,1,0:T(8,128)(2,1)S(1)}, u32[]{:S(2)}, u32[]{:S(2)}) collective-permute-start(bf16[4,288,128]{2,1,0:T(8,128)(2,1)S(1)} %pad_maximum_fusion.refs_1_), channel_id=1, source_target_pairs={{0,6},{1,7},{2,4},{3,5},{4,2},{5,3},{6,0},{7,1},{8,14},{9,15},{10,... | collective-permute-start | bytes 884744 | tf_op jit(solution)/shard_map/ppermute | solution.py:55
  205.9 10.8 %collective-permute-start.14 = (bf16[4,288,128]{2,1,0:T(8,128)(2,1)S(1)}, bf16[4,288,128]{2,1,0:T(8,128)(2,1)S(1)}, u32[]{:S(2)}, u32[]{:S(2)}) collective-permute-start(bf16[4,288,128]{2,1,0:T(8,128)(2,1)S(1)} %pad_maximum_fusion.refs_1_), channel_id=1, source_target_pairs={{0,4},{1,5},{2,6},{3,7},{4,0},{5,1},{6,2},{7,3},{8,12},{9,13},{10,... | collective-permute-start | bytes 884744 | tf_op jit(solution)/shard_map/ppermute | solution.py:55
  206.6 11.5 %collective-permute-start.13 = (bf16[4,288,128]{2,1,0:T(8,128)(2,1)S(1)}, bf16[4,288,128]{2,1,0:T(8,128)(2,1)S(1)}, u32[]{:S(2)}, u32[]{:S(2)}) collective-permute-start(bf16[4,288,128]{2,1,0:T(8,128)(2,1)S(1)} %pad_maximum_fusion.refs_1_), channel_id=1, source_target_pairs={{0,2},{1,3},{2,0},{3,1},{4,6},{5,7},{6,4},{7,5},{8,10},{9,11},{10,... | collective-permute-start | bytes 884744 | tf_op jit(solution)/shard_map/ppermute | solution.py:55
  207.9 10.2 %collective-permute-start.16 = (bf16[4,288,128]{2,1,0:T(8,128)(2,1)S(1)}, bf16[4,288,128]{2,1,0:T(8,128)(2,1)S(1)}, u32[]{:S(2)}, u32[]{:S(2)}) collective-permute-start(bf16[4,288,128]{2,1,0:T(8,128)(2,1)S(1)} %pad_maximum_fusion.refs_1_), channel_id=1, source_target_pairs={{0,1},{1,0},{2,3},{3,2},{4,5},{5,4},{6,7},{7,6},{8,9},{9,8},{10,11... | collective-permute-start | bytes 884744 | tf_op jit(solution)/shard_map/ppermute | solution.py:38
  215.0 3.1 %collective-permute-start.19 = (bf16[4,288,128]{2,1,0:T(8,128)(2,1)S(1)}, bf16[4,288,128]{2,1,0:T(8,128)(2,1)S(1)}, u32[]{:S(2)}, u32[]{:S(2)}) collective-permute-start(bf16[4,288,128]{2,1,0:T(8,128)(2,1)S(1)} %collective-permute-done.15.refs_4_), channel_id=1, source_target_pairs={{0,1},{1,0},{2,3},{3,2},{4,5},{5,4},{6,7},{7,6},{8,9},{9,8},{10,11... | collective-permute-start | bytes 884744 | tf_op jit(solution)/shard_map/ppermute | solution.py:38
  216.7 1.6 collective-permute-start.18
  218.1 1.6 collective-permute-start.17

commit v6 on v5

--- a/solution.py
+++ b/solution.py
@@ -38,29 +38,65 @@
     return lax.ppermute(block, "narrow", [(i, i ^ bit) for i in range(count)])
 
 
-def exchange_chips(block):
+def stages():
+    bits = list(range(device_count().bit_length() - 2, 0, -1))
+    pairs = [bits[k : k + 2] for k in range(0, len(bits), 2)]
+    return [
+        [sum(bit << pair[k] for k, bit in enumerate(pick)) for pick in product((0, 1), repeat=len(pair))]
+        for pair in pairs
+    ]
+
+
+def partners(blocks, steps):
     count = device_count()
-    groups = [[i for i in range(count) if i % 2 == core] for core in range(2)]
-    return lax.all_to_all(block, ALL, 0, 0, axis_index_groups=groups)
+    return [
+        lax.ppermute(block, ALL, [(i, i ^ step) for i in range(count)])
+        for block, step in zip(blocks[1:], steps[1:])
+    ]
+
+
+def slots():
+    order = [0]
+    for steps in reversed(stages()):
+        order = [place ^ (step >> 1) for place in order for step in steps]
+    return order
+
+
+def scatter_chips(meta, blocks, rows, large, after):
+    order = list(reversed(stages()))
+    for k, steps in enumerate(order):
+        count = 1 if k + 1 == len(order) else len(order[k + 1])
+        outs = [((blocks[0].shape[0] // count, rows, LANES), BF16)] * count
+        blocks = call(
+            sum_kernel,
+            outs,
+            [meta, blocks[0], *partners(blocks, steps)],
+            after=() if k else after,
+            large=0 if k else large,
+            others=[step >> 1 & 1 for step in steps],
+        )
+    return blocks[0]
 
 
 def gather_chips(share):
-    count = device_count()
-    bits = list(range(count.bit_length() - 2, 0, -1))
-    stages = [bits[k : k + 2] for k in range(0, len(bits), 2)]
-    block, places = share[None], [0]
-    for stage in stages:
-        steps = [sum(bit << stage[k] for k, bit in enumerate(pick)) for pick in product((0, 1), repeat=len(stage))]
-        blocks = [block] + [
-            lax.ppermute(block, ALL, [(i, i ^ step) for i in range(count)]) for step in steps[1:]
-        ]
+    block, places = share, [0]
+    for steps in stages():
+        blocks = [block] + partners([block] * len(steps), steps)
         lists = [[place ^ (step >> 1) for place in places] for step in steps]
         block, places = jnp.concatenate(blocks), sum(lists, [])
     return blocks, lists
 
 
-def sigmoid(values):
-    return 0.5 * jnp.tanh(0.5 * values) + 0.5
+def half_terms(center, inv, gain, shift):
+    scale = 0.5 * inv * gain
+    return scale, 0.5 * shift - scale * center
+
+
+def silu_of_half(half):
+    tanh = jnp.tanh(half)
+    more = 1.0 + tanh
+    silu = half * more
+    return silu, more + silu * (1.0 - tanh)
 
 
 def wide(mask, width):
@@ -87,6 +123,12 @@
 def put_row(ref, first, vector):
     for k in range(vector.shape[1] // LANES):
         ref[0, first + k : first + k + 1, :] = vector[:, k * LANES : (k + 1) * LANES]
+
+
+def put_sums(ref, rows, acc, center, inv):
+    plain = total(acc[0])
+    put_row(ref, 0, plain)
+    put_row(ref, rows, (total(acc[1]) - center * plain) * inv)
 
 
 def spread(ref):
@@ -210,19 +252,20 @@
     stat[0:1] = center
     stat[1:2] = inv
     stat[2:3] = counted
-    scale = inv * gain[...]
-    offset = shift[...]
+    scale, offset = half_terms(center, inv, gain[...], shift[...])
 
     def prepare(i, carry):
         edge = pl.ds(pl.multiple_of(i * COLS, COLS), COLS)
         own = pl.ds(pl.multiple_of(i * slab, slab), slab)
-        tall = jnp.concatenate([low[edge, :], pre[own, :], high[edge, :]], axis=0)
-        z = (tall - center) * scale + offset
-        mask = wide(inside(meta, i, -1, rows + 2), z.shape[1])
-        left, middle, right = shifted(z * sigmoid(z) * mask)
-        hid[0, i] = left
-        hid[1, i] = middle
-        hid[2, i] = right
+        mask = inside(meta, i, -1, rows + 2)
+        for k in range(2):
+            lanes = slice(k * LANES, k * LANES + LANES)
+            tall = jnp.concatenate([low[edge, lanes], pre[own, lanes], high[edge, lanes]], axis=0)
+            silu, _ = silu_of_half(tall * scale[:, lanes] + offset[:, lanes])
+            left, middle, right = shifted(silu * mask)
+            hid[0, i, :, lanes] = left
+            hid[1, i, :, lanes] = middle
+            hid[2, i, :, lanes] = right
         return carry
 
     lax.fori_loop(0, blocks, prepare, 0)
@@ -276,21 +319,20 @@
     stat2[0:1] = center
     stat2[1:2] = inv
     stat2[2:3] = counted
-    scale = inv * gain[...]
-    offset = shift[...]
+    scale, offset = half_terms(center, inv, gain[...], shift[...])
 
     def step(i, carry):
         own = pl.ds(pl.multiple_of(i * slab, slab), slab)
-        mask = wide(inside(meta, i, 0, rows), 256)
-        summed = None
-        for half in range(2):
-            lanes = slice(half * 256, half * 256 + 256)
-            z = (pre[own, lanes] - center[:, lanes]) * scale[:, lanes] + offset[:, lanes]
-            value = (z * sigmoid(z) * mask).astype(BF16)
+        mask = inside(meta, i, 0, rows)
+        summed = [None, None]
+        for k in range(4):
+            lanes = slice(k * LANES, k * LANES + LANES)
+            silu, _ = silu_of_half(pre[own, lanes] * scale[:, lanes] + offset[:, lanes])
+            value = (silu * mask).astype(BF16)
             hid[own, lanes] = value
             part = fold(value.astype(F32))
-            summed = part if summed is None else summed + part
-        pooled[pl.ds(i, 1), :] = total(summed) / area_of(meta, i)
+            summed[k % 2] = part if k < 2 else summed[k % 2] + part
+        pooled[pl.ds(i, 1), :] = total(jnp.concatenate(summed, axis=1)) / area_of(meta, i)
         return carry
 
     lax.fori_loop(0, blocks, step, 0)
@@ -370,27 +412,26 @@
     stat3[1:2] = inv
     stat3[2:3] = counted
     acc[...] = jnp.zeros_like(acc)
+    scale, offset = half_terms(center, inv, gain[...], shift[...])
 
     def step(i, carry):
         own = pl.ds(pl.multiple_of(i * slab, slab), slab)
-        mask = wide(inside(meta, i, 0, rows), 256)
-        for k in range(4):
-            lanes = slice(k * 256, k * 256 + 256)
-            normed = (pre[own, lanes].astype(F32) - center[:, lanes]) * inv[:, lanes]
-            value = normed * gain[:, lanes] + shift[:, lanes] + x[own, lanes].astype(F32)
-            part = sigmoid(value)
-            silu = value * part
+        mask = inside(meta, i, 0, rows)
+        half_mask = 0.5 * mask
+        for k in range(8):
+            lanes = slice(k * LANES, k * LANES + LANES)
+            values = pre[own, lanes].astype(F32)
+            half = values * scale[:, lanes] + offset[:, lanes] + 0.5 * x[own, lanes].astype(F32)
+            silu, slope = silu_of_half(half)
             out[own, lanes] = (silu * mask).astype(BF16)
-            slope = part + silu * (1.0 - part)
-            back = cot[own, lanes].astype(F32) * mask * slope
+            back = cot[own, lanes].astype(F32) * half_mask * slope
             grad[own, lanes] = back
             acc[0, :, lanes] += fold(back)
-            acc[1, :, lanes] += fold(back * normed)
+            acc[1, :, lanes] += fold(back * values)
         return carry
 
     lax.fori_loop(0, blocks, step, 0)
-    put_row(pay, 0, total(acc[0]))
-    put_row(pay, 8, total(acc[1]))
+    put_sums(pay, 8, acc, center, inv)
     spread(pay)
 
 
@@ -418,9 +459,9 @@
         for j in range(group):
             image = g * group + j
             own = pl.ds(pl.multiple_of(image * slab, slab), slab)
-            mask = wide(inside(meta, image, 0, rows), 256)
-            for k in range(4):
-                lanes = slice(k * 256, k * 256 + 256)
+            mask = inside(meta, image, 0, rows)
+            for k in range(8):
+                lanes = slice(k * LANES, k * LANES + LANES)
                 gexp[own, lanes] = (
                     mask
                     * (
@@ -480,25 +521,42 @@
     token[...] = jnp.zeros_like(token)
 
 
-def pack_kernel(meta, keep, got, keep1, got1, out):
-    chips = out.shape[0]
-    large, small = keep.shape[0] // chips, keep1.shape[0] // chips
-    out[:, :large, :] = (keep[...] + got[...].astype(F32)).astype(BF16).reshape(chips, large, LANES)
-    out[:, large:, :] = (keep1[...] + got1[...].astype(F32)).astype(BF16).reshape(chips, small, LANES)
-
-
-def share_kernel(meta, shares, out, *, large):
-    chips, rows, _ = shares.shape
-
-    def add(first, last, start, step):
-        value = shares[start, first:last, :].astype(F32)
-        for k in range(start + step, chips, step):
-            value = value + shares[k, first:last, :].astype(F32)
+def pack_kernel(meta, keep, got, keep1, got1, *refs, places):
+    *outs, flat, flat1 = refs
+    held = outs[0].shape[0]
+    large, small = flat.shape[0] // len(places), flat1.shape[0] // len(places)
+    flat[...] = (keep[...] + got[...].astype(F32)).astype(BF16)
+    flat1[...] = (keep1[...] + got1[...].astype(F32)).astype(BF16)
+    for k, place in enumerate(places):
+        chip = meta[4] ^ place
+        out = outs[k // held]
+        out[k % held, :large, :] = flat[pl.ds(pl.multiple_of(chip * large, large), large), :]
+        out[k % held, large:, :] = flat1[pl.ds(pl.multiple_of(chip * small, small), small), :]
+
+
+def sum_kernel(meta, *refs, large, others):
+    ins, outs = refs[: len(others)], refs[len(others) :]
+    held = outs[0].shape[0]
+
+    def add(pick, first, last):
+        value = None
+        for ref in pick:
+            part = ref[:, first:last, :].astype(F32)
+            value = part if value is None else value + part
         return value.astype(BF16)
 
-    out[:large, :] = add(0, large, 0, 2)
-    out[large : 2 * large, :] = add(0, large, 1, 2)
-    out[2 * large :, :] = add(large, rows, 0, 1)
+    def put(value, at, rows):
+        for k, out in enumerate(outs):
+            out[:, pl.ds(at, rows), :] = value[k * held : k * held + held]
+
+    total_rows = ins[0].shape[1]
+    if not large:
+        put(add(ins, 0, total_rows), 0, total_rows)
+        return
+    for other in range(2):
+        pick = [ref for ref, side in zip(ins, others) if side == other]
+        put(add(pick, 0, large), pl.multiple_of((meta[3] ^ other) * large, large), large)
+    put(add(ins, large, total_rows), 2 * large, total_rows - large)
 
 
 def hidden_kernel(
@@ -533,28 +591,28 @@
         gpool[i : i + 1, :] = gpool[i : i + 1, :] / area_of(meta, i)
     center, inv = stat2[0:1], stat2[1:2]
     acc[...] = jnp.zeros_like(acc)
+    scale, offset = half_terms(center, inv, gain[...], shift[...])
 
     def step(i, carry):
         own = pl.ds(pl.multiple_of(i * slab, slab), slab)
-        mask = wide(inside(meta, i, 0, rows), 256)
-        mixed = gmix[own, :].astype(F32)
+        half_mask = 0.5 * inside(meta, i, 0, rows)
+        weights = att[pl.ds(i, 1), :]
         pool = gpool[pl.ds(i, 1), :]
-        for half in range(2):
-            lanes = slice(half * 256, half * 256 + 256)
-            normed = (pre[own, lanes] - center[:, lanes]) * inv[:, lanes]
-            value = normed * gain[:, lanes] + shift[:, lanes]
-            sig = sigmoid(value)
-            slope = sig * (1.0 + value * (1.0 - sig))
-            hidden = (mixed * att[pl.ds(i, 1), lanes] + pool).astype(BF16).astype(F32)
-            back = hidden * mask * slope
+        for k in range(4):
+            lanes = slice(k * LANES, k * LANES + LANES)
+            mid = slice(k % 2 * LANES, k % 2 * LANES + LANES)
+            mixed = gmix[own, mid].astype(F32)
+            values = pre[own, lanes]
+            _, slope = silu_of_half(values * scale[:, lanes] + offset[:, lanes])
+            hidden = (mixed * weights[:, lanes] + pool[:, mid]).astype(BF16).astype(F32)
+            back = hidden * half_mask * slope
             dz[own, lanes] = back
             acc[0, :, lanes] += fold(back)
-            acc[1, :, lanes] += fold(back * normed)
+            acc[1, :, lanes] += fold(back * values)
         return carry
 
     lax.fori_loop(0, blocks, step, 0)
-    put_row(pay, 0, total(acc[0]))
-    put_row(pay, 4, total(acc[1]))
+    put_sums(pay, 4, acc, center, inv)
     pay[0, 8:, :] = jnp.zeros((pay.shape[1] - 8, LANES), F32)
     spread(pay)
     share = pay.shape[1] - 8
@@ -575,33 +633,30 @@
     shift_out[...] = shift_sum
     gain_out[...] = gain_sum
     a, b, d = back_terms(stat2, gain2[...], shift_sum, gain_sum)
-    center2, inv2 = stat2[0:1], stat2[1:2]
+    scale2, offset2 = half_terms(stat2[0:1], stat2[1:2], gain2[...], shift2[...])
 
     def prepare(i, carry):
         own = pl.ds(pl.multiple_of(i * slab, slab), slab)
         edge = pl.ds(pl.multiple_of(i * COLS, COLS), COLS)
         mask = inside(meta, i, -1, rows + 2)
-        for half in range(2):
-            lanes = slice(half * 256, half * 256 + 256)
+        weights = att[pl.ds(i, 1), :]
+        pool = gpool[pl.ds(i, 1), :]
+        for k in range(4):
+            lanes = slice(k * LANES, k * LANES + LANES)
+            mid = slice(k % 2 * LANES, k % 2 * LANES + LANES)
 
             def edge_grad(values, mixed, keep):
-                z = (values[edge, lanes] - center2[:, lanes]) * inv2[:, lanes]
-                z = z * gain2[:, lanes] + shift2[:, lanes]
-                sig = sigmoid(z)
-                slope = sig * (1.0 + z * (1.0 - sig))
-                hidden = (
-                    mixed[edge, :] * att[pl.ds(i, 1), lanes] + gpool[pl.ds(i, 1), :]
-                ).astype(BF16)
-                return hidden.astype(F32) * keep * slope
-
-            keep_low = wide(mask[:COLS], 256)
-            keep_high = wide(mask[slab + COLS :], 256)
+                _, slope = silu_of_half(values[edge, lanes] * scale2[:, lanes] + offset2[:, lanes])
+                hidden = mixed[edge, mid] * weights[:, lanes] + pool[:, mid]
+                return hidden.astype(BF16).astype(F32) * (0.5 * keep) * slope
+
+            keep_low, keep_high = mask[:COLS], mask[slab + COLS :]
             grads = jnp.concatenate(
                 [edge_grad(low2, lowm, keep_low), dz[own, lanes], edge_grad(high2, highm, keep_high)],
                 axis=0,
             )
             values = jnp.concatenate([low2[edge, lanes], pre2[own, lanes], high2[edge, lanes]], axis=0)
-            back = wide(mask, 256) * (a[:, lanes] * grads + b[:, lanes] + d[:, lanes] * values)
+            back = mask * (a[:, lanes] * grads + b[:, lanes] + d[:, lanes] * values)
             left, middle, right = shifted(back)
             tall[0, i, :, lanes] = left
             tall[1, i, :, lanes] = middle
@@ -635,6 +690,7 @@
         store.start()
     acc[...] = jnp.zeros_like(acc)
     center, inv = stat[0:1], stat[1:2]
+    scale, offset = half_terms(center, inv, gain[...], shift[...])
     group = 4
 
     def step(g, carry):
@@ -652,22 +708,18 @@
             for j in range(group):
                 image = g * group + j
                 own = pl.ds(pl.multiple_of(image * slab, slab), slab)
-                mask = inside(meta, image, 0, rows)
-                normed = (pre[own, outs] - center[:, outs]) * inv[:, outs]
-                z = normed * gain[:, outs] + shift[:, outs]
-                sig = sigmoid(z)
-                slope = sig * (1.0 + z * (1.0 - sig))
-                back = value[j * slab : (j + 1) * slab] * mask * slope
+                values = pre[own, outs]
+                _, slope = silu_of_half(values * scale[:, outs] + offset[:, outs])
+                back = value[j * slab : (j + 1) * slab] * (0.5 * inside(meta, image, 0, rows)) * slope
                 out[own, outs] = back
                 acc[0, :, outs] += fold(back)
-                acc[1, :, outs] += fold(back * normed)
+                acc[1, :, outs] += fold(back * values)
         return carry
 
     lax.fori_loop(0, blocks // group, step, 0)
     stores.append(pltpu.make_async_copy(out, out_hbm, sems.at[3]))
     stores[-1].start()
-    put_row(pay, 0, total(acc[0]))
-    put_row(pay, 2, total(acc[1]))
+    put_sums(pay, 2, acc, center, inv)
     put_row(pay, 4, total(glog[...]))
     pay[0, 8:, :] = sums[8:]
     spread(pay)
@@ -676,8 +728,8 @@
 
 
 def reduce_back_kernel(
-    meta, got, stat, gain, dz_in, pre_in, x_in, small_out, keep, send, gain_out, shift_out, bias_out, squeeze,
-    dz, pre, x, small, sems, *, blocks, rows
+    meta, got, stat, gain, dz_in, pre_in, x_in, small, keep, send, gain_out, shift_out, bias_out, squeeze,
+    dz, pre, x, sems, *, blocks, rows
 ):
     slab = rows * COLS
     fetches = [
@@ -705,8 +757,6 @@
         return carry
 
     lax.fori_loop(0, blocks, step, 0)
-    store = pltpu.make_async_copy(small, small_out, sems.at[3])
-    store.start()
     fetches[2].wait()
     for ref, core in ((send, 1 - meta[2]), (keep, meta[2])):
         lanes = pl.ds(pl.multiple_of(core * 512, 512), 512)
@@ -714,7 +764,6 @@
         for q in range(2):
             ref[q * 512 : q * 512 + 512, :] = value[:, q * 128 : q * 128 + 128]
         clear_from(ref, 1024)
-    store.wait()
 
 
 def input_kernel(meta, small, w, grad, out, token, *, blocks, rows):
@@ -1010,13 +1059,13 @@
     large, less = (-(-rows_in // (chips * 16)) * 16 for rows_in in (9 * 128 + 2 * mid + inter, channels))
     keep, send, token = call(
         add_kernel,
-        [((chips * large, LANES), F32, "hbm"), ((chips * large, LANES), BF16, "hbm"), TOKEN],
+        [((chips * large, LANES), F32), ((chips * large, LANES), BF16), TOKEN],
         [meta, keep2, swap(send2, 1), keep3, swap(send3, 1)],
     )
     small1, keep1, send1, gain1_grad, shift1_grad, bias_grad, squeeze_total = call(
         reduce_back_kernel,
         [
-            ((pixels, mid), BF16, "hbm"),
+            ((pixels, mid), BF16),
             ((chips * less, LANES), F32),
             ((chips * less, LANES), BF16),
             ((1, mid), F32),
@@ -1029,37 +1078,30 @@
             ((pixels, mid), F32),
             ((pixels, mid), F32),
             ((pixels, channels), BF16),
-            ((pixels, mid), BF16),
-            pltpu.SemaphoreType.DMA((4,)),
+            pltpu.SemaphoreType.DMA((3,)),
         ],
         raw_in=(4, 5, 6),
-        raw_out=(0,),
         flops=small,
         after=(token,),
         local="in",
         **sizes,
     )
-    (packed,) = call(
+    first = len(stages()[-1])
+    blocks = call(
         pack_kernel,
-        [((chips, large + less, LANES), BF16, "hbm")],
+        [((chips // first, large + less, LANES), BF16)] * first,
         [meta, keep, swap(send, 2), keep1, swap(send1, 1)],
+        [((chips * large, LANES), BF16), ((chips * less, LANES), BF16)],
+        places=slots(),
     )
     input_grad, token = call(
         input_kernel,
         [((pixels, channels), BF16, "hbm"), TOKEN],
         [meta, small1, weight_reduce, grad_res],
         flops=small,
-        after=(packed,),
         **sizes,
     )
-    (shared,) = call(
-        share_kernel,
-        [((2 * large + less, LANES), BF16)],
-        [meta, exchange_chips(packed)],
-        after=(token,),
-        local="out",
-        large=large,
-    )
+    shared = scatter_chips(meta, blocks, 2 * large + less, large, [token])
     parts, places = gather_chips(shared)
     expand_total, excite_total, split_total, reduce_total = call(
         total_kernel,

time: 224 us -> 217 us (0.969)
  waiting for transfers between devices: 36.8 us -> 33.5 us
  local copies, waits for them, and re-layouts: 8.04 us -> 4.75 us
    all_to_all x1 -> x0, waiting for transfers between devices: 11.4 us -> none  [exchange_chips(): return lax.all_to_all(block, ALL, 0, 0, axis_index_groups=groups)]
    ppermute x6 -> x12, waiting for transfers between devices: 14.3 us -> 22.4 us  [partners(): lax.ppermute(block, ALL, [(i, i ^ step) for i in range(count)])]
    ppermute x6 -> x12, starting transfers between devices: 8.01 us -> 16 us  [partners(): lax.ppermute(block, ALL, [(i, i ^ step) for i in range(count)])]
    all_to_all x1 -> x0, starting transfers between devices: 6.12 us -> none  [exchange_chips(): return lax.all_to_all(block, ALL, 0, 0, axis_index_groups=groups)]
    unnamed x50 -> x44, local copies, waits for them, and re-layouts: 7.3 us -> 4.01 us
    pallas_call x16 -> x17, Pallas kernels: 50.2 us -> 49 us  [call(): pl.pallas_call(run, grid=() if local == 'in out' else (1,), out_shape=[pl...]
  transfers between devices with their start and end apart: 22 -> 27, of which waited for: 13 -> 17; matrix products, arithmetic and copies ran while one was open for 0% -> 0% of each run, Pallas kernels for 5% -> 5%
where the time goes in v6:
time: 217 us
  blocking collectives  97.6 us (45%)
  Pallas kernels  49 us (23%)
  waiting for transfers between devices  33.5 us (15%)
  starting transfers between devices  30.9 us (14%)
  local copies, waits for them, and re-layouts  4.75 us (2%)
    all_to_all x7, blocking collectives, exchange(): return lax.all_to_all(block, ALL, 0, 0)  97.6 us
    pallas_call x17, Pallas kernels, call(): pl.pallas_call(run, grid=() if local == 'in out' else (1,), out_shape=[pl...  49 us
    ppermute x12, waiting for transfers between devices, partners(): lax.ppermute(block, ALL, [(i, i ^ step) for i in range(count)])  22.4 us
    ppermute x12, starting transfers between devices, partners(): lax.ppermute(block, ALL, [(i, i ^ step) for i in range(count)])  16 us
    ppermute x3, starting transfers between devices, halo(): low = lax.ppermute(bottom, 'narrow', [(i, i + 1) for i in range(count - 1)])  6.35 us
    ppermute x8, waiting for transfers between devices, swap(): return lax.ppermute(block, 'narrow', [(i, i ^ bit) for i in range(count)])  5.54 us
    all_to_all x1, waiting for transfers between devices, exchange(): return lax.all_to_all(block, ALL, 0, 0)  4.84 us
  transfers between devices with their start and end apart: 27, of which 17 were waited for; matrix products, arithmetic and copies ran while one was open for 0% of the time, Pallas kernels for 5%

profile of v6, /device:TPU:0, one launch (start us, length us, event | category | flops | bytes accessed | tf_op | source)
XLA Modules:
  0.0 216.9 jit_solution(5689478313076992735)
XLA Ops:
  1.4 1.6 copy-done
  4.1 1.9 shard_map.288
  6.1 2.4 %collective-permute-start = (f32[256,256]{1,0:T(8,128)S(1)}, f32[256,256]{1,0:T(8,128)S(1)}, u32[]{:S(2)}, u32[]{:S(2)}) collective-permute-start(f32[256,256]{1,0:T(8,128)S(1)} %get-tuple-element.88), channel_id=1, source_target_pairs={{0,1},{1,2},{2,3},{4,5},{5,6},{6,7},{8,9},{9,10},{10,11},{12,13},{... | collective-permute-start | bytes 786440 | tf_op jit(solution)/shard_map/ppermute | solution.py:27
  8.4 1.3 collective-permute-start.1
  9.7 17.2 %all_to_all.40.refs_1_ = f32[32,8,128]{2,1,0:T(8,128)S(1)} all-to-all(f32[32,8,128]{2,1,0:T(8,128)S(1)} %get-tuple-element.86), channel_id=1, replica_groups=mesh['batch'=8,'narrow'=4] {'batch','narrow'}, dimensions={0} | all-to-all | bytes 262144 | tf_op jit(solution)/shard_map/all_to_all | solution.py:33
  27.0 4.1 %shard_map.289 = (bf16[3,16,96,256]{3,2,1,0:T(8,128)(2,1)}, f32[1024,512]{1,0:T(8,128)S(1)}, f32[256,512]{1,0:T(8,128)S(1)}, f32[256,512]{1,0:T(8,128)S(1)}, f32...) custom-call(s32[21]{0:T(128)S(1)} %concatenate.6.refs_0_, f32[32,8,128]{2,1,0:T(8,128)S(1)} %all_to_all.40.refs_1_, ...), custom_call_target="tpu_custom_call" | custom-call | flops 1207959552 | bytes 8530004 | tf_op jit(solution)/shard_map/pallas_call | solution.py:199
  31.2 2.2 collective-permute-start.2
  33.3 1.3 collective-permute-start.3
  34.7 12.1 %all_to_all.41.refs_1_ = f32[32,8,128]{2,1,0:T(8,128)S(1)} all-to-all(f32[32,8,128]{2,1,0:T(8,128)S(1)} %get-tuple-element.90), channel_id=1, replica_groups=mesh['batch'=8,'narrow'=4] {'batch','narrow'}, dimensions={0} | all-to-all | bytes 262144 | tf_op jit(solution)/shard_map/all_to_all | solution.py:33
  46.9 2.0 shard_map.290
  48.9 12.4 %all_to_all.42.refs_1_ = f32[32,16,128]{2,1,0:T(8,128)S(1)} all-to-all(f32[32,16,128]{2,1,0:T(8,128)S(1)} %get-tuple-element.95), channel_id=1, replica_groups=mesh['batch'=8,'narrow'=4] {'batch','narrow'}, dimensions={0} | all-to-all | bytes 524288 | tf_op jit(solution)/shard_map/all_to_all | solution.py:33
  61.4 2.6 %shard_map.291 = (bf16[1024,256]{1,0:T(8,128)(2,1)S(1)}, bf16[1024,1024]{1,0:T(8,128)(2,1)S(1)}, f32[16,512]{1,0:T(8,128)S(1)}, f32[16,128]{1,0:T(8,128)S(1)}, f...) custom-call(s32[21]{0:T(128)S(1)} %concatenate.6.refs_0_, ...), custom_call_target="tpu_custom_call" | custom-call | flops 536870912 | bytes 5160020 | tf_op jit(solution)/shard_map/pallas_call | solution.py:199
  64.0 12.7 %all_to_all.43.refs_1_ = f32[32,16,128]{2,1,0:T(8,128)S(1)} all-to-all(f32[32,16,128]{2,1,0:T(8,128)S(1)} %get-tuple-element.97), channel_id=1, replica_groups=mesh['batch'=8,'narrow'=4] {'batch','narrow'}, dimensions={0} | all-to-all | bytes 524288 | tf_op jit(solution)/shard_map/all_to_all | solution.py:33
  76.8 5.4 %shard_map.292 = (bf16[1024,1024]{1,0:T(8,128)(2,1)}, f32[1024,1024]{1,0:T(8,128)S(1)}, f32[32,16,128]{2,1,0:T(8,128)S(1)}, f32[8,1024]{1,0:T(8,128)S(1)}) custom-call(s32[21]{0:T(128)S(1)} %concatenate.6.refs_0_, f32[32,16,128]{2,1,0:T(8,128)S(1)} %all_to_all.43.refs_1_, f32[8,256]{1,0:T(8,128)S(1)} %get-tuple-element.91.refs_2_.refs_15_, ...), custom_call_target="tpu_custom_call" | custom-call | bytes 13156436 | tf_op jit(solution)/shard_map/pallas_call | solution.py:199
  82.2 12.8 %all_to_all.44.refs_1_ = f32[32,16,128]{2,1,0:T(8,128)S(1)} all-to-all(f32[32,16,128]{2,1,0:T(8,128)S(1)} %get-tuple-element.100), channel_id=1, replica_groups=mesh['batch'=8,'narrow'=4] {'batch','narrow'}, dimensions={0} | all-to-all | bytes 524288 | tf_op jit(solution)/shard_map/all_to_all | solution.py:33
  95.0 3.4 %shard_map.293 = (bf16[1024,1024]{1,0:T(8,128)(2,1)S(1)}, bf16[1024,256]{1,0:T(8,128)(2,1)S(1)}, f32[256,256]{1,0:T(8,128)S(1)}, f32[256,256]{1,0:T(8,128)S(1)},...) custom-call(s32[21]{0:T(128)S(1)} %concatenate.6.refs_0_, f32[32,16,128]{2,1,0:T(8,128)S(1)} %all_to_all.44.refs_1_, ...), custom_call_target="tpu_custom_call" | custom-call | flops 536870912 | bytes 11382868 | tf_op jit(solution)/shard_map/pallas_call | solution.py:199
  98.4 1.8 collective-permute-start.4
  100.2 1.3 collective-permute-start.5
  101.5 1.5 shard_map.294
  104.6 17.4 %all_to_all.45.refs_1_ = f32[32,16,128]{2,1,0:T(8,128)S(1)} all-to-all(f32[32,16,128]{2,1,0:T(8,128)S(1)} %shard_map.295), channel_id=1, replica_groups=mesh['batch'=8,'narrow'=4] {'batch','narrow'}, dimensions={0} | all-to-all | bytes 524288 | tf_op jit(solution)/shard_map/all_to_all | solution.py:33
  122.0 3.3 %shard_map.296 = (f32[1024,512]{1,0:T(8,128)S(1)}, f32[16,256]{1,0:T(8,128)S(1)}, f32[32,16,128]{2,1,0:T(8,128)S(1)}, f32[1,128]{1,0:T(1,128)}, f32[1,128]{1,0:T(1,128)}) custom-call(s32[21]{0:T(128)S(1)} %concatenate.6.refs_0_, f32[32,16,128]{2,1,0:T(8,128)S(1)} %all_to_all.45.refs_1_, f32[128,128]{1,0:T(8,128)S(1)} %get-tuple-element.111.refs_2_, ...), custom_call_target="tpu_custom_call" | custom-call | bytes 5596756 | tf_op jit(solution)/shard_map/pallas_call | solution.py:199
  125.3 12.8 %all_to_all.46.refs_1_ = f32[32,16,128]{2,1,0:T(8,128)S(1)} all-to-all(f32[32,16,128]{2,1,0:T(8,128)S(1)} %get-tuple-element.117), channel_id=1, replica_groups=mesh['batch'=8,'narrow'=4] {'batch','narrow'}, dimensions={0} | all-to-all | bytes 524288 | tf_op jit(solution)/shard_map/all_to_all | solution.py:33
  138.1 9.8 %shard_map.297 = (f32[1024,256]{1,0:T(8,128)}, f32[2,1152,128]{2,1,0:T(8,128)}, bf16[2,1152,128]{2,1,0:T(8,128)(2,1)}, f32[32,16,128]{2,1,0:T(8,128)}, f32[1,512]{1,0:T(1,128)}, /*index=5*/f32[1,512]{1,0:T(1,128)}) custom-call(s32[21]{0:T(128)S(1)} %concatenate.6.refs_0_, f32[32,16,128]{2,1,0:T(8,128)S(1)} %all_to_all.46.refs_1_, ...), custom_call_target="tpu_custom_call" | custom-call | flops 2415919104 | bytes 13813844 | tf_op jit(solution)/shard_map/pallas_call | solution.py:199
  148.0 2.6 %all-to-all-start.7 = ((f32[32,16,128]{2,1,0:T(8,128)}), f32[32,16,128]{2,1,0:T(8,128)S(1)}, u32[]{:S(2)}, u32[]{:S(2)}) async-start(f32[32,16,128]{2,1,0:T(8,128)} %get-tuple-element.121), calls=%async_computation.7 | async-start | bytes 524288 | tf_op jit(solution)/shard_map/all_to_all | solution.py:33
  150.9 1.4 collective-permute-done.7.refs_4_
  152.3 1.3 copy-done.10
  153.6 1.2 shard_map.298
  154.8 1.7 collective-permute-start.8
  156.5 4.8 %all-to-all-done.7.refs_1_ = f32[32,16,128]{2,1,0:T(8,128)S(1)} async-done(((f32[32,16,128]{2,1,0:T(8,128)}), f32[32,16,128]{2,1,0:T(8,128)S(1)}, u32[]{:S(2)}, u32[]{:S(2)}) %all-to-all-start.7) | async-done | bytes 262176 | tf_op jit(solution)/shard_map/all_to_all | solution.py:33
  161.3 4.3 %shard_map.299 = (bf16[1024,256]{1,0:T(8,128)(2,1)S(1)}, f32[1024,128]{1,0:T(8,128)S(1)}, bf16[1024,128]{1,0:T(8,128)(2,1)S(1)}, f32[1,256]{1,0:T(1,128)}, f32[1...) custom-call(s32[21]{0:T(128)S(1)} %concatenate.6.refs_0_, f32[32,16,128]{2,1,0:T(8,128)S(1)} %all-to-all-done.7.refs_1_, ...), custom_call_target="tpu_custom_call" | custom-call | flops 536870912 | bytes 5911636 | tf_op jit(solution)/shard_map/pallas_call | solution.py:199
  165.7 1.5 collective-permute-done.9.refs_4_
  169.1 1.4 collective-permute-start.10
  170.5 1.4 collective-permute-start.11
  172.6 3.3 %shard_map.300 = (bf16[1024,1024]{1,0:T(8,128)(2,1)}, f32[8,128]{1,0:T(8,128)}) custom-call(s32[21]{0:T(128)S(1)} %concatenate.6.refs_0_, bf16[1024,256]{1,0:T(8,128)(2,1)S(1)} %get-tuple-element.127.refs_1_, bf16[1024,256]{1,0:T(8,128)(2,1)S(1)} %copy-done.7, f32[1024,1024]{1,0:T(8,128)S(1)} %copy-done.3), custom_call_target="tpu_custom_call" | custom-call | flops 536870912 | bytes 7344212 | tf_op jit(solution)/shard_map/pallas_call | solution.py:199
  175.9 2.1 collective-permute-done.11.refs_3_
  178.0 2.1 collective-permute-done.12.refs_4_
  180.7 1.8 collective-permute-start.13
  182.5 2.2 %collective-permute-start.14 = (bf16[1,288,128]{2,1,0:T(8,128)(2,1)S(1)}, bf16[1,288,128]{2,1,0:T(8,128)(2,1)S(1)}, u32[]{:S(2)}, u32[]{:S(2)}) collective-permute-start(bf16[1,288,128]{2,1,0:T(8,128)(2,1)S(1)} %get-tuple-element.140), channel_id=1, source_target_pairs={{0,16},{1,17},{2,18},{3,19},{4,20},{5,21},{6,22},{7,23},{8,24},{9,... | collective-permute-start | bytes 221192 | tf_op jit(solution)/shard_map/ppermute | solution.py:53
  185.7 3.6 %collective-permute-done.14.refs_3_ = bf16[1,288,128]{2,1,0:T(8,128)(2,1)S(1)} collective-permute-done((bf16[1,288,128]{2,1,0:T(8,128)(2,1)S(1)}, bf16[1,288,128]{2,1,0:T(8,128)(2,1)S(1)}, u32[]{:S(2)}, u32[]{:S(2)}) %collective-permute-start.14) | collective-permute-done | bytes 73760 | tf_op jit(solution)/shard_map/ppermute | solution.py:53
  189.3 1.6 collective-permute-done.15.refs_4_
  191.5 1.5 collective-permute-start.18
  193.0 2.9 %collective-permute-start.16 = (bf16[1,288,128]{2,1,0:T(8,128)(2,1)S(1)}, bf16[1,288,128]{2,1,0:T(8,128)(2,1)S(1)}, u32[]{:S(2)}, u32[]{:S(2)}) collective-permute-start(bf16[1,288,128]{2,1,0:T(8,128)(2,1)S(1)} %shard_map.303), channel_id=1, source_target_pairs={{0,8},{1,9},{2,10},{3,11},{4,12},{5,13},{6,14},{7,15},{8,0},{9,1},... | collective-permute-start | bytes 221192 | tf_op jit(solution)/shard_map/ppermute | solution.py:53
  195.9 1.8 collective-permute-done.18
  197.7 1.5 collective-permute-done.17
  199.3 1.8 collective-permute-start.21
  202.9 6.2 %collective-permute-done.21.refs_4_ = bf16[4,288,128]{2,1,0:T(8,128)(2,1)S(1)} collective-permute-done((bf16[4,288,128]{2,1,0:T(8,128)(2,1)S(1)}, bf16[4,288,128]{2,1,0:T(8,128)(2,1)S(1)}, u32[]{:S(2)}, u32[]{:S(2)}) %collective-permute-start.21) | collective-permute-done | bytes 294944 | tf_op jit(solution)/shard_map/ppermute | solution.py:53
  209.1 2.5 %collective-permute-done.20.refs_3_ = bf16[4,288,128]{2,1,0:T(8,128)(2,1)S(1)} collective-permute-done((bf16[4,288,128]{2,1,0:T(8,128)(2,1)S(1)}, bf16[4,288,128]{2,1,0:T(8,128)(2,1)S(1)}, u32[]{:S(2)}, u32[]{:S(2)}) %collective-permute-start.20) | collective-permute-done | bytes 294944 | tf_op jit(solution)/shard_map/ppermute | solution.py:53
  213.7 3.2 %shard_map.304 = (f32[256,1024]{1,0:T(8,128)}, f32[128,512]{1,0:T(8,128)}, f32[3,3,2,128,256]{4,3,2,1,0:T(8,128)}, f32[1024,256]{1,0:T(8,128)}) custom-call(s32[21]{0:T(128)S(1)} %concatenate.6.refs_0_, bf16[4,288,128]{2,1,0:T(8,128)(2,1)S(1)} %pad_maximum_fusion.refs_1_, bf16[4,288,128]{2,1,0:T(8,128)(2,1)S(1)} %collective-permute-done.19.refs_2_, ...), custom_call_target="tpu_custom_call" | custom-call | bytes 7077972 | tf_op jit(solution)/shard_map/pallas_call | solution.py:199
  (76 shorter events, 12.6 us)
Async XLA Ops:
  0.6 26.3 %copy-start.20 = (f32[256]{0:T(256)S(1)}, f32[256]{0:T(256)}, u32[]{:S(2)}) copy-start(f32[256]{0:T(256)} %param.21) | copy-start | bytes 3076
  0.7 26.3 %copy-start.16 = (f32[256]{0:T(256)S(1)}, f32[256]{0:T(256)}, u32[]{:S(2)}) copy-start(f32[256]{0:T(256)} %param.20) | copy-start | bytes 3076
  1.4 1.6 copy-start
  4.1 22.9 %copy-start.9 = (bf16[3,3,2,128,256]{4,3,2,1,0:T(8,128)(2,1)S(1)}, bf16[3,3,2,128,256]{4,3,2,1,0:T(8,128)(2,1)}, u32[]{:S(2)}) copy-start(bf16[3,3,2,128,256]{4,3,2,1,0:T(8,128)(2,1)} %refs_13_.1) | copy-start | bytes 3538948
  6.0 132.0 %copy-start.4 = (f32[1024,256]{1,0:T(8,128)}, f32[1024,256]{1,0:T(8,128)S(1)}, u32[]{:S(2)}) copy-start(f32[1024,256]{1,0:T(8,128)S(1)} %get-tuple-element.87.refs_2_.refs_14_.refs_5_) | copy-start | bytes 3145732
  6.1 20.9 %collective-permute-start = (f32[256,256]{1,0:T(8,128)S(1)}, f32[256,256]{1,0:T(8,128)S(1)}, u32[]{:S(2)}, u32[]{:S(2)}) collective-permute-start(f32[256,256]{1,0:T(8,128)S(1)} %get-tuple-element.88), channel_id=1, source_target_pairs={{0,1},{1,2},{2,3},{4,5},{5,6},{6,7},{8,9},{9,10},{10,11},{12,13},{... | collective-permute-start | bytes 786440 | tf_op jit(solution)/shard_map/ppermute | solution.py:27
  8.4 18.5 %collective-permute-start.1 = (f32[256,256]{1,0:T(8,128)S(1)}, f32[256,256]{1,0:T(8,128)S(1)}, u32[]{:S(2)}, u32[]{:S(2)}) collective-permute-start(f32[256,256]{1,0:T(8,128)S(1)} %get-tuple-element.89), channel_id=1, source_target_pairs={{1,0},{2,1},{3,2},{5,4},{6,5},{7,6},{9,8},{10,9},{11,10},{13,12},{... | collective-permute-start | bytes 786440 | tf_op jit(solution)/shard_map/ppermute | solution.py:28
  27.0 19.8 %copy-start.12 = (f32[256,128]{1,0:T(8,128)S(1)}, f32[256,128]{1,0:T(8,128)}, u32[]{:S(2)}) copy-start(f32[256,128]{1,0:T(8,128)} %refs_7_.5) | copy-start | bytes 393220
  27.0 19.8 %copy-start.13 = (f32[512]{0:T(512)S(1)}, f32[512]{0:T(512)}, u32[]{:S(2)}) copy-start(f32[512]{0:T(512)} %param.23) | copy-start | bytes 6148
  27.0 19.8 %copy-start.14 = (f32[512]{0:T(512)S(1)}, f32[512]{0:T(512)}, u32[]{:S(2)}) copy-start(f32[512]{0:T(512)} %param.24) | copy-start | bytes 6148
  31.2 15.6 %collective-permute-start.2 = (f32[256,512]{1,0:T(8,128)S(1)}, f32[256,512]{1,0:T(8,128)S(1)}, u32[]{:S(2)}, u32[]{:S(2)}) collective-permute-start(f32[256,512]{1,0:T(8,128)S(1)} %get-tuple-element.93), channel_id=1, source_target_pairs={{0,1},{1,2},{2,3},{4,5},{5,6},{6,7},{8,9},{9,10},{10,11},{12,13},{... | collective-permute-start | bytes 1572872 | tf_op jit(solution)/shard_map/ppermute | solution.py:27
  33.3 13.5 %collective-permute-start.3 = (f32[256,512]{1,0:T(8,128)S(1)}, f32[256,512]{1,0:T(8,128)S(1)}, u32[]{:S(2)}, u32[]{:S(2)}) collective-permute-start(f32[256,512]{1,0:T(8,128)S(1)} %get-tuple-element.94), channel_id=1, source_target_pairs={{1,0},{2,1},{3,2},{5,4},{6,5},{7,6},{9,8},{10,9},{11,10},{13,12},{... | collective-permute-start | bytes 1572872 | tf_op jit(solution)/shard_map/ppermute | solution.py:28
  34.6 26.7 %copy-start.8 = (bf16[256,1024]{1,0:T(8,128)(2,1)S(1)}, bf16[256,1024]{1,0:T(8,128)(2,1)}, u32[]{:S(2)}) copy-start(bf16[256,1024]{1,0:T(8,128)(2,1)} %refs_6_.3) | copy-start | bytes 1572868
  34.6 26.7 %copy-start.11 = (f32[128,512]{1,0:T(8,128)S(1)}, f32[128,512]{1,0:T(8,128)}, u32[]{:S(2)}) copy-start(f32[128,512]{1,0:T(8,128)} %refs_2_.4) | copy-start | bytes 786436
  34.7 26.7 %copy-start.18 = (f32[512]{0:T(512)S(1)}, f32[512]{0:T(512)}, u32[]{:S(2)}) copy-start(f32[512]{0:T(512)} %param.29) | copy-start | bytes 6148
  34.7 26.7 %copy-start.19 = (f32[128]{0:T(128)S(1)}, f32[128]{0:T(128)}, u32[]{:S(2)}) copy-start(f32[128]{0:T(128)} %param.26) | copy-start | bytes 1540
  34.7 26.7 %copy-start.21 = (f32[128]{0:T(128)S(1)}, f32[128]{0:T(128)}, u32[]{:S(2)}) copy-start(f32[128]{0:T(128)} %param.27) | copy-start | bytes 1540
  46.9 29.9 %copy-start.5 = (bf16[16,4,16,1024]{3,2,1,0:T(8,128)(2,1)S(1)}, bf16[16,4,16,1024]{3,2,1,0:T(8,128)(2,1)}, u32[]{:S(2)}) copy-start(bf16[16,4,16,1024]{3,2,1,0:T(8,128)(2,1)} %param.33) | copy-start | bytes 6291460
  48.9 27.9 %copy-start.1 = (bf16[16,4,16,1024]{3,2,1,0:T(8,128)(2,1)S(1)}, bf16[16,4,16,1024]{3,2,1,0:T(8,128)(2,1)}, u32[]{:S(2)}) copy-start(bf16[16,4,16,1024]{3,2,1,0:T(8,128)(2,1)} %param.17) | copy-start | bytes 6291460
  48.9 27.8 %copy-start.15 = (f32[1024]{0:T(1024)S(1)}, f32[1024]{0:T(1024)}, u32[]{:S(2)}) copy-start(f32[1024]{0:T(1024)} %param.31) | copy-start | bytes 12292
  48.9 27.8 %copy-start.17 = (f32[1024]{0:T(1024)S(1)}, f32[1024]{0:T(1024)}, u32[]{:S(2)}) copy-start(f32[1024]{0:T(1024)} %param.32) | copy-start | bytes 12292
  82.2 16.2 %copy-start.2 = (f32[1024,1024]{1,0:T(8,128)}, f32[1024,1024]{1,0:T(8,128)S(1)}, u32[]{:S(2)}) copy-start(f32[1024,1024]{1,0:T(8,128)S(1)} %get-tuple-element.102.refs_4_.refs_3_) | copy-start | bytes 12582916
  98.4 4.6 %collective-permute-start.4 = (f32[256,256]{1,0:T(8,128)S(1)}, f32[256,256]{1,0:T(8,128)S(1)}, u32[]{:S(2)}, u32[]{:S(2)}) collective-permute-start(f32[256,256]{1,0:T(8,128)S(1)} %get-tuple-element.105), channel_id=1, source_target_pairs={{0,1},{1,2},{2,3},{4,5},{5,6},{6,7},{8,9},{9,10},{10,11},{12,13},{... | collective-permute-start | bytes 786440 | tf_op jit(solution)/shard_map/ppermute | solution.py:27
  100.2 3.4 %collective-permute-start.5 = (f32[256,256]{1,0:T(8,128)S(1)}, f32[256,256]{1,0:T(8,128)S(1)}, u32[]{:S(2)}, u32[]{:S(2)}) collective-permute-start(f32[256,256]{1,0:T(8,128)S(1)} %get-tuple-element.106), channel_id=1, source_target_pairs={{1,0},{2,1},{3,2},{5,4},{6,5},{7,6},{9,8},{10,9},{11,10},{13,12},{... | collective-permute-start | bytes 786440 | tf_op jit(solution)/shard_map/ppermute | solution.py:28
  147.9 4.4 %collective-permute-start.6 = (bf16[2,1152,128]{2,1,0:T(8,128)(2,1)}, bf16[2,1152,128]{2,1,0:T(8,128)(2,1)S(1)}, u32[]{:S(2)}, u32[]{:S(2)}) collective-permute-start(bf16[2,1152,128]{2,1,0:T(8,128)(2,1)} %get-tuple-element.124), channel_id=1, source_target_pairs={{0,1},{1,0},{2,3},{3,2},{4,5},{5,4},{6,7},{7,6},{8,9},{9,8},{10,11... | collective-permute-start | bytes 1769480 | tf_op jit(solution)/shard_map/ppermute | solution.py:38
  148.0 13.3 %all-to-all-start.7 = ((f32[32,16,128]{2,1,0:T(8,128)}), f32[32,16,128]{2,1,0:T(8,128)S(1)}, u32[]{:S(2)}, u32[]{:S(2)}) async-start(f32[32,16,128]{2,1,0:T(8,128)} %get-tuple-element.121), calls=%async_computation.7 | async-start | bytes 524288 | tf_op jit(solution)/shard_map/all_to_all | solution.py:33
  150.6 1.7 collective-permute-start.7
  152.3 1.3 copy-start.10
  154.8 13.4 %collective-permute-start.8 = (bf16[1792,128]{1,0:T(8,128)(2,1)S(1)}, bf16[1792,128]{1,0:T(8,128)(2,1)S(1)}, u32[]{:S(2)}, u32[]{:S(2)}) collective-permute-start(bf16[1792,128]{1,0:T(8,128)(2,1)S(1)} %get-tuple-element.130), channel_id=1, source_target_pairs={{0,2},{1,3},{2,0},{3,1},{4,6},{5,7},{6,4},{7,5},{8,10},{9,11},{10,... | collective-permute-start | bytes 1376264 | tf_op jit(solution)/shard_map/ppermute | solution.py:38
  161.3 11.3 %copy-start.3 = (f32[1024,1024]{1,0:T(8,128)S(1)}, f32[1024,1024]{1,0:T(8,128)}, u32[]{:S(2)}) copy-start(f32[1024,1024]{1,0:T(8,128)} %copy-done.2) | copy-start | bytes 12582916
  165.6 7.0 %copy-start.7 = (bf16[1024,256]{1,0:T(8,128)(2,1)S(1)}, bf16[1024,256]{1,0:T(8,128)(2,1)}, u32[]{:S(2)}) copy-start(bf16[1024,256]{1,0:T(8,128)(2,1)} %refs_2_.5) | copy-start | bytes 1572868
  165.6 1.6 collective-permute-start.9
  169.1 6.9 %collective-permute-start.10 = (bf16[4,176,128]{2,1,0:T(8,128)(2,1)S(1)}, bf16[4,176,128]{2,1,0:T(8,128)(2,1)S(1)}, u32[]{:S(2)}, u32[]{:S(2)}) collective-permute-start(bf16[4,176,128]{2,1,0:T(8,128)(2,1)S(1)} %get-tuple-element.134), channel_id=1, source_target_pairs={{0,2},{1,3},{2,0},{3,1},{4,6},{5,7},{6,4},{7,5},{8,10},{9,11},{10,... | collective-permute-start | bytes 540680 | tf_op jit(solution)/shard_map/ppermute | solution.py:53
  170.5 7.5 %collective-permute-start.11 = (bf16[4,176,128]{2,1,0:T(8,128)(2,1)S(1)}, bf16[4,176,128]{2,1,0:T(8,128)(2,1)S(1)}, u32[]{:S(2)}, u32[]{:S(2)}) collective-permute-start(bf16[4,176,128]{2,1,0:T(8,128)(2,1)S(1)} %get-tuple-element.135), channel_id=1, source_target_pairs={{0,4},{1,5},{2,6},{3,7},{4,0},{5,1},{6,2},{7,3},{8,12},{9,13},{10,... | collective-permute-start | bytes 540680 | tf_op jit(solution)/shard_map/ppermute | solution.py:53
  171.9 8.2 %collective-permute-start.12 = (bf16[4,176,128]{2,1,0:T(8,128)(2,1)S(1)}, bf16[4,176,128]{2,1,0:T(8,128)(2,1)S(1)}, u32[]{:S(2)}, u32[]{:S(2)}) collective-permute-start(bf16[4,176,128]{2,1,0:T(8,128)(2,1)S(1)} %get-tuple-element.136), channel_id=1, source_target_pairs={{0,6},{1,7},{2,4},{3,5},{4,2},{5,3},{6,0},{7,1},{8,14},{9,15},{10,... | collective-permute-start | bytes 540680 | tf_op jit(solution)/shard_map/ppermute | solution.py:53
  180.7 4.9 %collective-permute-start.13 = (bf16[1,288,128]{2,1,0:T(8,128)(2,1)S(1)}, bf16[1,288,128]{2,1,0:T(8,128)(2,1)S(1)}, u32[]{:S(2)}, u32[]{:S(2)}) collective-permute-start(bf16[1,288,128]{2,1,0:T(8,128)(2,1)S(1)} %get-tuple-element.139), channel_id=1, source_target_pairs={{0,8},{1,9},{2,10},{3,11},{4,12},{5,13},{6,14},{7,15},{8,0},{9,1},... | collective-permute-start | bytes 221192 | tf_op jit(solution)/shard_map/ppermute | solution.py:53
  182.5 6.8 %collective-permute-start.14 = (bf16[1,288,128]{2,1,0:T(8,128)(2,1)S(1)}, bf16[1,288,128]{2,1,0:T(8,128)(2,1)S(1)}, u32[]{:S(2)}, u32[]{:S(2)}) collective-permute-start(bf16[1,288,128]{2,1,0:T(8,128)(2,1)S(1)} %get-tuple-element.140), channel_id=1, source_target_pairs={{0,16},{1,17},{2,18},{3,19},{4,20},{5,21},{6,22},{7,23},{8,24},{9,... | collective-permute-start | bytes 221192 | tf_op jit(solution)/shard_map/ppermute | solution.py:53
  184.7 6.2 %collective-permute-start.15 = (bf16[1,288,128]{2,1,0:T(8,128)(2,1)S(1)}, bf16[1,288,128]{2,1,0:T(8,128)(2,1)S(1)}, u32[]{:S(2)}, u32[]{:S(2)}) collective-permute-start(bf16[1,288,128]{2,1,0:T(8,128)(2,1)S(1)} %get-tuple-element.141), channel_id=1, source_target_pairs={{0,24},{1,25},{2,26},{3,27},{4,28},{5,29},{6,30},{7,31},{8,16},{9,... | collective-permute-start | bytes 221192 | tf_op jit(solution)/shard_map/ppermute | solution.py:53
  191.5 6.3 %collective-permute-start.18 = (bf16[1,288,128]{2,1,0:T(8,128)(2,1)S(1)}, bf16[1,288,128]{2,1,0:T(8,128)(2,1)S(1)}, u32[]{:S(2)}, u32[]{:S(2)}) collective-permute-start(bf16[1,288,128]{2,1,0:T(8,128)(2,1)S(1)} %shard_map.303), channel_id=1, source_target_pairs={{0,24},{1,25},{2,26},{3,27},{4,28},{5,29},{6,30},{7,31},{8,16},{9,... | collective-permute-start | bytes 221192 | tf_op jit(solution)/shard_map/ppermute | solution.py:53
  193.0 6.3 %collective-permute-start.17 = (bf16[1,288,128]{2,1,0:T(8,128)(2,1)S(1)}, bf16[1,288,128]{2,1,0:T(8,128)(2,1)S(1)}, u32[]{:S(2)}, u32[]{:S(2)}) collective-permute-start(bf16[1,288,128]{2,1,0:T(8,128)(2,1)S(1)} %shard_map.303), channel_id=1, source_target_pairs={{0,16},{1,17},{2,18},{3,19},{4,20},{5,21},{6,22},{7,23},{8,24},{9,... | collective-permute-start | bytes 221192 | tf_op jit(solution)/shard_map/ppermute | solution.py:53
  193.0 6.3 %collective-permute-start.16 = (bf16[1,288,128]{2,1,0:T(8,128)(2,1)S(1)}, bf16[1,288,128]{2,1,0:T(8,128)(2,1)S(1)}, u32[]{:S(2)}, u32[]{:S(2)}) collective-permute-start(bf16[1,288,128]{2,1,0:T(8,128)(2,1)S(1)} %shard_map.303), channel_id=1, source_target_pairs={{0,8},{1,9},{2,10},{3,11},{4,12},{5,13},{6,14},{7,15},{8,0},{9,1},... | collective-permute-start | bytes 221192 | tf_op jit(solution)/shard_map/ppermute | solution.py:53
  199.3 9.8 %collective-permute-start.21 = (bf16[4,288,128]{2,1,0:T(8,128)(2,1)S(1)}, bf16[4,288,128]{2,1,0:T(8,128)(2,1)S(1)}, u32[]{:S(2)}, u32[]{:S(2)}) collective-permute-start(bf16[4,288,128]{2,1,0:T(8,128)(2,1)S(1)} %pad_maximum_fusion.refs_1_), channel_id=1, source_target_pairs={{0,6},{1,7},{2,4},{3,5},{4,2},{5,3},{6,0},{7,1},{8,14},{9,15},{10,... | collective-permute-start | bytes 884744 | tf_op jit(solution)/shard_map/ppermute | solution.py:53
  201.1 10.5 %collective-permute-start.20 = (bf16[4,288,128]{2,1,0:T(8,128)(2,1)S(1)}, bf16[4,288,128]{2,1,0:T(8,128)(2,1)S(1)}, u32[]{:S(2)}, u32[]{:S(2)}) collective-permute-start(bf16[4,288,128]{2,1,0:T(8,128)(2,1)S(1)} %pad_maximum_fusion.refs_1_), channel_id=1, source_target_pairs={{0,4},{1,5},{2,6},{3,7},{4,0},{5,1},{6,2},{7,3},{8,12},{9,13},{10,... | collective-permute-start | bytes 884744 | tf_op jit(solution)/shard_map/ppermute | solution.py:53
  201.9 10.2 %collective-permute-start.19 = (bf16[4,288,128]{2,1,0:T(8,128)(2,1)S(1)}, bf16[4,288,128]{2,1,0:T(8,128)(2,1)S(1)}, u32[]{:S(2)}, u32[]{:S(2)}) collective-permute-start(bf16[4,288,128]{2,1,0:T(8,128)(2,1)S(1)} %pad_maximum_fusion.refs_1_), channel_id=1, source_target_pairs={{0,2},{1,3},{2,0},{3,1},{4,6},{5,7},{6,4},{7,5},{8,10},{9,11},{10,... | collective-permute-start | bytes 884744 | tf_op jit(solution)/shard_map/ppermute | solution.py:53
  202.9 9.3 %collective-permute-start.22 = (bf16[4,288,128]{2,1,0:T(8,128)(2,1)S(1)}, bf16[4,288,128]{2,1,0:T(8,128)(2,1)S(1)}, u32[]{:S(2)}, u32[]{:S(2)}) collective-permute-start(bf16[4,288,128]{2,1,0:T(8,128)(2,1)S(1)} %pad_maximum_fusion.refs_1_), channel_id=1, source_target_pairs={{0,1},{1,0},{2,3},{3,2},{4,5},{5,4},{6,7},{7,6},{8,9},{9,8},{10,11... | collective-permute-start | bytes 884744 | tf_op jit(solution)/shard_map/ppermute | solution.py:38
  209.1 3.0 %collective-permute-start.25 = (bf16[4,288,128]{2,1,0:T(8,128)(2,1)S(1)}, bf16[4,288,128]{2,1,0:T(8,128)(2,1)S(1)}, u32[]{:S(2)}, u32[]{:S(2)}) collective-permute-start(bf16[4,288,128]{2,1,0:T(8,128)(2,1)S(1)} %collective-permute-done.21.refs_4_), channel_id=1, source_target_pairs={{0,1},{1,0},{2,3},{3,2},{4,5},{5,4},{6,7},{7,6},{8,9},{9,8},{10,11... | collective-permute-start | bytes 884744 | tf_op jit(solution)/shard_map/ppermute | solution.py:38
  211.6 1.6 collective-permute-start.24
  212.1 1.6 collective-permute-start.23
  (1 other events, 1.0 us)

commit v7 on v6

--- a/solution.py
+++ b/solution.py
@@ -62,15 +62,17 @@
     return order
 
 
-def scatter_chips(meta, blocks, rows, large, after):
+def scatter_chips(meta, blocks, rows, large, extra, after):
     order = list(reversed(stages()))
     for k, steps in enumerate(order):
-        count = 1 if k + 1 == len(order) else len(order[k + 1])
-        outs = [((blocks[0].shape[0] // count, rows, LANES), BF16)] * count
+        last = k + 1 == len(order)
+        count = 1 if last else len(order[k + 1])
+        out_rows = rows + extra.shape[0] if last else rows
+        outs = [((blocks[0].shape[0] // count, out_rows, LANES), BF16)] * count
         blocks = call(
             sum_kernel,
             outs,
-            [meta, blocks[0], *partners(blocks, steps)],
+            [meta, blocks[0], *partners(blocks, steps)] + ([extra] if last else []),
             after=() if k else after,
             large=0 if k else large,
             others=[step >> 1 & 1 for step in steps],
@@ -148,6 +150,10 @@
 def clear_from(ref, first):
     if ref.shape[0] > first:
         ref[first:, :] = jnp.zeros((ref.shape[0] - first, LANES), ref.dtype)
+
+
+def own_of_tall(image, slab):
+    return pl.ds(pl.multiple_of(image * (slab + 2 * COLS) + COLS, COLS), slab)
 
 
 def total(block):
@@ -225,9 +231,9 @@
             mask = inside(meta, image, 0, rows)
             part = out[j * slab : (j + 1) * slab] * wide(mask, out.shape[1])
             pre[pl.ds(pl.multiple_of(image * slab, slab), slab), :] = part
-            edge = pl.ds(pl.multiple_of(image * COLS, COLS), COLS)
-            top[edge, :] = part[:COLS]
-            bottom[edge, :] = part[slab - COLS :]
+            edge = pl.ds(pl.multiple_of(image * 2 * COLS, 2 * COLS), 2 * COLS)
+            top[edge, :] = part[: 2 * COLS]
+            bottom[edge, :] = part[slab - 2 * COLS :]
             acc[0] += fold(part)
             acc[1] += fold(part * part)
             acc[2, :, :LANES] += fold(mask)
@@ -242,7 +248,7 @@
 
 
 def split_kernel(
-    meta, got, pre, low, high, gain, shift, w, hid_out, out, top, bottom, pay, stat, acc, hid, sem, *, blocks, rows
+    meta, got, pre, low, high, gain, shift, w, hid_out, out, pay, stat, acc, hid, sem, *, blocks, rows
 ):
     slab = rows * COLS
     sums = jnp.sum(got[...], 0)
@@ -255,9 +261,9 @@
     scale, offset = half_terms(center, inv, gain[...], shift[...])
 
     def prepare(i, carry):
-        edge = pl.ds(pl.multiple_of(i * COLS, COLS), COLS)
+        edge = pl.ds(pl.multiple_of(i * 2 * COLS, 2 * COLS), 2 * COLS)
         own = pl.ds(pl.multiple_of(i * slab, slab), slab)
-        mask = inside(meta, i, -1, rows + 2)
+        mask = inside(meta, i, -2, rows + 4)
         for k in range(2):
             lanes = slice(k * LANES, k * LANES + LANES)
             tall = jnp.concatenate([low[edge, lanes], pre[own, lanes], high[edge, lanes]], axis=0)
@@ -273,6 +279,7 @@
     copy.start()
     acc[...] = jnp.zeros_like(acc)
     group = 4
+    tall = slab + 2 * COLS
 
     def step(g, carry):
         for half in range(2):
@@ -280,8 +287,8 @@
             outs = slice(half * 256, half * 256 + 256)
             lhs = jnp.concatenate(
                 [
-                    hid[dx, pl.ds(g * group, group), dy * COLS : dy * COLS + slab, lanes].reshape(
-                        group * slab, 128
+                    hid[dx, pl.ds(g * group, group), dy * COLS : dy * COLS + tall, lanes].reshape(
+                        group * tall, 128
                     )
                     for dy in range(3)
                     for dx in range(3)
@@ -291,12 +298,10 @@
             value = dot(lhs, w[:, :, half].reshape(9 * 128, 256))
             for j in range(group):
                 image = g * group + j
-                mask = inside(meta, image, 0, rows)
-                part = value[j * slab : (j + 1) * slab] * wide(mask, 256)
-                out[pl.ds(pl.multiple_of(image * slab, slab), slab), outs] = part
-                edge = pl.ds(pl.multiple_of(image * COLS, COLS), COLS)
-                top[edge, outs] = part[:COLS]
-                bottom[edge, outs] = part[slab - COLS :]
+                mask = inside(meta, image, -1, rows + 2)
+                part = value[j * tall : (j + 1) * tall] * wide(mask, 256)
+                out[pl.ds(pl.multiple_of(image * tall, tall), tall), outs] = part
+                part = part[COLS : COLS + slab]
                 acc[0, :, outs] += fold(part)
                 acc[1, :, outs] += fold(part * part)
         return carry
@@ -327,7 +332,7 @@
         summed = [None, None]
         for k in range(4):
             lanes = slice(k * LANES, k * LANES + LANES)
-            silu, _ = silu_of_half(pre[own, lanes] * scale[:, lanes] + offset[:, lanes])
+            silu, _ = silu_of_half(pre[own_of_tall(i, slab), lanes] * scale[:, lanes] + offset[:, lanes])
             value = (silu * mask).astype(BF16)
             hid[own, lanes] = value
             part = fold(value.astype(F32))
@@ -444,7 +449,7 @@
 
 
 def mixture_kernel(
-    meta, got, stat3, pre, grad, gain, w, hid, att, gexp, gmix, top, bottom, glog, gain_out, shift_out, *, blocks, rows
+    meta, got, stat3, pre, grad, gain, w, hid, att, we, gexp, gmix, top, bottom, glog, keep, send, gain_out, shift_out, hidden, *, blocks, rows
 ):
     slab = rows * COLS
     sums = jnp.sum(got[...], 0)
@@ -478,8 +483,8 @@
             own = pl.ds(pl.multiple_of(image * slab, slab), slab)
             edge = pl.ds(pl.multiple_of(image * COLS, COLS), COLS)
             part = value[j * slab : (j + 1) * slab]
-            top[edge, :] = part[:COLS]
-            bottom[edge, :] = part[slab - COLS :]
+            top[edge, :] = part[:COLS].astype(BF16)
+            bottom[edge, :] = part[slab - COLS :].astype(BF16)
             for half in range(2):
                 lanes = slice(half * 256, half * 256 + 256)
                 glog[pl.ds(image, 1), lanes] = total(fold(part * hid[own, lanes].astype(F32)))
@@ -491,10 +496,14 @@
     glog[...] = jnp.concatenate(
         [first * (glog[:, :256] - inner), second * (glog[:, 256:] - inner)], axis=1
     )
-
-
-def logits_kernel(meta, glog, we, pay):
-    pay[0] = dot(glog[...], we[...], ((1,), (1,)), HIGHEST)
+    hidden[...] = dot(glog[...], we[...], ((1,), (1,)), HIGHEST)
+    many = blocks // 2
+    keep[...] = hidden[pl.ds(pl.multiple_of(meta[2] * many, many), many), :]
+    send[...] = hidden[pl.ds(pl.multiple_of((1 - meta[2]) * many, many), many), :]
+
+
+def logits_kernel(meta, keep, got, pay):
+    pay[0] = keep[...] + got[...]
     spread(pay)
 
 
@@ -536,6 +545,9 @@
 
 def sum_kernel(meta, *refs, large, others):
     ins, outs = refs[: len(others)], refs[len(others) :]
+    if len(outs[0].shape) == 2:
+        extra, *outs = outs
+        outs[0][0, ins[0].shape[1] :, :] = extra[...].astype(BF16)
     held = outs[0].shape[0]
 
     def add(pick, first, last):
@@ -561,15 +573,18 @@
 
 def hidden_kernel(
     meta, got, znorm, zall, hsq_gain, stat_sq, pooled, wsq, att, gmix, pre, stat2, gain, shift,
-    dz, gpool, pay, gain_out, shift_out, acc, full, squeeze, *, blocks, rows, parts
+    dz, gpool, squeeze, pay, gain_out, shift_out, acc, full, *, blocks, rows, parts
 ):
     slab = rows * COLS
     bands = got.shape[0] // parts
+    many = blocks // 2
     for b in range(bands):
-        block = got[b * parts]
-        for k in range(1, parts):
-            block = block + got[b * parts + k]
-        full[b * blocks : (b + 1) * blocks, :] = block
+        for core in range(2):
+            block = got[b * parts + core]
+            for k in range(core + 2, parts, 2):
+                block = block + got[b * parts + k]
+            at = b * blocks + core * many
+            full[at : at + many, :] = block
     z = zall[...]
     part = jax.nn.sigmoid(z)
     grad_z = full[...] * (part * (1.0 + z * (1.0 - part)))
@@ -602,7 +617,7 @@
             lanes = slice(k * LANES, k * LANES + LANES)
             mid = slice(k % 2 * LANES, k % 2 * LANES + LANES)
             mixed = gmix[own, mid].astype(F32)
-            values = pre[own, lanes]
+            values = pre[own_of_tall(i, slab), lanes]
             _, slope = silu_of_half(values * scale[:, lanes] + offset[:, lanes])
             hidden = (mixed * weights[:, lanes] + pool[:, mid]).astype(BF16).astype(F32)
             back = hidden * half_mask * slope
@@ -613,16 +628,12 @@
 
     lax.fori_loop(0, blocks, step, 0)
     put_sums(pay, 4, acc, center, inv)
-    pay[0, 8:, :] = jnp.zeros((pay.shape[1] - 8, LANES), F32)
     spread(pay)
-    share = pay.shape[1] - 8
-    for n in range(pay.shape[0]):
-        pay[n, 8:, :] = squeeze[n * share : (n + 1) * share, :]
 
 
 def conv_kernel(
-    meta, got, stat2, gain2, shift2, dz, pre2, low2, high2, lowm, highm, att, gpool, w, pre, stat,
-    gain, shift, glog, hid_in, out_hbm, keep_hbm, send_hbm, pay, gain_out, shift_out, tall, acc,
+    meta, got, stat2, gain2, shift2, dz, pre2, lowm, highm, att, gpool, w, pre, stat,
+    gain, shift, glog, squeeze, hid_in, out_hbm, keep_hbm, send_hbm, pay, gain_out, shift_out, tall, acc,
     hid, out, keep, send, sems, *, blocks, rows
 ):
     slab = rows * COLS
@@ -638,6 +649,7 @@
     def prepare(i, carry):
         own = pl.ds(pl.multiple_of(i * slab, slab), slab)
         edge = pl.ds(pl.multiple_of(i * COLS, COLS), COLS)
+        whole_image = pl.ds(pl.multiple_of(i * (slab + 2 * COLS), COLS), slab + 2 * COLS)
         mask = inside(meta, i, -1, rows + 2)
         weights = att[pl.ds(i, 1), :]
         pool = gpool[pl.ds(i, 1), :]
@@ -646,16 +658,20 @@
             mid = slice(k % 2 * LANES, k % 2 * LANES + LANES)
 
             def edge_grad(values, mixed, keep):
-                _, slope = silu_of_half(values[edge, lanes] * scale2[:, lanes] + offset2[:, lanes])
-                hidden = mixed[edge, mid] * weights[:, lanes] + pool[:, mid]
+                _, slope = silu_of_half(values * scale2[:, lanes] + offset2[:, lanes])
+                hidden = mixed[edge, mid].astype(F32) * weights[:, lanes] + pool[:, mid]
                 return hidden.astype(BF16).astype(F32) * (0.5 * keep) * slope
 
             keep_low, keep_high = mask[:COLS], mask[slab + COLS :]
+            values = pre2[whole_image, lanes]
             grads = jnp.concatenate(
-                [edge_grad(low2, lowm, keep_low), dz[own, lanes], edge_grad(high2, highm, keep_high)],
+                [
+                    edge_grad(values[:COLS], lowm, keep_low),
+                    dz[own, lanes],
+                    edge_grad(values[slab + COLS :], highm, keep_high),
+                ],
                 axis=0,
             )
-            values = jnp.concatenate([low2[edge, lanes], pre2[own, lanes], high2[edge, lanes]], axis=0)
             back = mask * (a[:, lanes] * grads + b[:, lanes] + d[:, lanes] * values)
             left, middle, right = shifted(back)
             tall[0, i, :, lanes] = left
@@ -667,7 +683,7 @@
     fetch.wait()
 
     def weights(dy, carry):
-        rows_at = pl.ds(pl.multiple_of(dy * COLS, COLS), slab)
+        rows_at = pl.ds(pl.multiple_of((dy + 1) * COLS, COLS), slab)
         for ref, core in ((send, 1 - meta[2]), (keep, meta[2])):
             lanes = pl.ds(pl.multiple_of(core * 128, 128), 128)
             wide_lanes = pl.ds(pl.multiple_of(core * 256, 256), 256)
@@ -721,8 +737,11 @@
     stores[-1].start()
     put_sums(pay, 2, acc, center, inv)
     put_row(pay, 4, total(glog[...]))
-    pay[0, 8:, :] = sums[8:]
+    pay[0, 8:, :] = jnp.zeros((pay.shape[1] - 8, LANES), F32)
     spread(pay)
+    share = pay.shape[1] - 8
+    for n in range(pay.shape[0]):
+        pay[n, 8:, :] = squeeze[n * share : (n + 1) * share, :]
     for store in stores:
         store.wait()
 
@@ -738,10 +757,10 @@
     ]
     for fetch in fetches:
         fetch.start()
-    sums = jnp.sum(got[:, :8, :], 0)
+    sums = jnp.sum(got[...], 0)
     share = got.shape[1] - 8
-    for n in range(got.shape[0]):
-        squeeze[n * share : (n + 1) * share, :] = got[n, 8:, :]
+    squeeze[...] = jnp.zeros_like(squeeze)
+    squeeze[:share, :] = sums[8:]
     shift_sum, gain_sum = row_of(sums, 0, 2), row_of(sums, 2, 2)
     shift_out[...] = shift_sum
     gain_out[...] = gain_sum
@@ -788,10 +807,12 @@
     lax.fori_loop(0, blocks // group, step, 0)
 
 
-def total_kernel(meta, *refs, places, large):
+def total_kernel(meta, *refs, places, large, less):
     arrays = len(places)
-    expand, excite, split, reduce, wide_part, narrow_part = refs[2 * arrays :]
-    small = refs[0].shape[1] - 2 * large
+    expand, excite, split, reduce, squeeze, wide_part, narrow_part = refs[2 * arrays :]
+    chips_in_all = wide_part.shape[1] // large
+    share = squeeze.shape[0] // (2 * chips_in_all)
+    behind = 2 * large + less
     for parts, core in ((refs[:arrays], meta[2]), (refs[arrays : 2 * arrays], 1 - meta[2])):
         for part, chips in zip(parts, places):
             for k, chip in enumerate(chips):
@@ -800,7 +821,9 @@
                     wide_part[q, pl.ds(pl.multiple_of(at * large, large), large), :] = part[
                         k, q * large : q * large + large, :
                     ]
-                narrow_part[pl.ds(pl.multiple_of(at * small, small), small), :] = part[k, 2 * large :, :]
+                narrow_part[pl.ds(pl.multiple_of(at * less, less), less), :] = part[k, 2 * large : behind, :]
+                device = pl.multiple_of((2 * at + core) * share, share)
+                squeeze[pl.ds(device, share), :] = part[k, behind:, :].astype(F32)[:share]
         for q in range(2):
             lanes = slice(q * 128, q * 128 + 128)
             for tap in range(9):
@@ -867,7 +890,7 @@
 
     pre1, top, bottom, pay = call(
         reduce_kernel,
-        [((pixels, mid), F32), ((edge, mid), F32), ((edge, mid), F32), ((count, 8, LANES), F32)],
+        [((pixels, mid), F32), ((2 * edge, mid), F32), ((2 * edge, mid), F32), ((count, 8, LANES), F32)],
         [meta, x, weight_reduce],
         [((3, 8, mid), F32)],
         flops=small,
@@ -875,24 +898,21 @@
         **sizes,
     )
     low, high = halo(top, bottom)
-    hid1, pre2, top, bottom, pay, stat1 = call(
+    hid1, pre2, pay, stat1 = call(
         split_kernel,
         [
-            ((3, blocks, slab + 2 * cols, mid), BF16, "hbm"),
-            ((pixels, 2 * mid), F32),
-            ((edge, 2 * mid), F32),
-            ((edge, 2 * mid), F32),
+            ((3, blocks, slab + 4 * cols, mid), BF16, "hbm"),
+            ((pixels + 2 * edge, 2 * mid), F32),
             ((count, 8, LANES), F32),
             ((8, mid), F32),
         ],
         [meta, exchange(pay), pre1, low, high, gain1, shift1, weight_split],
-        [((2, 8, 2 * mid), F32), ((3, blocks, slab + 2 * cols, mid), BF16), pltpu.SemaphoreType.DMA],
+        [((2, 8, 2 * mid), F32), ((3, blocks, slab + 4 * cols, mid), BF16), pltpu.SemaphoreType.DMA],
         raw_out=(0,),
         flops=large,
         local="in out",
         **sizes,
     )
-    low2, high2 = halo(top, bottom)
     hid2, pooled, pay, stat2 = call(
         pool_kernel,
         [
@@ -903,7 +923,6 @@
         ],
         [meta, exchange(pay), stat1, pre2, gain2, shift2, weight_squeeze],
         local="in out",
-        after=(low2, high2),
         **sizes,
     )
     mix, pre3, att, hsq, znorm, zall, pay, stat_sq = call(
@@ -947,18 +966,21 @@
         local="in out",
         **sizes,
     )
-    gexp, gmix, top, bottom, glog, gain3_grad, shift3_grad = call(
+    gexp, gmix, top, bottom, glog, keep6, send6, gain3_grad, shift3_grad = call(
         mixture_kernel,
         [
             ((pixels, channels), BF16),
             ((pixels, mid), BF16),
-            ((edge, mid), F32),
-            ((edge, mid), F32),
+            ((edge, mid), BF16),
+            ((edge, mid), BF16),
             ((blocks, 2 * mid), F32),
+            ((blocks // 2, inter), F32),
+            ((blocks // 2, inter), F32),
             ((1, channels), F32),
             ((1, channels), F32),
         ],
-        [meta, exchange(pay), stat3, pre3, grad_res, gain3, weight_expand, hid2, att],
+        [meta, exchange(pay), stat3, pre3, grad_res, gain3, weight_expand, hid2, att, weight_excite],
+        [((blocks, inter), F32)],
         flops=small,
         local="in out",
         **sizes,
@@ -973,17 +995,18 @@
     )
     (pay,) = call(
         logits_kernel,
-        [((count, blocks, inter), F32)],
-        [meta, glog, weight_excite],
+        [((count, blocks // 2, inter), F32)],
+        [meta, keep6, swap(send6, 1)],
         after=(lowm, highm, send3),
         local="in out",
     )
-    dz2, gpool, pay, gain_sq_grad, shift_sq_grad = call(
+    dz2, gpool, squeeze_part, pay, gain_sq_grad, shift_sq_grad = call(
         hidden_kernel,
         [
             ((pixels, 2 * mid), F32),
             ((blocks, mid), F32),
-            ((count, 8 + share, LANES), F32),
+            ((mid, inter), F32),
+            ((count, 8, LANES), F32),
             ((1, inter), F32),
             ((1, inter), F32),
         ],
@@ -1003,7 +1026,7 @@
             gain2,
             shift2,
         ],
-        [((2, 8, 2 * mid), F32), ((images, inter), F32), ((mid, inter), F32)],
+        [((2, 8, 2 * mid), F32), ((images, inter), F32)],
         parts=lax.axis_size("narrow"),
         local="in out",
         **sizes,
@@ -1026,8 +1049,6 @@
             shift2,
             dz2,
             pre2,
-            low2,
-            high2,
             lowm,
             highm,
             att,
@@ -1038,6 +1059,7 @@
             gain1,
             shift1,
             glog,
+            squeeze_part,
             hid1,
         ],
         [
@@ -1049,7 +1071,7 @@
             ((2, 9 * 128, LANES), BF16),
             pltpu.SemaphoreType.DMA((4,)),
         ],
-        raw_in=(19,),
+        raw_in=(18,),
         raw_out=(0, 1, 2),
         flops=2 * large,
         local="in",
@@ -1062,7 +1084,7 @@
         [((chips * large, LANES), F32), ((chips * large, LANES), BF16), TOKEN],
         [meta, keep2, swap(send2, 1), keep3, swap(send3, 1)],
     )
-    small1, keep1, send1, gain1_grad, shift1_grad, bias_grad, squeeze_total = call(
+    small1, keep1, send1, gain1_grad, shift1_grad, bias_grad, squeeze_share = call(
         reduce_back_kernel,
         [
             ((pixels, mid), BF16),
@@ -1071,7 +1093,7 @@
             ((1, mid), F32),
             ((1, mid), F32),
             ((1, 2 * mid), F32),
-            ((mid, inter), F32),
+            ((16, inter), F32),
         ],
         [meta, exchange(pay), stat1, gain1, dz1, pre1, x],
         [
@@ -1101,21 +1123,23 @@
         flops=small,
         **sizes,
     )
-    shared = scatter_chips(meta, blocks, 2 * large + less, large, [token])
+    shared = scatter_chips(meta, blocks, 2 * large + less, large, squeeze_share, [token])
     parts, places = gather_chips(shared)
-    expand_total, excite_total, split_total, reduce_total = call(
+    expand_total, excite_total, split_total, reduce_total, squeeze_total = call(
         total_kernel,
         [
             ((mid, channels), F32),
             ((inter, 2 * mid), F32),
             (weight_split.shape, F32),
             ((channels, mid), F32),
+            ((mid, inter), F32),
         ],
         [meta] + parts + [swap(part, 1) for part in parts],
         [((2, chips * large, LANES), BF16), ((chips * less, LANES), BF16)],
         local="in",
         places=places,
         large=large,
+        less=less,
     )
     flat = lambda v: v.reshape(-1)
     return (

time: 217 us -> 207 us (0.954)
  blocking collectives: 97.6 us -> 88.3 us
    all_to_all x7, blocking collectives: 97.6 us -> 88.3 us  [exchange(): return lax.all_to_all(block, ALL, 0, 0)]
    ppermute x3 -> x2, starting transfers between devices: 6.35 us -> 4.21 us  [halo(): low = lax.ppermute(bottom, 'narrow', [(i, i + 1) for i in range(count - 1)])]
    ppermute x8 -> x9, waiting for transfers between devices: 5.54 us -> 6.05 us  [swap(): return lax.ppermute(block, 'narrow', [(i, i ^ bit) for i in range(count)])]
  transfers between devices with their start and end apart: 27 -> 26, of which waited for: 17 -> 16; matrix products, arithmetic and copies ran while one was open for 0% -> 0% of each run, Pallas kernels for 5% -> 5%
where the time goes in v7:
time: 207 us
  blocking collectives  88.3 us (43%)
  Pallas kernels  49.5 us (24%)
  waiting for transfers between devices  34.3 us (17%)
  starting transfers between devices  28.8 us (14%)
  local copies, waits for them, and re-layouts  4.75 us (2%)
    all_to_all x7, blocking collectives, exchange(): return lax.all_to_all(block, ALL, 0, 0)  88.3 us
    pallas_call x17, Pallas kernels, call(): pl.pallas_call(run, grid=() if local == 'in out' else (1,), out_shape=[pl...  49.5 us
    ppermute x12, waiting for transfers between devices, partners(): lax.ppermute(block, ALL, [(i, i ^ step) for i in range(count)])  23.4 us
    ppermute x12, starting transfers between devices, partners(): lax.ppermute(block, ALL, [(i, i ^ step) for i in range(count)])  16 us
    ppermute x9, waiting for transfers between devices, swap(): return lax.ppermute(block, 'narrow', [(i, i ^ bit) for i in range(count)])  6.05 us
    all_to_all x1, waiting for transfers between devices, exchange(): return lax.all_to_all(block, ALL, 0, 0)  4.88 us
    ppermute x2, starting transfers between devices, halo(): low = lax.ppermute(bottom, 'narrow', [(i, i + 1) for i in range(count - 1)])  4.21 us
  transfers between devices with their start and end apart: 26, of which 16 were waited for; matrix products, arithmetic and copies ran while one was open for 0% of the time, Pallas kernels for 5%

profile of v7, /device:TPU:0, one launch (start us, length us, event | category | flops | bytes accessed | tf_op | source)
XLA Modules:
  0.0 206.8 jit_solution(13000754959121188556)
XLA Ops:
  1.4 1.6 copy-done
  4.1 1.9 shard_map.288
  6.0 2.4 %collective-permute-start = (f32[512,256]{1,0:T(8,128)S(1)}, f32[512,256]{1,0:T(8,128)S(1)}, u32[]{:S(2)}, u32[]{:S(2)}) collective-permute-start(f32[512,256]{1,0:T(8,128)S(1)} %get-tuple-element.90), channel_id=1, source_target_pairs={{0,1},{1,2},{2,3},{4,5},{5,6},{6,7},{8,9},{9,10},{10,11},{12,13},{... | collective-permute-start | bytes 1572872 | tf_op jit(solution)/shard_map/ppermute | solution.py:27
  8.4 1.3 collective-permute-start.1
  9.7 17.2 %all_to_all.40.refs_1_ = f32[32,8,128]{2,1,0:T(8,128)S(1)} all-to-all(f32[32,8,128]{2,1,0:T(8,128)S(1)} %get-tuple-element.88), channel_id=1, replica_groups=mesh['batch'=8,'narrow'=4] {'batch','narrow'}, dimensions={0} | all-to-all | bytes 262144 | tf_op jit(solution)/shard_map/all_to_all | solution.py:33
  27.0 5.1 %shard_map.289 = (bf16[3,16,128,256]{3,2,1,0:T(8,128)(2,1)}, f32[1536,512]{1,0:T(8,128)S(1)}, f32[32,8,128]{2,1,0:T(8,128)S(1)}, f32[8,256]{1,0:T(8,128)S(1)}) custom-call(s32[21]{0:T(128)S(1)} %concatenate.6.refs_0_, f32[32,8,128]{2,1,0:T(8,128)S(1)} %all_to_all.40.refs_1_, f32[1024,256]{1,0:T(8,128)S(1)} %get-tuple-element.89.refs_2_.refs_12_.refs_5_, ...), custom_call_target="tpu_custom_call" | custom-call | flops 1207959552 | bytes 9840724 | tf_op jit(solution)/shard_map/pallas_call | solution.py:205
  32.2 10.1 %all_to_all.41.refs_1_ = f32[32,8,128]{2,1,0:T(8,128)S(1)} all-to-all(f32[32,8,128]{2,1,0:T(8,128)S(1)} %get-tuple-element.92), channel_id=1, replica_groups=mesh['batch'=8,'narrow'=4] {'batch','narrow'}, dimensions={0} | all-to-all | bytes 262144 | tf_op jit(solution)/shard_map/all_to_all | solution.py:33
  42.3 2.0 shard_map.290
  44.3 12.4 %all_to_all.42.refs_1_ = f32[32,16,128]{2,1,0:T(8,128)S(1)} all-to-all(f32[32,16,128]{2,1,0:T(8,128)S(1)} %get-tuple-element.95), channel_id=1, replica_groups=mesh['batch'=8,'narrow'=4] {'batch','narrow'}, dimensions={0} | all-to-all | bytes 524288 | tf_op jit(solution)/shard_map/all_to_all | solution.py:33
  56.8 2.6 %shard_map.291 = (bf16[1024,256]{1,0:T(8,128)(2,1)S(1)}, bf16[1024,1024]{1,0:T(8,128)(2,1)S(1)}, f32[16,512]{1,0:T(8,128)S(1)}, f32[16,128]{1,0:T(8,128)S(1)}, f...) custom-call(s32[21]{0:T(128)S(1)} %concatenate.6.refs_0_, ...), custom_call_target="tpu_custom_call" | custom-call | flops 536870912 | bytes 5160020 | tf_op jit(solution)/shard_map/pallas_call | solution.py:205
  59.4 12.7 %all_to_all.43.refs_1_ = f32[32,16,128]{2,1,0:T(8,128)S(1)} all-to-all(f32[32,16,128]{2,1,0:T(8,128)S(1)} %get-tuple-element.97), channel_id=1, replica_groups=mesh['batch'=8,'narrow'=4] {'batch','narrow'}, dimensions={0} | all-to-all | bytes 524288 | tf_op jit(solution)/shard_map/all_to_all | solution.py:33
  72.1 5.4 %shard_map.292 = (bf16[1024,1024]{1,0:T(8,128)(2,1)}, f32[1024,1024]{1,0:T(8,128)S(1)}, f32[32,16,128]{2,1,0:T(8,128)S(1)}, f32[8,1024]{1,0:T(8,128)S(1)}) custom-call(s32[21]{0:T(128)S(1)} %concatenate.6.refs_0_, f32[32,16,128]{2,1,0:T(8,128)S(1)} %all_to_all.43.refs_1_, f32[8,256]{1,0:T(8,128)S(1)} %get-tuple-element.93.refs_2_.refs_13_, ...), custom_call_target="tpu_custom_call" | custom-call | bytes 13156436 | tf_op jit(solution)/shard_map/pallas_call | solution.py:205
  77.5 12.8 %all_to_all.44.refs_1_ = f32[32,16,128]{2,1,0:T(8,128)S(1)} all-to-all(f32[32,16,128]{2,1,0:T(8,128)S(1)} %get-tuple-element.100), channel_id=1, replica_groups=mesh['batch'=8,'narrow'=4] {'batch','narrow'}, dimensions={0} | all-to-all | bytes 524288 | tf_op jit(solution)/shard_map/all_to_all | solution.py:33
  90.3 3.7 %shard_map.293 = (bf16[1024,1024]{1,0:T(8,128)(2,1)S(1)}, bf16[1024,256]{1,0:T(8,128)(2,1)S(1)}, bf16[256,256]{1,0:T(8,128)(2,1)S(1)}, bf16[256,256]{1,0:T(8,128...) custom-call(s32[21]{0:T(128)S(1)} %concatenate.6.refs_0_, ...), custom_call_target="tpu_custom_call" | custom-call | flops 536870912 | bytes 11391060 | tf_op jit(solution)/shard_map/pallas_call | solution.py:205
  94.0 1.8 collective-permute-start.3
  95.9 1.3 collective-permute-start.4
  97.2 1.2 collective-permute-start.2
  98.3 1.5 shard_map.294
  100.6 13.1 %all_to_all.45.refs_1_ = f32[32,8,128]{2,1,0:T(8,128)S(1)} all-to-all(f32[32,8,128]{2,1,0:T(8,128)S(1)} %shard_map.295), channel_id=1, replica_groups=mesh['batch'=8,'narrow'=4] {'batch','narrow'}, dimensions={0} | all-to-all | bytes 262144 | tf_op jit(solution)/shard_map/all_to_all | solution.py:33
  113.7 3.2 %shard_map.296 = (f32[1024,512]{1,0:T(8,128)S(1)}, f32[16,256]{1,0:T(8,128)S(1)}, f32[256,128]{1,0:T(8,128)S(1)}, f32[32,8,128]{2,1,0:T(8,128)S(1)}, f32[1,128]{1,0:T(1,128)}, /*index=5*/f32[1,128]{1,0:T(1,128)}) custom-call(s32[21]{0:T(128)S(1)} %concatenate.6.refs_0_, f32[32,8,128]{2,1,0:T(8,128)S(1)} %all_to_all.45.refs_1_, ...), custom_call_target="tpu_custom_call" | custom-call | bytes 6514260 | tf_op jit(solution)/shard_map/pallas_call | solution.py:205
  116.9 10.0 %all_to_all.46.refs_1_ = f32[32,8,128]{2,1,0:T(8,128)S(1)} all-to-all(f32[32,8,128]{2,1,0:T(8,128)S(1)} %get-tuple-element.119), channel_id=1, replica_groups=mesh['batch'=8,'narrow'=4] {'batch','narrow'}, dimensions={0} | all-to-all | bytes 262144 | tf_op jit(solution)/shard_map/all_to_all | solution.py:33
  126.9 9.9 %shard_map.297 = (f32[1024,256]{1,0:T(8,128)}, f32[2,1152,128]{2,1,0:T(8,128)}, bf16[2,1152,128]{2,1,0:T(8,128)(2,1)}, f32[32,16,128]{2,1,0:T(8,128)}, f32[1,512]{1,0:T(1,128)}, /*index=5*/f32[1,512]{1,0:T(1,128)}) custom-call(s32[21]{0:T(128)S(1)} %concatenate.6.refs_0_, f32[32,8,128]{2,1,0:T(8,128)S(1)} %all_to_all.46.refs_1_, ...), custom_call_target="tpu_custom_call" | custom-call | flops 2415919104 | bytes 14338132 | tf_op jit(solution)/shard_map/pallas_call | solution.py:205
  137.1 2.6 %all-to-all-start.7 = ((f32[32,16,128]{2,1,0:T(8,128)}), f32[32,16,128]{2,1,0:T(8,128)S(1)}, u32[]{:S(2)}, u32[]{:S(2)}) async-start(f32[32,16,128]{2,1,0:T(8,128)} %get-tuple-element.124), calls=%async_computation.7 | async-start | bytes 524288 | tf_op jit(solution)/shard_map/all_to_all | solution.py:33
  139.8 1.5 collective-permute-done.6.refs_4_
  141.3 1.3 copy-done.10
  142.6 1.2 shard_map.298
  143.8 1.7 collective-permute-start.7
  145.5 4.9 %all-to-all-done.7.refs_1_ = f32[32,16,128]{2,1,0:T(8,128)S(1)} async-done(((f32[32,16,128]{2,1,0:T(8,128)}), f32[32,16,128]{2,1,0:T(8,128)S(1)}, u32[]{:S(2)}, u32[]{:S(2)}) %all-to-all-start.7) | async-done | bytes 262176 | tf_op jit(solution)/shard_map/all_to_all | solution.py:33
  150.3 3.9 %shard_map.299 = (bf16[1024,256]{1,0:T(8,128)(2,1)S(1)}, f32[1024,128]{1,0:T(8,128)S(1)}, bf16[1024,128]{1,0:T(8,128)(2,1)S(1)}, f32[1,256]{1,0:T(1,128)}, f32[1...) custom-call(s32[21]{0:T(128)S(1)} %concatenate.6.refs_0_, f32[32,16,128]{2,1,0:T(8,128)S(1)} %all-to-all-done.7.refs_1_, ...), custom_call_target="tpu_custom_call" | custom-call | flops 536870912 | bytes 5788756 | tf_op jit(solution)/shard_map/pallas_call | solution.py:205
  154.3 1.5 collective-permute-done.8.refs_4_
  155.8 1.4 collective-permute-done.7.refs_2_
  158.1 1.4 collective-permute-start.9
  159.5 1.4 collective-permute-start.10
  161.7 3.3 %shard_map.300 = (bf16[1024,1024]{1,0:T(8,128)(2,1)}, f32[8,128]{1,0:T(8,128)}) custom-call(s32[21]{0:T(128)S(1)} %concatenate.6.refs_0_, bf16[1024,256]{1,0:T(8,128)(2,1)S(1)} %get-tuple-element.130.refs_1_, bf16[1024,256]{1,0:T(8,128)(2,1)S(1)} %copy-done.7, f32[1024,1024]{1,0:T(8,128)S(1)} %copy-done.3), custom_call_target="tpu_custom_call" | custom-call | flops 536870912 | bytes 7344212 | tf_op jit(solution)/shard_map/pallas_call | solution.py:205
  165.0 2.0 collective-permute-done.10.refs_3_
  167.0 2.2 %collective-permute-done.11.refs_4_ = bf16[4,176,128]{2,1,0:T(8,128)(2,1)S(1)} collective-permute-done((bf16[4,176,128]{2,1,0:T(8,128)(2,1)S(1)}, bf16[4,176,128]{2,1,0:T(8,128)(2,1)S(1)}, u32[]{:S(2)}, u32[]{:S(2)}) %collective-permute-start.11) | collective-permute-done | bytes 180256 | tf_op jit(solution)/shard_map/ppermute | solution.py:53
  169.8 1.7 collective-permute-start.12
  171.5 2.2 %collective-permute-start.13 = (bf16[1,288,128]{2,1,0:T(8,128)(2,1)S(1)}, bf16[1,288,128]{2,1,0:T(8,128)(2,1)S(1)}, u32[]{:S(2)}, u32[]{:S(2)}) collective-permute-start(bf16[1,288,128]{2,1,0:T(8,128)(2,1)S(1)} %get-tuple-element.143), channel_id=1, source_target_pairs={{0,16},{1,17},{2,18},{3,19},{4,20},{5,21},{6,22},{7,23},{8,24},{9,... | collective-permute-start | bytes 221192 | tf_op jit(solution)/shard_map/ppermute | solution.py:53
  174.7 3.7 %collective-permute-done.13.refs_3_ = bf16[1,288,128]{2,1,0:T(8,128)(2,1)S(1)} collective-permute-done((bf16[1,288,128]{2,1,0:T(8,128)(2,1)S(1)}, bf16[1,288,128]{2,1,0:T(8,128)(2,1)S(1)}, u32[]{:S(2)}, u32[]{:S(2)}) %collective-permute-start.13) | collective-permute-done | bytes 73760 | tf_op jit(solution)/shard_map/ppermute | solution.py:53
  178.3 1.6 collective-permute-done.14.refs_4_
  180.5 1.5 collective-permute-start.17
  182.0 2.9 %collective-permute-start.15 = (bf16[1,304,128]{2,1,0:T(8,128)(2,1)S(1)}, bf16[1,304,128]{2,1,0:T(8,128)(2,1)S(1)}, u32[]{:S(2)}, u32[]{:S(2)}) collective-permute-start(bf16[1,304,128]{2,1,0:T(8,128)(2,1)S(1)} %shard_map.303), channel_id=1, source_target_pairs={{0,8},{1,9},{2,10},{3,11},{4,12},{5,13},{6,14},{7,15},{8,0},{9,1},... | collective-permute-start | bytes 233480 | tf_op jit(solution)/shard_map/ppermute | solution.py:53
  185.0 1.9 collective-permute-done.17
  186.8 1.6 collective-permute-done.16
  188.5 1.8 collective-permute-start.20
  192.0 6.8 %collective-permute-done.20.refs_4_ = bf16[4,304,128]{2,1,0:T(8,128)(2,1)S(1)} collective-permute-done((bf16[4,304,128]{2,1,0:T(8,128)(2,1)S(1)}, bf16[4,304,128]{2,1,0:T(8,128)(2,1)S(1)}, u32[]{:S(2)}, u32[]{:S(2)}) %collective-permute-start.20) | collective-permute-done | bytes 311328 | tf_op jit(solution)/shard_map/ppermute | solution.py:53
  198.9 2.6 %collective-permute-done.19.refs_3_ = bf16[4,304,128]{2,1,0:T(8,128)(2,1)S(1)} collective-permute-done((bf16[4,304,128]{2,1,0:T(8,128)(2,1)S(1)}, bf16[4,304,128]{2,1,0:T(8,128)(2,1)S(1)}, u32[]{:S(2)}, u32[]{:S(2)}) %collective-permute-start.19) | collective-permute-done | bytes 311328 | tf_op jit(solution)/shard_map/ppermute | solution.py:53
  203.7 3.1 %shard_map.304 = (f32[256,1024]{1,0:T(8,128)}, f32[128,512]{1,0:T(8,128)}, f32[3,3,2,128,256]{4,3,2,1,0:T(8,128)}, f32[1024,256]{1,0:T(8,128)}, f32[256,128]{1,0:T(8,128)}) custom-call(s32[21]{0:T(128)S(1)} %concatenate.6.refs_0_, bf16[4,304,128]{2,1,0:T(8,128)(2,1)S(1)} %pad_maximum_fusion.refs_1_, ...), custom_call_target="tpu_custom_call" | custom-call | bytes 7340116 | tf_op jit(solution)/shard_map/pallas_call | solution.py:205
  (74 shorter events, 10.9 us)
Async XLA Ops:
  0.6 26.3 %copy-start.20 = (f32[256]{0:T(256)S(1)}, f32[256]{0:T(256)}, u32[]{:S(2)}) copy-start(f32[256]{0:T(256)} %param.21) | copy-start | bytes 3076
  0.7 26.3 %copy-start.16 = (f32[256]{0:T(256)S(1)}, f32[256]{0:T(256)}, u32[]{:S(2)}) copy-start(f32[256]{0:T(256)} %param.20) | copy-start | bytes 3076
  1.4 1.6 copy-start
  3.0 1.0 copy-start.6
  4.1 22.9 %copy-start.9 = (bf16[3,3,2,128,256]{4,3,2,1,0:T(8,128)(2,1)S(1)}, bf16[3,3,2,128,256]{4,3,2,1,0:T(8,128)(2,1)}, u32[]{:S(2)}) copy-start(bf16[3,3,2,128,256]{4,3,2,1,0:T(8,128)(2,1)} %refs_11_.1) | copy-start | bytes 3538948
  6.0 120.9 %copy-start.4 = (f32[1024,256]{1,0:T(8,128)}, f32[1024,256]{1,0:T(8,128)S(1)}, u32[]{:S(2)}) copy-start(f32[1024,256]{1,0:T(8,128)S(1)} %get-tuple-element.89.refs_2_.refs_12_.refs_5_) | copy-start | bytes 3145732
  6.0 20.9 %collective-permute-start = (f32[512,256]{1,0:T(8,128)S(1)}, f32[512,256]{1,0:T(8,128)S(1)}, u32[]{:S(2)}, u32[]{:S(2)}) collective-permute-start(f32[512,256]{1,0:T(8,128)S(1)} %get-tuple-element.90), channel_id=1, source_target_pairs={{0,1},{1,2},{2,3},{4,5},{5,6},{6,7},{8,9},{9,10},{10,11},{12,13},{... | collective-permute-start | bytes 1572872 | tf_op jit(solution)/shard_map/ppermute | solution.py:27
  8.4 18.5 %collective-permute-start.1 = (f32[512,256]{1,0:T(8,128)S(1)}, f32[512,256]{1,0:T(8,128)S(1)}, u32[]{:S(2)}, u32[]{:S(2)}) collective-permute-start(f32[512,256]{1,0:T(8,128)S(1)} %get-tuple-element.91), channel_id=1, source_target_pairs={{1,0},{2,1},{3,2},{5,4},{6,5},{7,6},{9,8},{10,9},{11,10},{13,12},{... | collective-permute-start | bytes 1572872 | tf_op jit(solution)/shard_map/ppermute | solution.py:28
  27.0 15.3 %copy-start.12 = (f32[256,128]{1,0:T(8,128)S(1)}, f32[256,128]{1,0:T(8,128)}, u32[]{:S(2)}) copy-start(f32[256,128]{1,0:T(8,128)} %refs_7_.5) | copy-start | bytes 393220
  27.0 15.3 %copy-start.13 = (f32[512]{0:T(512)S(1)}, f32[512]{0:T(512)}, u32[]{:S(2)}) copy-start(f32[512]{0:T(512)} %param.23) | copy-start | bytes 6148
  27.0 15.3 %copy-start.14 = (f32[512]{0:T(512)S(1)}, f32[512]{0:T(512)}, u32[]{:S(2)}) copy-start(f32[512]{0:T(512)} %param.24) | copy-start | bytes 6148
  32.1 24.6 %copy-start.8 = (bf16[256,1024]{1,0:T(8,128)(2,1)S(1)}, bf16[256,1024]{1,0:T(8,128)(2,1)}, u32[]{:S(2)}) copy-start(bf16[256,1024]{1,0:T(8,128)(2,1)} %refs_6_.3) | copy-start | bytes 1572868
  32.2 24.6 %copy-start.11 = (f32[128,512]{1,0:T(8,128)S(1)}, f32[128,512]{1,0:T(8,128)}, u32[]{:S(2)}) copy-start(f32[128,512]{1,0:T(8,128)} %refs_9_.1) | copy-start | bytes 786436
  32.2 24.6 %copy-start.18 = (f32[512]{0:T(512)S(1)}, f32[512]{0:T(512)}, u32[]{:S(2)}) copy-start(f32[512]{0:T(512)} %param.29) | copy-start | bytes 6148
  32.2 24.6 %copy-start.19 = (f32[128]{0:T(128)S(1)}, f32[128]{0:T(128)}, u32[]{:S(2)}) copy-start(f32[128]{0:T(128)} %param.26) | copy-start | bytes 1540
  32.2 24.6 %copy-start.21 = (f32[128]{0:T(128)S(1)}, f32[128]{0:T(128)}, u32[]{:S(2)}) copy-start(f32[128]{0:T(128)} %param.27) | copy-start | bytes 1540
  42.3 29.8 %copy-start.5 = (bf16[16,4,16,1024]{3,2,1,0:T(8,128)(2,1)S(1)}, bf16[16,4,16,1024]{3,2,1,0:T(8,128)(2,1)}, u32[]{:S(2)}) copy-start(bf16[16,4,16,1024]{3,2,1,0:T(8,128)(2,1)} %param.33) | copy-start | bytes 6291460
  44.3 27.8 %copy-start.1 = (bf16[16,4,16,1024]{3,2,1,0:T(8,128)(2,1)S(1)}, bf16[16,4,16,1024]{3,2,1,0:T(8,128)(2,1)}, u32[]{:S(2)}) copy-start(bf16[16,4,16,1024]{3,2,1,0:T(8,128)(2,1)} %param.17) | copy-start | bytes 6291460
  44.3 27.8 %copy-start.15 = (f32[1024]{0:T(1024)S(1)}, f32[1024]{0:T(1024)}, u32[]{:S(2)}) copy-start(f32[1024]{0:T(1024)} %param.31) | copy-start | bytes 12292
  44.3 27.8 %copy-start.17 = (f32[1024]{0:T(1024)S(1)}, f32[1024]{0:T(1024)}, u32[]{:S(2)}) copy-start(f32[1024]{0:T(1024)} %param.32) | copy-start | bytes 12292
  77.5 16.5 %copy-start.2 = (f32[1024,1024]{1,0:T(8,128)}, f32[1024,1024]{1,0:T(8,128)S(1)}, u32[]{:S(2)}) copy-start(f32[1024,1024]{1,0:T(8,128)S(1)} %get-tuple-element.102.refs_4_.refs_3_) | copy-start | bytes 12582916
  94.0 5.8 %collective-permute-start.3 = (bf16[256,256]{1,0:T(8,128)(2,1)S(1)}, bf16[256,256]{1,0:T(8,128)(2,1)S(1)}, u32[]{:S(2)}, u32[]{:S(2)}) collective-permute-start(bf16[256,256]{1,0:T(8,128)(2,1)S(1)} %get-tuple-element.106), channel_id=1, source_target_pairs={{0,1},{1,2},{2,3},{4,5},{5,6},{6,7},{8,9},{9,10},{10,11},{12,13},{... | collective-permute-start | bytes 393224 | tf_op jit(solution)/shard_map/ppermute | solution.py:27
  95.9 4.0 %collective-permute-start.4 = (bf16[256,256]{1,0:T(8,128)(2,1)S(1)}, bf16[256,256]{1,0:T(8,128)(2,1)S(1)}, u32[]{:S(2)}, u32[]{:S(2)}) collective-permute-start(bf16[256,256]{1,0:T(8,128)(2,1)S(1)} %get-tuple-element.107), channel_id=1, source_target_pairs={{1,0},{2,1},{3,2},{5,4},{6,5},{7,6},{9,8},{10,9},{11,10},{13,12},{... | collective-permute-start | bytes 393224 | tf_op jit(solution)/shard_map/ppermute | solution.py:28
  97.2 2.7 %collective-permute-start.2 = (f32[8,128]{1,0:T(8,128)S(1)}, f32[8,128]{1,0:T(8,128)S(1)}, u32[]{:S(2)}, u32[]{:S(2)}) collective-permute-start(f32[8,128]{1,0:T(8,128)S(1)} %get-tuple-element.105), channel_id=1, source_target_pairs={{0,1},{1,0},{2,3},{3,2},{4,5},{5,4},{6,7},{7,6},{8,9},{9,8},{10,11... | collective-permute-start | bytes 12296 | tf_op jit(solution)/shard_map/ppermute | solution.py:38
  136.8 4.6 %collective-permute-start.5 = (bf16[2,1152,128]{2,1,0:T(8,128)(2,1)}, bf16[2,1152,128]{2,1,0:T(8,128)(2,1)S(1)}, u32[]{:S(2)}, u32[]{:S(2)}) collective-permute-start(bf16[2,1152,128]{2,1,0:T(8,128)(2,1)} %get-tuple-element.127), channel_id=1, source_target_pairs={{0,1},{1,0},{2,3},{3,2},{4,5},{5,4},{6,7},{7,6},{8,9},{9,8},{10,11... | collective-permute-start | bytes 1769480 | tf_op jit(solution)/shard_map/ppermute | solution.py:38
  137.1 13.3 %all-to-all-start.7 = ((f32[32,16,128]{2,1,0:T(8,128)}), f32[32,16,128]{2,1,0:T(8,128)S(1)}, u32[]{:S(2)}, u32[]{:S(2)}) async-start(f32[32,16,128]{2,1,0:T(8,128)} %get-tuple-element.124), calls=%async_computation.7 | async-start | bytes 524288 | tf_op jit(solution)/shard_map/all_to_all | solution.py:33
  139.6 1.7 collective-permute-start.6
  141.3 1.3 copy-start.10
  143.8 13.4 %collective-permute-start.7 = (bf16[1792,128]{1,0:T(8,128)(2,1)S(1)}, bf16[1792,128]{1,0:T(8,128)(2,1)S(1)}, u32[]{:S(2)}, u32[]{:S(2)}) collective-permute-start(bf16[1792,128]{1,0:T(8,128)(2,1)S(1)} %get-tuple-element.133), channel_id=1, source_target_pairs={{0,2},{1,3},{2,0},{3,1},{4,6},{5,7},{6,4},{7,5},{8,10},{9,11},{10,... | collective-permute-start | bytes 1376264 | tf_op jit(solution)/shard_map/ppermute | solution.py:38
  150.3 11.3 %copy-start.3 = (f32[1024,1024]{1,0:T(8,128)S(1)}, f32[1024,1024]{1,0:T(8,128)}, u32[]{:S(2)}) copy-start(f32[1024,1024]{1,0:T(8,128)} %copy-done.2) | copy-start | bytes 12582916
  154.2 7.4 %copy-start.7 = (bf16[1024,256]{1,0:T(8,128)(2,1)S(1)}, bf16[1024,256]{1,0:T(8,128)(2,1)}, u32[]{:S(2)}) copy-start(bf16[1024,256]{1,0:T(8,128)(2,1)} %refs_2_.3) | copy-start | bytes 1572868
  154.2 1.6 collective-permute-start.8
  158.1 6.9 %collective-permute-start.9 = (bf16[4,176,128]{2,1,0:T(8,128)(2,1)S(1)}, bf16[4,176,128]{2,1,0:T(8,128)(2,1)S(1)}, u32[]{:S(2)}, u32[]{:S(2)}) collective-permute-start(bf16[4,176,128]{2,1,0:T(8,128)(2,1)S(1)} %get-tuple-element.137), channel_id=1, source_target_pairs={{0,2},{1,3},{2,0},{3,1},{4,6},{5,7},{6,4},{7,5},{8,10},{9,11},{10,... | collective-permute-start | bytes 540680 | tf_op jit(solution)/shard_map/ppermute | solution.py:53
  159.5 7.5 %collective-permute-start.10 = (bf16[4,176,128]{2,1,0:T(8,128)(2,1)S(1)}, bf16[4,176,128]{2,1,0:T(8,128)(2,1)S(1)}, u32[]{:S(2)}, u32[]{:S(2)}) collective-permute-start(bf16[4,176,128]{2,1,0:T(8,128)(2,1)S(1)} %get-tuple-element.138), channel_id=1, source_target_pairs={{0,4},{1,5},{2,6},{3,7},{4,0},{5,1},{6,2},{7,3},{8,12},{9,13},{10,... | collective-permute-start | bytes 540680 | tf_op jit(solution)/shard_map/ppermute | solution.py:53
  161.0 8.2 %collective-permute-start.11 = (bf16[4,176,128]{2,1,0:T(8,128)(2,1)S(1)}, bf16[4,176,128]{2,1,0:T(8,128)(2,1)S(1)}, u32[]{:S(2)}, u32[]{:S(2)}) collective-permute-start(bf16[4,176,128]{2,1,0:T(8,128)(2,1)S(1)} %get-tuple-element.139), channel_id=1, source_target_pairs={{0,6},{1,7},{2,4},{3,5},{4,2},{5,3},{6,0},{7,1},{8,14},{9,15},{10,... | collective-permute-start | bytes 540680 | tf_op jit(solution)/shard_map/ppermute | solution.py:53
  169.8 4.9 %collective-permute-start.12 = (bf16[1,288,128]{2,1,0:T(8,128)(2,1)S(1)}, bf16[1,288,128]{2,1,0:T(8,128)(2,1)S(1)}, u32[]{:S(2)}, u32[]{:S(2)}) collective-permute-start(bf16[1,288,128]{2,1,0:T(8,128)(2,1)S(1)} %get-tuple-element.142), channel_id=1, source_target_pairs={{0,8},{1,9},{2,10},{3,11},{4,12},{5,13},{6,14},{7,15},{8,0},{9,1},... | collective-permute-start | bytes 221192 | tf_op jit(solution)/shard_map/ppermute | solution.py:53
  171.5 6.8 %collective-permute-start.13 = (bf16[1,288,128]{2,1,0:T(8,128)(2,1)S(1)}, bf16[1,288,128]{2,1,0:T(8,128)(2,1)S(1)}, u32[]{:S(2)}, u32[]{:S(2)}) collective-permute-start(bf16[1,288,128]{2,1,0:T(8,128)(2,1)S(1)} %get-tuple-element.143), channel_id=1, source_target_pairs={{0,16},{1,17},{2,18},{3,19},{4,20},{5,21},{6,22},{7,23},{8,24},{9,... | collective-permute-start | bytes 221192 | tf_op jit(solution)/shard_map/ppermute | solution.py:53
  173.7 6.2 %collective-permute-start.14 = (bf16[1,288,128]{2,1,0:T(8,128)(2,1)S(1)}, bf16[1,288,128]{2,1,0:T(8,128)(2,1)S(1)}, u32[]{:S(2)}, u32[]{:S(2)}) collective-permute-start(bf16[1,288,128]{2,1,0:T(8,128)(2,1)S(1)} %get-tuple-element.144), channel_id=1, source_target_pairs={{0,24},{1,25},{2,26},{3,27},{4,28},{5,29},{6,30},{7,31},{8,16},{9,... | collective-permute-start | bytes 221192 | tf_op jit(solution)/shard_map/ppermute | solution.py:53
  180.5 6.3 %collective-permute-start.17 = (bf16[1,304,128]{2,1,0:T(8,128)(2,1)S(1)}, bf16[1,304,128]{2,1,0:T(8,128)(2,1)S(1)}, u32[]{:S(2)}, u32[]{:S(2)}) collective-permute-start(bf16[1,304,128]{2,1,0:T(8,128)(2,1)S(1)} %shard_map.303), channel_id=1, source_target_pairs={{0,24},{1,25},{2,26},{3,27},{4,28},{5,29},{6,30},{7,31},{8,16},{9,... | collective-permute-start | bytes 233480 | tf_op jit(solution)/shard_map/ppermute | solution.py:53
  182.0 6.4 %collective-permute-start.16 = (bf16[1,304,128]{2,1,0:T(8,128)(2,1)S(1)}, bf16[1,304,128]{2,1,0:T(8,128)(2,1)S(1)}, u32[]{:S(2)}, u32[]{:S(2)}) collective-permute-start(bf16[1,304,128]{2,1,0:T(8,128)(2,1)S(1)} %shard_map.303), channel_id=1, source_target_pairs={{0,16},{1,17},{2,18},{3,19},{4,20},{5,21},{6,22},{7,23},{8,24},{9,... | collective-permute-start | bytes 233480 | tf_op jit(solution)/shard_map/ppermute | solution.py:53
  182.0 6.4 %collective-permute-start.15 = (bf16[1,304,128]{2,1,0:T(8,128)(2,1)S(1)}, bf16[1,304,128]{2,1,0:T(8,128)(2,1)S(1)}, u32[]{:S(2)}, u32[]{:S(2)}) collective-permute-start(bf16[1,304,128]{2,1,0:T(8,128)(2,1)S(1)} %shard_map.303), channel_id=1, source_target_pairs={{0,8},{1,9},{2,10},{3,11},{4,12},{5,13},{6,14},{7,15},{8,0},{9,1},... | collective-permute-start | bytes 233480 | tf_op jit(solution)/shard_map/ppermute | solution.py:53
  188.5 10.4 %collective-permute-start.20 = (bf16[4,304,128]{2,1,0:T(8,128)(2,1)S(1)}, bf16[4,304,128]{2,1,0:T(8,128)(2,1)S(1)}, u32[]{:S(2)}, u32[]{:S(2)}) collective-permute-start(bf16[4,304,128]{2,1,0:T(8,128)(2,1)S(1)} %pad_maximum_fusion.refs_1_), channel_id=1, source_target_pairs={{0,6},{1,7},{2,4},{3,5},{4,2},{5,3},{6,0},{7,1},{8,14},{9,15},{10,... | collective-permute-start | bytes 933896 | tf_op jit(solution)/shard_map/ppermute | solution.py:53
  190.2 11.2 %collective-permute-start.19 = (bf16[4,304,128]{2,1,0:T(8,128)(2,1)S(1)}, bf16[4,304,128]{2,1,0:T(8,128)(2,1)S(1)}, u32[]{:S(2)}, u32[]{:S(2)}) collective-permute-start(bf16[4,304,128]{2,1,0:T(8,128)(2,1)S(1)} %pad_maximum_fusion.refs_1_), channel_id=1, source_target_pairs={{0,4},{1,5},{2,6},{3,7},{4,0},{5,1},{6,2},{7,3},{8,12},{9,13},{10,... | collective-permute-start | bytes 933896 | tf_op jit(solution)/shard_map/ppermute | solution.py:53
  191.1 11.0 %collective-permute-start.18 = (bf16[4,304,128]{2,1,0:T(8,128)(2,1)S(1)}, bf16[4,304,128]{2,1,0:T(8,128)(2,1)S(1)}, u32[]{:S(2)}, u32[]{:S(2)}) collective-permute-start(bf16[4,304,128]{2,1,0:T(8,128)(2,1)S(1)} %pad_maximum_fusion.refs_1_), channel_id=1, source_target_pairs={{0,2},{1,3},{2,0},{3,1},{4,6},{5,7},{6,4},{7,5},{8,10},{9,11},{10,... | collective-permute-start | bytes 933896 | tf_op jit(solution)/shard_map/ppermute | solution.py:53
  192.0 10.0 %collective-permute-start.21 = (bf16[4,304,128]{2,1,0:T(8,128)(2,1)S(1)}, bf16[4,304,128]{2,1,0:T(8,128)(2,1)S(1)}, u32[]{:S(2)}, u32[]{:S(2)}) collective-permute-start(bf16[4,304,128]{2,1,0:T(8,128)(2,1)S(1)} %pad_maximum_fusion.refs_1_), channel_id=1, source_target_pairs={{0,1},{1,0},{2,3},{3,2},{4,5},{5,4},{6,7},{7,6},{8,9},{9,8},{10,11... | collective-permute-start | bytes 933896 | tf_op jit(solution)/shard_map/ppermute | solution.py:38
  198.9 3.2 %collective-permute-start.24 = (bf16[4,304,128]{2,1,0:T(8,128)(2,1)S(1)}, bf16[4,304,128]{2,1,0:T(8,128)(2,1)S(1)}, u32[]{:S(2)}, u32[]{:S(2)}) collective-permute-start(bf16[4,304,128]{2,1,0:T(8,128)(2,1)S(1)} %collective-permute-done.20.refs_4_), channel_id=1, source_target_pairs={{0,1},{1,0},{2,3},{3,2},{4,5},{5,4},{6,7},{7,6},{8,9},{9,8},{10,11... | collective-permute-start | bytes 933896 | tf_op jit(solution)/shard_map/ppermute | solution.py:38
  201.5 1.6 collective-permute-start.23
  202.1 1.6 collective-permute-start.22

commit v8 on v7

--- a/solution.py
+++ b/solution.py
@@ -184,7 +184,7 @@
 
 
 def call(
-    kernel, outs, args, scratch=(), megabytes=24, flops=0, after=(), local="", raw_in=(), raw_out=(), **sizes
+    kernel, outs, args, scratch=(), megabytes=24, flops=0, after=(), local="", raw_in=(), raw_out=(), aliases=None, **sizes
 ):
     moved = sum(a.size * a.dtype.itemsize for a in args) + sum(
         functools.reduce(lambda x, y: x * y, o[0]) * jnp.dtype(o[1]).itemsize for o in outs
@@ -212,6 +212,7 @@
         + [spec(k, a.shape, "in" in local, raw_in) for k, a in enumerate(args) if k]
         + [anywhere] * len(after),
         out_specs=[spec(k, o[0], "out" in local, raw_out) for k, o in enumerate(outs)],
+        input_output_aliases=aliases or {},
         scratch_shapes=[pltpu.VMEM(*entry) if isinstance(entry, tuple) else entry for entry in scratch],
         compiler_params=pltpu.CompilerParams(vmem_limit_bytes=megabytes << 20),
         cost_estimate=pl.CostEstimate(flops=flops, bytes_accessed=moved, transcendentals=0),
@@ -239,7 +240,7 @@
             acc[2, :, :LANES] += fold(mask)
         return carry
 
-    lax.fori_loop(0, blocks // group, step, 0)
+    lax.fori_loop(0, blocks // group, step, 0, unroll=True)
     put_row(pay, 0, total(acc[0]))
     put_row(pay, 2, total(acc[1]))
     put_row(pay, 4, total(acc[2, :, :LANES]))
@@ -274,7 +275,7 @@
             hid[2, i, :, lanes] = right
         return carry
 
-    lax.fori_loop(0, blocks, prepare, 0)
+    lax.fori_loop(0, blocks, prepare, 0, unroll=4)
     copy = pltpu.make_async_copy(hid, hid_out, sem)
     copy.start()
     acc[...] = jnp.zeros_like(acc)
@@ -306,7 +307,7 @@
                 acc[1, :, outs] += fold(part * part)
         return carry
 
-    lax.fori_loop(0, blocks // group, step, 0)
+    lax.fori_loop(0, blocks // group, step, 0, unroll=2)
     put_row(pay, 0, total(acc[0]))
     put_row(pay, 4, total(acc[1]))
     spread(pay)
@@ -340,7 +341,7 @@
         pooled[pl.ds(i, 1), :] = total(jnp.concatenate(summed, axis=1)) / area_of(meta, i)
         return carry
 
-    lax.fori_loop(0, blocks, step, 0)
+    lax.fori_loop(0, blocks, step, 0, unroll=4)
     pay[0] = dot(pooled[...], w[...], precision=HIGHEST)
     spread(pay)
 
@@ -399,7 +400,7 @@
             acc[1, :, lanes] += fold(value * value)
         return carry
 
-    lax.fori_loop(0, blocks // group, step, 0)
+    lax.fori_loop(0, blocks // group, step, 0, unroll=True)
     put_row(pay, 0, total(acc[0]))
     put_row(pay, 8, total(acc[1]))
     spread(pay)
@@ -490,7 +491,7 @@
                 glog[pl.ds(image, 1), lanes] = total(fold(part * hid[own, lanes].astype(F32)))
         return carry
 
-    lax.fori_loop(0, blocks // group, step, 0)
+    lax.fori_loop(0, blocks // group, step, 0, unroll=2)
     first, second = att[:, :256], att[:, 256:]
     inner = first * glog[:, :256] + second * glog[:, 256:]
     glog[...] = jnp.concatenate(
@@ -626,19 +627,17 @@
             acc[1, :, lanes] += fold(back * values)
         return carry
 
-    lax.fori_loop(0, blocks, step, 0)
+    lax.fori_loop(0, blocks, step, 0, unroll=4)
     put_sums(pay, 4, acc, center, inv)
     spread(pay)
 
 
 def conv_kernel(
     meta, got, stat2, gain2, shift2, dz, pre2, lowm, highm, att, gpool, w, pre, stat,
-    gain, shift, glog, squeeze, hid_in, out_hbm, keep_hbm, send_hbm, pay, gain_out, shift_out, tall, acc,
-    hid, out, keep, send, sems, *, blocks, rows
+    gain, shift, glog, squeeze, hid, out_hbm, keep_hbm, send_hbm, pay_hbm, gain_out, shift_out, tall, acc,
+    out, keep, send, pay, sems, *, blocks, rows
 ):
     slab = rows * COLS
-    fetch = pltpu.make_async_copy(hid_in, hid, sems.at[0])
-    fetch.start()
     sums = jnp.sum(got[...], 0)
     shift_sum, gain_sum = row_of(sums, 0, 4), row_of(sums, 4, 4)
     shift_out[...] = shift_sum
@@ -679,8 +678,7 @@
             tall[2, i, :, lanes] = right
         return carry
 
-    lax.fori_loop(0, blocks, prepare, 0)
-    fetch.wait()
+    lax.fori_loop(0, blocks, prepare, 0, unroll=4)
 
     def weights(dy, carry):
         rows_at = pl.ds(pl.multiple_of((dy + 1) * COLS, COLS), slab)
@@ -709,18 +707,26 @@
     scale, offset = half_terms(center, inv, gain[...], shift[...])
     group = 4
 
+    def store_group(g):
+        many = pl.ds(pl.multiple_of(g * group * slab, group * slab), group * slab)
+        return pltpu.make_async_copy(out.at[many], out_hbm.at[many], sems.at[3 + g])
+
     def step(g, carry):
         for half in range(2):
             lanes = slice(half * 256, half * 256 + 256)
             outs = slice(half * 128, half * 128 + 128)
-            value = None
-            for dy in range(3):
-                for dx in range(3):
-                    lhs = tall[
+            taps = [(dy, dx) for dy in range(3) for dx in range(3)]
+            lhs = jnp.concatenate(
+                [
+                    tall[
                         2 - dx, pl.ds(g * group, group), (2 - dy) * COLS : (2 - dy) * COLS + slab, lanes
                     ].reshape(group * slab, 256)
-                    part = dot(lhs, w[dy, dx, half], ((1,), (1,)))
-                    value = part if value is None else value + part
+                    for dy, dx in taps
+                ],
+                axis=1,
+            )
+            rhs = jnp.concatenate([w[dy, dx, half] for dy, dx in taps], axis=1)
+            value = dot(lhs, rhs, ((1,), (1,)))
             for j in range(group):
                 image = g * group + j
                 own = pl.ds(pl.multiple_of(image * slab, slab), slab)
@@ -730,11 +736,10 @@
                 out[own, outs] = back
                 acc[0, :, outs] += fold(back)
                 acc[1, :, outs] += fold(back * values)
-        return carry
-
-    lax.fori_loop(0, blocks // group, step, 0)
-    stores.append(pltpu.make_async_copy(out, out_hbm, sems.at[3]))
-    stores[-1].start()
+        store_group(g).start()
+        return carry
+
+    lax.fori_loop(0, blocks // group, step, 0, unroll=2)
     put_sums(pay, 2, acc, center, inv)
     put_row(pay, 4, total(glog[...]))
     pay[0, 8:, :] = jnp.zeros((pay.shape[1] - 8, LANES), F32)
@@ -742,6 +747,9 @@
     share = pay.shape[1] - 8
     for n in range(pay.shape[0]):
         pay[n, 8:, :] = squeeze[n * share : (n + 1) * share, :]
+    stores.append(pltpu.make_async_copy(pay, pay_hbm, sems.at[0]))
+    stores[-1].start()
+    stores += [store_group(g) for g in range(blocks // group)]
     for store in stores:
         store.wait()
 
@@ -807,36 +815,48 @@
     lax.fori_loop(0, blocks // group, step, 0)
 
 
-def total_kernel(meta, *refs, places, large, less):
+def total_kernel(meta, *refs, places, large, less, other):
     arrays = len(places)
-    expand, excite, split, reduce, squeeze, wide_part, narrow_part = refs[2 * arrays :]
-    chips_in_all = wide_part.shape[1] // large
-    share = squeeze.shape[0] // (2 * chips_in_all)
+    *outs, wide_part, narrow_part, expand, excite, split, reduce, squeeze, sems = refs[arrays + 5 * other :]
+    share = squeeze.shape[1]
     behind = 2 * large + less
-    for parts, core in ((refs[:arrays], meta[2]), (refs[arrays : 2 * arrays], 1 - meta[2])):
-        for part, chips in zip(parts, places):
-            for k, chip in enumerate(chips):
-                at = meta[4] ^ chip
-                for q in range(2):
-                    wide_part[q, pl.ds(pl.multiple_of(at * large, large), large), :] = part[
-                        k, q * large : q * large + large, :
-                    ]
-                narrow_part[pl.ds(pl.multiple_of(at * less, less), less), :] = part[k, 2 * large : behind, :]
-                device = pl.multiple_of((2 * at + core) * share, share)
-                squeeze[pl.ds(device, share), :] = part[k, behind:, :].astype(F32)[:share]
-        for q in range(2):
-            lanes = slice(q * 128, q * 128 + 128)
-            for tap in range(9):
-                split[tap // 3, tap % 3, core, :, lanes] = wide_part[q, tap * 128 : tap * 128 + 128].astype(F32)
-            for k in range(2):
-                first = 1152 + k * 256
-                out = pl.ds(pl.multiple_of(core * 512 + (k * 256 + q * 128), 128), 128)
-                expand[:, out] = wide_part[q, first : first + 256].astype(F32)
-            out = pl.ds(pl.multiple_of(core * 256 + q * 128, 128), 128)
-            excite[:, out] = wide_part[q, 1664:1792].astype(F32)
-        own_rows = pl.ds(pl.multiple_of(core * 512, 512), 512)
-        for q in range(2):
-            reduce[own_rows, q * 128 : q * 128 + 128] = narrow_part[q * 512 : q * 512 + 512].astype(F32)
+    core = meta[2] ^ other
+    for part, chips in zip(refs[:arrays], places):
+        for k, chip in enumerate(chips):
+            at = meta[4] ^ chip
+            for q in range(2):
+                wide_part[q, pl.ds(pl.multiple_of(at * large, large), large), :] = part[
+                    k, q * large : q * large + large, :
+                ]
+            narrow_part[pl.ds(pl.multiple_of(at * less, less), less), :] = part[k, 2 * large : behind, :]
+            squeeze[at] = part[k, behind:, :].astype(F32)[:share]
+    expand_out, excite_out, split_out, reduce_out, squeeze_out = outs
+    copies = []
+
+    def send(source, target):
+        copies.append(pltpu.make_async_copy(source, target, sems.at[len(copies)]))
+        copies[-1].start()
+
+    send(squeeze, squeeze_out.at[:, core])
+    for q in range(2):
+        reduce[:, q * 128 : q * 128 + 128] = narrow_part[q * 512 : q * 512 + 512].astype(F32)
+    send(reduce, reduce_out.at[pl.ds(pl.multiple_of(core * 512, 512), 512)])
+    for dy in range(3):
+        for dx in range(3):
+            first = (3 * dy + dx) * 128
+            for q in range(2):
+                split[dy, dx, :, q * 128 : q * 128 + 128] = wide_part[q, first : first + 128].astype(F32)
+        send(split.at[dy], split_out.at[dy, :, core])
+    for q in range(2):
+        for k in range(2):
+            first = 1152 + k * 256
+            at = k * 256 + q * 128
+            expand[:, at : at + 128] = wide_part[q, first : first + 256].astype(F32)
+        excite[:, q * 128 : q * 128 + 128] = wide_part[q, 1664:1792].astype(F32)
+    send(expand, expand_out.at[:, pl.ds(pl.multiple_of(core * 512, 512), 512)])
+    send(excite, excite_out.at[:, pl.ds(pl.multiple_of(core * 256, 256), 256)])
+    for copy in copies:
+        copy.wait()
 
 
 def body(
@@ -1065,14 +1085,13 @@
         [
             ((3, blocks, slab + 2 * cols, 2 * mid), BF16),
             ((2, 8, mid), F32),
-            (hid1.shape, BF16),
             ((pixels, mid), F32),
             ((2, 9 * 128, LANES), F32),
             ((2, 9 * 128, LANES), BF16),
-            pltpu.SemaphoreType.DMA((4,)),
-        ],
-        raw_in=(18,),
-        raw_out=(0, 1, 2),
+            ((count, 8 + share, LANES), F32),
+            pltpu.SemaphoreType.DMA((3 + blocks // 4,)),
+        ],
+        raw_out=(0, 1, 2, 3),
         flops=2 * large,
         local="in",
         **sizes,
@@ -1105,7 +1124,7 @@
         raw_in=(4, 5, 6),
         flops=small,
         after=(token,),
-        local="in",
+        local="in out",
         **sizes,
     )
     first = len(stages()[-1])
@@ -1125,22 +1144,41 @@
     )
     shared = scatter_chips(meta, blocks, 2 * large + less, large, squeeze_share, [token])
     parts, places = gather_chips(shared)
-    expand_total, excite_total, split_total, reduce_total, squeeze_total = call(
-        total_kernel,
-        [
-            ((mid, channels), F32),
-            ((inter, 2 * mid), F32),
-            (weight_split.shape, F32),
-            ((channels, mid), F32),
-            ((mid, inter), F32),
-        ],
-        [meta] + parts + [swap(part, 1) for part in parts],
-        [((2, chips * large, LANES), BF16), ((chips * less, LANES), BF16)],
-        local="in",
-        places=places,
-        large=large,
-        less=less,
-    )
+    swapped = [swap(part, 1) for part in parts]
+    totals = ()
+    for other, half in enumerate((parts, swapped)):
+        args = [meta, *half, *totals]
+        totals = call(
+            total_kernel,
+            [
+                ((mid, channels), F32, "hbm"),
+                ((inter, 2 * mid), F32, "hbm"),
+                (weight_split.shape, F32, "hbm"),
+                ((channels, mid), F32, "hbm"),
+                ((chips, 2, share, inter), F32, "hbm"),
+            ],
+            args,
+            [
+                ((2, chips * large, LANES), BF16),
+                ((chips * less, LANES), BF16),
+                ((mid, channels // 2), F32),
+                ((inter, mid), F32),
+                ((3, 3, 128, mid), F32),
+                ((channels // 2, mid), F32),
+                ((chips, share, inter), F32),
+                pltpu.SemaphoreType.DMA((7,)),
+            ],
+            local="in",
+            raw_in=range(1 + len(half), len(args)),
+            raw_out=range(5),
+            aliases={1 + len(half) + k: k for k in range(len(totals))},
+            places=places,
+            large=large,
+            less=less,
+            other=other,
+        )
+    expand_total, excite_total, split_total, reduce_total, squeeze_total = totals
+    squeeze_total = squeeze_total.reshape(mid, inter)
     flat = lambda v: v.reshape(-1)
     return (
         out.reshape(inputs.shape),

time: 207 us -> 204 us (0.986)
    pallas_call x17 -> x18, Pallas kernels: 49.5 us -> 48 us  [call(): pl.pallas_call(run, grid=() if local == 'in out' else (1,), out_shape=[pl...]
  transfers between devices with their start and end apart: 26 -> 26, of which waited for: 16 -> 14; matrix products, arithmetic and copies ran while one was open for 0% -> 0% of each run, Pallas kernels for 5% -> 6%
where the time goes in v8:
time: 204 us
  blocking collectives  88.3 us (43%)
  Pallas kernels  48 us (24%)
  waiting for transfers between devices  32.8 us (16%)
  starting transfers between devices  28.7 us (14%)
  local copies, waits for them, and re-layouts  4.75 us (2%)
    all_to_all x7, blocking collectives, exchange(): return lax.all_to_all(block, ALL, 0, 0)  88.3 us
    pallas_call x18, Pallas kernels, call(): pl.pallas_call(run, grid=() if local == 'in out' else (1,), out_shape=[pl...  48 us
    ppermute x12, waiting for transfers between devices, partners(): lax.ppermute(block, ALL, [(i, i ^ step) for i in range(count)])  23.3 us
    ppermute x12, starting transfers between devices, partners(): lax.ppermute(block, ALL, [(i, i ^ step) for i in range(count)])  16 us
    all_to_all x1, waiting for transfers between devices, exchange(): return lax.all_to_all(block, ALL, 0, 0)  4.86 us
    ppermute x9, waiting for transfers between devices, swap(): return lax.ppermute(block, 'narrow', [(i, i ^ bit) for i in range(count)])  4.65 us
    ppermute x2, starting transfers between devices, halo(): low = lax.ppermute(bottom, 'narrow', [(i, i + 1) for i in range(count - 1)])  4.2 us
  transfers between devices with their start and end apart: 26, of which 14 were waited for; matrix products, arithmetic and copies ran while one was open for 0% of the time, Pallas kernels for 6%

profile of v8, /device:TPU:0, one launch (start us, length us, event | category | flops | bytes accessed | tf_op | source)
XLA Modules:
  0.0 203.9 jit_solution(7232027600138963328)
XLA Ops:
  1.4 1.6 copy-done
  4.1 1.5 shard_map.288
  5.6 2.4 %collective-permute-start = (f32[512,256]{1,0:T(8,128)S(1)}, f32[512,256]{1,0:T(8,128)S(1)}, u32[]{:S(2)}, u32[]{:S(2)}) collective-permute-start(f32[512,256]{1,0:T(8,128)S(1)} %get-tuple-element.95), channel_id=1, source_target_pairs={{0,1},{1,2},{2,3},{4,5},{5,6},{6,7},{8,9},{9,10},{10,11},{12,13},{... | collective-permute-start | bytes 1572872 | tf_op jit(solution)/shard_map/ppermute | solution.py:27
  8.0 1.3 collective-permute-start.1
  9.3 17.2 %all_to_all.40.refs_1_ = f32[32,8,128]{2,1,0:T(8,128)S(1)} all-to-all(f32[32,8,128]{2,1,0:T(8,128)S(1)} %get-tuple-element.93), channel_id=1, replica_groups=mesh['batch'=8,'narrow'=4] {'batch','narrow'}, dimensions={0} | all-to-all | bytes 262144 | tf_op jit(solution)/shard_map/all_to_all | solution.py:33
  26.5 4.6 %shard_map.289 = (bf16[3,16,128,256]{3,2,1,0:T(8,128)(2,1)}, f32[1536,512]{1,0:T(8,128)S(1)}, f32[32,8,128]{2,1,0:T(8,128)S(1)}, f32[8,256]{1,0:T(8,128)S(1)}) custom-call(s32[21]{0:T(128)S(1)} %concatenate.6.refs_0_, f32[32,8,128]{2,1,0:T(8,128)S(1)} %all_to_all.40.refs_1_, f32[1024,256]{1,0:T(8,128)S(1)} %get-tuple-element.94.refs_2_.refs_12_.refs_5_, ...), custom_call_target="tpu_custom_call" | custom-call | flops 1207959552 | bytes 9840724 | tf_op jit(solution)/shard_map/pallas_call | solution.py:205
  31.2 10.1 %all_to_all.41.refs_1_ = f32[32,8,128]{2,1,0:T(8,128)S(1)} all-to-all(f32[32,8,128]{2,1,0:T(8,128)S(1)} %get-tuple-element.97), channel_id=1, replica_groups=mesh['batch'=8,'narrow'=4] {'batch','narrow'}, dimensions={0} | all-to-all | bytes 262144 | tf_op jit(solution)/shard_map/all_to_all | solution.py:33
  41.3 1.8 shard_map.290
  43.1 12.4 %all_to_all.42.refs_1_ = f32[32,16,128]{2,1,0:T(8,128)S(1)} all-to-all(f32[32,16,128]{2,1,0:T(8,128)S(1)} %get-tuple-element.100), channel_id=1, replica_groups=mesh['batch'=8,'narrow'=4] {'batch','narrow'}, dimensions={0} | all-to-all | bytes 524288 | tf_op jit(solution)/shard_map/all_to_all | solution.py:33
  55.6 2.1 %shard_map.291 = (bf16[1024,256]{1,0:T(8,128)(2,1)S(1)}, bf16[1024,1024]{1,0:T(8,128)(2,1)S(1)}, f32[16,512]{1,0:T(8,128)S(1)}, f32[16,128]{1,0:T(8,128)S(1)}, f...) custom-call(s32[21]{0:T(128)S(1)} %concatenate.6.refs_0_, ...), custom_call_target="tpu_custom_call" | custom-call | flops 536870912 | bytes 5160020 | tf_op jit(solution)/shard_map/pallas_call | solution.py:205
  57.7 12.7 %all_to_all.43.refs_1_ = f32[32,16,128]{2,1,0:T(8,128)S(1)} all-to-all(f32[32,16,128]{2,1,0:T(8,128)S(1)} %get-tuple-element.102), channel_id=1, replica_groups=mesh['batch'=8,'narrow'=4] {'batch','narrow'}, dimensions={0} | all-to-all | bytes 524288 | tf_op jit(solution)/shard_map/all_to_all | solution.py:33
  70.5 5.4 %shard_map.292 = (bf16[1024,1024]{1,0:T(8,128)(2,1)}, f32[1024,1024]{1,0:T(8,128)S(1)}, f32[32,16,128]{2,1,0:T(8,128)S(1)}, f32[8,1024]{1,0:T(8,128)S(1)}) custom-call(s32[21]{0:T(128)S(1)} %concatenate.6.refs_0_, f32[32,16,128]{2,1,0:T(8,128)S(1)} %all_to_all.43.refs_1_, f32[8,256]{1,0:T(8,128)S(1)} %get-tuple-element.98.refs_2_.refs_13_, ...), custom_call_target="tpu_custom_call" | custom-call | bytes 13156436 | tf_op jit(solution)/shard_map/pallas_call | solution.py:205
  75.9 12.8 %all_to_all.44.refs_1_ = f32[32,16,128]{2,1,0:T(8,128)S(1)} all-to-all(f32[32,16,128]{2,1,0:T(8,128)S(1)} %get-tuple-element.105), channel_id=1, replica_groups=mesh['batch'=8,'narrow'=4] {'batch','narrow'}, dimensions={0} | all-to-all | bytes 524288 | tf_op jit(solution)/shard_map/all_to_all | solution.py:33
  88.7 3.6 %shard_map.293 = (bf16[1024,1024]{1,0:T(8,128)(2,1)S(1)}, bf16[1024,256]{1,0:T(8,128)(2,1)S(1)}, bf16[256,256]{1,0:T(8,128)(2,1)S(1)}, bf16[256,256]{1,0:T(8,128...) custom-call(s32[21]{0:T(128)S(1)} %concatenate.6.refs_0_, ...), custom_call_target="tpu_custom_call" | custom-call | flops 536870912 | bytes 11391060 | tf_op jit(solution)/shard_map/pallas_call | solution.py:205
  92.3 1.8 collective-permute-start.3
  94.1 1.3 collective-permute-start.4
  96.6 1.5 shard_map.294
  98.8 13.1 %all_to_all.45.refs_1_ = f32[32,8,128]{2,1,0:T(8,128)S(1)} all-to-all(f32[32,8,128]{2,1,0:T(8,128)S(1)} %shard_map.295), channel_id=1, replica_groups=mesh['batch'=8,'narrow'=4] {'batch','narrow'}, dimensions={0} | all-to-all | bytes 262144 | tf_op jit(solution)/shard_map/all_to_all | solution.py:33
  111.9 3.1 %shard_map.296 = (f32[1024,512]{1,0:T(8,128)S(1)}, f32[16,256]{1,0:T(8,128)S(1)}, f32[256,128]{1,0:T(8,128)S(1)}, f32[32,8,128]{2,1,0:T(8,128)S(1)}, f32[1,128]{1,0:T(1,128)}, /*index=5*/f32[1,128]{1,0:T(1,128)}) custom-call(s32[21]{0:T(128)S(1)} %concatenate.6.refs_0_, f32[32,8,128]{2,1,0:T(8,128)S(1)} %all_to_all.45.refs_1_, ...), custom_call_target="tpu_custom_call" | custom-call | bytes 6514260 | tf_op jit(solution)/shard_map/pallas_call | solution.py:205
  115.0 10.0 %all_to_all.46.refs_1_ = f32[32,8,128]{2,1,0:T(8,128)S(1)} all-to-all(f32[32,8,128]{2,1,0:T(8,128)S(1)} %get-tuple-element.124), channel_id=1, replica_groups=mesh['batch'=8,'narrow'=4] {'batch','narrow'}, dimensions={0} | all-to-all | bytes 262144 | tf_op jit(solution)/shard_map/all_to_all | solution.py:33
  125.0 9.0 %shard_map.297 = (f32[1024,256]{1,0:T(8,128)}, f32[2,1152,128]{2,1,0:T(8,128)}, bf16[2,1152,128]{2,1,0:T(8,128)(2,1)}, f32[32,16,128]{2,1,0:T(8,128)}, f32[1,512]{1,0:T(1,128)}, /*index=5*/f32[1,512]{1,0:T(1,128)}) custom-call(s32[21]{0:T(128)S(1)} %concatenate.6.refs_0_, f32[32,8,128]{2,1,0:T(8,128)S(1)} %all_to_all.46.refs_1_, ...), custom_call_target="tpu_custom_call" | custom-call | flops 2415919104 | bytes 14338132 | tf_op jit(solution)/shard_map/pallas_call | solution.py:205
  134.3 2.8 %all-to-all-start.7 = ((f32[32,16,128]{2,1,0:T(8,128)}), f32[32,16,128]{2,1,0:T(8,128)S(1)}, u32[]{:S(2)}, u32[]{:S(2)}) async-start(f32[32,16,128]{2,1,0:T(8,128)} %get-tuple-element.129), calls=%async_computation.7 | async-start | bytes 524288 | tf_op jit(solution)/shard_map/all_to_all | solution.py:33
  137.2 1.6 collective-permute-done.6.refs_4_
  138.8 1.3 copy-done.11
  140.1 1.2 shard_map.298
  141.3 1.5 collective-permute-start.7
  142.8 4.9 %all-to-all-done.7.refs_1_ = f32[32,16,128]{2,1,0:T(8,128)S(1)} async-done(((f32[32,16,128]{2,1,0:T(8,128)}), f32[32,16,128]{2,1,0:T(8,128)S(1)}, u32[]{:S(2)}, u32[]{:S(2)}) %all-to-all-start.7) | async-done | bytes 262176 | tf_op jit(solution)/shard_map/all_to_all | solution.py:33
  147.6 3.9 %shard_map.299 = (bf16[1024,256]{1,0:T(8,128)(2,1)S(1)}, f32[1024,128]{1,0:T(8,128)S(1)}, bf16[1024,128]{1,0:T(8,128)(2,1)S(1)}, f32[1,256]{1,0:T(1,128)}, f32[1...) custom-call(s32[21]{0:T(128)S(1)} %concatenate.6.refs_0_, f32[32,16,128]{2,1,0:T(8,128)S(1)} %all-to-all-done.7.refs_1_, ...), custom_call_target="tpu_custom_call" | custom-call | flops 536870912 | bytes 5788756 | tf_op jit(solution)/shard_map/pallas_call | solution.py:205
  151.6 1.5 collective-permute-done.8.refs_4_
  153.1 1.5 collective-permute-done.7.refs_2_
  155.5 1.4 collective-permute-start.9
  156.8 1.4 collective-permute-start.10
  159.1 3.3 %shard_map.300 = (bf16[1024,1024]{1,0:T(8,128)(2,1)}, f32[8,128]{1,0:T(8,128)}) custom-call(s32[21]{0:T(128)S(1)} %concatenate.6.refs_0_, bf16[1024,256]{1,0:T(8,128)(2,1)S(1)} %get-tuple-element.135.refs_1_, bf16[1024,256]{1,0:T(8,128)(2,1)S(1)} %copy-done.8, f32[1024,1024]{1,0:T(8,128)S(1)} %copy-done.3), custom_call_target="tpu_custom_call" | custom-call | flops 536870912 | bytes 7344212 | tf_op jit(solution)/shard_map/pallas_call | solution.py:205
  162.4 1.9 collective-permute-done.10.refs_3_
  164.3 2.2 %collective-permute-done.11.refs_4_ = bf16[4,176,128]{2,1,0:T(8,128)(2,1)S(1)} collective-permute-done((bf16[4,176,128]{2,1,0:T(8,128)(2,1)S(1)}, bf16[4,176,128]{2,1,0:T(8,128)(2,1)S(1)}, u32[]{:S(2)}, u32[]{:S(2)}) %collective-permute-start.11) | collective-permute-done | bytes 180256 | tf_op jit(solution)/shard_map/ppermute | solution.py:53
  167.2 1.7 collective-permute-start.12
  168.8 2.2 %collective-permute-start.13 = (bf16[1,288,128]{2,1,0:T(8,128)(2,1)S(1)}, bf16[1,288,128]{2,1,0:T(8,128)(2,1)S(1)}, u32[]{:S(2)}, u32[]{:S(2)}) collective-permute-start(bf16[1,288,128]{2,1,0:T(8,128)(2,1)S(1)} %get-tuple-element.148), channel_id=1, source_target_pairs={{0,16},{1,17},{2,18},{3,19},{4,20},{5,21},{6,22},{7,23},{8,24},{9,... | collective-permute-start | bytes 221192 | tf_op jit(solution)/shard_map/ppermute | solution.py:53
  172.0 3.6 %collective-permute-done.13.refs_3_ = bf16[1,288,128]{2,1,0:T(8,128)(2,1)S(1)} collective-permute-done((bf16[1,288,128]{2,1,0:T(8,128)(2,1)S(1)}, bf16[1,288,128]{2,1,0:T(8,128)(2,1)S(1)}, u32[]{:S(2)}, u32[]{:S(2)}) %collective-permute-start.13) | collective-permute-done | bytes 73760 | tf_op jit(solution)/shard_map/ppermute | solution.py:53
  175.7 1.6 collective-permute-done.14.refs_4_
  177.8 1.5 collective-permute-start.17
  179.3 2.9 %collective-permute-start.15 = (bf16[1,304,128]{2,1,0:T(8,128)(2,1)S(1)}, bf16[1,304,128]{2,1,0:T(8,128)(2,1)S(1)}, u32[]{:S(2)}, u32[]{:S(2)}) collective-permute-start(bf16[1,304,128]{2,1,0:T(8,128)(2,1)S(1)} %shard_map.303), channel_id=1, source_target_pairs={{0,8},{1,9},{2,10},{3,11},{4,12},{5,13},{6,14},{7,15},{8,0},{9,1},... | collective-permute-start | bytes 233480 | tf_op jit(solution)/shard_map/ppermute | solution.py:53
  182.3 1.9 collective-permute-done.17
  184.1 1.6 collective-permute-done.16
  185.8 1.8 collective-permute-start.23
  189.4 6.9 %collective-permute-done.23.refs_4_ = bf16[4,304,128]{2,1,0:T(8,128)(2,1)S(1)} collective-permute-done((bf16[4,304,128]{2,1,0:T(8,128)(2,1)S(1)}, bf16[4,304,128]{2,1,0:T(8,128)(2,1)S(1)}, u32[]{:S(2)}, u32[]{:S(2)}) %collective-permute-start.23) | collective-permute-done | bytes 311328 | tf_op jit(solution)/shard_map/ppermute | solution.py:53
  196.2 2.5 %collective-permute-done.21.refs_3_ = bf16[4,304,128]{2,1,0:T(8,128)(2,1)S(1)} collective-permute-done((bf16[4,304,128]{2,1,0:T(8,128)(2,1)S(1)}, bf16[4,304,128]{2,1,0:T(8,128)(2,1)S(1)}, u32[]{:S(2)}, u32[]{:S(2)}) %collective-permute-start.21) | collective-permute-done | bytes 311328 | tf_op jit(solution)/shard_map/ppermute | solution.py:53
  199.4 2.1 %shard_map.304 = (f32[256,1024]{1,0:T(8,128)}, f32[128,512]{1,0:T(8,128)}, f32[3,3,2,128,256]{4,3,2,1,0:T(8,128)}, f32[1024,256]{1,0:T(8,128)}, f32[16,2,8,128]{3,2,1,0:T(8,128)}) custom-call(s32[21]{0:T(128)S(1)} %concatenate.6.refs_0_, bf16[4,304,128]{2,1,0:T(8,128)(2,1)S(1)} %pad_maximum_fusion.refs_1_, ...), custom_call_target="tpu_custom_call" | custom-call | bytes 6094932 | tf_op jit(solution)/shard_map/pallas_call | solution.py:205
  201.6 2.1 %shard_map.305 = (f32[256,1024]{1,0:T(8,128)}, f32[128,512]{1,0:T(8,128)}, f32[3,3,2,128,256]{4,3,2,1,0:T(8,128)}, f32[1024,256]{1,0:T(8,128)}, f32[16,2,8,128]{3,2,1,0:T(8,128)}) custom-call(s32[21]{0:T(128)S(1)} %concatenate.6.refs_0_, ...), custom_call_target="tpu_custom_call", output_to_operand_aliasing={{0}: (5, {}), {1}: (6, {}), {2}: (7, {}), {3}: (8, {}), {4}... | custom-call | bytes 10944596 | tf_op jit(solution)/shard_map/pallas_call | solution.py:205
  (77 shorter events, 10.6 us)
Async XLA Ops:
  0.6 25.8 %copy-start.21 = (f32[256]{0:T(256)S(1)}, f32[256]{0:T(256)}, u32[]{:S(2)}) copy-start(f32[256]{0:T(256)} %param.21) | copy-start | bytes 3076
  0.7 25.8 %copy-start.17 = (f32[256]{0:T(256)S(1)}, f32[256]{0:T(256)}, u32[]{:S(2)}) copy-start(f32[256]{0:T(256)} %param.20) | copy-start | bytes 3076
  1.4 1.6 copy-start
  4.1 22.4 %copy-start.10 = (bf16[3,3,2,128,256]{4,3,2,1,0:T(8,128)(2,1)S(1)}, bf16[3,3,2,128,256]{4,3,2,1,0:T(8,128)(2,1)}, u32[]{:S(2)}) copy-start(bf16[3,3,2,128,256]{4,3,2,1,0:T(8,128)(2,1)} %refs_11_.1) | copy-start | bytes 3538948
  5.6 119.5 %copy-start.4 = (f32[1024,256]{1,0:T(8,128)}, f32[1024,256]{1,0:T(8,128)S(1)}, u32[]{:S(2)}) copy-start(f32[1024,256]{1,0:T(8,128)S(1)} %get-tuple-element.94.refs_2_.refs_12_.refs_5_) | copy-start | bytes 3145732
  5.6 20.9 %collective-permute-start = (f32[512,256]{1,0:T(8,128)S(1)}, f32[512,256]{1,0:T(8,128)S(1)}, u32[]{:S(2)}, u32[]{:S(2)}) collective-permute-start(f32[512,256]{1,0:T(8,128)S(1)} %get-tuple-element.95), channel_id=1, source_target_pairs={{0,1},{1,2},{2,3},{4,5},{5,6},{6,7},{8,9},{9,10},{10,11},{12,13},{... | collective-permute-start | bytes 1572872 | tf_op jit(solution)/shard_map/ppermute | solution.py:27
  8.0 18.5 %collective-permute-start.1 = (f32[512,256]{1,0:T(8,128)S(1)}, f32[512,256]{1,0:T(8,128)S(1)}, u32[]{:S(2)}, u32[]{:S(2)}) collective-permute-start(f32[512,256]{1,0:T(8,128)S(1)} %get-tuple-element.96), channel_id=1, source_target_pairs={{1,0},{2,1},{3,2},{5,4},{6,5},{7,6},{9,8},{10,9},{11,10},{13,12},{... | collective-permute-start | bytes 1572872 | tf_op jit(solution)/shard_map/ppermute | solution.py:28
  26.5 14.8 %copy-start.13 = (f32[256,128]{1,0:T(8,128)S(1)}, f32[256,128]{1,0:T(8,128)}, u32[]{:S(2)}) copy-start(f32[256,128]{1,0:T(8,128)} %refs_7_.5) | copy-start | bytes 393220
  26.5 14.8 %copy-start.14 = (f32[512]{0:T(512)S(1)}, f32[512]{0:T(512)}, u32[]{:S(2)}) copy-start(f32[512]{0:T(512)} %param.23) | copy-start | bytes 6148
  26.5 14.7 %copy-start.15 = (f32[512]{0:T(512)S(1)}, f32[512]{0:T(512)}, u32[]{:S(2)}) copy-start(f32[512]{0:T(512)} %param.24) | copy-start | bytes 6148
  31.1 24.4 %copy-start.9 = (bf16[256,1024]{1,0:T(8,128)(2,1)S(1)}, bf16[256,1024]{1,0:T(8,128)(2,1)}, u32[]{:S(2)}) copy-start(bf16[256,1024]{1,0:T(8,128)(2,1)} %refs_6_.3) | copy-start | bytes 1572868
  31.2 24.4 %copy-start.12 = (f32[128,512]{1,0:T(8,128)S(1)}, f32[128,512]{1,0:T(8,128)}, u32[]{:S(2)}) copy-start(f32[128,512]{1,0:T(8,128)} %refs_9_.1) | copy-start | bytes 786436
  31.2 24.4 %copy-start.19 = (f32[512]{0:T(512)S(1)}, f32[512]{0:T(512)}, u32[]{:S(2)}) copy-start(f32[512]{0:T(512)} %param.29) | copy-start | bytes 6148
  31.2 24.4 %copy-start.20 = (f32[128]{0:T(128)S(1)}, f32[128]{0:T(128)}, u32[]{:S(2)}) copy-start(f32[128]{0:T(128)} %param.26) | copy-start | bytes 1540
  31.2 24.4 %copy-start.22 = (f32[128]{0:T(128)S(1)}, f32[128]{0:T(128)}, u32[]{:S(2)}) copy-start(f32[128]{0:T(128)} %param.27) | copy-start | bytes 1540
  41.3 29.2 %copy-start.6 = (bf16[16,4,16,1024]{3,2,1,0:T(8,128)(2,1)S(1)}, bf16[16,4,16,1024]{3,2,1,0:T(8,128)(2,1)}, u32[]{:S(2)}) copy-start(bf16[16,4,16,1024]{3,2,1,0:T(8,128)(2,1)} %param.33) | copy-start | bytes 6291460
  43.1 27.4 %copy-start.1 = (bf16[16,4,16,1024]{3,2,1,0:T(8,128)(2,1)S(1)}, bf16[16,4,16,1024]{3,2,1,0:T(8,128)(2,1)}, u32[]{:S(2)}) copy-start(bf16[16,4,16,1024]{3,2,1,0:T(8,128)(2,1)} %param.17) | copy-start | bytes 6291460
  43.1 27.4 %copy-start.16 = (f32[1024]{0:T(1024)S(1)}, f32[1024]{0:T(1024)}, u32[]{:S(2)}) copy-start(f32[1024]{0:T(1024)} %param.31) | copy-start | bytes 12292
  43.1 27.4 %copy-start.18 = (f32[1024]{0:T(1024)S(1)}, f32[1024]{0:T(1024)}, u32[]{:S(2)}) copy-start(f32[1024]{0:T(1024)} %param.32) | copy-start | bytes 12292
  75.9 16.4 %copy-start.2 = (f32[1024,1024]{1,0:T(8,128)}, f32[1024,1024]{1,0:T(8,128)S(1)}, u32[]{:S(2)}) copy-start(f32[1024,1024]{1,0:T(8,128)S(1)} %get-tuple-element.107.refs_4_.refs_3_) | copy-start | bytes 12582916
  92.3 5.8 %collective-permute-start.3 = (bf16[256,256]{1,0:T(8,128)(2,1)S(1)}, bf16[256,256]{1,0:T(8,128)(2,1)S(1)}, u32[]{:S(2)}, u32[]{:S(2)}) collective-permute-start(bf16[256,256]{1,0:T(8,128)(2,1)S(1)} %get-tuple-element.111), channel_id=1, source_target_pairs={{0,1},{1,2},{2,3},{4,5},{5,6},{6,7},{8,9},{9,10},{10,11},{12,13},{... | collective-permute-start | bytes 393224 | tf_op jit(solution)/shard_map/ppermute | solution.py:27
  94.1 4.0 %collective-permute-start.4 = (bf16[256,256]{1,0:T(8,128)(2,1)S(1)}, bf16[256,256]{1,0:T(8,128)(2,1)S(1)}, u32[]{:S(2)}, u32[]{:S(2)}) collective-permute-start(bf16[256,256]{1,0:T(8,128)(2,1)S(1)} %get-tuple-element.112), channel_id=1, source_target_pairs={{1,0},{2,1},{3,2},{5,4},{6,5},{7,6},{9,8},{10,9},{11,10},{13,12},{... | collective-permute-start | bytes 393224 | tf_op jit(solution)/shard_map/ppermute | solution.py:28
  95.4 2.7 %collective-permute-start.2 = (f32[8,128]{1,0:T(8,128)S(1)}, f32[8,128]{1,0:T(8,128)S(1)}, u32[]{:S(2)}, u32[]{:S(2)}) collective-permute-start(f32[8,128]{1,0:T(8,128)S(1)} %get-tuple-element.110), channel_id=1, source_target_pairs={{0,1},{1,0},{2,3},{3,2},{4,5},{5,4},{6,7},{7,6},{8,9},{9,8},{10,11... | collective-permute-start | bytes 12296 | tf_op jit(solution)/shard_map/ppermute | solution.py:38
  111.9 13.1 %copy-start.5 = (bf16[3,16,128,256]{3,2,1,0:T(8,128)(2,1)S(1)}, bf16[3,16,128,256]{3,2,1,0:T(8,128)(2,1)}, u32[]{:S(2)}) copy-start(bf16[3,16,128,256]{3,2,1,0:T(8,128)(2,1)} %get-tuple-element.128.refs_18_) | copy-start | bytes 9437188
  134.1 4.8 %collective-permute-start.5 = (bf16[2,1152,128]{2,1,0:T(8,128)(2,1)}, bf16[2,1152,128]{2,1,0:T(8,128)(2,1)S(1)}, u32[]{:S(2)}, u32[]{:S(2)}) collective-permute-start(bf16[2,1152,128]{2,1,0:T(8,128)(2,1)} %get-tuple-element.132), channel_id=1, source_target_pairs={{0,1},{1,0},{2,3},{3,2},{4,5},{5,4},{6,7},{7,6},{8,9},{9,8},{10,11... | collective-permute-start | bytes 1769480 | tf_op jit(solution)/shard_map/ppermute | solution.py:38
  134.3 13.3 %all-to-all-start.7 = ((f32[32,16,128]{2,1,0:T(8,128)}), f32[32,16,128]{2,1,0:T(8,128)S(1)}, u32[]{:S(2)}, u32[]{:S(2)}) async-start(f32[32,16,128]{2,1,0:T(8,128)} %get-tuple-element.129), calls=%async_computation.7 | async-start | bytes 524288 | tf_op jit(solution)/shard_map/all_to_all | solution.py:33
  137.1 1.7 collective-permute-start.6
  138.8 1.3 copy-start.11
  141.3 13.4 %collective-permute-start.7 = (bf16[1792,128]{1,0:T(8,128)(2,1)S(1)}, bf16[1792,128]{1,0:T(8,128)(2,1)S(1)}, u32[]{:S(2)}, u32[]{:S(2)}) collective-permute-start(bf16[1792,128]{1,0:T(8,128)(2,1)S(1)} %get-tuple-element.138), channel_id=1, source_target_pairs={{0,2},{1,3},{2,0},{3,1},{4,6},{5,7},{6,4},{7,5},{8,10},{9,11},{10,... | collective-permute-start | bytes 1376264 | tf_op jit(solution)/shard_map/ppermute | solution.py:38
  147.6 11.4 %copy-start.3 = (f32[1024,1024]{1,0:T(8,128)S(1)}, f32[1024,1024]{1,0:T(8,128)}, u32[]{:S(2)}) copy-start(f32[1024,1024]{1,0:T(8,128)} %copy-done.2) | copy-start | bytes 12582916
  151.5 7.5 %copy-start.8 = (bf16[1024,256]{1,0:T(8,128)(2,1)S(1)}, bf16[1024,256]{1,0:T(8,128)(2,1)}, u32[]{:S(2)}) copy-start(bf16[1024,256]{1,0:T(8,128)(2,1)} %refs_2_.3) | copy-start | bytes 1572868
  151.5 1.6 collective-permute-start.8
  155.5 6.9 %collective-permute-start.9 = (bf16[4,176,128]{2,1,0:T(8,128)(2,1)S(1)}, bf16[4,176,128]{2,1,0:T(8,128)(2,1)S(1)}, u32[]{:S(2)}, u32[]{:S(2)}) collective-permute-start(bf16[4,176,128]{2,1,0:T(8,128)(2,1)S(1)} %get-tuple-element.142), channel_id=1, source_target_pairs={{0,2},{1,3},{2,0},{3,1},{4,6},{5,7},{6,4},{7,5},{8,10},{9,11},{10,... | collective-permute-start | bytes 540680 | tf_op jit(solution)/shard_map/ppermute | solution.py:53
  156.8 7.5 %collective-permute-start.10 = (bf16[4,176,128]{2,1,0:T(8,128)(2,1)S(1)}, bf16[4,176,128]{2,1,0:T(8,128)(2,1)S(1)}, u32[]{:S(2)}, u32[]{:S(2)}) collective-permute-start(bf16[4,176,128]{2,1,0:T(8,128)(2,1)S(1)} %get-tuple-element.143), channel_id=1, source_target_pairs={{0,4},{1,5},{2,6},{3,7},{4,0},{5,1},{6,2},{7,3},{8,12},{9,13},{10,... | collective-permute-start | bytes 540680 | tf_op jit(solution)/shard_map/ppermute | solution.py:53
  158.3 8.3 %collective-permute-start.11 = (bf16[4,176,128]{2,1,0:T(8,128)(2,1)S(1)}, bf16[4,176,128]{2,1,0:T(8,128)(2,1)S(1)}, u32[]{:S(2)}, u32[]{:S(2)}) collective-permute-start(bf16[4,176,128]{2,1,0:T(8,128)(2,1)S(1)} %get-tuple-element.144), channel_id=1, source_target_pairs={{0,6},{1,7},{2,4},{3,5},{4,2},{5,3},{6,0},{7,1},{8,14},{9,15},{10,... | collective-permute-start | bytes 540680 | tf_op jit(solution)/shard_map/ppermute | solution.py:53
  167.2 4.9 %collective-permute-start.12 = (bf16[1,288,128]{2,1,0:T(8,128)(2,1)S(1)}, bf16[1,288,128]{2,1,0:T(8,128)(2,1)S(1)}, u32[]{:S(2)}, u32[]{:S(2)}) collective-permute-start(bf16[1,288,128]{2,1,0:T(8,128)(2,1)S(1)} %get-tuple-element.147), channel_id=1, source_target_pairs={{0,8},{1,9},{2,10},{3,11},{4,12},{5,13},{6,14},{7,15},{8,0},{9,1},... | collective-permute-start | bytes 221192 | tf_op jit(solution)/shard_map/ppermute | solution.py:53
  168.8 6.8 %collective-permute-start.13 = (bf16[1,288,128]{2,1,0:T(8,128)(2,1)S(1)}, bf16[1,288,128]{2,1,0:T(8,128)(2,1)S(1)}, u32[]{:S(2)}, u32[]{:S(2)}) collective-permute-start(bf16[1,288,128]{2,1,0:T(8,128)(2,1)S(1)} %get-tuple-element.148), channel_id=1, source_target_pairs={{0,16},{1,17},{2,18},{3,19},{4,20},{5,21},{6,22},{7,23},{8,24},{9,... | collective-permute-start | bytes 221192 | tf_op jit(solution)/shard_map/ppermute | solution.py:53
  171.0 6.2 %collective-permute-start.14 = (bf16[1,288,128]{2,1,0:T(8,128)(2,1)S(1)}, bf16[1,288,128]{2,1,0:T(8,128)(2,1)S(1)}, u32[]{:S(2)}, u32[]{:S(2)}) collective-permute-start(bf16[1,288,128]{2,1,0:T(8,128)(2,1)S(1)} %get-tuple-element.149), channel_id=1, source_target_pairs={{0,24},{1,25},{2,26},{3,27},{4,28},{5,29},{6,30},{7,31},{8,16},{9,... | collective-permute-start | bytes 221192 | tf_op jit(solution)/shard_map/ppermute | solution.py:53
  177.8 6.3 %collective-permute-start.17 = (bf16[1,304,128]{2,1,0:T(8,128)(2,1)S(1)}, bf16[1,304,128]{2,1,0:T(8,128)(2,1)S(1)}, u32[]{:S(2)}, u32[]{:S(2)}) collective-permute-start(bf16[1,304,128]{2,1,0:T(8,128)(2,1)S(1)} %shard_map.303), channel_id=1, source_target_pairs={{0,24},{1,25},{2,26},{3,27},{4,28},{5,29},{6,30},{7,31},{8,16},{9,... | collective-permute-start | bytes 233480 | tf_op jit(solution)/shard_map/ppermute | solution.py:53
  179.3 6.4 %collective-permute-start.16 = (bf16[1,304,128]{2,1,0:T(8,128)(2,1)S(1)}, bf16[1,304,128]{2,1,0:T(8,128)(2,1)S(1)}, u32[]{:S(2)}, u32[]{:S(2)}) collective-permute-start(bf16[1,304,128]{2,1,0:T(8,128)(2,1)S(1)} %shard_map.303), channel_id=1, source_target_pairs={{0,16},{1,17},{2,18},{3,19},{4,20},{5,21},{6,22},{7,23},{8,24},{9,... | collective-permute-start | bytes 233480 | tf_op jit(solution)/shard_map/ppermute | solution.py:53
  179.3 6.4 %collective-permute-start.15 = (bf16[1,304,128]{2,1,0:T(8,128)(2,1)S(1)}, bf16[1,304,128]{2,1,0:T(8,128)(2,1)S(1)}, u32[]{:S(2)}, u32[]{:S(2)}) collective-permute-start(bf16[1,304,128]{2,1,0:T(8,128)(2,1)S(1)} %shard_map.303), channel_id=1, source_target_pairs={{0,8},{1,9},{2,10},{3,11},{4,12},{5,13},{6,14},{7,15},{8,0},{9,1},... | collective-permute-start | bytes 233480 | tf_op jit(solution)/shard_map/ppermute | solution.py:53
  185.8 10.4 %collective-permute-start.23 = (bf16[4,304,128]{2,1,0:T(8,128)(2,1)S(1)}, bf16[4,304,128]{2,1,0:T(8,128)(2,1)S(1)}, u32[]{:S(2)}, u32[]{:S(2)}) collective-permute-start(bf16[4,304,128]{2,1,0:T(8,128)(2,1)S(1)} %pad_maximum_fusion.refs_1_), channel_id=1, source_target_pairs={{0,6},{1,7},{2,4},{3,5},{4,2},{5,3},{6,0},{7,1},{8,14},{9,15},{10,... | collective-permute-start | bytes 933896 | tf_op jit(solution)/shard_map/ppermute | solution.py:53
  187.6 11.2 %collective-permute-start.21 = (bf16[4,304,128]{2,1,0:T(8,128)(2,1)S(1)}, bf16[4,304,128]{2,1,0:T(8,128)(2,1)S(1)}, u32[]{:S(2)}, u32[]{:S(2)}) collective-permute-start(bf16[4,304,128]{2,1,0:T(8,128)(2,1)S(1)} %pad_maximum_fusion.refs_1_), channel_id=1, source_target_pairs={{0,4},{1,5},{2,6},{3,7},{4,0},{5,1},{6,2},{7,3},{8,12},{9,13},{10,... | collective-permute-start | bytes 933896 | tf_op jit(solution)/shard_map/ppermute | solution.py:53
  188.4 11.0 %collective-permute-start.19 = (bf16[4,304,128]{2,1,0:T(8,128)(2,1)S(1)}, bf16[4,304,128]{2,1,0:T(8,128)(2,1)S(1)}, u32[]{:S(2)}, u32[]{:S(2)}) collective-permute-start(bf16[4,304,128]{2,1,0:T(8,128)(2,1)S(1)} %pad_maximum_fusion.refs_1_), channel_id=1, source_target_pairs={{0,2},{1,3},{2,0},{3,1},{4,6},{5,7},{6,4},{7,5},{8,10},{9,11},{10,... | collective-permute-start | bytes 933896 | tf_op jit(solution)/shard_map/ppermute | solution.py:53
  189.4 12.2 %collective-permute-start.18 = (bf16[4,304,128]{2,1,0:T(8,128)(2,1)S(1)}, bf16[4,304,128]{2,1,0:T(8,128)(2,1)S(1)}, u32[]{:S(2)}, u32[]{:S(2)}) collective-permute-start(bf16[4,304,128]{2,1,0:T(8,128)(2,1)S(1)} %pad_maximum_fusion.refs_1_), channel_id=1, source_target_pairs={{0,1},{1,0},{2,3},{3,2},{4,5},{5,4},{6,7},{7,6},{8,9},{9,8},{10,11... | collective-permute-start | bytes 933896 | tf_op jit(solution)/shard_map/ppermute | solution.py:38
  196.2 5.3 %collective-permute-start.24 = (bf16[4,304,128]{2,1,0:T(8,128)(2,1)S(1)}, bf16[4,304,128]{2,1,0:T(8,128)(2,1)S(1)}, u32[]{:S(2)}, u32[]{:S(2)}) collective-permute-start(bf16[4,304,128]{2,1,0:T(8,128)(2,1)S(1)} %collective-permute-done.23.refs_4_), channel_id=1, source_target_pairs={{0,1},{1,0},{2,3},{3,2},{4,5},{5,4},{6,7},{7,6},{8,9},{9,8},{10,11... | collective-permute-start | bytes 933896 | tf_op jit(solution)/shard_map/ppermute | solution.py:38
  198.8 2.8 %collective-permute-start.22 = (bf16[4,304,128]{2,1,0:T(8,128)(2,1)S(1)}, bf16[4,304,128]{2,1,0:T(8,128)(2,1)S(1)}, u32[]{:S(2)}, u32[]{:S(2)}) collective-permute-start(bf16[4,304,128]{2,1,0:T(8,128)(2,1)S(1)} %collective-permute-done.21.refs_3_), channel_id=1, source_target_pairs={{0,1},{1,0},{2,3},{3,2},{4,5},{5,4},{6,7},{7,6},{8,9},{9,8},{10,11... | collective-permute-start | bytes 933896 | tf_op jit(solution)/shard_map/ppermute | solution.py:38
  199.4 2.2 %collective-permute-start.20 = (bf16[4,304,128]{2,1,0:T(8,128)(2,1)S(1)}, bf16[4,304,128]{2,1,0:T(8,128)(2,1)S(1)}, u32[]{:S(2)}, u32[]{:S(2)}) collective-permute-start(bf16[4,304,128]{2,1,0:T(8,128)(2,1)S(1)} %collective-permute-done.19.refs_2_), channel_id=1, source_target_pairs={{0,1},{1,0},{2,3},{3,2},{4,5},{5,4},{6,7},{7,6},{8,9},{9,8},{10,11... | collective-permute-start | bytes 933896 | tf_op jit(solution)/shard_map/ppermute | solution.py:38
  (1 other events, 1.0 us)

commit v9 on v8

--- a/solution.py
+++ b/solution.py
@@ -140,7 +140,7 @@
         ref[k] = block
         return carry
 
-    lax.fori_loop(1, ref.shape[0], step, 0)
+    lax.fori_loop(1, ref.shape[0], step, 0, unroll=31)
 
 
 def fold(values):
@@ -634,8 +634,8 @@
 
 def conv_kernel(
     meta, got, stat2, gain2, shift2, dz, pre2, lowm, highm, att, gpool, w, pre, stat,
-    gain, shift, glog, squeeze, hid, out_hbm, keep_hbm, send_hbm, pay_hbm, gain_out, shift_out, tall, acc,
-    out, keep, send, pay, sems, *, blocks, rows
+    gain, shift, glog, squeeze, hid, out_hbm, keep_hbm, send_hbm, pay_hbm, gain_hbm, shift_hbm, tall, acc,
+    out, keep, send, pay, gain_out, shift_out, sems, *, blocks, rows
 ):
     slab = rows * COLS
     sums = jnp.sum(got[...], 0)
@@ -699,6 +699,8 @@
     stores = [
         pltpu.make_async_copy(send, send_hbm, sems.at[1]),
         pltpu.make_async_copy(keep, keep_hbm, sems.at[2]),
+        pltpu.make_async_copy(gain_out, gain_hbm, sems.at[3]),
+        pltpu.make_async_copy(shift_out, shift_hbm, sems.at[4]),
     ]
     for store in stores:
         store.start()
@@ -709,7 +711,7 @@
 
     def store_group(g):
         many = pl.ds(pl.multiple_of(g * group * slab, group * slab), group * slab)
-        return pltpu.make_async_copy(out.at[many], out_hbm.at[many], sems.at[3 + g])
+        return pltpu.make_async_copy(out.at[many], out_hbm.at[many], sems.at[5 + g])
 
     def step(g, carry):
         for half in range(2):
@@ -1058,8 +1060,8 @@
             ((2, 9 * 128, LANES), F32, "hbm"),
             ((2, 9 * 128, LANES), BF16, "hbm"),
             ((count, 8 + share, LANES), F32, "hbm"),
-            ((1, 2 * mid), F32),
-            ((1, 2 * mid), F32),
+            ((1, 2 * mid), F32, "hbm"),
+            ((1, 2 * mid), F32, "hbm"),
         ],
         [
             meta,
@@ -1089,11 +1091,13 @@
             ((2, 9 * 128, LANES), F32),
             ((2, 9 * 128, LANES), BF16),
             ((count, 8 + share, LANES), F32),
-            pltpu.SemaphoreType.DMA((3 + blocks // 4,)),
-        ],
-        raw_out=(0, 1, 2, 3),
+            ((1, 2 * mid), F32),
+            ((1, 2 * mid), F32),
+            pltpu.SemaphoreType.DMA((5 + blocks // 4,)),
+        ],
+        raw_out=range(6),
         flops=2 * large,
-        local="in",
+        local="in out",
         **sizes,
     )
     chips = count // 2

time: 204 us -> 203 us (level)
  no operation moved by 1% of the time
where the time goes in v9:
time: 203 us; the launch traced here: 202 us
  blocking collectives  88.3 us (43%)
  Pallas kernels  46.1 us (23%)
  waiting for transfers between devices  32.8 us (16%)
  starting transfers between devices  28.7 us (14%)
  local copies, waits for them, and re-layouts  4.75 us (2%)
    all_to_all x7, blocking collectives, exchange(): return lax.all_to_all(block, ALL, 0, 0)  88.3 us
    pallas_call x18, Pallas kernels, call(): pl.pallas_call(run, grid=() if local == 'in out' else (1,), out_shape=[pl...  46.1 us
    ppermute x12, waiting for transfers between devices, partners(): lax.ppermute(block, ALL, [(i, i ^ step) for i in range(count)])  23.3 us
    ppermute x12, starting transfers between devices, partners(): lax.ppermute(block, ALL, [(i, i ^ step) for i in range(count)])  16 us
    all_to_all x1, waiting for transfers between devices, exchange(): return lax.all_to_all(block, ALL, 0, 0)  4.86 us
    ppermute x9, waiting for transfers between devices, swap(): return lax.ppermute(block, 'narrow', [(i, i ^ bit) for i in range(count)])  4.65 us
    ppermute x2, starting transfers between devices, halo(): low = lax.ppermute(bottom, 'narrow', [(i, i + 1) for i in range(count - 1)])  4.2 us
  transfers between devices with their start and end apart: 26, of which 14 were waited for; matrix products, arithmetic and copies ran while one was open for 0% of the time, Pallas kernels for 6%

profile of v9, /device:TPU:0, one launch (start us, length us, event | category | flops | bytes accessed | tf_op | source)
XLA Modules:
  0.0 202.0 jit_solution(11948586112334905645)
XLA Ops:
  1.4 1.6 copy-done
  4.1 1.3 shard_map.288
  5.4 2.4 %collective-permute-start = (f32[512,256]{1,0:T(8,128)S(1)}, f32[512,256]{1,0:T(8,128)S(1)}, u32[]{:S(2)}, u32[]{:S(2)}) collective-permute-start(f32[512,256]{1,0:T(8,128)S(1)} %get-tuple-element.95), channel_id=1, source_target_pairs={{0,1},{1,2},{2,3},{4,5},{5,6},{6,7},{8,9},{9,10},{10,11},{12,13},{... | collective-permute-start | bytes 1572872 | tf_op jit(solution)/shard_map/ppermute | solution.py:27
  7.8 1.3 collective-permute-start.1
  9.1 17.2 %all_to_all.40.refs_1_ = f32[32,8,128]{2,1,0:T(8,128)S(1)} all-to-all(f32[32,8,128]{2,1,0:T(8,128)S(1)} %get-tuple-element.93), channel_id=1, replica_groups=mesh['batch'=8,'narrow'=4] {'batch','narrow'}, dimensions={0} | all-to-all | bytes 262144 | tf_op jit(solution)/shard_map/all_to_all | solution.py:33
  26.4 4.4 %shard_map.289 = (bf16[3,16,128,256]{3,2,1,0:T(8,128)(2,1)}, f32[1536,512]{1,0:T(8,128)S(1)}, f32[32,8,128]{2,1,0:T(8,128)S(1)}, f32[8,256]{1,0:T(8,128)S(1)}) custom-call(s32[21]{0:T(128)S(1)} %concatenate.6.refs_0_, f32[32,8,128]{2,1,0:T(8,128)S(1)} %all_to_all.40.refs_1_, f32[1024,256]{1,0:T(8,128)S(1)} %get-tuple-element.94.refs_2_.refs_12_.refs_5_, ...), custom_call_target="tpu_custom_call" | custom-call | flops 1207959552 | bytes 9840724 | tf_op jit(solution)/shard_map/pallas_call | solution.py:205
  30.9 10.1 %all_to_all.41.refs_1_ = f32[32,8,128]{2,1,0:T(8,128)S(1)} all-to-all(f32[32,8,128]{2,1,0:T(8,128)S(1)} %get-tuple-element.97), channel_id=1, replica_groups=mesh['batch'=8,'narrow'=4] {'batch','narrow'}, dimensions={0} | all-to-all | bytes 262144 | tf_op jit(solution)/shard_map/all_to_all | solution.py:33
  41.0 1.6 shard_map.290
  42.7 12.4 %all_to_all.42.refs_1_ = f32[32,16,128]{2,1,0:T(8,128)S(1)} all-to-all(f32[32,16,128]{2,1,0:T(8,128)S(1)} %get-tuple-element.100), channel_id=1, replica_groups=mesh['batch'=8,'narrow'=4] {'batch','narrow'}, dimensions={0} | all-to-all | bytes 524288 | tf_op jit(solution)/shard_map/all_to_all | solution.py:33
  55.2 2.0 shard_map.291
  57.2 12.7 %all_to_all.43.refs_1_ = f32[32,16,128]{2,1,0:T(8,128)S(1)} all-to-all(f32[32,16,128]{2,1,0:T(8,128)S(1)} %get-tuple-element.102), channel_id=1, replica_groups=mesh['batch'=8,'narrow'=4] {'batch','narrow'}, dimensions={0} | all-to-all | bytes 524288 | tf_op jit(solution)/shard_map/all_to_all | solution.py:33
  69.9 5.2 %shard_map.292 = (bf16[1024,1024]{1,0:T(8,128)(2,1)}, f32[1024,1024]{1,0:T(8,128)S(1)}, f32[32,16,128]{2,1,0:T(8,128)S(1)}, f32[8,1024]{1,0:T(8,128)S(1)}) custom-call(s32[21]{0:T(128)S(1)} %concatenate.6.refs_0_, f32[32,16,128]{2,1,0:T(8,128)S(1)} %all_to_all.43.refs_1_, f32[8,256]{1,0:T(8,128)S(1)} %get-tuple-element.98.refs_2_.refs_13_, ...), custom_call_target="tpu_custom_call" | custom-call | bytes 13156436 | tf_op jit(solution)/shard_map/pallas_call | solution.py:205
  75.1 12.8 %all_to_all.44.refs_1_ = f32[32,16,128]{2,1,0:T(8,128)S(1)} all-to-all(f32[32,16,128]{2,1,0:T(8,128)S(1)} %get-tuple-element.105), channel_id=1, replica_groups=mesh['batch'=8,'narrow'=4] {'batch','narrow'}, dimensions={0} | all-to-all | bytes 524288 | tf_op jit(solution)/shard_map/all_to_all | solution.py:33
  87.9 3.6 %shard_map.293 = (bf16[1024,1024]{1,0:T(8,128)(2,1)S(1)}, bf16[1024,256]{1,0:T(8,128)(2,1)S(1)}, bf16[256,256]{1,0:T(8,128)(2,1)S(1)}, bf16[256,256]{1,0:T(8,128...) custom-call(s32[21]{0:T(128)S(1)} %concatenate.6.refs_0_, ...), custom_call_target="tpu_custom_call" | custom-call | flops 536870912 | bytes 11391060 | tf_op jit(solution)/shard_map/pallas_call | solution.py:205
  91.5 1.8 collective-permute-start.3
  93.3 1.3 collective-permute-start.4
  95.8 1.5 shard_map.294
  97.9 13.1 %all_to_all.45.refs_1_ = f32[32,8,128]{2,1,0:T(8,128)S(1)} all-to-all(f32[32,8,128]{2,1,0:T(8,128)S(1)} %shard_map.295), channel_id=1, replica_groups=mesh['batch'=8,'narrow'=4] {'batch','narrow'}, dimensions={0} | all-to-all | bytes 262144 | tf_op jit(solution)/shard_map/all_to_all | solution.py:33
  111.0 2.9 %shard_map.296 = (f32[1024,512]{1,0:T(8,128)S(1)}, f32[16,256]{1,0:T(8,128)S(1)}, f32[256,128]{1,0:T(8,128)S(1)}, f32[32,8,128]{2,1,0:T(8,128)S(1)}, f32[1,128]{1,0:T(1,128)}, /*index=5*/f32[1,128]{1,0:T(1,128)}) custom-call(s32[21]{0:T(128)S(1)} %concatenate.6.refs_0_, f32[32,8,128]{2,1,0:T(8,128)S(1)} %all_to_all.45.refs_1_, ...), custom_call_target="tpu_custom_call" | custom-call | bytes 6514260 | tf_op jit(solution)/shard_map/pallas_call | solution.py:205
  113.8 10.0 %all_to_all.46.refs_1_ = f32[32,8,128]{2,1,0:T(8,128)S(1)} all-to-all(f32[32,8,128]{2,1,0:T(8,128)S(1)} %get-tuple-element.124), channel_id=1, replica_groups=mesh['batch'=8,'narrow'=4] {'batch','narrow'}, dimensions={0} | all-to-all | bytes 262144 | tf_op jit(solution)/shard_map/all_to_all | solution.py:33
  123.8 8.4 %shard_map.297 = (f32[1024,256]{1,0:T(8,128)}, f32[2,1152,128]{2,1,0:T(8,128)}, bf16[2,1152,128]{2,1,0:T(8,128)(2,1)}, f32[32,16,128]{2,1,0:T(8,128)}, f32[1,512]{1,0:T(1,128)}, /*index=5*/f32[1,512]{1,0:T(1,128)}) custom-call(s32[21]{0:T(128)S(1)} %concatenate.6.refs_0_, f32[32,8,128]{2,1,0:T(8,128)S(1)} %all_to_all.46.refs_1_, ...), custom_call_target="tpu_custom_call" | custom-call | flops 2415919104 | bytes 14338132 | tf_op jit(solution)/shard_map/pallas_call | solution.py:205
  132.5 2.8 %all-to-all-start.7 = ((f32[32,16,128]{2,1,0:T(8,128)}), f32[32,16,128]{2,1,0:T(8,128)S(1)}, u32[]{:S(2)}, u32[]{:S(2)}) async-start(f32[32,16,128]{2,1,0:T(8,128)} %get-tuple-element.129), calls=%async_computation.7 | async-start | bytes 524288 | tf_op jit(solution)/shard_map/all_to_all | solution.py:33
  135.4 1.6 collective-permute-done.6.refs_4_
  137.0 1.3 copy-done.11
  138.2 1.2 shard_map.298
  139.4 1.5 collective-permute-start.7
  140.9 4.9 %all-to-all-done.7.refs_1_ = f32[32,16,128]{2,1,0:T(8,128)S(1)} async-done(((f32[32,16,128]{2,1,0:T(8,128)}), f32[32,16,128]{2,1,0:T(8,128)S(1)}, u32[]{:S(2)}, u32[]{:S(2)}) %all-to-all-start.7) | async-done | bytes 262176 | tf_op jit(solution)/shard_map/all_to_all | solution.py:33
  145.8 3.9 %shard_map.299 = (bf16[1024,256]{1,0:T(8,128)(2,1)S(1)}, f32[1024,128]{1,0:T(8,128)S(1)}, bf16[1024,128]{1,0:T(8,128)(2,1)S(1)}, f32[1,256]{1,0:T(1,128)}, f32[1...) custom-call(s32[21]{0:T(128)S(1)} %concatenate.6.refs_0_, f32[32,16,128]{2,1,0:T(8,128)S(1)} %all-to-all-done.7.refs_1_, ...), custom_call_target="tpu_custom_call" | custom-call | flops 536870912 | bytes 5788756 | tf_op jit(solution)/shard_map/pallas_call | solution.py:205
  149.8 1.5 collective-permute-done.8.refs_4_
  151.3 1.5 collective-permute-done.7.refs_2_
  153.6 1.4 collective-permute-start.9
  155.0 1.4 collective-permute-start.10
  157.2 3.3 %shard_map.300 = (bf16[1024,1024]{1,0:T(8,128)(2,1)}, f32[8,128]{1,0:T(8,128)}) custom-call(s32[21]{0:T(128)S(1)} %concatenate.6.refs_0_, bf16[1024,256]{1,0:T(8,128)(2,1)S(1)} %get-tuple-element.135.refs_1_, bf16[1024,256]{1,0:T(8,128)(2,1)S(1)} %copy-done.8, f32[1024,1024]{1,0:T(8,128)S(1)} %copy-done.3), custom_call_target="tpu_custom_call" | custom-call | flops 536870912 | bytes 7344212 | tf_op jit(solution)/shard_map/pallas_call | solution.py:205
  160.5 1.9 collective-permute-done.10.refs_3_
  162.5 2.2 %collective-permute-done.11.refs_4_ = bf16[4,176,128]{2,1,0:T(8,128)(2,1)S(1)} collective-permute-done((bf16[4,176,128]{2,1,0:T(8,128)(2,1)S(1)}, bf16[4,176,128]{2,1,0:T(8,128)(2,1)S(1)}, u32[]{:S(2)}, u32[]{:S(2)}) %collective-permute-start.11) | collective-permute-done | bytes 180256 | tf_op jit(solution)/shard_map/ppermute | solution.py:53
  165.3 1.7 collective-permute-start.12
  167.0 2.2 %collective-permute-start.13 = (bf16[1,288,128]{2,1,0:T(8,128)(2,1)S(1)}, bf16[1,288,128]{2,1,0:T(8,128)(2,1)S(1)}, u32[]{:S(2)}, u32[]{:S(2)}) collective-permute-start(bf16[1,288,128]{2,1,0:T(8,128)(2,1)S(1)} %get-tuple-element.148), channel_id=1, source_target_pairs={{0,16},{1,17},{2,18},{3,19},{4,20},{5,21},{6,22},{7,23},{8,24},{9,... | collective-permute-start | bytes 221192 | tf_op jit(solution)/shard_map/ppermute | solution.py:53
  170.2 3.6 %collective-permute-done.13.refs_3_ = bf16[1,288,128]{2,1,0:T(8,128)(2,1)S(1)} collective-permute-done((bf16[1,288,128]{2,1,0:T(8,128)(2,1)S(1)}, bf16[1,288,128]{2,1,0:T(8,128)(2,1)S(1)}, u32[]{:S(2)}, u32[]{:S(2)}) %collective-permute-start.13) | collective-permute-done | bytes 73760 | tf_op jit(solution)/shard_map/ppermute | solution.py:53
  173.8 1.6 collective-permute-done.14.refs_4_
  176.0 1.5 collective-permute-start.17
  177.5 2.9 %collective-permute-start.15 = (bf16[1,304,128]{2,1,0:T(8,128)(2,1)S(1)}, bf16[1,304,128]{2,1,0:T(8,128)(2,1)S(1)}, u32[]{:S(2)}, u32[]{:S(2)}) collective-permute-start(bf16[1,304,128]{2,1,0:T(8,128)(2,1)S(1)} %shard_map.303), channel_id=1, source_target_pairs={{0,8},{1,9},{2,10},{3,11},{4,12},{5,13},{6,14},{7,15},{8,0},{9,1},... | collective-permute-start | bytes 233480 | tf_op jit(solution)/shard_map/ppermute | solution.py:53
  180.4 1.9 collective-permute-done.17
  182.3 1.6 collective-permute-done.16
  183.9 1.8 collective-permute-start.23
  187.5 6.9 %collective-permute-done.23.refs_4_ = bf16[4,304,128]{2,1,0:T(8,128)(2,1)S(1)} collective-permute-done((bf16[4,304,128]{2,1,0:T(8,128)(2,1)S(1)}, bf16[4,304,128]{2,1,0:T(8,128)(2,1)S(1)}, u32[]{:S(2)}, u32[]{:S(2)}) %collective-permute-start.23) | collective-permute-done | bytes 311328 | tf_op jit(solution)/shard_map/ppermute | solution.py:53
  194.4 2.5 %collective-permute-done.21.refs_3_ = bf16[4,304,128]{2,1,0:T(8,128)(2,1)S(1)} collective-permute-done((bf16[4,304,128]{2,1,0:T(8,128)(2,1)S(1)}, bf16[4,304,128]{2,1,0:T(8,128)(2,1)S(1)}, u32[]{:S(2)}, u32[]{:S(2)}) %collective-permute-start.21) | collective-permute-done | bytes 311328 | tf_op jit(solution)/shard_map/ppermute | solution.py:53
  197.6 2.1 %shard_map.304 = (f32[256,1024]{1,0:T(8,128)}, f32[128,512]{1,0:T(8,128)}, f32[3,3,2,128,256]{4,3,2,1,0:T(8,128)}, f32[1024,256]{1,0:T(8,128)}, f32[16,2,8,128]{3,2,1,0:T(8,128)}) custom-call(s32[21]{0:T(128)S(1)} %concatenate.6.refs_0_, bf16[4,304,128]{2,1,0:T(8,128)(2,1)S(1)} %pad_maximum_fusion.refs_1_, ...), custom_call_target="tpu_custom_call" | custom-call | bytes 6094932 | tf_op jit(solution)/shard_map/pallas_call | solution.py:205
  199.7 2.1 %shard_map.305 = (f32[256,1024]{1,0:T(8,128)}, f32[128,512]{1,0:T(8,128)}, f32[3,3,2,128,256]{4,3,2,1,0:T(8,128)}, f32[1024,256]{1,0:T(8,128)}, f32[16,2,8,128]{3,2,1,0:T(8,128)}) custom-call(s32[21]{0:T(128)S(1)} %concatenate.6.refs_0_, ...), custom_call_target="tpu_custom_call", output_to_operand_aliasing={{0}: (5, {}), {1}: (6, {}), {2}: (7, {}), {3}: (8, {}), {4}... | custom-call | bytes 10944596 | tf_op jit(solution)/shard_map/pallas_call | solution.py:205
  (77 shorter events, 10.4 us)
Async XLA Ops:
  0.6 25.7 %copy-start.21 = (f32[256]{0:T(256)S(1)}, f32[256]{0:T(256)}, u32[]{:S(2)}) copy-start(f32[256]{0:T(256)} %param.21) | copy-start | bytes 3076
  0.7 25.7 %copy-start.17 = (f32[256]{0:T(256)S(1)}, f32[256]{0:T(256)}, u32[]{:S(2)}) copy-start(f32[256]{0:T(256)} %param.20) | copy-start | bytes 3076
  1.4 1.6 copy-start
  4.1 22.3 %copy-start.10 = (bf16[3,3,2,128,256]{4,3,2,1,0:T(8,128)(2,1)S(1)}, bf16[3,3,2,128,256]{4,3,2,1,0:T(8,128)(2,1)}, u32[]{:S(2)}) copy-start(bf16[3,3,2,128,256]{4,3,2,1,0:T(8,128)(2,1)} %refs_11_.1) | copy-start | bytes 3538948
  5.4 118.4 %copy-start.4 = (f32[1024,256]{1,0:T(8,128)}, f32[1024,256]{1,0:T(8,128)S(1)}, u32[]{:S(2)}) copy-start(f32[1024,256]{1,0:T(8,128)S(1)} %get-tuple-element.94.refs_2_.refs_12_.refs_5_) | copy-start | bytes 3145732
  5.4 20.9 %collective-permute-start = (f32[512,256]{1,0:T(8,128)S(1)}, f32[512,256]{1,0:T(8,128)S(1)}, u32[]{:S(2)}, u32[]{:S(2)}) collective-permute-start(f32[512,256]{1,0:T(8,128)S(1)} %get-tuple-element.95), channel_id=1, source_target_pairs={{0,1},{1,2},{2,3},{4,5},{5,6},{6,7},{8,9},{9,10},{10,11},{12,13},{... | collective-permute-start | bytes 1572872 | tf_op jit(solution)/shard_map/ppermute | solution.py:27
  7.8 18.5 %collective-permute-start.1 = (f32[512,256]{1,0:T(8,128)S(1)}, f32[512,256]{1,0:T(8,128)S(1)}, u32[]{:S(2)}, u32[]{:S(2)}) collective-permute-start(f32[512,256]{1,0:T(8,128)S(1)} %get-tuple-element.96), channel_id=1, source_target_pairs={{1,0},{2,1},{3,2},{5,4},{6,5},{7,6},{9,8},{10,9},{11,10},{13,12},{... | collective-permute-start | bytes 1572872 | tf_op jit(solution)/shard_map/ppermute | solution.py:28
  26.4 14.6 %copy-start.13 = (f32[256,128]{1,0:T(8,128)S(1)}, f32[256,128]{1,0:T(8,128)}, u32[]{:S(2)}) copy-start(f32[256,128]{1,0:T(8,128)} %refs_7_.5) | copy-start | bytes 393220
  26.4 14.6 %copy-start.14 = (f32[512]{0:T(512)S(1)}, f32[512]{0:T(512)}, u32[]{:S(2)}) copy-start(f32[512]{0:T(512)} %param.23) | copy-start | bytes 6148
  26.4 14.6 %copy-start.15 = (f32[512]{0:T(512)S(1)}, f32[512]{0:T(512)}, u32[]{:S(2)}) copy-start(f32[512]{0:T(512)} %param.24) | copy-start | bytes 6148
  30.9 24.3 %copy-start.9 = (bf16[256,1024]{1,0:T(8,128)(2,1)S(1)}, bf16[256,1024]{1,0:T(8,128)(2,1)}, u32[]{:S(2)}) copy-start(bf16[256,1024]{1,0:T(8,128)(2,1)} %refs_6_.3) | copy-start | bytes 1572868
  30.9 24.3 %copy-start.12 = (f32[128,512]{1,0:T(8,128)S(1)}, f32[128,512]{1,0:T(8,128)}, u32[]{:S(2)}) copy-start(f32[128,512]{1,0:T(8,128)} %refs_9_.1) | copy-start | bytes 786436
  30.9 24.3 %copy-start.19 = (f32[512]{0:T(512)S(1)}, f32[512]{0:T(512)}, u32[]{:S(2)}) copy-start(f32[512]{0:T(512)} %param.29) | copy-start | bytes 6148
  30.9 24.3 %copy-start.20 = (f32[128]{0:T(128)S(1)}, f32[128]{0:T(128)}, u32[]{:S(2)}) copy-start(f32[128]{0:T(128)} %param.26) | copy-start | bytes 1540
  30.9 24.3 %copy-start.22 = (f32[128]{0:T(128)S(1)}, f32[128]{0:T(128)}, u32[]{:S(2)}) copy-start(f32[128]{0:T(128)} %param.27) | copy-start | bytes 1540
  41.0 28.9 %copy-start.6 = (bf16[16,4,16,1024]{3,2,1,0:T(8,128)(2,1)S(1)}, bf16[16,4,16,1024]{3,2,1,0:T(8,128)(2,1)}, u32[]{:S(2)}) copy-start(bf16[16,4,16,1024]{3,2,1,0:T(8,128)(2,1)} %param.33) | copy-start | bytes 6291460
  42.7 27.2 %copy-start.1 = (bf16[16,4,16,1024]{3,2,1,0:T(8,128)(2,1)S(1)}, bf16[16,4,16,1024]{3,2,1,0:T(8,128)(2,1)}, u32[]{:S(2)}) copy-start(bf16[16,4,16,1024]{3,2,1,0:T(8,128)(2,1)} %param.17) | copy-start | bytes 6291460
  42.7 27.2 %copy-start.16 = (f32[1024]{0:T(1024)S(1)}, f32[1024]{0:T(1024)}, u32[]{:S(2)}) copy-start(f32[1024]{0:T(1024)} %param.31) | copy-start | bytes 12292
  42.7 27.2 %copy-start.18 = (f32[1024]{0:T(1024)S(1)}, f32[1024]{0:T(1024)}, u32[]{:S(2)}) copy-start(f32[1024]{0:T(1024)} %param.32) | copy-start | bytes 12292
  75.1 16.4 %copy-start.2 = (f32[1024,1024]{1,0:T(8,128)}, f32[1024,1024]{1,0:T(8,128)S(1)}, u32[]{:S(2)}) copy-start(f32[1024,1024]{1,0:T(8,128)S(1)} %get-tuple-element.107.refs_4_.refs_3_) | copy-start | bytes 12582916
  91.5 5.8 %collective-permute-start.3 = (bf16[256,256]{1,0:T(8,128)(2,1)S(1)}, bf16[256,256]{1,0:T(8,128)(2,1)S(1)}, u32[]{:S(2)}, u32[]{:S(2)}) collective-permute-start(bf16[256,256]{1,0:T(8,128)(2,1)S(1)} %get-tuple-element.111), channel_id=1, source_target_pairs={{0,1},{1,2},{2,3},{4,5},{5,6},{6,7},{8,9},{9,10},{10,11},{12,13},{... | collective-permute-start | bytes 393224 | tf_op jit(solution)/shard_map/ppermute | solution.py:27
  93.3 4.0 %collective-permute-start.4 = (bf16[256,256]{1,0:T(8,128)(2,1)S(1)}, bf16[256,256]{1,0:T(8,128)(2,1)S(1)}, u32[]{:S(2)}, u32[]{:S(2)}) collective-permute-start(bf16[256,256]{1,0:T(8,128)(2,1)S(1)} %get-tuple-element.112), channel_id=1, source_target_pairs={{1,0},{2,1},{3,2},{5,4},{6,5},{7,6},{9,8},{10,9},{11,10},{13,12},{... | collective-permute-start | bytes 393224 | tf_op jit(solution)/shard_map/ppermute | solution.py:28
  94.6 2.7 %collective-permute-start.2 = (f32[8,128]{1,0:T(8,128)S(1)}, f32[8,128]{1,0:T(8,128)S(1)}, u32[]{:S(2)}, u32[]{:S(2)}) collective-permute-start(f32[8,128]{1,0:T(8,128)S(1)} %get-tuple-element.110), channel_id=1, source_target_pairs={{0,1},{1,0},{2,3},{3,2},{4,5},{5,4},{6,7},{7,6},{8,9},{9,8},{10,11... | collective-permute-start | bytes 12296 | tf_op jit(solution)/shard_map/ppermute | solution.py:38
  111.0 12.9 %copy-start.5 = (bf16[3,16,128,256]{3,2,1,0:T(8,128)(2,1)S(1)}, bf16[3,16,128,256]{3,2,1,0:T(8,128)(2,1)}, u32[]{:S(2)}) copy-start(bf16[3,16,128,256]{3,2,1,0:T(8,128)(2,1)} %get-tuple-element.128.refs_18_) | copy-start | bytes 9437188
  132.2 4.8 %collective-permute-start.5 = (bf16[2,1152,128]{2,1,0:T(8,128)(2,1)}, bf16[2,1152,128]{2,1,0:T(8,128)(2,1)S(1)}, u32[]{:S(2)}, u32[]{:S(2)}) collective-permute-start(bf16[2,1152,128]{2,1,0:T(8,128)(2,1)} %get-tuple-element.132), channel_id=1, source_target_pairs={{0,1},{1,0},{2,3},{3,2},{4,5},{5,4},{6,7},{7,6},{8,9},{9,8},{10,11... | collective-permute-start | bytes 1769480 | tf_op jit(solution)/shard_map/ppermute | solution.py:38
  132.5 13.3 %all-to-all-start.7 = ((f32[32,16,128]{2,1,0:T(8,128)}), f32[32,16,128]{2,1,0:T(8,128)S(1)}, u32[]{:S(2)}, u32[]{:S(2)}) async-start(f32[32,16,128]{2,1,0:T(8,128)} %get-tuple-element.129), calls=%async_computation.7 | async-start | bytes 524288 | tf_op jit(solution)/shard_map/all_to_all | solution.py:33
  135.3 1.7 collective-permute-start.6
  137.0 1.3 copy-start.11
  139.4 13.4 %collective-permute-start.7 = (bf16[1792,128]{1,0:T(8,128)(2,1)S(1)}, bf16[1792,128]{1,0:T(8,128)(2,1)S(1)}, u32[]{:S(2)}, u32[]{:S(2)}) collective-permute-start(bf16[1792,128]{1,0:T(8,128)(2,1)S(1)} %get-tuple-element.138), channel_id=1, source_target_pairs={{0,2},{1,3},{2,0},{3,1},{4,6},{5,7},{6,4},{7,5},{8,10},{9,11},{10,... | collective-permute-start | bytes 1376264 | tf_op jit(solution)/shard_map/ppermute | solution.py:38
  145.8 11.4 %copy-start.3 = (f32[1024,1024]{1,0:T(8,128)S(1)}, f32[1024,1024]{1,0:T(8,128)}, u32[]{:S(2)}) copy-start(f32[1024,1024]{1,0:T(8,128)} %copy-done.2) | copy-start | bytes 12582916
  149.7 7.5 %copy-start.8 = (bf16[1024,256]{1,0:T(8,128)(2,1)S(1)}, bf16[1024,256]{1,0:T(8,128)(2,1)}, u32[]{:S(2)}) copy-start(bf16[1024,256]{1,0:T(8,128)(2,1)} %refs_2_.3) | copy-start | bytes 1572868
  149.7 1.6 collective-permute-start.8
  153.6 6.9 %collective-permute-start.9 = (bf16[4,176,128]{2,1,0:T(8,128)(2,1)S(1)}, bf16[4,176,128]{2,1,0:T(8,128)(2,1)S(1)}, u32[]{:S(2)}, u32[]{:S(2)}) collective-permute-start(bf16[4,176,128]{2,1,0:T(8,128)(2,1)S(1)} %get-tuple-element.142), channel_id=1, source_target_pairs={{0,2},{1,3},{2,0},{3,1},{4,6},{5,7},{6,4},{7,5},{8,10},{9,11},{10,... | collective-permute-start | bytes 540680 | tf_op jit(solution)/shard_map/ppermute | solution.py:53
  155.0 7.5 %collective-permute-start.10 = (bf16[4,176,128]{2,1,0:T(8,128)(2,1)S(1)}, bf16[4,176,128]{2,1,0:T(8,128)(2,1)S(1)}, u32[]{:S(2)}, u32[]{:S(2)}) collective-permute-start(bf16[4,176,128]{2,1,0:T(8,128)(2,1)S(1)} %get-tuple-element.143), channel_id=1, source_target_pairs={{0,4},{1,5},{2,6},{3,7},{4,0},{5,1},{6,2},{7,3},{8,12},{9,13},{10,... | collective-permute-start | bytes 540680 | tf_op jit(solution)/shard_map/ppermute | solution.py:53
  156.4 8.3 %collective-permute-start.11 = (bf16[4,176,128]{2,1,0:T(8,128)(2,1)S(1)}, bf16[4,176,128]{2,1,0:T(8,128)(2,1)S(1)}, u32[]{:S(2)}, u32[]{:S(2)}) collective-permute-start(bf16[4,176,128]{2,1,0:T(8,128)(2,1)S(1)} %get-tuple-element.144), channel_id=1, source_target_pairs={{0,6},{1,7},{2,4},{3,5},{4,2},{5,3},{6,0},{7,1},{8,14},{9,15},{10,... | collective-permute-start | bytes 540680 | tf_op jit(solution)/shard_map/ppermute | solution.py:53
  165.3 4.9 %collective-permute-start.12 = (bf16[1,288,128]{2,1,0:T(8,128)(2,1)S(1)}, bf16[1,288,128]{2,1,0:T(8,128)(2,1)S(1)}, u32[]{:S(2)}, u32[]{:S(2)}) collective-permute-start(bf16[1,288,128]{2,1,0:T(8,128)(2,1)S(1)} %get-tuple-element.147), channel_id=1, source_target_pairs={{0,8},{1,9},{2,10},{3,11},{4,12},{5,13},{6,14},{7,15},{8,0},{9,1},... | collective-permute-start | bytes 221192 | tf_op jit(solution)/shard_map/ppermute | solution.py:53
  167.0 6.8 %collective-permute-start.13 = (bf16[1,288,128]{2,1,0:T(8,128)(2,1)S(1)}, bf16[1,288,128]{2,1,0:T(8,128)(2,1)S(1)}, u32[]{:S(2)}, u32[]{:S(2)}) collective-permute-start(bf16[1,288,128]{2,1,0:T(8,128)(2,1)S(1)} %get-tuple-element.148), channel_id=1, source_target_pairs={{0,16},{1,17},{2,18},{3,19},{4,20},{5,21},{6,22},{7,23},{8,24},{9,... | collective-permute-start | bytes 221192 | tf_op jit(solution)/shard_map/ppermute | solution.py:53
  169.2 6.2 %collective-permute-start.14 = (bf16[1,288,128]{2,1,0:T(8,128)(2,1)S(1)}, bf16[1,288,128]{2,1,0:T(8,128)(2,1)S(1)}, u32[]{:S(2)}, u32[]{:S(2)}) collective-permute-start(bf16[1,288,128]{2,1,0:T(8,128)(2,1)S(1)} %get-tuple-element.149), channel_id=1, source_target_pairs={{0,24},{1,25},{2,26},{3,27},{4,28},{5,29},{6,30},{7,31},{8,16},{9,... | collective-permute-start | bytes 221192 | tf_op jit(solution)/shard_map/ppermute | solution.py:53
  176.0 6.3 %collective-permute-start.17 = (bf16[1,304,128]{2,1,0:T(8,128)(2,1)S(1)}, bf16[1,304,128]{2,1,0:T(8,128)(2,1)S(1)}, u32[]{:S(2)}, u32[]{:S(2)}) collective-permute-start(bf16[1,304,128]{2,1,0:T(8,128)(2,1)S(1)} %shard_map.303), channel_id=1, source_target_pairs={{0,24},{1,25},{2,26},{3,27},{4,28},{5,29},{6,30},{7,31},{8,16},{9,... | collective-permute-start | bytes 233480 | tf_op jit(solution)/shard_map/ppermute | solution.py:53
  177.5 6.4 %collective-permute-start.16 = (bf16[1,304,128]{2,1,0:T(8,128)(2,1)S(1)}, bf16[1,304,128]{2,1,0:T(8,128)(2,1)S(1)}, u32[]{:S(2)}, u32[]{:S(2)}) collective-permute-start(bf16[1,304,128]{2,1,0:T(8,128)(2,1)S(1)} %shard_map.303), channel_id=1, source_target_pairs={{0,16},{1,17},{2,18},{3,19},{4,20},{5,21},{6,22},{7,23},{8,24},{9,... | collective-permute-start | bytes 233480 | tf_op jit(solution)/shard_map/ppermute | solution.py:53
  177.5 6.4 %collective-permute-start.15 = (bf16[1,304,128]{2,1,0:T(8,128)(2,1)S(1)}, bf16[1,304,128]{2,1,0:T(8,128)(2,1)S(1)}, u32[]{:S(2)}, u32[]{:S(2)}) collective-permute-start(bf16[1,304,128]{2,1,0:T(8,128)(2,1)S(1)} %shard_map.303), channel_id=1, source_target_pairs={{0,8},{1,9},{2,10},{3,11},{4,12},{5,13},{6,14},{7,15},{8,0},{9,1},... | collective-permute-start | bytes 233480 | tf_op jit(solution)/shard_map/ppermute | solution.py:53
  183.9 10.4 %collective-permute-start.23 = (bf16[4,304,128]{2,1,0:T(8,128)(2,1)S(1)}, bf16[4,304,128]{2,1,0:T(8,128)(2,1)S(1)}, u32[]{:S(2)}, u32[]{:S(2)}) collective-permute-start(bf16[4,304,128]{2,1,0:T(8,128)(2,1)S(1)} %pad_maximum_fusion.refs_1_), channel_id=1, source_target_pairs={{0,6},{1,7},{2,4},{3,5},{4,2},{5,3},{6,0},{7,1},{8,14},{9,15},{10,... | collective-permute-start | bytes 933896 | tf_op jit(solution)/shard_map/ppermute | solution.py:53
  185.7 11.2 %collective-permute-start.21 = (bf16[4,304,128]{2,1,0:T(8,128)(2,1)S(1)}, bf16[4,304,128]{2,1,0:T(8,128)(2,1)S(1)}, u32[]{:S(2)}, u32[]{:S(2)}) collective-permute-start(bf16[4,304,128]{2,1,0:T(8,128)(2,1)S(1)} %pad_maximum_fusion.refs_1_), channel_id=1, source_target_pairs={{0,4},{1,5},{2,6},{3,7},{4,0},{5,1},{6,2},{7,3},{8,12},{9,13},{10,... | collective-permute-start | bytes 933896 | tf_op jit(solution)/shard_map/ppermute | solution.py:53
  186.6 11.0 %collective-permute-start.19 = (bf16[4,304,128]{2,1,0:T(8,128)(2,1)S(1)}, bf16[4,304,128]{2,1,0:T(8,128)(2,1)S(1)}, u32[]{:S(2)}, u32[]{:S(2)}) collective-permute-start(bf16[4,304,128]{2,1,0:T(8,128)(2,1)S(1)} %pad_maximum_fusion.refs_1_), channel_id=1, source_target_pairs={{0,2},{1,3},{2,0},{3,1},{4,6},{5,7},{6,4},{7,5},{8,10},{9,11},{10,... | collective-permute-start | bytes 933896 | tf_op jit(solution)/shard_map/ppermute | solution.py:53
  187.5 12.2 %collective-permute-start.18 = (bf16[4,304,128]{2,1,0:T(8,128)(2,1)S(1)}, bf16[4,304,128]{2,1,0:T(8,128)(2,1)S(1)}, u32[]{:S(2)}, u32[]{:S(2)}) collective-permute-start(bf16[4,304,128]{2,1,0:T(8,128)(2,1)S(1)} %pad_maximum_fusion.refs_1_), channel_id=1, source_target_pairs={{0,1},{1,0},{2,3},{3,2},{4,5},{5,4},{6,7},{7,6},{8,9},{9,8},{10,11... | collective-permute-start | bytes 933896 | tf_op jit(solution)/shard_map/ppermute | solution.py:38
  194.4 5.3 %collective-permute-start.24 = (bf16[4,304,128]{2,1,0:T(8,128)(2,1)S(1)}, bf16[4,304,128]{2,1,0:T(8,128)(2,1)S(1)}, u32[]{:S(2)}, u32[]{:S(2)}) collective-permute-start(bf16[4,304,128]{2,1,0:T(8,128)(2,1)S(1)} %collective-permute-done.23.refs_4_), channel_id=1, source_target_pairs={{0,1},{1,0},{2,3},{3,2},{4,5},{5,4},{6,7},{7,6},{8,9},{9,8},{10,11... | collective-permute-start | bytes 933896 | tf_op jit(solution)/shard_map/ppermute | solution.py:38
  196.9 2.8 %collective-permute-start.22 = (bf16[4,304,128]{2,1,0:T(8,128)(2,1)S(1)}, bf16[4,304,128]{2,1,0:T(8,128)(2,1)S(1)}, u32[]{:S(2)}, u32[]{:S(2)}) collective-permute-start(bf16[4,304,128]{2,1,0:T(8,128)(2,1)S(1)} %collective-permute-done.21.refs_3_), channel_id=1, source_target_pairs={{0,1},{1,0},{2,3},{3,2},{4,5},{5,4},{6,7},{7,6},{8,9},{9,8},{10,11... | collective-permute-start | bytes 933896 | tf_op jit(solution)/shard_map/ppermute | solution.py:38
  197.6 2.2 %collective-permute-start.20 = (bf16[4,304,128]{2,1,0:T(8,128)(2,1)S(1)}, bf16[4,304,128]{2,1,0:T(8,128)(2,1)S(1)}, u32[]{:S(2)}, u32[]{:S(2)}) collective-permute-start(bf16[4,304,128]{2,1,0:T(8,128)(2,1)S(1)} %collective-permute-done.19.refs_2_), channel_id=1, source_target_pairs={{0,1},{1,0},{2,3},{3,2},{4,5},{5,4},{6,7},{7,6},{8,9},{9,8},{10,11... | collective-permute-start | bytes 933896 | tf_op jit(solution)/shard_map/ppermute | solution.py:38
  (1 other events, 1.0 us)

commit v10 on v9

--- a/solution.py
+++ b/solution.py
@@ -307,7 +307,7 @@
                 acc[1, :, outs] += fold(part * part)
         return carry
 
-    lax.fori_loop(0, blocks // group, step, 0, unroll=2)
+    lax.fori_loop(0, blocks // group, step, 0, unroll=True)
     put_row(pay, 0, total(acc[0]))
     put_row(pay, 4, total(acc[1]))
     spread(pay)
@@ -491,7 +491,7 @@
                 glog[pl.ds(image, 1), lanes] = total(fold(part * hid[own, lanes].astype(F32)))
         return carry
 
-    lax.fori_loop(0, blocks // group, step, 0, unroll=2)
+    lax.fori_loop(0, blocks // group, step, 0, unroll=True)
     first, second = att[:, :256], att[:, 256:]
     inner = first * glog[:, :256] + second * glog[:, 256:]
     glog[...] = jnp.concatenate(
@@ -741,7 +741,7 @@
         store_group(g).start()
         return carry
 
-    lax.fori_loop(0, blocks // group, step, 0, unroll=2)
+    lax.fori_loop(0, blocks // group, step, 0, unroll=True)
     put_sums(pay, 2, acc, center, inv)
     put_row(pay, 4, total(glog[...]))
     pay[0, 8:, :] = jnp.zeros((pay.shape[1] - 8, LANES), F32)
@@ -757,13 +757,13 @@
 
 
 def reduce_back_kernel(
-    meta, got, stat, gain, dz_in, pre_in, x_in, small, keep, send, gain_out, shift_out, bias_out, squeeze,
-    dz, pre, x, sems, *, blocks, rows
+    meta, got, stat, gain, dz_in, pre_in, x, small, keep, send, gain_out, shift_out, bias_out, squeeze,
+    dz, pre, sems, *, blocks, rows
 ):
     slab = rows * COLS
     fetches = [
         pltpu.make_async_copy(source, target, sems.at[k])
-        for k, (source, target) in enumerate(((dz_in, dz), (pre_in, pre), (x_in, x)))
+        for k, (source, target) in enumerate(((dz_in, dz), (pre_in, pre)))
     ]
     for fetch in fetches:
         fetch.start()
@@ -785,8 +785,7 @@
         small[own, :] = (mask * (a * dz[own, :] + b + d * pre[own, :])).astype(BF16)
         return carry
 
-    lax.fori_loop(0, blocks, step, 0)
-    fetches[2].wait()
+    lax.fori_loop(0, blocks, step, 0, unroll=4)
     for ref, core in ((send, 1 - meta[2]), (keep, meta[2])):
         lanes = pl.ds(pl.multiple_of(core * 512, 512), 512)
         value = dot(x[:, lanes], small[...], ((0,), (0,))).astype(ref.dtype)
@@ -1122,10 +1121,9 @@
         [
             ((pixels, mid), F32),
             ((pixels, mid), F32),
-            ((pixels, channels), BF16),
-            pltpu.SemaphoreType.DMA((3,)),
-        ],
-        raw_in=(4, 5, 6),
+            pltpu.SemaphoreType.DMA((2,)),
+        ],
+        raw_in=(4, 5),
         flops=small,
         after=(token,),
         local="in out",

time: 203 us -> 206 us (1.015)
  local copies, waits for them, and re-layouts: 4.75 us -> 7.75 us
    all_to_all x1, waiting for transfers between devices: 4.86 us -> 1.64 us  [exchange(): return lax.all_to_all(block, ALL, 0, 0)]
    ppermute x9, waiting for transfers between devices: 4.65 us -> 7.71 us  [swap(): return lax.ppermute(block, 'narrow', [(i, i ^ bit) for i in range(count)])]
    unnamed x46 -> x54, local copies, waits for them, and re-layouts: 4.02 us -> 7.01 us
where the time goes in v10:
time: 206 us; the launch traced here: 205 us
  blocking collectives  88.3 us (43%)
  Pallas kernels  46.4 us (23%)
  waiting for transfers between devices  32.8 us (16%)
  starting transfers between devices  28.8 us (14%)
  local copies, waits for them, and re-layouts  7.75 us (4%)
    all_to_all x7, blocking collectives, exchange(): return lax.all_to_all(block, ALL, 0, 0)  88.3 us
    pallas_call x18, Pallas kernels, call(): pl.pallas_call(run, grid=() if local == 'in out' else (1,), out_shape=[pl...  46.4 us
    ppermute x12, waiting for transfers between devices, partners(): lax.ppermute(block, ALL, [(i, i ^ step) for i in range(count)])  23.4 us
    ppermute x12, starting transfers between devices, partners(): lax.ppermute(block, ALL, [(i, i ^ step) for i in range(count)])  16 us
    ppermute x9, waiting for transfers between devices, swap(): return lax.ppermute(block, 'narrow', [(i, i ^ bit) for i in range(count)])  7.71 us
    unnamed x54, local copies, waits for them, and re-layouts  7.01 us
    ppermute x2, starting transfers between devices, halo(): low = lax.ppermute(bottom, 'narrow', [(i, i + 1) for i in range(count - 1)])  4.2 us
  transfers between devices with their start and end apart: 26, of which 14 were waited for; matrix products, arithmetic and copies ran while one was open for 0% of the time, Pallas kernels for 6%

profile of v10, /device:TPU:0, one launch (start us, length us, event | category | flops | bytes accessed | tf_op | source)
XLA Modules:
  0.0 205.3 jit_solution(5183688753807339797)
XLA Ops:
  1.4 1.6 copy-done
  4.1 1.3 shard_map.288
  5.4 2.4 %collective-permute-start = (f32[512,256]{1,0:T(8,128)S(1)}, f32[512,256]{1,0:T(8,128)S(1)}, u32[]{:S(2)}, u32[]{:S(2)}) collective-permute-start(f32[512,256]{1,0:T(8,128)S(1)} %get-tuple-element.95), channel_id=1, source_target_pairs={{0,1},{1,2},{2,3},{4,5},{5,6},{6,7},{8,9},{9,10},{10,11},{12,13},{... | collective-permute-start | bytes 1572872 | tf_op jit(solution)/shard_map/ppermute | solution.py:27
  7.8 1.3 collective-permute-start.1
  9.1 17.2 %all_to_all.40.refs_1_ = f32[32,8,128]{2,1,0:T(8,128)S(1)} all-to-all(f32[32,8,128]{2,1,0:T(8,128)S(1)} %get-tuple-element.93), channel_id=1, replica_groups=mesh['batch'=8,'narrow'=4] {'batch','narrow'}, dimensions={0} | all-to-all | bytes 262144 | tf_op jit(solution)/shard_map/all_to_all | solution.py:33
  26.4 4.6 %shard_map.289 = (bf16[3,16,128,256]{3,2,1,0:T(8,128)(2,1)}, f32[1536,512]{1,0:T(8,128)S(1)}, f32[32,8,128]{2,1,0:T(8,128)S(1)}, f32[8,256]{1,0:T(8,128)S(1)}) custom-call(s32[21]{0:T(128)S(1)} %concatenate.6.refs_0_, f32[32,8,128]{2,1,0:T(8,128)S(1)} %all_to_all.40.refs_1_, f32[1024,256]{1,0:T(8,128)S(1)} %get-tuple-element.94.refs_2_.refs_12_.refs_5_, ...), custom_call_target="tpu_custom_call" | custom-call | flops 1207959552 | bytes 9840724 | tf_op jit(solution)/shard_map/pallas_call | solution.py:205
  31.0 10.1 %all_to_all.41.refs_1_ = f32[32,8,128]{2,1,0:T(8,128)S(1)} all-to-all(f32[32,8,128]{2,1,0:T(8,128)S(1)} %get-tuple-element.97), channel_id=1, replica_groups=mesh['batch'=8,'narrow'=4] {'batch','narrow'}, dimensions={0} | all-to-all | bytes 262144 | tf_op jit(solution)/shard_map/all_to_all | solution.py:33
  41.1 1.6 shard_map.290
  42.8 12.4 %all_to_all.42.refs_1_ = f32[32,16,128]{2,1,0:T(8,128)S(1)} all-to-all(f32[32,16,128]{2,1,0:T(8,128)S(1)} %get-tuple-element.100), channel_id=1, replica_groups=mesh['batch'=8,'narrow'=4] {'batch','narrow'}, dimensions={0} | all-to-all | bytes 524288 | tf_op jit(solution)/shard_map/all_to_all | solution.py:33
  55.3 2.0 shard_map.291
  57.3 12.7 %all_to_all.43.refs_1_ = f32[32,16,128]{2,1,0:T(8,128)S(1)} all-to-all(f32[32,16,128]{2,1,0:T(8,128)S(1)} %get-tuple-element.102), channel_id=1, replica_groups=mesh['batch'=8,'narrow'=4] {'batch','narrow'}, dimensions={0} | all-to-all | bytes 524288 | tf_op jit(solution)/shard_map/all_to_all | solution.py:33
  70.0 5.2 %shard_map.292 = (bf16[1024,1024]{1,0:T(8,128)(2,1)}, f32[1024,1024]{1,0:T(8,128)S(1)}, f32[32,16,128]{2,1,0:T(8,128)S(1)}, f32[8,1024]{1,0:T(8,128)S(1)}) custom-call(s32[21]{0:T(128)S(1)} %concatenate.6.refs_0_, f32[32,16,128]{2,1,0:T(8,128)S(1)} %all_to_all.43.refs_1_, f32[8,256]{1,0:T(8,128)S(1)} %get-tuple-element.98.refs_2_.refs_13_, ...), custom_call_target="tpu_custom_call" | custom-call | bytes 13156436 | tf_op jit(solution)/shard_map/pallas_call | solution.py:205
  75.2 12.8 %all_to_all.44.refs_1_ = f32[32,16,128]{2,1,0:T(8,128)S(1)} all-to-all(f32[32,16,128]{2,1,0:T(8,128)S(1)} %get-tuple-element.105), channel_id=1, replica_groups=mesh['batch'=8,'narrow'=4] {'batch','narrow'}, dimensions={0} | all-to-all | bytes 524288 | tf_op jit(solution)/shard_map/all_to_all | solution.py:33
  88.0 3.6 %shard_map.293 = (bf16[1024,1024]{1,0:T(8,128)(2,1)S(1)}, bf16[1024,256]{1,0:T(8,128)(2,1)S(1)}, bf16[256,256]{1,0:T(8,128)(2,1)S(1)}, bf16[256,256]{1,0:T(8,128...) custom-call(s32[21]{0:T(128)S(1)} %concatenate.6.refs_0_, ...), custom_call_target="tpu_custom_call" | custom-call | flops 536870912 | bytes 11391060 | tf_op jit(solution)/shard_map/pallas_call | solution.py:205
  91.6 1.8 collective-permute-start.3
  93.5 1.3 collective-permute-start.4
  95.9 1.5 shard_map.294
  98.0 13.1 %all_to_all.45.refs_1_ = f32[32,8,128]{2,1,0:T(8,128)S(1)} all-to-all(f32[32,8,128]{2,1,0:T(8,128)S(1)} %shard_map.295), channel_id=1, replica_groups=mesh['batch'=8,'narrow'=4] {'batch','narrow'}, dimensions={0} | all-to-all | bytes 262144 | tf_op jit(solution)/shard_map/all_to_all | solution.py:33
  111.1 2.9 %shard_map.296 = (f32[1024,512]{1,0:T(8,128)S(1)}, f32[16,256]{1,0:T(8,128)S(1)}, f32[256,128]{1,0:T(8,128)S(1)}, f32[32,8,128]{2,1,0:T(8,128)S(1)}, f32[1,128]{1,0:T(1,128)}, /*index=5*/f32[1,128]{1,0:T(1,128)}) custom-call(s32[21]{0:T(128)S(1)} %concatenate.6.refs_0_, f32[32,8,128]{2,1,0:T(8,128)S(1)} %all_to_all.45.refs_1_, ...), custom_call_target="tpu_custom_call" | custom-call | bytes 6514260 | tf_op jit(solution)/shard_map/pallas_call | solution.py:205
  114.0 10.0 %all_to_all.46.refs_1_ = f32[32,8,128]{2,1,0:T(8,128)S(1)} all-to-all(f32[32,8,128]{2,1,0:T(8,128)S(1)} %get-tuple-element.124), channel_id=1, replica_groups=mesh['batch'=8,'narrow'=4] {'batch','narrow'}, dimensions={0} | all-to-all | bytes 262144 | tf_op jit(solution)/shard_map/all_to_all | solution.py:33
  124.0 8.1 %shard_map.297 = (f32[1024,256]{1,0:T(8,128)}, f32[2,1152,128]{2,1,0:T(8,128)}, bf16[2,1152,128]{2,1,0:T(8,128)(2,1)}, f32[32,16,128]{2,1,0:T(8,128)}, f32[1,512]{1,0:T(1,128)}, /*index=5*/f32[1,512]{1,0:T(1,128)}) custom-call(s32[21]{0:T(128)S(1)} %concatenate.6.refs_0_, f32[32,8,128]{2,1,0:T(8,128)S(1)} %all_to_all.46.refs_1_, ...), custom_call_target="tpu_custom_call" | custom-call | flops 2415919104 | bytes 14338132 | tf_op jit(solution)/shard_map/pallas_call | solution.py:205
  132.4 2.6 %all-to-all-start.7 = ((f32[32,16,128]{2,1,0:T(8,128)}), f32[32,16,128]{2,1,0:T(8,128)S(1)}, u32[]{:S(2)}, u32[]{:S(2)}) async-start(f32[32,16,128]{2,1,0:T(8,128)} %get-tuple-element.129), calls=%async_computation.7 | async-start | bytes 524288 | tf_op jit(solution)/shard_map/all_to_all | solution.py:33
  135.2 1.5 collective-permute-done.6.refs_4_
  137.5 1.3 copy-done.11
  141.0 1.4 shard_map.298
  142.4 1.7 collective-permute-start.7
  144.1 1.6 all-to-all-done.7.refs_1_
  145.7 3.5 %shard_map.299 = (bf16[1024,256]{1,0:T(8,128)(2,1)S(1)}, f32[1024,128]{1,0:T(8,128)S(1)}, bf16[1024,128]{1,0:T(8,128)(2,1)S(1)}, f32[1,256]{1,0:T(1,128)}, f32[1...) custom-call(s32[21]{0:T(128)S(1)} %concatenate.6.refs_0_, f32[32,16,128]{2,1,0:T(8,128)S(1)} %all-to-all-done.7.refs_1_, ...), custom_call_target="tpu_custom_call" | custom-call | flops 536870912 | bytes 5788756 | tf_op jit(solution)/shard_map/pallas_call | solution.py:205
  149.2 1.5 collective-permute-done.8.refs_4_
  150.8 4.7 %collective-permute-done.7.refs_2_ = bf16[1792,128]{1,0:T(8,128)(2,1)} collective-permute-done((bf16[1792,128]{1,0:T(8,128)(2,1)}, bf16[1792,128]{1,0:T(8,128)(2,1)}, u32[]{:S(2)}, u32[]{:S(2)}) %collective-permute-start.7) | collective-permute-done | bytes 458784 | tf_op jit(solution)/shard_map/ppermute | solution.py:38
  155.4 1.3 shard_map.301
  156.7 1.6 collective-permute-start.9
  158.3 1.5 collective-permute-start.10
  160.3 3.3 %shard_map.300 = (bf16[1024,1024]{1,0:T(8,128)(2,1)}, f32[8,128]{1,0:T(8,128)}) custom-call(s32[21]{0:T(128)S(1)} %concatenate.6.refs_0_, bf16[1024,256]{1,0:T(8,128)(2,1)S(1)} %get-tuple-element.135.refs_1_, bf16[1024,256]{1,0:T(8,128)(2,1)S(1)} %copy-done.8, f32[1024,1024]{1,0:T(8,128)S(1)} %copy-done.3), custom_call_target="tpu_custom_call" | custom-call | flops 536870912 | bytes 7344212 | tf_op jit(solution)/shard_map/pallas_call | solution.py:205
  163.6 2.1 %collective-permute-done.10.refs_3_ = bf16[4,176,128]{2,1,0:T(8,128)(2,1)S(1)} collective-permute-done((bf16[4,176,128]{2,1,0:T(8,128)(2,1)S(1)}, bf16[4,176,128]{2,1,0:T(8,128)(2,1)S(1)}, u32[]{:S(2)}, u32[]{:S(2)}) %collective-permute-start.10) | collective-permute-done | bytes 180256 | tf_op jit(solution)/shard_map/ppermute | solution.py:53
  165.8 2.0 collective-permute-done.11.refs_4_
  168.4 1.5 collective-permute-start.12
  169.9 2.5 %collective-permute-start.13 = (bf16[1,288,128]{2,1,0:T(8,128)(2,1)S(1)}, bf16[1,288,128]{2,1,0:T(8,128)(2,1)S(1)}, u32[]{:S(2)}, u32[]{:S(2)}) collective-permute-start(bf16[1,288,128]{2,1,0:T(8,128)(2,1)S(1)} %get-tuple-element.148), channel_id=1, source_target_pairs={{0,16},{1,17},{2,18},{3,19},{4,20},{5,21},{6,22},{7,23},{8,24},{9,... | collective-permute-start | bytes 221192 | tf_op jit(solution)/shard_map/ppermute | solution.py:53
  173.0 3.8 %collective-permute-done.13.refs_3_ = bf16[1,288,128]{2,1,0:T(8,128)(2,1)S(1)} collective-permute-done((bf16[1,288,128]{2,1,0:T(8,128)(2,1)S(1)}, bf16[1,288,128]{2,1,0:T(8,128)(2,1)S(1)}, u32[]{:S(2)}, u32[]{:S(2)}) %collective-permute-start.13) | collective-permute-done | bytes 73760 | tf_op jit(solution)/shard_map/ppermute | solution.py:53
  176.7 1.9 collective-permute-done.14.refs_4_
  181.1 2.6 %collective-permute-start.15 = (bf16[1,304,128]{2,1,0:T(8,128)(2,1)S(1)}, bf16[1,304,128]{2,1,0:T(8,128)(2,1)S(1)}, u32[]{:S(2)}, u32[]{:S(2)}) collective-permute-start(bf16[1,304,128]{2,1,0:T(8,128)(2,1)S(1)} %shard_map.303), channel_id=1, source_target_pairs={{0,8},{1,9},{2,10},{3,11},{4,12},{5,13},{6,14},{7,15},{8,0},{9,1},... | collective-permute-start | bytes 233480 | tf_op jit(solution)/shard_map/ppermute | solution.py:53
  183.7 1.9 collective-permute-done.17
  185.6 1.6 collective-permute-done.16
  187.2 2.4 %collective-permute-start.23 = (bf16[4,304,128]{2,1,0:T(8,128)(2,1)S(1)}, bf16[4,304,128]{2,1,0:T(8,128)(2,1)S(1)}, u32[]{:S(2)}, u32[]{:S(2)}) collective-permute-start(bf16[4,304,128]{2,1,0:T(8,128)(2,1)S(1)} %pad_maximum_fusion.refs_1_), channel_id=1, source_target_pairs={{0,6},{1,7},{2,4},{3,5},{4,2},{5,3},{6,0},{7,1},{8,14},{9,15},{10,... | collective-permute-start | bytes 933896 | tf_op jit(solution)/shard_map/ppermute | solution.py:53
  190.8 6.9 %collective-permute-done.23.refs_4_ = bf16[4,304,128]{2,1,0:T(8,128)(2,1)S(1)} collective-permute-done((bf16[4,304,128]{2,1,0:T(8,128)(2,1)S(1)}, bf16[4,304,128]{2,1,0:T(8,128)(2,1)S(1)}, u32[]{:S(2)}, u32[]{:S(2)}) %collective-permute-start.23) | collective-permute-done | bytes 311328 | tf_op jit(solution)/shard_map/ppermute | solution.py:53
  197.6 2.3 %collective-permute-done.21.refs_3_ = bf16[4,304,128]{2,1,0:T(8,128)(2,1)S(1)} collective-permute-done((bf16[4,304,128]{2,1,0:T(8,128)(2,1)S(1)}, bf16[4,304,128]{2,1,0:T(8,128)(2,1)S(1)}, u32[]{:S(2)}, u32[]{:S(2)}) %collective-permute-start.21) | collective-permute-done | bytes 311328 | tf_op jit(solution)/shard_map/ppermute | solution.py:53
  200.8 2.1 %shard_map.304 = (f32[256,1024]{1,0:T(8,128)}, f32[128,512]{1,0:T(8,128)}, f32[3,3,2,128,256]{4,3,2,1,0:T(8,128)}, f32[1024,256]{1,0:T(8,128)}, f32[16,2,8,128]{3,2,1,0:T(8,128)}) custom-call(s32[21]{0:T(128)S(1)} %concatenate.6.refs_0_, bf16[4,304,128]{2,1,0:T(8,128)(2,1)S(1)} %pad_maximum_fusion.refs_1_, ...), custom_call_target="tpu_custom_call" | custom-call | bytes 6094932 | tf_op jit(solution)/shard_map/pallas_call | solution.py:205
  203.0 2.1 %shard_map.305 = (f32[256,1024]{1,0:T(8,128)}, f32[128,512]{1,0:T(8,128)}, f32[3,3,2,128,256]{4,3,2,1,0:T(8,128)}, f32[1024,256]{1,0:T(8,128)}, f32[16,2,8,128]{3,2,1,0:T(8,128)}) custom-call(s32[21]{0:T(128)S(1)} %concatenate.6.refs_0_, ...), custom_call_target="tpu_custom_call", output_to_operand_aliasing={{0}: (5, {}), {1}: (6, {}), {2}: (7, {}), {3}: (8, {}), {4}... | custom-call | bytes 10944596 | tf_op jit(solution)/shard_map/pallas_call | solution.py:205
  (85 shorter events, 13.4 us)
Async XLA Ops:
  0.6 25.7 %copy-start.25 = (f32[256]{0:T(256)S(1)}, f32[256]{0:T(256)}, u32[]{:S(2)}) copy-start(f32[256]{0:T(256)} %param.21) | copy-start | bytes 3076
  0.7 25.7 %copy-start.21 = (f32[256]{0:T(256)S(1)}, f32[256]{0:T(256)}, u32[]{:S(2)}) copy-start(f32[256]{0:T(256)} %param.20) | copy-start | bytes 3076
  1.4 1.6 copy-start
  4.1 22.3 %copy-start.10 = (bf16[3,3,2,128,256]{4,3,2,1,0:T(8,128)(2,1)S(1)}, bf16[3,3,2,128,256]{4,3,2,1,0:T(8,128)(2,1)}, u32[]{:S(2)}) copy-start(bf16[3,3,2,128,256]{4,3,2,1,0:T(8,128)(2,1)} %refs_11_.1) | copy-start | bytes 3538948
  5.4 118.6 %copy-start.4 = (f32[1024,256]{1,0:T(8,128)}, f32[1024,256]{1,0:T(8,128)S(1)}, u32[]{:S(2)}) copy-start(f32[1024,256]{1,0:T(8,128)S(1)} %get-tuple-element.94.refs_2_.refs_12_.refs_5_) | copy-start | bytes 3145732
  5.4 20.9 %collective-permute-start = (f32[512,256]{1,0:T(8,128)S(1)}, f32[512,256]{1,0:T(8,128)S(1)}, u32[]{:S(2)}, u32[]{:S(2)}) collective-permute-start(f32[512,256]{1,0:T(8,128)S(1)} %get-tuple-element.95), channel_id=1, source_target_pairs={{0,1},{1,2},{2,3},{4,5},{5,6},{6,7},{8,9},{9,10},{10,11},{12,13},{... | collective-permute-start | bytes 1572872 | tf_op jit(solution)/shard_map/ppermute | solution.py:27
  7.8 18.5 %collective-permute-start.1 = (f32[512,256]{1,0:T(8,128)S(1)}, f32[512,256]{1,0:T(8,128)S(1)}, u32[]{:S(2)}, u32[]{:S(2)}) collective-permute-start(f32[512,256]{1,0:T(8,128)S(1)} %get-tuple-element.96), channel_id=1, source_target_pairs={{1,0},{2,1},{3,2},{5,4},{6,5},{7,6},{9,8},{10,9},{11,10},{13,12},{... | collective-permute-start | bytes 1572872 | tf_op jit(solution)/shard_map/ppermute | solution.py:28
  26.4 14.7 %copy-start.17 = (f32[256,128]{1,0:T(8,128)S(1)}, f32[256,128]{1,0:T(8,128)}, u32[]{:S(2)}) copy-start(f32[256,128]{1,0:T(8,128)} %refs_7_.5) | copy-start | bytes 393220
  26.4 14.7 %copy-start.18 = (f32[512]{0:T(512)S(1)}, f32[512]{0:T(512)}, u32[]{:S(2)}) copy-start(f32[512]{0:T(512)} %param.23) | copy-start | bytes 6148
  26.4 14.7 %copy-start.19 = (f32[512]{0:T(512)S(1)}, f32[512]{0:T(512)}, u32[]{:S(2)}) copy-start(f32[512]{0:T(512)} %param.24) | copy-start | bytes 6148
  31.0 24.3 %copy-start.9 = (bf16[256,1024]{1,0:T(8,128)(2,1)S(1)}, bf16[256,1024]{1,0:T(8,128)(2,1)}, u32[]{:S(2)}) copy-start(bf16[256,1024]{1,0:T(8,128)(2,1)} %refs_6_.3) | copy-start | bytes 1572868
  31.0 24.3 %copy-start.12 = (f32[128,512]{1,0:T(8,128)S(1)}, f32[128,512]{1,0:T(8,128)}, u32[]{:S(2)}) copy-start(f32[128,512]{1,0:T(8,128)} %refs_9_.1) | copy-start | bytes 786436
  31.0 24.3 %copy-start.23 = (f32[512]{0:T(512)S(1)}, f32[512]{0:T(512)}, u32[]{:S(2)}) copy-start(f32[512]{0:T(512)} %param.29) | copy-start | bytes 6148
  31.0 24.3 %copy-start.24 = (f32[128]{0:T(128)S(1)}, f32[128]{0:T(128)}, u32[]{:S(2)}) copy-start(f32[128]{0:T(128)} %param.26) | copy-start | bytes 1540
  31.0 24.3 %copy-start.26 = (f32[128]{0:T(128)S(1)}, f32[128]{0:T(128)}, u32[]{:S(2)}) copy-start(f32[128]{0:T(128)} %param.27) | copy-start | bytes 1540
  41.1 28.9 %copy-start.6 = (bf16[16,4,16,1024]{3,2,1,0:T(8,128)(2,1)S(1)}, bf16[16,4,16,1024]{3,2,1,0:T(8,128)(2,1)}, u32[]{:S(2)}) copy-start(bf16[16,4,16,1024]{3,2,1,0:T(8,128)(2,1)} %param.33) | copy-start | bytes 6291460
  42.8 27.2 %copy-start.1 = (bf16[16,4,16,1024]{3,2,1,0:T(8,128)(2,1)S(1)}, bf16[16,4,16,1024]{3,2,1,0:T(8,128)(2,1)}, u32[]{:S(2)}) copy-start(bf16[16,4,16,1024]{3,2,1,0:T(8,128)(2,1)} %param.17) | copy-start | bytes 6291460
  42.8 27.2 %copy-start.20 = (f32[1024]{0:T(1024)S(1)}, f32[1024]{0:T(1024)}, u32[]{:S(2)}) copy-start(f32[1024]{0:T(1024)} %param.31) | copy-start | bytes 12292
  42.8 27.2 %copy-start.22 = (f32[1024]{0:T(1024)S(1)}, f32[1024]{0:T(1024)}, u32[]{:S(2)}) copy-start(f32[1024]{0:T(1024)} %param.32) | copy-start | bytes 12292
  75.2 16.4 %copy-start.2 = (f32[1024,1024]{1,0:T(8,128)}, f32[1024,1024]{1,0:T(8,128)S(1)}, u32[]{:S(2)}) copy-start(f32[1024,1024]{1,0:T(8,128)S(1)} %get-tuple-element.107.refs_4_.refs_3_) | copy-start | bytes 12582916
  91.6 5.8 %collective-permute-start.3 = (bf16[256,256]{1,0:T(8,128)(2,1)S(1)}, bf16[256,256]{1,0:T(8,128)(2,1)S(1)}, u32[]{:S(2)}, u32[]{:S(2)}) collective-permute-start(bf16[256,256]{1,0:T(8,128)(2,1)S(1)} %get-tuple-element.111), channel_id=1, source_target_pairs={{0,1},{1,2},{2,3},{4,5},{5,6},{6,7},{8,9},{9,10},{10,11},{12,13},{... | collective-permute-start | bytes 393224 | tf_op jit(solution)/shard_map/ppermute | solution.py:27
  93.5 4.0 %collective-permute-start.4 = (bf16[256,256]{1,0:T(8,128)(2,1)S(1)}, bf16[256,256]{1,0:T(8,128)(2,1)S(1)}, u32[]{:S(2)}, u32[]{:S(2)}) collective-permute-start(bf16[256,256]{1,0:T(8,128)(2,1)S(1)} %get-tuple-element.112), channel_id=1, source_target_pairs={{1,0},{2,1},{3,2},{5,4},{6,5},{7,6},{9,8},{10,9},{11,10},{13,12},{... | collective-permute-start | bytes 393224 | tf_op jit(solution)/shard_map/ppermute | solution.py:28
  94.8 2.7 %collective-permute-start.2 = (f32[8,128]{1,0:T(8,128)S(1)}, f32[8,128]{1,0:T(8,128)S(1)}, u32[]{:S(2)}, u32[]{:S(2)}) collective-permute-start(f32[8,128]{1,0:T(8,128)S(1)} %get-tuple-element.110), channel_id=1, source_target_pairs={{0,1},{1,0},{2,3},{3,2},{4,5},{5,4},{6,7},{7,6},{8,9},{9,8},{10,11... | collective-permute-start | bytes 12296 | tf_op jit(solution)/shard_map/ppermute | solution.py:38
  97.4 13.7 %copy-start.13 = (f32[2,640,128]{2,1,0:T(8,128)}, f32[2,640,128]{2,1,0:T(8,128)S(1)}, u32[]{:S(2)}) copy-start(f32[2,640,128]{2,1,0:T(8,128)S(1)} %get-tuple-element.133.refs_3_) | copy-start | bytes 1966084
  111.1 12.9 %copy-start.5 = (bf16[3,16,128,256]{3,2,1,0:T(8,128)(2,1)S(1)}, bf16[3,16,128,256]{3,2,1,0:T(8,128)(2,1)}, u32[]{:S(2)}) copy-start(bf16[3,16,128,256]{3,2,1,0:T(8,128)(2,1)} %get-tuple-element.128.refs_18_) | copy-start | bytes 9437188
  132.1 4.6 %collective-permute-start.5 = (bf16[2,1152,128]{2,1,0:T(8,128)(2,1)}, bf16[2,1152,128]{2,1,0:T(8,128)(2,1)S(1)}, u32[]{:S(2)}, u32[]{:S(2)}) collective-permute-start(bf16[2,1152,128]{2,1,0:T(8,128)(2,1)} %get-tuple-element.132), channel_id=1, source_target_pairs={{0,1},{1,0},{2,3},{3,2},{4,5},{5,4},{6,7},{7,6},{8,9},{9,8},{10,11... | collective-permute-start | bytes 1769480 | tf_op jit(solution)/shard_map/ppermute | solution.py:38
  132.4 13.3 %all-to-all-start.7 = ((f32[32,16,128]{2,1,0:T(8,128)}), f32[32,16,128]{2,1,0:T(8,128)S(1)}, u32[]{:S(2)}, u32[]{:S(2)}) async-start(f32[32,16,128]{2,1,0:T(8,128)} %get-tuple-element.129), calls=%async_computation.7 | async-start | bytes 524288 | tf_op jit(solution)/shard_map/all_to_all | solution.py:33
  135.0 1.7 collective-permute-start.6
  142.4 13.0 %collective-permute-start.7 = (bf16[1792,128]{1,0:T(8,128)(2,1)}, bf16[1792,128]{1,0:T(8,128)(2,1)}, u32[]{:S(2)}, u32[]{:S(2)}) collective-permute-start(bf16[1792,128]{1,0:T(8,128)(2,1)} %get-tuple-element.138), channel_id=1, source_target_pairs={{0,2},{1,3},{2,0},{3,1},{4,6},{5,7},{6,4},{7,5},{8,10},{9,11},{10,... | collective-permute-start | bytes 1376264 | tf_op jit(solution)/shard_map/ppermute | solution.py:38
  145.7 14.6 %copy-start.3 = (f32[1024,1024]{1,0:T(8,128)S(1)}, f32[1024,1024]{1,0:T(8,128)}, u32[]{:S(2)}) copy-start(f32[1024,1024]{1,0:T(8,128)} %copy-done.2) | copy-start | bytes 12582916
  149.2 11.2 %copy-start.8 = (bf16[1024,256]{1,0:T(8,128)(2,1)S(1)}, bf16[1024,256]{1,0:T(8,128)(2,1)}, u32[]{:S(2)}) copy-start(bf16[1024,256]{1,0:T(8,128)(2,1)} %refs_2_.3) | copy-start | bytes 1572868
  149.2 1.6 collective-permute-start.8
  156.7 6.9 %collective-permute-start.9 = (bf16[4,176,128]{2,1,0:T(8,128)(2,1)S(1)}, bf16[4,176,128]{2,1,0:T(8,128)(2,1)S(1)}, u32[]{:S(2)}, u32[]{:S(2)}) collective-permute-start(bf16[4,176,128]{2,1,0:T(8,128)(2,1)S(1)} %get-tuple-element.142), channel_id=1, source_target_pairs={{0,2},{1,3},{2,0},{3,1},{4,6},{5,7},{6,4},{7,5},{8,10},{9,11},{10,... | collective-permute-start | bytes 540680 | tf_op jit(solution)/shard_map/ppermute | solution.py:53
  158.3 7.4 %collective-permute-start.10 = (bf16[4,176,128]{2,1,0:T(8,128)(2,1)S(1)}, bf16[4,176,128]{2,1,0:T(8,128)(2,1)S(1)}, u32[]{:S(2)}, u32[]{:S(2)}) collective-permute-start(bf16[4,176,128]{2,1,0:T(8,128)(2,1)S(1)} %get-tuple-element.143), channel_id=1, source_target_pairs={{0,4},{1,5},{2,6},{3,7},{4,0},{5,1},{6,2},{7,3},{8,12},{9,13},{10,... | collective-permute-start | bytes 540680 | tf_op jit(solution)/shard_map/ppermute | solution.py:53
  159.8 8.0 %collective-permute-start.11 = (bf16[4,176,128]{2,1,0:T(8,128)(2,1)S(1)}, bf16[4,176,128]{2,1,0:T(8,128)(2,1)S(1)}, u32[]{:S(2)}, u32[]{:S(2)}) collective-permute-start(bf16[4,176,128]{2,1,0:T(8,128)(2,1)S(1)} %get-tuple-element.144), channel_id=1, source_target_pairs={{0,6},{1,7},{2,4},{3,5},{4,2},{5,3},{6,0},{7,1},{8,14},{9,15},{10,... | collective-permute-start | bytes 540680 | tf_op jit(solution)/shard_map/ppermute | solution.py:53
  168.4 4.5 %collective-permute-start.12 = (bf16[1,288,128]{2,1,0:T(8,128)(2,1)S(1)}, bf16[1,288,128]{2,1,0:T(8,128)(2,1)S(1)}, u32[]{:S(2)}, u32[]{:S(2)}) collective-permute-start(bf16[1,288,128]{2,1,0:T(8,128)(2,1)S(1)} %get-tuple-element.147), channel_id=1, source_target_pairs={{0,8},{1,9},{2,10},{3,11},{4,12},{5,13},{6,14},{7,15},{8,0},{9,1},... | collective-permute-start | bytes 221192 | tf_op jit(solution)/shard_map/ppermute | solution.py:53
  169.9 6.8 %collective-permute-start.13 = (bf16[1,288,128]{2,1,0:T(8,128)(2,1)S(1)}, bf16[1,288,128]{2,1,0:T(8,128)(2,1)S(1)}, u32[]{:S(2)}, u32[]{:S(2)}) collective-permute-start(bf16[1,288,128]{2,1,0:T(8,128)(2,1)S(1)} %get-tuple-element.148), channel_id=1, source_target_pairs={{0,16},{1,17},{2,18},{3,19},{4,20},{5,21},{6,22},{7,23},{8,24},{9,... | collective-permute-start | bytes 221192 | tf_op jit(solution)/shard_map/ppermute | solution.py:53
  172.4 6.3 %collective-permute-start.14 = (bf16[1,288,128]{2,1,0:T(8,128)(2,1)S(1)}, bf16[1,288,128]{2,1,0:T(8,128)(2,1)S(1)}, u32[]{:S(2)}, u32[]{:S(2)}) collective-permute-start(bf16[1,288,128]{2,1,0:T(8,128)(2,1)S(1)} %get-tuple-element.149), channel_id=1, source_target_pairs={{0,24},{1,25},{2,26},{3,27},{4,28},{5,29},{6,30},{7,31},{8,16},{9,... | collective-permute-start | bytes 221192 | tf_op jit(solution)/shard_map/ppermute | solution.py:53
  179.2 6.4 %collective-permute-start.17 = (bf16[1,304,128]{2,1,0:T(8,128)(2,1)S(1)}, bf16[1,304,128]{2,1,0:T(8,128)(2,1)S(1)}, u32[]{:S(2)}, u32[]{:S(2)}) collective-permute-start(bf16[1,304,128]{2,1,0:T(8,128)(2,1)S(1)} %shard_map.303), channel_id=1, source_target_pairs={{0,24},{1,25},{2,26},{3,27},{4,28},{5,29},{6,30},{7,31},{8,16},{9,... | collective-permute-start | bytes 233480 | tf_op jit(solution)/shard_map/ppermute | solution.py:53
  180.3 6.9 %collective-permute-start.16 = (bf16[1,304,128]{2,1,0:T(8,128)(2,1)S(1)}, bf16[1,304,128]{2,1,0:T(8,128)(2,1)S(1)}, u32[]{:S(2)}, u32[]{:S(2)}) collective-permute-start(bf16[1,304,128]{2,1,0:T(8,128)(2,1)S(1)} %shard_map.303), channel_id=1, source_target_pairs={{0,16},{1,17},{2,18},{3,19},{4,20},{5,21},{6,22},{7,23},{8,24},{9,... | collective-permute-start | bytes 233480 | tf_op jit(solution)/shard_map/ppermute | solution.py:53
  181.1 6.1 %collective-permute-start.15 = (bf16[1,304,128]{2,1,0:T(8,128)(2,1)S(1)}, bf16[1,304,128]{2,1,0:T(8,128)(2,1)S(1)}, u32[]{:S(2)}, u32[]{:S(2)}) collective-permute-start(bf16[1,304,128]{2,1,0:T(8,128)(2,1)S(1)} %shard_map.303), channel_id=1, source_target_pairs={{0,8},{1,9},{2,10},{3,11},{4,12},{5,13},{6,14},{7,15},{8,0},{9,1},... | collective-permute-start | bytes 233480 | tf_op jit(solution)/shard_map/ppermute | solution.py:53
  187.2 10.4 %collective-permute-start.23 = (bf16[4,304,128]{2,1,0:T(8,128)(2,1)S(1)}, bf16[4,304,128]{2,1,0:T(8,128)(2,1)S(1)}, u32[]{:S(2)}, u32[]{:S(2)}) collective-permute-start(bf16[4,304,128]{2,1,0:T(8,128)(2,1)S(1)} %pad_maximum_fusion.refs_1_), channel_id=1, source_target_pairs={{0,6},{1,7},{2,4},{3,5},{4,2},{5,3},{6,0},{7,1},{8,14},{9,15},{10,... | collective-permute-start | bytes 933896 | tf_op jit(solution)/shard_map/ppermute | solution.py:53
  189.6 10.4 %collective-permute-start.21 = (bf16[4,304,128]{2,1,0:T(8,128)(2,1)S(1)}, bf16[4,304,128]{2,1,0:T(8,128)(2,1)S(1)}, u32[]{:S(2)}, u32[]{:S(2)}) collective-permute-start(bf16[4,304,128]{2,1,0:T(8,128)(2,1)S(1)} %pad_maximum_fusion.refs_1_), channel_id=1, source_target_pairs={{0,4},{1,5},{2,6},{3,7},{4,0},{5,1},{6,2},{7,3},{8,12},{9,13},{10,... | collective-permute-start | bytes 933896 | tf_op jit(solution)/shard_map/ppermute | solution.py:53
  190.1 10.7 %collective-permute-start.19 = (bf16[4,304,128]{2,1,0:T(8,128)(2,1)S(1)}, bf16[4,304,128]{2,1,0:T(8,128)(2,1)S(1)}, u32[]{:S(2)}, u32[]{:S(2)}) collective-permute-start(bf16[4,304,128]{2,1,0:T(8,128)(2,1)S(1)} %pad_maximum_fusion.refs_1_), channel_id=1, source_target_pairs={{0,2},{1,3},{2,0},{3,1},{4,6},{5,7},{6,4},{7,5},{8,10},{9,11},{10,... | collective-permute-start | bytes 933896 | tf_op jit(solution)/shard_map/ppermute | solution.py:53
  190.8 12.2 %collective-permute-start.18 = (bf16[4,304,128]{2,1,0:T(8,128)(2,1)S(1)}, bf16[4,304,128]{2,1,0:T(8,128)(2,1)S(1)}, u32[]{:S(2)}, u32[]{:S(2)}) collective-permute-start(bf16[4,304,128]{2,1,0:T(8,128)(2,1)S(1)} %pad_maximum_fusion.refs_1_), channel_id=1, source_target_pairs={{0,1},{1,0},{2,3},{3,2},{4,5},{5,4},{6,7},{7,6},{8,9},{9,8},{10,11... | collective-permute-start | bytes 933896 | tf_op jit(solution)/shard_map/ppermute | solution.py:38
  197.6 5.3 %collective-permute-start.24 = (bf16[4,304,128]{2,1,0:T(8,128)(2,1)S(1)}, bf16[4,304,128]{2,1,0:T(8,128)(2,1)S(1)}, u32[]{:S(2)}, u32[]{:S(2)}) collective-permute-start(bf16[4,304,128]{2,1,0:T(8,128)(2,1)S(1)} %collective-permute-done.23.refs_4_), channel_id=1, source_target_pairs={{0,1},{1,0},{2,3},{3,2},{4,5},{5,4},{6,7},{7,6},{8,9},{9,8},{10,11... | collective-permute-start | bytes 933896 | tf_op jit(solution)/shard_map/ppermute | solution.py:38
  200.0 3.0 %collective-permute-start.22 = (bf16[4,304,128]{2,1,0:T(8,128)(2,1)S(1)}, bf16[4,304,128]{2,1,0:T(8,128)(2,1)S(1)}, u32[]{:S(2)}, u32[]{:S(2)}) collective-permute-start(bf16[4,304,128]{2,1,0:T(8,128)(2,1)S(1)} %collective-permute-done.21.refs_3_), channel_id=1, source_target_pairs={{0,1},{1,0},{2,3},{3,2},{4,5},{5,4},{6,7},{7,6},{8,9},{9,8},{10,11... | collective-permute-start | bytes 933896 | tf_op jit(solution)/shard_map/ppermute | solution.py:38
  200.8 2.2 %collective-permute-start.20 = (bf16[4,304,128]{2,1,0:T(8,128)(2,1)S(1)}, bf16[4,304,128]{2,1,0:T(8,128)(2,1)S(1)}, u32[]{:S(2)}, u32[]{:S(2)}) collective-permute-start(bf16[4,304,128]{2,1,0:T(8,128)(2,1)S(1)} %collective-permute-done.19.refs_2_), channel_id=1, source_target_pairs={{0,1},{1,0},{2,3},{3,2},{4,5},{5,4},{6,7},{7,6},{8,9},{9,8},{10,11... | collective-permute-start | bytes 933896 | tf_op jit(solution)/shard_map/ppermute | solution.py:38
  (5 other events, 5.3 us)
